TPU v7x, 32 devices: a whole 2x2x4 slice. The times are simulated.
32 devices in a mesh: group: 2 (over x), tp: 16 (over z, y, core).
Axes of the slice: x: 2, y: 2, z: 4, core: 2. Of those that a mesh axis runs over, the one named last changes fastest.
Arguments:
- hidden_states: bfloat16 [16, 2, 8192], P('group'), parts along dimension 0, may hold values from -6 to 6
- qkv_weight: bfloat16 [10240, 8192], P('tp'), may hold values from -0.0625 to 0.0625
- out_weight: bfloat16 [8192, 8192], P('tp'), may hold values from -0.0625 to 0.0625
- cache_pages: bfloat16 [2048, 128, 256], P(('group', 'tp')), parts along dimension 0, may hold values from -6 to 6
- context_lengths: int32 [16], P('group'), parts along dimension 0, may hold values from 1 to 2046, 8184 in all
- new_units: int32 [128], P('group'), parts along dimension 0, may hold values from 0 to 63, as said below
- old_pages: int32 [2048], P('group'), parts along dimension 0, may hold values from 0 to 1023, as said below
Outputs:
- mixed_out: bfloat16 [16, 2, 8192], P('group', None, 'tp'), parts along dimension 0
- cache_out: bfloat16 [2048, 128, 256], P(('group', 'tp')), parts along dimension 0
There are 2 independent parts, one for each index of `group`. A program takes and returns all parts, laid end to end along the dimension named above; an argument that names none is the same for every part. Nothing has to cross between parts.
Inputs may be any that keep to these rules, and one draw needn't show every extreme that they name: `new_units`: A permutation of all request head groups; slot q of the new layout is on device q // 4. `old_pages`: A permutation of all logical pages (page u * 16 + i is page i of unit u); position p is on device p // 64. The pages that one device holds go to exactly 16 devices of the new layout, exactly 4 to each.
All inputs are finite; a program needn't handle non-finite values.
Results may differ from a plain program's by a relative error of at most 0.013.
Values may be sent and summed in bfloat16 or wider, within the bound.
No kernel may reach another device: no remote copies, remote signals or barrier semaphores. Data moves between devices by JAX's collectives and lax.ppermute only.
A program may use at most 128 MiB of HBM per device.

v0:
```python
import math

import jax
import jax.numpy as jnp
from jax import lax
from jax.sharding import PartitionSpec as P

D = 8192
HEADS = 64
KVH = 8
HD = 128
U_DEV = 4
MAXCTX = 2048
PAGE = 128


rope_base = 10000.0


def rotate_positions(values, positions):
    half_dim = values.shape[-1] // 2
    frequency = rope_base ** (-(jnp.arange(half_dim, dtype=jnp.float32) * 2.0 / values.shape[-1]))
    angles = positions.astype(jnp.float32)[..., None] * frequency
    cosine = jnp.concatenate([jnp.cos(angles), jnp.cos(angles)], axis=-1)
    sine_table = jnp.concatenate([jnp.sin(angles), jnp.sin(angles)], axis=-1)
    turned = jnp.concatenate([-values[..., half_dim:], values[..., :half_dim]], axis=-1)
    return values * cosine + turned * sine_table


def prepare(unit_qkv, base_lengths):
    group_count = HEADS // KVH
    count_units = unit_qkv.shape[0]
    positions = base_lengths[:, None] + jnp.arange(2, dtype=jnp.int32)[None, :]
    widened = unit_qkv.astype(jnp.float32)
    queries = widened[..., : group_count * HD].reshape(count_units, 2, group_count, HD)
    queries = rotate_positions(queries, positions[:, :, None]).astype(jnp.bfloat16)
    new_keys = rotate_positions(
        widened[..., group_count * HD : (group_count + 1) * HD], positions
    ).astype(jnp.bfloat16)
    new_values = unit_qkv[..., (group_count + 1) * HD :]
    return (queries, new_keys, new_values)


def context_terms(context, queries, valid_count):
    score_scale = 1.0 / math.sqrt(HD)
    cached_keys = context[..., :HD]
    cached_values = context[..., HD:]
    scores = (
        jnp.einsum("psgd,ptd->psgt", queries, cached_keys, preferred_element_type=jnp.float32)
        * score_scale
    )
    visible = jnp.arange(context.shape[1], dtype=jnp.int32)[None, :] < valid_count[:, None]
    weights = jnp.where(visible[:, None, None, :], jnp.exp(scores), 0.0)
    totals = jnp.sum(weights, axis=-1)
    weighted = jnp.einsum(
        "psgt,ptd->psgd",
        weights.astype(jnp.bfloat16),
        cached_values,
        preferred_element_type=jnp.float32,
    )
    return (weighted, totals)


def own_terms(queries, new_keys, new_values):
    score_scale = 1.0 / math.sqrt(HD)
    scores = (
        jnp.einsum("usgd,ujd->usgj", queries, new_keys, preferred_element_type=jnp.float32)
        * score_scale
    )
    recent = jnp.arange(2, dtype=jnp.int32)[None, :] <= jnp.arange(2, dtype=jnp.int32)[:, None]
    weights = jnp.where(recent[None, :, None, :], jnp.exp(scores), 0.0)
    totals = jnp.sum(weights, axis=-1)
    weighted = jnp.einsum(
        "usgj,ujd->usgd",
        weights.astype(jnp.bfloat16),
        new_values,
        preferred_element_type=jnp.float32,
    )
    return (weighted, totals)


def body(hidden_states, qkv_weight, out_weight, cache_pages, context_lengths, new_units, old_pages):
    devices = lax.axis_size("tp")
    device = lax.axis_index("tp")
    requests = hidden_states.shape[0]
    rows_dev = qkv_weight.shape[0]
    pages_dev, page_rows, page_width = cache_pages.shape
    group_count = HEADS // KVH
    unit_rows = (group_count + 2) * HD
    per_unit = MAXCTX // PAGE
    unit_slots = U_DEV
    capacity = max(1, pages_dev // devices)
    total_units = new_units.shape[0]
    total_pages = old_pages.shape[0]
    flat_rows = hidden_states.reshape(requests * 2, D)
    partial_qkv = lax.dot_general(
        flat_rows, qkv_weight, (((1,), (1,)), ((), ())), preferred_element_type=jnp.float32
    )
    partial_qkv = partial_qkv.astype(jnp.bfloat16).reshape(requests, 2, rows_dev)
    slot_index = (
        jnp.zeros((total_units,), jnp.int32)
        .at[new_units]
        .set(jnp.arange(total_units, dtype=jnp.int32))
    )
    own_units = lax.dynamic_slice_in_dim(new_units, device * unit_slots, unit_slots)
    own_requests = own_units // KVH
    own_heads = own_units % KVH
    own_lengths = context_lengths[own_requests]
    local_ids = lax.dynamic_slice_in_dim(old_pages, device * pages_dev, pages_dev)
    local_units = local_ids // per_unit
    local_index = local_ids % per_unit
    target_dev = (slot_index[local_units] * per_unit + local_index) // pages_dev
    local_order = jnp.arange(pages_dev, dtype=jnp.int32)
    send_rank = jnp.sum(
        (
            (target_dev[:, None] == target_dev[None, :])
            & (local_order[None, :] < local_order[:, None])
        ).astype(jnp.int32),
        axis=1,
    )
    outgoing = (
        jnp.zeros((devices, capacity, page_rows, page_width), jnp.bfloat16)
        .at[target_dev, send_rank]
        .set(cache_pages)
    )
    arrived = lax.all_to_all(outgoing, "tp", split_axis=0, concat_axis=0, tiled=True)
    stored_position = (
        jnp.zeros((total_pages,), jnp.int32)
        .at[old_pages]
        .set(jnp.arange(total_pages, dtype=jnp.int32))
    )
    wanted = (
        own_units[:, None] * per_unit + jnp.arange(per_unit, dtype=jnp.int32)[None, :]
    ).reshape(pages_dev)
    source_pos = stored_position[wanted]
    source_dev = source_pos // pages_dev
    source_slot = source_pos % pages_dev
    arrival_rank = jnp.sum(
        (
            (source_dev[:, None] == source_dev[None, :])
            & (source_slot[None, :] < source_slot[:, None])
        ).astype(jnp.int32),
        axis=1,
    )
    relaid = arrived[source_dev, arrival_rank]
    contexts = relaid.reshape(unit_slots, MAXCTX, page_width)
    sources_per_head = unit_rows // rows_dev
    request_table = (new_units // KVH).reshape(devices, unit_slots)
    outgoing_rows = partial_qkv[request_table]
    incoming = lax.all_to_all(outgoing_rows, "tp", split_axis=0, concat_axis=0, tiled=True)
    grouped = jnp.moveaxis(incoming.reshape(KVH, sources_per_head, unit_slots, 2, rows_dev), 2, 0)
    chosen = jnp.take_along_axis(grouped, own_heads[:, None, None, None, None], axis=1)[:, 0]
    own_rows = chosen.transpose(0, 2, 1, 3).reshape(unit_slots, 2, unit_rows)
    queries, new_keys, new_values = prepare(own_rows, own_lengths)
    cache_sums, cache_totals = context_terms(contexts, queries, own_lengths)
    own_sums, own_totals = own_terms(queries, new_keys, new_values)
    attended = ((cache_sums + own_sums) / (cache_totals + own_totals)[..., None]).astype(
        jnp.bfloat16
    )
    attended = attended.reshape(unit_slots, 2, group_count * HD)
    all_heads = lax.all_gather(attended, "tp", axis=0, tiled=True)
    logical = (
        all_heads[slot_index]
        .reshape(requests, KVH, 2, group_count * HD)
        .transpose(0, 2, 1, 3)
        .reshape(requests * 2, HEADS * HD)
    )
    mixed_rows = lax.dot_general(
        logical, out_weight, (((1,), (1,)), ((), ())), preferred_element_type=jnp.float32
    )
    mixed_rows = mixed_rows.astype(jnp.bfloat16).reshape(requests, 2, out_weight.shape[0])
    fresh_rows = jnp.concatenate([new_keys, new_values], axis=-1)
    positions = jnp.arange(MAXCTX, dtype=jnp.int32)[None, :]
    contexts = jnp.where(
        (positions == own_lengths[:, None])[..., None], fresh_rows[:, 0:1], contexts
    )
    contexts = jnp.where(
        (positions == own_lengths[:, None] + 1)[..., None], fresh_rows[:, 1:2], contexts
    )
    return (mixed_rows, contexts.reshape(pages_dev, page_rows, page_width))


def solution(mesh):
    in_specs = (
        P("group", None, None),
        P("tp", None),
        P("tp", None),
        P(("group", "tp"), None, None),
        P("group"),
        P("group"),
        P("group"),
    )
    out_specs = (P("group", None, "tp"), P(("group", "tp"), None, None))
    return jax.shard_map(body, mesh=mesh, in_specs=in_specs, out_specs=out_specs, check_vma=False)
```

profile of v0, /device:TPU:0, one launch (start us, length us, event | category | flops | bytes accessed | tf_op | source)
XLA Modules:
  0.0 180.0 jit_solution(12315859373717689695)
XLA Ops:
  0.6 0.0 copy-start
  0.6 0.7 and_select_fusion.6
  1.3 1.0 reshape.412
  2.4 0.0 copy-start.1
  2.4 6.8 %convolution_convert_fusion = bf16[16,640]{1,0:T(8,128)(2,1)S(1)} fusion(bf16[16,8192]{1,0:T(8,128)(2,1)S(1)} %reshape.412, bf16[640,8192]{1,0:T(8,128)(2,1)} %param.8), kind=kOutput, calls=%fused_computation.19 | convolution fusion | flops 167782400 | bytes 10768384 | tf_op jit(solution)/shard_map/dot_general | solution.py:96
  9.2 0.1 reshape.414
  9.3 0.1 reshape.434
  9.4 1.6 gather_fusion.1
  11.0 7.4 %all-to-all-start = ((bf16[16,4,2,640]{3,2,1,0:T(2,128)(2,1)}), bf16[16,4,2,640]{3,2,1,0:T(2,128)(2,1)S(1)}, u32[]{:S(2)}, u32[]{:S(2)}) async-start(bf16[16,4,2,640]{3,2,1,0:T(2,128)(2,1)} %bitcast), calls=%async_computation | async-start | bytes 327680 | tf_op jit(solution)/shard_map/all_to_all | solution.py:150
  18.4 0.0 copy-done.1
  18.4 0.1 compare_select_fusion.8
  18.5 0.8 scatter_custom_fusion
  19.3 0.8 gather_fusion.2
  20.1 0.2 convert_reduce_fusion.1
  20.3 2.5 %broadcast_in_dim.130 = bf16[16,4,128,256]{3,2,1,0:T(8,128)(2,1)} broadcast(bf16[]{:T(256)} %constant.132.clone.1), dimensions={} | broadcast | bytes 4194306 | tf_op jit(solution)/shard_map/broadcast_in_dim | solution.py:122
  22.8 12.5 %scatter_fusion = bf16[16,4,128,256]{3,2,1,0:T(8,128)(2,1)} fusion(bf16[16,4,128,256]{3,2,1,0:T(8,128)(2,1)} %broadcast_in_dim.130, s32[64]{0:T(128)S(1)} %fusion.28, bf16[64,128,256]{2,1,0:T(8,128)(2,1)} %param.10), kind=kCustom, calls=%fused_computation.8 | custom fusion | bytes 12583424 | tf_op jit(solution)/shard_map/scatter | solution.py:124
  35.2 0.0 copy-start.2
  35.2 0.0 all-to-all-done
  35.3 6.2 %all-to-all-start.1 = ((bf16[16,4,128,256]{3,2,1,0:T(8,128)(2,1)}), bf16[16,4,128,256]{3,2,1,0:T(8,128)(2,1)}, u32[]{:S(2)}, u32[]{:S(2)}) async-start(bf16[16,4,128,256]{3,2,1,0:T(8,128)(2,1)} %scatter_fusion), calls=%async_computation.1 | async-start | bytes 8388608 | tf_op jit(solution)/shard_map/all_to_all | solution.py:126
  41.4 0.0 copy-done.2
  41.5 0.1 compare_select_fusion.10
  41.5 0.1 iota_add_fusion
  41.6 0.1 add.228
  41.7 0.0 copy-done
  41.7 0.6 gather_fusion
  42.4 0.1 eq.69
  42.4 0.1 eq.70
  42.5 0.1 lt.204
  42.6 0.1 lt.205
  42.7 4.3 %scatter_custom_fusion.2 = s32[1024]{0:T(1024)S(1)} fusion(s32[1024]{0:T(1024)S(1)} %compare_select_fusion.1, s32[1024]{0:T(1024)S(1)} %iota.73, s32[]{:T(128)} %constant.122.clone.1), kind=kCustom, calls=%fused_computation.75 | custom fusion | bytes 4100 | tf_op jit(solution)/shard_map/scatter | solution.py:130
  47.0 0.7 gather_fusion.3
  47.8 0.1 bitcast_compare_fusion.1
  48.0 0.1 add_convert_fusion
  48.0 0.1 multiply_cosine_fusion.1
  48.2 0.1 maximum_bitcast_fusion
  48.3 0.2 convert_reduce_fusion
  48.5 0.1 iota_compare_fusion.1
  48.6 0.1 copy.18
  48.7 0.6 gather_fusion.6
  49.3 0.1 broadcast_select_fusion
  49.5 0.1 multiply_sine_fusion
  49.6 0.1 fusion.12
  49.8 0.1 slice_negate_fusion
  49.9 0.1 fusion.9
  49.9 0.2 fusion.33
  50.2 69.0 %all-to-all-done.1 = bf16[16,4,128,256]{3,2,1,0:T(8,128)(2,1)} async-done(((bf16[16,4,128,256]{3,2,1,0:T(8,128)(2,1)}), bf16[16,4,128,256]{3,2,1,0:T(8,128)(2,1)}, u32[]{:S(2)}, u32[]{:S(2)}) %all-to-all-start.1) | async-done | bytes 4194336 | tf_op jit(solution)/shard_map/all_to_all | solution.py:126
  119.1 5.0 %gather_fusion.4 = bf16[64,128,256]{2,1,0:T(8,128)(2,1)} fusion(bf16[16,4,128,256]{3,2,1,0:T(8,128)(2,1)} %all-to-all-done.1, s32[64]{0:T(128)S(1)} %fusion.27), kind=kCustom, calls=%fused_computation.4 | custom fusion | bytes 8389120 | tf_op jit(solution)/shard_map/gather | solution.py:145
  124.1 2.3 %fusion.32 = (f32[4,2,8]{2,1,0:T(2,128)S(1)}, bf16[4,2,8,2048]{3,2,1,0:T(8,128)(2,1)S(1)}) fusion(bf16[4,2,8,128]{3,2,1,0:T(8,128)(2,1)S(1)} %fusion.9, bf16[4,2048,256]{2,1,0:T(8,128)(2,1)} %bitcast.104, pred[4,2048]{1,0:T(4,128)(4,1)S(1)} %iota_compare_fusion.1), kind=kOutput, calls=%fused_computation.131 | convolution fusion | flops 34078656 | bytes 2384128 | tf_op jit(solution)/shard_map/psgd,ptd->psgt/dot_general | solution.py:49
  126.5 2.0 %fusion.2 = f32[4,2,8,128]{3,2,1,0:T(8,128)S(1)} fusion(bf16[4,2048,256]{2,1,0:T(8,128)(2,1)} %bitcast.105, bf16[4,2,8,2048]{3,2,1,0:T(8,128)(2,1)S(1)} %get-tuple-element.24), kind=kOutput, calls=%fused_computation.15 | convolution fusion | flops 33554432 | bytes 2392064 | tf_op jit(solution)/shard_map/psgt,ptd->psgd/dot_general | solution.py:55
  128.5 0.2 fusion.4
  128.7 36.1 %all_gather.3 = bf16[64,2,1024]{2,1,0:T(2,128)(2,1)S(1)} all-gather(bf16[4,2,1024]{2,1,0:T(2,128)(2,1)S(1)} %reshape.420), channel_id=1, replica_groups=mesh['group'=2,'tp'=16] {'tp'}, dimensions={0}, use_global_device_ids=true | all-gather | bytes 278528 | tf_op jit(solution)/shard_map/all_gather | solution.py:161
  164.7 1.1 gather_fusion.5
  165.9 0.2 copy.27
  166.1 5.6 %convolution_convert_fusion.1 = bf16[16,512]{1,0:T(8,128)(2,1)S(1)} fusion(bf16[16,8192]{1,0:T(8,128)(2,1)S(1)} %bitcast.106, bf16[512,8192]{1,0:T(8,128)(2,1)} %param.9), kind=kOutput, calls=%fused_computation.21 | convolution fusion | flops 134225920 | bytes 8667136 | tf_op jit(solution)/shard_map/dot_general | solution.py:168
  171.7 0.6 reshape.423
  172.4 7.6 %select_select_fusion = bf16[64,128,256]{2,1,0:T(8,128)(2,1)} fusion(bf16[64,128,256]{2,1,0:T(8,128)(2,1)} %gather_fusion.4, pred[64,128]{1,0:T(8,128)(4,1)S(1)} %get-tuple-element.11, pred[64,128]{1,0:T(8,128)(4,1)S(1)} %get-tuple-element.10, bf16[64,256]{1,0:T(8,128)(2,1)S(1)} %bitcast.115, bf16[64,256]{1,0:T(8,128)(2,1)S(1)} %bitcast.116), kind=kLoop, calls=%fused_computation.10 | loop fusion | flops 4194304 | bytes 8470528 | tf_op jit(solution)/shard_map/jit(_where)/select_n | solution.py:177
  (38 shorter events, 0.4 us)
Async XLA Ops:
  0.6 41.1 %copy-start = (s32[8]{0:T(128)S(1)}, s32[8]{0:T(128)}, u32[]{:S(2)}) copy-start(s32[8]{0:T(128)} %param.11) | copy-start | bytes 100
  2.4 16.0 %copy-start.1 = (s32[1024]{0:T(1024)S(1)}, s32[1024]{0:T(1024)}, u32[]{:S(2)}) copy-start(s32[1024]{0:T(1024)} %param.13) | copy-start | bytes 12292
  11.0 24.3 %all-to-all-start = ((bf16[16,4,2,640]{3,2,1,0:T(2,128)(2,1)}), bf16[16,4,2,640]{3,2,1,0:T(2,128)(2,1)S(1)}, u32[]{:S(2)}, u32[]{:S(2)}) async-start(bf16[16,4,2,640]{3,2,1,0:T(2,128)(2,1)} %bitcast), calls=%async_computation | async-start | bytes 327680 | tf_op jit(solution)/shard_map/all_to_all | solution.py:150
  35.2 6.2 %copy-start.2 = (s32[64]{0:T(128)S(1)}, s32[64]{0:T(128)}, u32[]{:S(2)}) copy-start(s32[64]{0:T(128)} %param.12) | copy-start | bytes 772
  35.3 83.9 %all-to-all-start.1 = ((bf16[16,4,128,256]{3,2,1,0:T(8,128)(2,1)}), bf16[16,4,128,256]{3,2,1,0:T(8,128)(2,1)}, u32[]{:S(2)}, u32[]{:S(2)}) async-start(bf16[16,4,128,256]{3,2,1,0:T(8,128)(2,1)} %scatter_fusion), calls=%async_computation.1 | async-start | bytes 8388608 | tf_op jit(solution)/shard_map/all_to_all | solution.py:126
where the time goes:
time: 181 us; the launch traced here: 180 us
  waiting for transfers between devices  69 us (38%)
  blocking collectives  36.1 us (20%)
  local copies, waits for them, and re-layouts  33.2 us (18%)
  matrix products  17.2 us (10%)
  starting transfers between devices  13.6 us (8%)
  other arithmetic  10 us (6%)
    all_to_all x1, waiting for transfers between devices, body(): lax.all_to_all(outgoing, 'tp', split_axis=0, concat_axis=0, tiled=True)  69 us
    all_gather x1, blocking collectives, body(): all_heads = lax.all_gather(attended, 'tp', axis=0, tiled=True)  36.1 us
    scatter x1, local copies, waits for them, and re-layouts, body(): outgoing = jnp.zeros((devices, capacity, page_rows, page_width), jnp.bflo...  12.5 us
    select_n x1, other arithmetic, body(): jnp.where((positions == own_lengths[:, None] + 1)[..., None], fresh_rows[...  7.63 us
    all_to_all x1, starting transfers between devices, body(): lax.all_to_all(outgoing_rows, 'tp', split_axis=0, concat_axis=0, tiled=True)  7.39 us
    dot_general x1, matrix products, body(): lax.dot_general(flat_rows, qkv_weight, (((1,), (1,)), ((), ())), preferre...  6.81 us
    all_to_all x1, starting transfers between devices, body(): lax.all_to_all(outgoing, 'tp', split_axis=0, concat_axis=0, tiled=True)  6.18 us
    dot_general x1, matrix products, body(): lax.dot_general(logical, out_weight, (((1,), (1,)), ((), ())), preferred_...  5.64 us
  transfers between devices with their start and end apart: 2, of which 1 were waited for; matrix products, arithmetic and copies ran while one was open for 14% of the time, Pallas kernels for 0%

commit v1 on v0

v1 whole, which is shorter than its diff:
```python
import functools
import math

import jax
import jax.numpy as jnp
from jax import lax
from jax.experimental import pallas as pl
from jax.experimental.pallas import tpu as pltpu
from jax.sharding import PartitionSpec as P

D = 8192
HEADS = 64
KVH = 8
HD = 128
U_DEV = 4
MAXCTX = 2048
PAGE = 128
GROUP = HEADS // KVH
QROWS = 2 * GROUP
PER_UNIT = MAXCTX // PAGE
VMEM_LIMIT = 32 * 1024 * 1024
FIRST = 3
LATE = 0
GROUPS = (5, 4, 4, 2)

rope_base = 10000.0


def rope_tables(positions):
    half_dim = HD // 2
    frequency = rope_base ** (-(jnp.arange(half_dim, dtype=jnp.float32) * 2.0 / HD))
    angles = positions.astype(jnp.float32)[..., None] * frequency
    cosine = jnp.concatenate([jnp.cos(angles), jnp.cos(angles)], axis=-1)
    sine = jnp.concatenate([-jnp.sin(angles), jnp.sin(angles)], axis=-1)
    return cosine, sine


def rotate(values, cosine, sine):
    half_dim = HD // 2
    turned = jnp.concatenate([values[..., half_dim:], values[..., :half_dim]], axis=-1)
    return values * cosine + turned * sine


def any_spec():
    return pl.BlockSpec(memory_space=pl.ANY)


def smem_spec():
    return pl.BlockSpec(memory_space=pltpu.SMEM)


def vmem_spec():
    return pl.BlockSpec(memory_space=pltpu.VMEM)


def load_order(devices, capacity, relative, units_ref, old_ref, order_ref, slots, count):
    device = lax.axis_index("tp")
    total_units = units_ref.shape[0]
    pages_dev = old_ref.shape[0] // devices

    def clear(t, carry):
        count[t] = 0
        return carry

    def empty(t, carry):
        order_ref[t] = 0
        return carry

    def invert(q, carry):
        slots[units_ref[q]] = q
        return carry

    def assign(i, carry):
        unit = old_ref[device * pages_dev + i] // PER_UNIT
        target = slots[unit] // U_DEV
        if relative:
            target = target ^ device
        rank = count[target]
        count[target] = rank + 1
        order_ref[target * capacity + rank] = i
        return carry

    lax.fori_loop(0, devices, clear, 0, unroll=8)
    if devices * capacity > pages_dev:
        lax.fori_loop(0, devices * capacity, empty, 0, unroll=8)
    lax.fori_loop(0, total_units, invert, 0, unroll=8)
    lax.fori_loop(0, pages_dev, assign, 0, unroll=8)


def move_pages(capacity, keys, order_ref, pages_ref, outs, stage, load_sem, store_sem):
    loads, stores = [], []
    for n, key in enumerate(keys):
        for r in range(capacity):
            copy = pltpu.make_async_copy(
                pages_ref.at[order_ref[key * capacity + r]],
                stage.at[n * capacity + r],
                load_sem.at[n * capacity + r],
            )
            copy.start()
            loads.append(copy)
    for n, key in enumerate(keys):
        for r in range(capacity):
            loads[n * capacity + r].wait()
        target = outs[n] if len(outs) > 1 else outs[0].at[pl.ds(n * capacity, capacity)]
        copy = pltpu.make_async_copy(
            stage.at[pl.ds(n * capacity, capacity)], target, store_sem.at[n]
        )
        copy.start()
        stores.append(copy)
    for copy in stores:
        copy.wait()


def first_pack_kernel(devices, capacity, keys, relative, units_ref, old_ref, pages_ref, *rest):
    outs = rest[:-6]
    order_ref, slots, count, stage, load_sem, store_sem = rest[-6:]
    load_order(devices, capacity, relative, units_ref, old_ref, order_ref, slots, count)
    move_pages(capacity, keys, order_ref, pages_ref, outs, stage, load_sem, store_sem)


def next_pack_kernel(capacity, keys, order_ref, pages_ref, *rest):
    outs = rest[:-3]
    stage, load_sem, store_sem = rest[-3:]
    move_pages(capacity, keys, order_ref, pages_ref, outs, stage, load_sem, store_sem)


def pack_scratch(count, pages):
    return [
        pltpu.VMEM((count,) + pages.shape[1:], pages.dtype),
        pltpu.SemaphoreType.DMA((count,)),
        pltpu.SemaphoreType.DMA((count,)),
    ]


def first_pack(new_units, old_pages, pages, devices, capacity, keys, relative):
    chunk = (capacity,) + pages.shape[1:]
    if relative:
        outs = [jax.ShapeDtypeStruct(chunk, pages.dtype) for _ in keys]
    else:
        outs = [jax.ShapeDtypeStruct((len(keys) * capacity,) + chunk[1:], pages.dtype)]
    result = pl.pallas_call(
        functools.partial(first_pack_kernel, devices, capacity, keys, relative),
        out_shape=tuple(outs) + (jax.ShapeDtypeStruct((devices * capacity,), jnp.int32),),
        in_specs=[smem_spec(), smem_spec(), any_spec()],
        out_specs=tuple(any_spec() for _ in outs) + (smem_spec(),),
        scratch_shapes=[
            pltpu.SMEM(new_units.shape, jnp.int32),
            pltpu.SMEM((devices,), jnp.int32),
        ]
        + pack_scratch(len(keys) * capacity, pages),
        compiler_params=pltpu.CompilerParams(vmem_limit_bytes=VMEM_LIMIT),
        name="first_pack",
    )(new_units, old_pages, pages)
    return result[:-1], result[-1]


def next_pack(order, pages, capacity, keys):
    chunk = (capacity,) + pages.shape[1:]
    return pl.pallas_call(
        functools.partial(next_pack_kernel, capacity, keys),
        out_shape=tuple(jax.ShapeDtypeStruct(chunk, pages.dtype) for _ in keys),
        in_specs=[smem_spec(), any_spec()],
        out_specs=tuple(any_spec() for _ in keys),
        scratch_shapes=pack_scratch(len(keys) * capacity, pages),
        compiler_params=pltpu.CompilerParams(vmem_limit_bytes=VMEM_LIMIT),
        name="next_pack",
    )(order, pages)


def attend(query, keys, values, limit):
    scale = 1.0 / math.sqrt(HD)
    scores = (
        lax.dot_general(query, keys, (((1,), (1,)), ((), ())), preferred_element_type=jnp.float32)
        * scale
    )
    lane = lax.broadcasted_iota(jnp.int32, scores.shape, 1)
    weights = jnp.where(lane < limit, jnp.exp(scores), 0.0)
    total = jnp.sum(weights, axis=1, keepdims=True)
    weighted = jnp.dot(weights.astype(jnp.bfloat16), values, preferred_element_type=jnp.float32)
    return weighted, total


def partial_kernel(
    capacity, keys, order_ref, old_ref, lengths_ref, queries_ref, pages_ref, *rest
):
    outs = rest[: len(keys)]
    stage, load_sem = rest[len(keys) :]
    device = lax.axis_index("tp")
    pages_dev = pages_ref.shape[0]
    lane = lax.broadcasted_iota(jnp.int32, (QROWS, HD), 1)
    loads = []
    for n, key in enumerate(keys):
        for r in range(capacity):
            copy = pltpu.make_async_copy(
                pages_ref.at[order_ref[key * capacity + r]],
                stage.at[n * capacity + r],
                load_sem.at[n * capacity + r],
            )
            copy.start()
            loads.append(copy)
    for n, key in enumerate(keys):
        sums = jnp.zeros((QROWS, HD), jnp.float32)
        for r in range(capacity):
            page = old_ref[device * pages_dev + order_ref[key * capacity + r]]
            unit = page // PER_UNIT
            limit = lengths_ref[unit // KVH] - (page % PER_UNIT) * PAGE
            slot = n * capacity + r
            loads[slot].wait()
            weighted, total = attend(
                queries_ref[unit], stage[slot, :, :HD], stage[slot, :, HD:], limit
            )
            outs[n][r * QROWS : (r + 1) * QROWS, :] = weighted.astype(jnp.bfloat16)
            high = total.astype(jnp.bfloat16).astype(jnp.float32)
            sums = jnp.where(lane == 2 * r, high, sums)
            sums = jnp.where(lane == 2 * r + 1, total - high, sums)
        outs[n][capacity * QROWS :, :] = sums.astype(jnp.bfloat16)


def partial_terms(order, old_pages, lengths, queries, pages, capacity, keys):
    rows = (capacity + 1) * QROWS
    count = len(keys) * capacity
    return pl.pallas_call(
        functools.partial(partial_kernel, capacity, keys),
        out_shape=tuple(jax.ShapeDtypeStruct((rows, HD), jnp.bfloat16) for _ in keys),
        in_specs=[smem_spec()] * 3 + [vmem_spec(), any_spec()],
        out_specs=tuple(vmem_spec() for _ in keys),
        scratch_shapes=[
            pltpu.VMEM((count,) + pages.shape[1:], pages.dtype),
            pltpu.SemaphoreType.DMA((count,)),
        ],
        compiler_params=pltpu.CompilerParams(vmem_limit_bytes=VMEM_LIMIT),
        name="partial_terms",
    )(order, old_pages, lengths, queries, pages)


ALIGN = 16


def place_kernel(entries, attends, started, *refs):
    refs = list(refs)
    table_ref, order_ref, length_ref, fresh_ref = refs[:4]
    refs = refs[4:]
    queries_ref = refs.pop(0) if attends else None
    if started and attends:
        weighted_in, total_in = refs.pop(0), refs.pop(0)
    sources = 1 + max(source for source, _, _ in entries)
    source_refs, refs = refs[:sources], refs[sources:]
    if started:
        refs.pop(0)
    out_ref = refs.pop(0)
    if attends:
        weighted_ref, total_ref = refs.pop(0), refs.pop(0)
    stage, load_sem, store_sem = refs
    if attends:
        if started:
            weighted_ref[...] = weighted_in[...]
            total_ref[...] = total_in[...]
        else:
            weighted_ref[...] = jnp.zeros_like(weighted_ref)
            total_ref[...] = jnp.zeros_like(total_ref)
    loads = []
    for n, (source, index, _) in enumerate(entries):
        index = order_ref[index[0]] if isinstance(index, tuple) else index
        copy = pltpu.make_async_copy(
            source_refs[source].at[index], stage.at[n], load_sem.at[n]
        )
        copy.start()
        loads.append(copy)
    row = lax.broadcasted_iota(jnp.int32, (ALIGN, 2 * HD), 0)
    stores = []
    for n, (_, _, key) in enumerate(entries):
        w = table_ref[key[0]] if isinstance(key, tuple) else key
        unit, part = w // PER_UNIT, w % PER_UNIT
        length = length_ref[unit]
        loads[n].wait()
        for j in range(2):
            position = length + j

            @pl.when(position // PAGE == part)
            def _():
                inside = position % PAGE
                rows = pl.ds(pl.multiple_of(inside // ALIGN * ALIGN, ALIGN), ALIGN)
                block = stage[n, rows, :].astype(jnp.float32)
                token = fresh_ref[unit, j : j + 1, :].astype(jnp.float32)
                block = jnp.where(row == inside % ALIGN, token, block)
                stage[n, rows, :] = block.astype(jnp.bfloat16)

        copy = pltpu.make_async_copy(stage.at[n], out_ref.at[w], store_sem.at[n])
        copy.start()
        stores.append(copy)
    if attends:
        group = 4
        for first in range(0, len(entries), group):
            found = []
            for n in range(first, min(first + group, len(entries))):
                key = entries[n][2]
                w = table_ref[key[0]] if isinstance(key, tuple) else key
                unit, part = w // PER_UNIT, w % PER_UNIT
                weighted, total = attend(
                    queries_ref[unit],
                    stage[n, :, :HD],
                    stage[n, :, HD:],
                    length_ref[unit] - part * PAGE,
                )
                found.append((unit, weighted, total))
            for unit, weighted, total in found:
                weighted_ref[unit] += weighted
                total_ref[unit] += jnp.broadcast_to(total, (QROWS, HD))
    for copy in stores:
        copy.wait()


def place_pages(table, order, lengths, fresh, queries, sums, sources, entries, cache):
    attends, started = queries is not None, cache is not None
    page_shape = sources[0].shape[1:]
    pages_dev = U_DEV * PER_UNIT
    args = [table, order, lengths, fresh]
    specs = [smem_spec()] * 3 + [vmem_spec()]
    if attends:
        args.append(queries)
        specs.append(vmem_spec())
        if started:
            args += list(sums)
            specs += [vmem_spec()] * 2
    args += list(sources)
    specs += [any_spec()] * len(sources)
    aliases = {}
    if started:
        aliases = {len(args): 0}
        args.append(cache)
        specs.append(any_spec())
    outs = [jax.ShapeDtypeStruct((pages_dev,) + page_shape, jnp.bfloat16)]
    out_specs = [any_spec()]
    if attends:
        outs += [jax.ShapeDtypeStruct((U_DEV, QROWS, HD), jnp.float32)] * 2
        out_specs += [vmem_spec()] * 2
    count = len(entries)
    result = pl.pallas_call(
        functools.partial(place_kernel, entries, attends, started),
        out_shape=tuple(outs),
        in_specs=specs,
        out_specs=tuple(out_specs),
        input_output_aliases=aliases,
        scratch_shapes=[
            pltpu.VMEM((count,) + page_shape, jnp.bfloat16),
            pltpu.SemaphoreType.DMA((count,)),
            pltpu.SemaphoreType.DMA((count,)),
        ],
        compiler_params=pltpu.CompilerParams(vmem_limit_bytes=VMEM_LIMIT),
        name="place_pages",
    )(*args)
    return result[0], result[1:]


def combine_kernel(capacity, late, table_ref, weighted_ref, total_ref, queries_ref, fresh_ref, *rest):
    parts, out_ref, weighted_sum, total_sum = rest[:-3], rest[-3], rest[-2], rest[-1]
    scale = 1.0 / math.sqrt(HD)
    lane = lax.broadcasted_iota(jnp.int32, (QROWS, HD), 1)
    row = lax.broadcasted_iota(jnp.int32, (QROWS, 1), 0)
    weighted_sum[...] = weighted_ref[...]
    total_sum[...] = total_ref[...]
    for part, key in zip(parts, late):
        sums = part[capacity * QROWS :, :].astype(jnp.float32)
        for r in range(capacity):
            unit = table_ref[key * capacity + r] // PER_UNIT
            mine = (lane == 2 * r) | (lane == 2 * r + 1)
            total = jnp.sum(jnp.where(mine, sums, 0.0), axis=1, keepdims=True)
            weighted_sum[unit] += part[r * QROWS : (r + 1) * QROWS, :].astype(jnp.float32)
            total_sum[unit] += jnp.broadcast_to(total, (QROWS, HD))
    for unit in range(U_DEV):
        query = queries_ref[unit].astype(jnp.float32)
        weighted = weighted_sum[unit]
        total = total_sum[unit]
        for j in range(2):
            key = fresh_ref[unit, j : j + 1, :HD].astype(jnp.float32)
            value = fresh_ref[unit, j : j + 1, HD:].astype(jnp.float32)
            score = jnp.sum(query * key, axis=1, keepdims=True) * scale
            weight = jnp.where(row >= j * GROUP, jnp.exp(score), 0.0)
            total = total + weight
            weighted = weighted + weight.astype(jnp.bfloat16).astype(jnp.float32) * value
        out_ref[unit] = (weighted / total).astype(jnp.bfloat16)


def combine(table, sums, queries, fresh, parts, late, capacity):
    return pl.pallas_call(
        functools.partial(combine_kernel, capacity, late),
        out_shape=jax.ShapeDtypeStruct((U_DEV, QROWS, HD), jnp.bfloat16),
        in_specs=[smem_spec()] + [vmem_spec()] * (4 + len(parts)),
        out_specs=vmem_spec(),
        scratch_shapes=[pltpu.VMEM((U_DEV, QROWS, HD), jnp.float32)] * 2,
        name="combine",
    )(table, *sums, queries, fresh, *parts)


def swap(values, key, devices):
    return lax.ppermute(values, "tp", [(i, i ^ key) for i in range(devices)])


def gather_swaps(values, devices):
    values = values[None]
    step = devices // 2
    span = [0]
    while step:
        values = jnp.concatenate([values, swap(values, step, devices)], axis=0)
        span = span + [s ^ step for s in span]
        step //= 2
    return values, span


def exchange_plan(devices):
    half = devices // 2
    far = sorted(range(half, devices), key=lambda k: (k & 1, k & 2, k))
    near = sorted(range(1, half), key=lambda k: (-(k & (half // 2)), k & 1, k))
    plan = far[:3]
    far = far[3:]
    while far:
        take = -(-len(near) // len(far))
        plan += near[:take] + far[:1]
        near, far = near[take:], far[1:]
    return plan + near


def body(hidden_states, qkv_weight, out_weight, cache_pages, context_lengths, new_units, old_pages):
    devices = lax.axis_size("tp")
    device = lax.axis_index("tp")
    requests = hidden_states.shape[0]
    pages_dev, page_rows, page_width = cache_pages.shape
    capacity = max(1, pages_dev // devices)
    total_units = new_units.shape[0]
    total_pages = old_pages.shape[0]
    pairwise = devices <= 16 and devices & (devices - 1) == 0

    if pairwise:
        plan = exchange_plan(devices)
        first, order = first_pack(
            new_units, old_pages, cache_pages, devices, capacity, plan[:FIRST], True
        )
        second = next_pack(order, cache_pages, capacity, plan[FIRST:])
        moved = [swap(c, k, devices) for c, k in zip(tuple(first) + tuple(second), plan)]
    else:
        keys = list(range(devices))
        (packed,), order = first_pack(
            new_units, old_pages, cache_pages, devices, capacity, keys, False
        )
        arrived = lax.all_to_all(
            packed.reshape(devices, capacity, page_rows, page_width),
            "tp",
            split_axis=0,
            concat_axis=0,
            tiled=True,
        ).reshape(devices * capacity, page_rows, page_width)

    own_units = lax.dynamic_slice_in_dim(new_units, device * U_DEV, U_DEV)
    own_lengths = context_lengths[own_units // KVH]
    wanted = (
        own_units[:, None] * PER_UNIT + jnp.arange(PER_UNIT, dtype=jnp.int32)[None, :]
    ).reshape(pages_dev)
    source_pos = jnp.sum(
        jnp.where(
            wanted[:, None] == old_pages[None, :],
            jnp.arange(total_pages, dtype=jnp.int32)[None, :],
            0,
        ),
        axis=1,
    )
    source_dev = source_pos // pages_dev
    rank = jnp.sum(
        (
            (source_dev[:, None] == source_dev[None, :])
            & (source_pos[None, :] < source_pos[:, None])
        ).astype(jnp.int32),
        axis=1,
    )
    if pairwise:
        where = (source_dev ^ device) * capacity + rank
        spots = jnp.arange(devices * capacity, dtype=jnp.int32)
        slots = jnp.arange(pages_dev, dtype=jnp.int32)
        table = jnp.sum(jnp.where(where[None, :] == spots[:, None], slots[None, :], 0), axis=1)
    else:
        table = source_dev * capacity + rank

    flat_rows = hidden_states.reshape(requests * 2, D)
    own_part = lax.dot_general(
        flat_rows, qkv_weight, (((1,), (1,)), ((), ())), preferred_element_type=jnp.float32
    ).astype(jnp.bfloat16)
    if pairwise:
        rows, span = gather_swaps(own_part, devices)
        turn = jnp.array([span.index(i) for i in range(devices)], jnp.int32)
        rows = rows[turn[jnp.arange(devices, dtype=jnp.int32) ^ device]]
        rows = rows.transpose(1, 0, 2)
    else:
        rows = lax.all_gather(own_part, "tp", axis=1, tiled=True)
    rows = rows.reshape(requests, 2, KVH, GROUP + 2, HD)

    positions = context_lengths[:, None] + jnp.arange(2, dtype=jnp.int32)[None, :]
    cosine, sine = rope_tables(positions)
    turned = rotate(
        rows[..., : GROUP + 1, :].astype(jnp.float32),
        cosine[:, :, None, None, :],
        sine[:, :, None, None, :],
    ).astype(jnp.bfloat16)
    by_unit = turned.transpose(0, 2, 1, 3, 4).reshape(total_units, 2, GROUP + 1, HD)
    queries = by_unit[:, :, :GROUP].reshape(total_units, QROWS, HD)
    new_keys = by_unit[:, :, GROUP]
    new_values = rows[..., GROUP + 1, :].transpose(0, 2, 1, 3).reshape(total_units, 2, HD)
    own_queries = queries[own_units]
    fresh = jnp.concatenate([new_keys[own_units], new_values[own_units]], axis=-1)

    late, parts, sums, new_cache = [], [], None, None
    if pairwise:
        late = plan[len(plan) - LATE :]
        if late:
            sent = partial_terms(
                order, old_pages, context_lengths, queries, cache_pages, capacity, late
            )
            parts = [swap(p, k, devices) for p, k in zip(sent, late)]
        at = 0
        for size in GROUPS:
            keys, at = plan[at : at + size], at + size
            entries, sources = [], []
            for key, array in zip(keys, moved[at - size : at]):
                entries += [(len(sources), r, (key * capacity + r,)) for r in range(capacity)]
                sources.append(array)
            if at == size:
                entries = [(len(sources), (r,), (r,)) for r in range(capacity)] + entries
                sources.append(cache_pages)
            attending = at <= len(plan) - len(late)
            new_cache, found = place_pages(
                table,
                order,
                own_lengths,
                fresh,
                own_queries if attending else None,
                sums,
                sources,
                entries,
                new_cache,
            )
            sums = found if attending else sums
    else:
        entries = [(0, (w,), w) for w in range(pages_dev)]
        new_cache, sums = place_pages(
            table, table, own_lengths, fresh, own_queries, None, [arrived], entries, None
        )
    attended = combine(table, sums, own_queries, fresh, parts, late, capacity)

    slot_index = jnp.sum(
        jnp.where(
            new_units[None, :] == jnp.arange(total_units, dtype=jnp.int32)[:, None],
            jnp.arange(total_units, dtype=jnp.int32)[None, :],
            0,
        ),
        axis=1,
    )
    attended = attended.reshape(U_DEV, 2, GROUP * HD)
    if pairwise:
        heads, span = gather_swaps(attended, devices)
        holder = turn[(slot_index // U_DEV) ^ device]
        heads = heads.reshape(total_units, 2, GROUP * HD)[holder * U_DEV + slot_index % U_DEV]
    else:
        heads = lax.all_gather(attended, "tp", axis=0, tiled=True)[slot_index]
    logical = (
        heads.reshape(requests, KVH, 2, GROUP * HD)
        .transpose(0, 2, 1, 3)
        .reshape(requests * 2, HEADS * HD)
    )
    mixed_rows = lax.dot_general(
        logical, out_weight, (((1,), (1,)), ((), ())), preferred_element_type=jnp.float32
    )
    mixed_rows = mixed_rows.astype(jnp.bfloat16).reshape(requests, 2, out_weight.shape[0])
    return (mixed_rows, new_cache)


def solution(mesh):
    in_specs = (
        P("group", None, None),
        P("tp", None),
        P("tp", None),
        P(("group", "tp"), None, None),
        P("group"),
        P("group"),
        P("group"),
    )
    out_specs = (P("group", None, "tp"), P(("group", "tp"), None, None))
    return jax.shard_map(body, mesh=mesh, in_specs=in_specs, out_specs=out_specs, check_vma=False)
```

time: 181 us -> 147 us (0.81)
  blocking collectives: 36.1 us -> 0 us
  Pallas kernels: 0 us -> 34.8 us
  waiting for transfers between devices: 69 us -> 37.1 us
  starting transfers between devices: 13.6 us -> 34.6 us
  local copies, waits for them, and re-layouts: 33.2 us -> 21.6 us
  other arithmetic: 10 us -> 4.24 us
  matrix products: 17.2 us -> 13.2 us
    all_to_all x2 -> x0, waiting for transfers between devices: 69 us -> none  [the longest x1 69 us: body(): lax.all_to_all(outgoing, 'tp', split_axis=0, concat_axis=0, tiled=True)]
    ppermute x0 -> x23, waiting for transfers between devices: none -> 37.1 us  [swap(): return lax.ppermute(values, 'tp', [(i, i ^ key) for i in range(devices)])]
    all_gather x1 -> x0, blocking collectives: 36.1 us -> none  [body(): all_heads = lax.all_gather(attended, 'tp', axis=0, tiled=True)]
    pallas_call x0 -> x7, Pallas kernels: none -> 34.8 us  [the longest x4 22.8 us: place_pages(): pl.pallas_call(functools.partial(place_kernel, entries, attends, started)...]
    ppermute x0 -> x23, starting transfers between devices: none -> 34.6 us  [swap(): return lax.ppermute(values, 'tp', [(i, i ^ key) for i in range(devices)])]
    scatter x3 -> x0, local copies, waits for them, and re-layouts: 17.5 us -> none  [the longest x1 12.5 us: body(): outgoing = jnp.zeros((devices, capacity, page_rows, page_width), jnp.bflo...]
    all_to_all x2 -> x0, starting transfers between devices: 13.6 us -> none  [the longest x1 7.39 us: body(): lax.all_to_all(outgoing_rows, 'tp', split_axis=0, concat_axis=0, tiled=True)]
    select_n x10 -> x5, other arithmetic: 8.6 us -> 0.13 us  [the longest x1 0.09 us: body(): new_keys[own_units]]
  transfers between devices with their start and end apart: 2 -> 23, of which waited for: 1 -> 11; matrix products, arithmetic and copies ran while one was open for 14% -> 12% of each run, Pallas kernels for 0% -> 20%
where the time goes in v1:
time: 147 us
  waiting for transfers between devices  37.1 us (25%)
  Pallas kernels  34.8 us (24%)
  starting transfers between devices  34.6 us (24%)
  local copies, waits for them, and re-layouts  21.6 us (15%)
  matrix products  13.2 us (9%)
  other arithmetic  4.24 us (3%)
    ppermute x23, waiting for transfers between devices, swap(): return lax.ppermute(values, 'tp', [(i, i ^ key) for i in range(devices)])  37.1 us
    ppermute x23, starting transfers between devices, swap(): return lax.ppermute(values, 'tp', [(i, i ^ key) for i in range(devices)])  34.6 us
    pallas_call x4, Pallas kernels, place_pages(): pl.pallas_call(functools.partial(place_kernel, entries, attends, started)...  22.8 us
    dot_general x1, matrix products, body(): lax.dot_general(flat_rows, qkv_weight, (((1,), (1,)), ((), ())), preferre...  7.56 us
    pallas_call x1, Pallas kernels, next_pack(): pl.pallas_call(functools.partial(next_pack_kernel, capacity, keys), out_s...  7 us
    dot_general x1, matrix products, body(): lax.dot_general(logical, out_weight, (((1,), (1,)), ((), ())), preferred_...  5.64 us
    unnamed x31, local copies, waits for them, and re-layouts  5.58 us
    pallas_call x1, Pallas kernels, first_pack(): pl.pallas_call(functools.partial(first_pack_kernel, devices, capacity, ke...  3.5 us
  transfers between devices with their start and end apart: 23, of which 11 were waited for; matrix products, arithmetic and copies ran while one was open for 12% of the time, Pallas kernels for 20%

profile of v1, /device:TPU:0, one launch (start us, length us, event | category | flops | bytes accessed | tf_op | source)
XLA Modules:
  0.0 146.7 jit_solution(2947309715434324813)
XLA Ops:
  0.6 1.1 reshape.256
  1.8 7.6 %constant_dynamic-update-slice_fusion.4 = (bf16[16,16,640]{2,1,0:T(8,128)(2,1)}, bf16[1,16,640]{2,1,0:T(8,128)(2,1)S(1)}) fusion(bf16[16,8192]{1,0:T(8,128)(2,1)S(1)} %reshape.256, bf16[640,8192]{1,0:T(8,128)(2,1)} %param.9), kind=kOutput, calls=%fused_computation.37 | convolution fusion | flops 167782400 | bytes 10788864 | tf_op jit(solution)/shard_map/dot_general | solution.py:483
  9.3 4.0 %collective-permute-start = (bf16[1,16,640]{2,1,0:T(8,128)(2,1)S(1)}, bf16[1,16,640]{2,1,0:T(8,128)(2,1)S(1)}, u32[]{:S(2)}, u32[]{:S(2)}) collective-permute-start(bf16[1,16,640]{2,1,0:T(8,128)(2,1)S(1)} %get-tuple-element.67), channel_id=1, source_target_pairs={{0,8},{1,9},{2,10},{3,11},{4,12},{5,13},{6,14},{7,15},{8,0},{9,1},... | collective-permute-start | bytes 61448 | tf_op jit(solution)/shard_map/ppermute | solution.py:396
  13.4 3.5 %first_pack.1 = (bf16[4,128,256]{2,1,0:T(8,128)(2,1)S(1)}, bf16[4,128,256]{2,1,0:T(8,128)(2,1)S(1)}, bf16[4,128,256]{2,1,0:T(8,128)(2,1)S(1)}, s32[64]{0:T(128)S(1)}) custom-call(s32[64]{0:T(128)S(1)} %copy-done.8, s32[1024]{0:T(1024)S(1)} %copy-done.6, bf16[64,128,256]{2,1,0:T(8,128)(2,1)S(1)} %copy-done), custom_call_target="tpu_custom_call" | custom-call | tf_op jit(solution)/shard_map/first_pack/pallas_call | solution.py:141
  16.9 3.9 %collective-permute-start.5 = (bf16[4,128,256]{2,1,0:T(8,128)(2,1)S(1)}, bf16[4,128,256]{2,1,0:T(8,128)(2,1)S(1)}, u32[]{:S(2)}, u32[]{:S(2)}) collective-permute-start(bf16[4,128,256]{2,1,0:T(8,128)(2,1)S(1)} %get-tuple-element.32), channel_id=1, source_target_pairs={{0,12},{1,13},{2,14},{3,15},{4,8},{5,9},{6,10},{7,11},{8,4},{9,5},... | collective-permute-start | bytes 786440 | tf_op jit(solution)/shard_map/ppermute | solution.py:396
  20.9 0.4 collective-permute-start.6
  21.3 7.0 %next_pack.1 = (bf16[4,128,256]{2,1,0:T(8,128)(2,1)S(1)}, bf16[4,128,256]{2,1,0:T(8,128)(2,1)}, bf16[4,128,256]{2,1,0:T(8,128)(2,1)S(1)}, bf16[4,128,256]{2,1,0:...) custom-call(s32[64]{0:T(128)S(1)} %get-tuple-element.30.order_ref.re, ...), custom_call_target="tpu_custom_call" | custom-call | tf_op jit(solution)/shard_map/next_pack/pallas_call | solution.py:159
  28.3 1.4 collective-permute-start.7
  30.1 0.2 select_reduce_fusion
  30.3 0.2 convert_reduce_fusion
  30.7 0.8 gather_fusion.6
  31.5 0.7 gather_fusion.1
  32.2 0.2 multiply_cosine_fusion
  32.5 0.7 collective-permute-start.1
  33.3 0.6 gather_fusion
  33.9 9.1 %collective-permute-done.1 = bf16[2,16,640]{2,1,0:T(8,128)(2,1)S(1)} collective-permute-done((bf16[2,16,640]{2,1,0:T(8,128)(2,1)S(1)}, bf16[2,16,640]{2,1,0:T(8,128)(2,1)S(1)}, u32[]{:S(2)}, u32[]{:S(2)}) %collective-permute-start.1) | collective-permute-done | bytes 40992 | tf_op jit(solution)/shard_map/ppermute | solution.py:396
  43.0 1.6 %collective-permute-start.2 = (bf16[4,16,640]{2,1,0:T(8,128)(2,1)S(1)}, bf16[4,16,640]{2,1,0:T(8,128)(2,1)S(1)}, u32[]{:S(2)}, u32[]{:S(2)}) collective-permute-start(bf16[4,16,640]{2,1,0:T(8,128)(2,1)S(1)} %pad_maximum_fusion.2), channel_id=1, source_target_pairs={{0,2},{1,3},{2,0},{3,1},{4,6},{5,7},{6,4},{7,5},{8,10},{9,11},{10,... | collective-permute-start | bytes 245768 | tf_op jit(solution)/shard_map/ppermute | solution.py:396
  44.6 0.6 constant_dynamic-update-slice_fusion.3
  45.2 2.3 %collective-permute-done.2 = bf16[4,16,640]{2,1,0:T(8,128)(2,1)S(1)} collective-permute-done((bf16[4,16,640]{2,1,0:T(8,128)(2,1)S(1)}, bf16[4,16,640]{2,1,0:T(8,128)(2,1)S(1)}, u32[]{:S(2)}, u32[]{:S(2)}) %collective-permute-start.2) | collective-permute-done | bytes 81952 | tf_op jit(solution)/shard_map/ppermute | solution.py:396
  47.6 0.6 constant_dynamic-update-slice_fusion.2
  48.2 0.6 constant_dynamic-update-slice_fusion.1
  49.0 0.8 collective-permute-start.8
  49.8 0.7 constant_dynamic-update-slice_fusion
  50.5 1.6 %gather_fusion.2 = bf16[16,16,640]{2,1,0:T(8,128)(2,1)S(1)} fusion(bf16[16,16,640]{2,1,0:T(8,128)(2,1)} %constant_dynamic-update-slice_fusion, s32[1024]{0:T(1024)S(1)} %pad_clamp_fusion.3), kind=kCustom, calls=%fused_computation.2 | custom fusion | bytes 655424 | tf_op jit(solution)/shard_map/gather | solution.py:489
  52.1 0.8 copy.31
  52.8 2.0 %reshape.257 = bf16[8,2,8,10,128]{4,3,2,1,0:T(8,128)(2,1)} reshape(bf16[16,16,640]{2,1,0:T(8,128)(2,1)} %copy.31) | data formatting | bytes 655360 | tf_op jit(solution)/shard_map/reshape | solution.py:493
  54.9 1.1 slice_convert_fusion
  56.0 7.8 %collective-permute-start.9 = (bf16[4,128,256]{2,1,0:T(8,128)(2,1)S(1)}, bf16[4,128,256]{2,1,0:T(8,128)(2,1)S(1)}, u32[]{:S(2)}, u32[]{:S(2)}) collective-permute-start(bf16[4,128,256]{2,1,0:T(8,128)(2,1)S(1)} %get-tuple-element.38), channel_id=1, source_target_pairs={{0,14},{1,15},{2,12},{3,13},{4,10},{5,11},{6,8},{7,9},{8,6},{9,7},... | collective-permute-start | bytes 786440 | tf_op jit(solution)/shard_map/ppermute | solution.py:396
  63.9 1.5 %collective-permute-start.11 = (bf16[4,128,256]{2,1,0:T(8,128)(2,1)}, bf16[4,128,256]{2,1,0:T(8,128)(2,1)S(1)}, u32[]{:S(2)}, u32[]{:S(2)}) collective-permute-start(bf16[4,128,256]{2,1,0:T(8,128)(2,1)} %get-tuple-element.40), channel_id=1, source_target_pairs={{0,7},{1,6},{2,5},{3,4},{4,3},{5,2},{6,1},{7,0},{8,15},{9,14},{10,... | collective-permute-start | bytes 786440 | tf_op jit(solution)/shard_map/ppermute | solution.py:396
  65.4 2.0 %collective-permute-start.13 = (bf16[4,128,256]{2,1,0:T(8,128)(2,1)S(1)}, bf16[4,128,256]{2,1,0:T(8,128)(2,1)S(1)}, u32[]{:S(2)}, u32[]{:S(2)}) collective-permute-start(bf16[4,128,256]{2,1,0:T(8,128)(2,1)S(1)} %get-tuple-element.45), channel_id=1, source_target_pairs={{0,2},{1,3},{2,0},{3,1},{4,6},{5,7},{6,4},{7,5},{8,10},{9,11},{10,... | collective-permute-start | bytes 786440 | tf_op jit(solution)/shard_map/ppermute | solution.py:396
  67.4 0.4 fusion.10
  67.8 1.5 %fusion.3 = bf16[8,8,2,9,128]{4,3,1,2,0:T(8,128)(2,1)S(1)} fusion(f32[8,2,8,9,64]{4,3,2,1,0:T(8,128)S(1)} %get-tuple-element.59, f32[8,2,8,9,64]{4,3,2,1,0:T(8,128)S(1)} %get-tuple-element.58, f32[8,2,128]{2,1,0:T(2,128)S(1)} %get-tuple-element.73, f32[8,2,128]{2,1,0:T(2,128)S(1)} %get-tuple-element.72, bf16[8,2,8,10,128]{4,3,2,1,0:T(8,128)(2,1)} %reshape.257), kind=kLoop, calls=%fused_computation.14 | loop fusion | flops 884736 | bytes 1196032 | tf_op jit(solution)/shard_map/transpose | solution.py:502
  69.4 1.7 %collective-permute-done.9.refs_7_ = bf16[4,128,256]{2,1,0:T(8,128)(2,1)S(1)} collective-permute-done((bf16[4,128,256]{2,1,0:T(8,128)(2,1)S(1)}, bf16[4,128,256]{2,1,0:T(8,128)(2,1)S(1)}, u32[]{:S(2)}, u32[]{:S(2)}) %collective-permute-start.9) | collective-permute-done | bytes 262176 | tf_op jit(solution)/shard_map/ppermute | solution.py:396
  71.1 0.7 collective-permute-start.14
  71.8 4.5 %collective-permute-done.10.refs_8_ = bf16[4,128,256]{2,1,0:T(8,128)(2,1)S(1)} collective-permute-done((bf16[4,128,256]{2,1,0:T(8,128)(2,1)}, bf16[4,128,256]{2,1,0:T(8,128)(2,1)S(1)}, u32[]{:S(2)}, u32[]{:S(2)}) %collective-permute-start.10) | collective-permute-done | bytes 262176 | tf_op jit(solution)/shard_map/ppermute | solution.py:396
  76.3 11.3 %collective-permute-done.11.refs_9_ = bf16[4,128,256]{2,1,0:T(8,128)(2,1)S(1)} collective-permute-done((bf16[4,128,256]{2,1,0:T(8,128)(2,1)}, bf16[4,128,256]{2,1,0:T(8,128)(2,1)S(1)}, u32[]{:S(2)}, u32[]{:S(2)}) %collective-permute-start.11) | collective-permute-done | bytes 262176 | tf_op jit(solution)/shard_map/ppermute | solution.py:396
  87.6 1.3 collective-permute-start.17
  89.0 1.5 %collective-permute-start.18 = (bf16[4,128,256]{2,1,0:T(8,128)(2,1)}, bf16[4,128,256]{2,1,0:T(8,128)(2,1)S(1)}, u32[]{:S(2)}, u32[]{:S(2)}) collective-permute-start(bf16[4,128,256]{2,1,0:T(8,128)(2,1)} %get-tuple-element.53), channel_id=1, source_target_pairs={{0,15},{1,14},{2,13},{3,12},{4,11},{5,10},{6,9},{7,8},{8,7},{9,6},... | collective-permute-start | bytes 786440 | tf_op jit(solution)/shard_map/ppermute | solution.py:396
  90.5 1.0 slice.44
  91.6 0.9 copy.48
  92.5 0.6 gather_fusion.4
  93.0 1.5 %gather_fusion.5 = bf16[4,16,128]{2,1,0:T(8,128)(2,1)S(1)} fusion(bf16[64,16,128]{2,1,0:T(8,128)(2,1)} %bitcast.72, s32[1024]{0:T(1024)S(1)} %get-tuple-element.68), kind=kCustom, calls=%fused_computation.5 | custom fusion | bytes 32784 | tf_op jit(solution)/shard_map/gather | solution.py:506
  94.6 0.6 gather_fusion.3
  95.2 2.2 %copy-done.1 = bf16[64,128,256]{2,1,0:T(8,128)(2,1)S(1)} copy-done((bf16[64,128,256]{2,1,0:T(8,128)(2,1)S(1)}, bf16[64,128,256]{2,1,0:T(8,128)(2,1)}, u32[]{:S(2)}) %copy-start.1) | copy-done | bytes 4194328
  97.4 8.1 %place_pages.4 = (bf16[64,128,256]{2,1,0:T(8,128)(2,1)}, f32[4,16,128]{2,1,0:T(8,128)S(1)}, f32[4,16,128]{2,1,0:T(8,128)S(1)}) custom-call(s32[64]{0:T(128)S(1)} %select_reduce_fusion.2.refs_0_.table_ref, s32[64]{0:T(128)S(1)} %get-tuple-element.30.order_ref.refs_1_, s32[4]{0:T(128)S(1)} %gather_fusion, ...), custom_call_target="tpu_custom_call" | custom-call | tf_op jit(solution)/shard_map/place_pages/pallas_call | solution.py:338
  105.5 5.9 %place_pages.5 = (bf16[64,128,256]{2,1,0:T(8,128)(2,1)}, f32[4,16,128]{2,1,0:T(8,128)S(1)}, f32[4,16,128]{2,1,0:T(8,128)S(1)}) custom-call(s32[64]{0:T(128)S(1)} %select_reduce_fusion.2.refs_0_.table_ref, s32[64]{0:T(128)S(1)} %get-tuple-element.30.order_ref.refs_1_, s32[4]{0:T(128)S(1)} %gather_fusion, ...), custom_call_target="tpu_custom_call", output_to_operand_aliasing={{0}: (11, {})} | custom-call | tf_op jit(solution)/shard_map/place_pages/pallas_call | solution.py:338
  111.4 0.4 collective-permute-done.16.refs_10_
  111.8 5.6 %place_pages.6 = (bf16[64,128,256]{2,1,0:T(8,128)(2,1)}, f32[4,16,128]{2,1,0:T(8,128)S(1)}, f32[4,16,128]{2,1,0:T(8,128)S(1)}) custom-call(s32[64]{0:T(128)S(1)} %select_reduce_fusion.2.refs_0_.table_ref, s32[64]{0:T(128)S(1)} %get-tuple-element.30.order_ref.refs_1_, s32[4]{0:T(128)S(1)} %gather_fusion, ...), custom_call_target="tpu_custom_call", output_to_operand_aliasing={{0}: (11, {})} | custom-call | tf_op jit(solution)/shard_map/place_pages/pallas_call | solution.py:338
  117.4 3.3 %place_pages.7 = (bf16[64,128,256]{2,1,0:T(8,128)(2,1)}, f32[4,16,128]{2,1,0:T(8,128)S(1)}, f32[4,16,128]{2,1,0:T(8,128)S(1)}) custom-call(s32[64]{0:T(128)S(1)} %select_reduce_fusion.2.refs_0_.table_ref, s32[64]{0:T(128)S(1)} %get-tuple-element.30.order_ref.refs_1_, s32[4]{0:T(128)S(1)} %gather_fusion, ...), custom_call_target="tpu_custom_call", output_to_operand_aliasing={{0}: (9, {})} | custom-call | tf_op jit(solution)/shard_map/place_pages/pallas_call | solution.py:338
  120.8 0.6 copy-done.4
  121.4 0.6 copy-done.5
  122.0 1.5 %combine.1 = bf16[4,16,128]{2,1,0:T(8,128)(2,1)} custom-call(s32[64]{0:T(128)} %copy-done.7, f32[4,16,128]{2,1,0:T(8,128)} %copy-done.4, f32[4,16,128]{2,1,0:T(8,128)} %copy-done.5, bf16[4,16,128]{2,1,0:T(8,128)(2,1)} %copy-done.2, bf16[4,2,256]{2,1,0:T(2,128)(2,1)} %copy-done.3), custom_call_target="tpu_custom_call" | custom-call | tf_op jit(solution)/shard_map/combine/pallas_call | solution.py:385
  123.5 0.7 broadcast_in_dim_reshape.4
  124.2 3.0 %collective-permute-start.19 = (bf16[1,4,2,1024]{3,2,1,0:T(2,128)(2,1)S(1)}, bf16[1,4,2,1024]{3,2,1,0:T(2,128)(2,1)S(1)}, u32[]{:S(2)}, u32[]{:S(2)}) collective-permute-start(bf16[1,4,2,1024]{3,2,1,0:T(2,128)(2,1)S(1)} %broadcast_in_dim_reshape.4), channel_id=1, source_target_pairs={{0,8},{1,9},{2,10},{3,11},{4,12},{5,13},{6,14},{7,15},{8,0},{9,1},... | collective-permute-start | bytes 49160 | tf_op jit(solution)/shard_map/ppermute | solution.py:396
  127.2 1.7 %collective-permute-done.19 = bf16[1,4,2,1024]{3,2,1,0:T(2,128)(2,1)S(1)} collective-permute-done((bf16[1,4,2,1024]{3,2,1,0:T(2,128)(2,1)S(1)}, bf16[1,4,2,1024]{3,2,1,0:T(2,128)(2,1)S(1)}, u32[]{:S(2)}, u32[]{:S(2)}) %collective-permute-start.19) | collective-permute-done | bytes 16416 | tf_op jit(solution)/shard_map/ppermute | solution.py:396
  128.9 1.6 %collective-permute-start.20 = (bf16[2,4,2,1024]{3,2,1,0:T(2,128)(2,1)S(1)}, bf16[2,4,2,1024]{3,2,1,0:T(2,128)(2,1)S(1)}, u32[]{:S(2)}, u32[]{:S(2)}) collective-permute-start(bf16[2,4,2,1024]{3,2,1,0:T(2,128)(2,1)S(1)} %pad_maximum_fusion.5), channel_id=1, source_target_pairs={{0,4},{1,5},{2,6},{3,7},{4,0},{5,1},{6,2},{7,3},{8,12},{9,13},{10,... | collective-permute-start | bytes 98312 | tf_op jit(solution)/shard_map/ppermute | solution.py:396
  130.6 2.4 %collective-permute-done.20 = bf16[2,4,2,1024]{3,2,1,0:T(2,128)(2,1)S(1)} collective-permute-done((bf16[2,4,2,1024]{3,2,1,0:T(2,128)(2,1)S(1)}, bf16[2,4,2,1024]{3,2,1,0:T(2,128)(2,1)S(1)}, u32[]{:S(2)}, u32[]{:S(2)}) %collective-permute-start.20) | collective-permute-done | bytes 32800 | tf_op jit(solution)/shard_map/ppermute | solution.py:396
  133.0 2.0 %collective-permute-start.21 = (bf16[4,4,2,1024]{3,2,1,0:T(2,128)(2,1)S(1)}, bf16[4,4,2,1024]{3,2,1,0:T(2,128)(2,1)S(1)}, u32[]{:S(2)}, u32[]{:S(2)}) collective-permute-start(bf16[4,4,2,1024]{3,2,1,0:T(2,128)(2,1)S(1)} %pad_maximum_fusion.3), channel_id=1, source_target_pairs={{0,2},{1,3},{2,0},{3,1},{4,6},{5,7},{6,4},{7,5},{8,10},{9,11},{10,... | collective-permute-start | bytes 196616 | tf_op jit(solution)/shard_map/ppermute | solution.py:396
  135.1 2.3 %collective-permute-done.21 = bf16[4,4,2,1024]{3,2,1,0:T(2,128)(2,1)S(1)} collective-permute-done((bf16[4,4,2,1024]{3,2,1,0:T(2,128)(2,1)S(1)}, bf16[4,4,2,1024]{3,2,1,0:T(2,128)(2,1)S(1)}, u32[]{:S(2)}, u32[]{:S(2)}) %collective-permute-start.21) | collective-permute-done | bytes 65568 | tf_op jit(solution)/shard_map/ppermute | solution.py:396
  137.4 0.2 pad_maximum_fusion.1
  137.7 1.2 collective-permute-done.22
  139.1 1.1 gather_fusion.7
  140.4 5.6 %convolution_convert_fusion.1 = bf16[16,512]{1,0:T(8,128)(2,1)S(1)} fusion(bf16[16,8192]{1,0:T(8,128)(2,1)S(1)} %bitcast.68, bf16[512,8192]{1,0:T(8,128)(2,1)} %param.10), kind=kOutput, calls=%fused_computation.9 | convolution fusion | flops 134225920 | bytes 8667136 | tf_op jit(solution)/shard_map/dot_general | solution.py:567
  146.1 0.6 reshape.264
  (78 shorter events, 2.0 us)
Async XLA Ops:
  0.6 12.7 %copy-start.8 = (s32[64]{0:T(128)S(1)}, s32[64]{0:T(128)}, u32[]{:S(2)}) copy-start(s32[64]{0:T(128)} %units_ref.1) | copy-start | bytes 772
  0.6 12.7 %copy-start.6 = (s32[1024]{0:T(1024)S(1)}, s32[1024]{0:T(1024)}, u32[]{:S(2)}) copy-start(s32[1024]{0:T(1024)} %old_ref.1) | copy-start | bytes 12292
  1.7 11.6 %copy-start = (bf16[64,128,256]{2,1,0:T(8,128)(2,1)S(1)}, bf16[64,128,256]{2,1,0:T(8,128)(2,1)}, u32[]{:S(2)}) copy-start(bf16[64,128,256]{2,1,0:T(8,128)(2,1)} %refs_10_.1) | copy-start | bytes 12582916
  1.7 28.9 %copy-start.10 = (s32[8]{0:T(128)S(1)}, s32[8]{0:T(128)}, u32[]{:S(2)}) copy-start(s32[8]{0:T(128)} %param.12) | copy-start | bytes 100
  1.7 29.0 %copy-start.9 = (s32[16]{0:T(128)S(1)}, s32[16]{0:T(128)}, u32[]{:S(2)}) copy-start(s32[16]{0:T(128)} %constant.78.clone) | copy-start | bytes 196
  9.3 23.2 %collective-permute-start = (bf16[1,16,640]{2,1,0:T(8,128)(2,1)S(1)}, bf16[1,16,640]{2,1,0:T(8,128)(2,1)S(1)}, u32[]{:S(2)}, u32[]{:S(2)}) collective-permute-start(bf16[1,16,640]{2,1,0:T(8,128)(2,1)S(1)} %get-tuple-element.67), channel_id=1, source_target_pairs={{0,8},{1,9},{2,10},{3,11},{4,12},{5,13},{6,14},{7,15},{8,0},{9,1},... | collective-permute-start | bytes 61448 | tf_op jit(solution)/shard_map/ppermute | solution.py:396
  16.9 39.2 %collective-permute-start.4 = (bf16[4,128,256]{2,1,0:T(8,128)(2,1)S(1)}, bf16[4,128,256]{2,1,0:T(8,128)(2,1)S(1)}, u32[]{:S(2)}, u32[]{:S(2)}) collective-permute-start(bf16[4,128,256]{2,1,0:T(8,128)(2,1)S(1)} %get-tuple-element.31), channel_id=1, source_target_pairs={{0,8},{1,9},{2,10},{3,11},{4,12},{5,13},{6,14},{7,15},{8,0},{9,1},... | collective-permute-start | bytes 786440 | tf_op jit(solution)/shard_map/ppermute | solution.py:396
  16.9 46.9 %collective-permute-start.5 = (bf16[4,128,256]{2,1,0:T(8,128)(2,1)S(1)}, bf16[4,128,256]{2,1,0:T(8,128)(2,1)S(1)}, u32[]{:S(2)}, u32[]{:S(2)}) collective-permute-start(bf16[4,128,256]{2,1,0:T(8,128)(2,1)S(1)} %get-tuple-element.32), channel_id=1, source_target_pairs={{0,12},{1,13},{2,14},{3,15},{4,8},{5,9},{6,10},{7,11},{8,4},{9,5},... | collective-permute-start | bytes 786440 | tf_op jit(solution)/shard_map/ppermute | solution.py:396
  20.9 43.0 %collective-permute-start.6 = (bf16[4,128,256]{2,1,0:T(8,128)(2,1)S(1)}, bf16[4,128,256]{2,1,0:T(8,128)(2,1)S(1)}, u32[]{:S(2)}, u32[]{:S(2)}) collective-permute-start(bf16[4,128,256]{2,1,0:T(8,128)(2,1)S(1)} %get-tuple-element.33), channel_id=1, source_target_pairs={{0,10},{1,11},{2,8},{3,9},{4,14},{5,15},{6,12},{7,13},{8,2},{9,3},... | collective-permute-start | bytes 786440 | tf_op jit(solution)/shard_map/ppermute | solution.py:396
  28.3 37.1 %collective-permute-start.7 = (bf16[4,128,256]{2,1,0:T(8,128)(2,1)S(1)}, bf16[4,128,256]{2,1,0:T(8,128)(2,1)S(1)}, u32[]{:S(2)}, u32[]{:S(2)}) collective-permute-start(bf16[4,128,256]{2,1,0:T(8,128)(2,1)S(1)} %get-tuple-element.34), channel_id=1, source_target_pairs={{0,4},{1,5},{2,6},{3,7},{4,0},{5,1},{6,2},{7,3},{8,12},{9,13},{10,... | collective-permute-start | bytes 786440 | tf_op jit(solution)/shard_map/ppermute | solution.py:396
  30.6 86.8 %copy-start.7 = (s32[64]{0:T(128)}, s32[64]{0:T(128)S(1)}, u32[]{:S(2)}) copy-start(s32[64]{0:T(128)S(1)} %select_reduce_fusion.2.refs_0_.table_ref) | copy-start | bytes 772
  32.5 10.5 %collective-permute-start.1 = (bf16[2,16,640]{2,1,0:T(8,128)(2,1)S(1)}, bf16[2,16,640]{2,1,0:T(8,128)(2,1)S(1)}, u32[]{:S(2)}, u32[]{:S(2)}) collective-permute-start(bf16[2,16,640]{2,1,0:T(8,128)(2,1)S(1)} %pad_maximum_fusion.4), channel_id=1, source_target_pairs={{0,4},{1,5},{2,6},{3,7},{4,0},{5,1},{6,2},{7,3},{8,12},{9,13},{10,... | collective-permute-start | bytes 122888 | tf_op jit(solution)/shard_map/ppermute | solution.py:396
  43.0 4.5 %collective-permute-start.2 = (bf16[4,16,640]{2,1,0:T(8,128)(2,1)S(1)}, bf16[4,16,640]{2,1,0:T(8,128)(2,1)S(1)}, u32[]{:S(2)}, u32[]{:S(2)}) collective-permute-start(bf16[4,16,640]{2,1,0:T(8,128)(2,1)S(1)} %pad_maximum_fusion.2), channel_id=1, source_target_pairs={{0,2},{1,3},{2,0},{3,1},{4,6},{5,7},{6,4},{7,5},{8,10},{9,11},{10,... | collective-permute-start | bytes 245768 | tf_op jit(solution)/shard_map/ppermute | solution.py:396
  47.5 1.5 collective-permute-start.3
  49.0 16.4 %collective-permute-start.8 = (bf16[4,128,256]{2,1,0:T(8,128)(2,1)}, bf16[4,128,256]{2,1,0:T(8,128)(2,1)S(1)}, u32[]{:S(2)}, u32[]{:S(2)}) collective-permute-start(bf16[4,128,256]{2,1,0:T(8,128)(2,1)} %get-tuple-element.35), channel_id=1, source_target_pairs={{0,6},{1,7},{2,4},{3,5},{4,2},{5,3},{6,0},{7,1},{8,14},{9,15},{10,... | collective-permute-start | bytes 786440 | tf_op jit(solution)/shard_map/ppermute | solution.py:396
  56.0 15.1 %collective-permute-start.9 = (bf16[4,128,256]{2,1,0:T(8,128)(2,1)S(1)}, bf16[4,128,256]{2,1,0:T(8,128)(2,1)S(1)}, u32[]{:S(2)}, u32[]{:S(2)}) collective-permute-start(bf16[4,128,256]{2,1,0:T(8,128)(2,1)S(1)} %get-tuple-element.38), channel_id=1, source_target_pairs={{0,14},{1,15},{2,12},{3,13},{4,10},{5,11},{6,8},{7,9},{8,6},{9,7},... | collective-permute-start | bytes 786440 | tf_op jit(solution)/shard_map/ppermute | solution.py:396
  63.9 12.4 %collective-permute-start.10 = (bf16[4,128,256]{2,1,0:T(8,128)(2,1)}, bf16[4,128,256]{2,1,0:T(8,128)(2,1)S(1)}, u32[]{:S(2)}, u32[]{:S(2)}) collective-permute-start(bf16[4,128,256]{2,1,0:T(8,128)(2,1)} %get-tuple-element.39), channel_id=1, source_target_pairs={{0,5},{1,4},{2,7},{3,6},{4,1},{5,0},{6,3},{7,2},{8,13},{9,12},{10,... | collective-permute-start | bytes 786440 | tf_op jit(solution)/shard_map/ppermute | solution.py:396
  63.9 23.8 %collective-permute-start.11 = (bf16[4,128,256]{2,1,0:T(8,128)(2,1)}, bf16[4,128,256]{2,1,0:T(8,128)(2,1)S(1)}, u32[]{:S(2)}, u32[]{:S(2)}) collective-permute-start(bf16[4,128,256]{2,1,0:T(8,128)(2,1)} %get-tuple-element.40), channel_id=1, source_target_pairs={{0,7},{1,6},{2,5},{3,4},{4,3},{5,2},{6,1},{7,0},{8,15},{9,14},{10,... | collective-permute-start | bytes 786440 | tf_op jit(solution)/shard_map/ppermute | solution.py:396
  65.4 22.3 %collective-permute-start.12 = (bf16[4,128,256]{2,1,0:T(8,128)(2,1)S(1)}, bf16[4,128,256]{2,1,0:T(8,128)(2,1)S(1)}, u32[]{:S(2)}, u32[]{:S(2)}) collective-permute-start(bf16[4,128,256]{2,1,0:T(8,128)(2,1)S(1)} %get-tuple-element.41), channel_id=1, source_target_pairs={{0,9},{1,8},{2,11},{3,10},{4,13},{5,12},{6,15},{7,14},{8,1},{9,0},... | collective-permute-start | bytes 786440 | tf_op jit(solution)/shard_map/ppermute | solution.py:396
  65.4 23.6 %collective-permute-start.13 = (bf16[4,128,256]{2,1,0:T(8,128)(2,1)S(1)}, bf16[4,128,256]{2,1,0:T(8,128)(2,1)S(1)}, u32[]{:S(2)}, u32[]{:S(2)}) collective-permute-start(bf16[4,128,256]{2,1,0:T(8,128)(2,1)S(1)} %get-tuple-element.45), channel_id=1, source_target_pairs={{0,2},{1,3},{2,0},{3,1},{4,6},{5,7},{6,4},{7,5},{8,10},{9,11},{10,... | collective-permute-start | bytes 786440 | tf_op jit(solution)/shard_map/ppermute | solution.py:396
  71.1 40.3 %collective-permute-start.14 = (bf16[4,128,256]{2,1,0:T(8,128)(2,1)}, bf16[4,128,256]{2,1,0:T(8,128)(2,1)S(1)}, u32[]{:S(2)}, u32[]{:S(2)}) collective-permute-start(bf16[4,128,256]{2,1,0:T(8,128)(2,1)} %get-tuple-element.46), channel_id=1, source_target_pairs={{0,13},{1,12},{2,15},{3,14},{4,9},{5,8},{6,11},{7,10},{8,5},{9,4},... | collective-permute-start | bytes 786440 | tf_op jit(solution)/shard_map/ppermute | solution.py:396
  76.3 35.1 %collective-permute-start.15 = (bf16[4,128,256]{2,1,0:T(8,128)(2,1)}, bf16[4,128,256]{2,1,0:T(8,128)(2,1)}, u32[]{:S(2)}, u32[]{:S(2)}) collective-permute-start(bf16[4,128,256]{2,1,0:T(8,128)(2,1)} %get-tuple-element.47), channel_id=1, source_target_pairs={{0,1},{1,0},{2,3},{3,2},{4,5},{5,4},{6,7},{7,6},{8,9},{9,8},{10,11... | collective-permute-start | bytes 786440 | tf_op jit(solution)/shard_map/ppermute | solution.py:396
  87.6 24.2 %collective-permute-start.16 = (bf16[4,128,256]{2,1,0:T(8,128)(2,1)}, bf16[4,128,256]{2,1,0:T(8,128)(2,1)}, u32[]{:S(2)}, u32[]{:S(2)}) collective-permute-start(bf16[4,128,256]{2,1,0:T(8,128)(2,1)} %get-tuple-element.48), channel_id=1, source_target_pairs={{0,11},{1,10},{2,9},{3,8},{4,15},{5,14},{6,13},{7,12},{8,3},{9,2},... | collective-permute-start | bytes 786440 | tf_op jit(solution)/shard_map/ppermute | solution.py:396
  87.6 29.8 %collective-permute-start.17 = (bf16[4,128,256]{2,1,0:T(8,128)(2,1)}, bf16[4,128,256]{2,1,0:T(8,128)(2,1)S(1)}, u32[]{:S(2)}, u32[]{:S(2)}) collective-permute-start(bf16[4,128,256]{2,1,0:T(8,128)(2,1)} %get-tuple-element.52), channel_id=1, source_target_pairs={{0,3},{1,2},{2,1},{3,0},{4,7},{5,6},{6,5},{7,4},{8,11},{9,10},{10,... | collective-permute-start | bytes 786440 | tf_op jit(solution)/shard_map/ppermute | solution.py:396
  89.0 28.5 %collective-permute-start.18 = (bf16[4,128,256]{2,1,0:T(8,128)(2,1)}, bf16[4,128,256]{2,1,0:T(8,128)(2,1)S(1)}, u32[]{:S(2)}, u32[]{:S(2)}) collective-permute-start(bf16[4,128,256]{2,1,0:T(8,128)(2,1)} %get-tuple-element.53), channel_id=1, source_target_pairs={{0,15},{1,14},{2,13},{3,12},{4,11},{5,10},{6,9},{7,8},{8,7},{9,6},... | collective-permute-start | bytes 786440 | tf_op jit(solution)/shard_map/ppermute | solution.py:396
  94.5 26.2 %copy-start.2 = (bf16[4,16,128]{2,1,0:T(8,128)(2,1)}, bf16[4,16,128]{2,1,0:T(8,128)(2,1)S(1)}, u32[]{:S(2)}) copy-start(bf16[4,16,128]{2,1,0:T(8,128)(2,1)S(1)} %gather_fusion.5) | copy-start | bytes 49156
  95.2 2.2 %copy-start.1 = (bf16[64,128,256]{2,1,0:T(8,128)(2,1)S(1)}, bf16[64,128,256]{2,1,0:T(8,128)(2,1)}, u32[]{:S(2)}) copy-start(bf16[64,128,256]{2,1,0:T(8,128)(2,1)} %refs_10_.1) | copy-start | bytes 12582916
  97.4 23.4 %copy-start.3 = (bf16[4,2,256]{2,1,0:T(2,128)(2,1)}, bf16[4,2,256]{2,1,0:T(2,128)(2,1)S(1)}, u32[]{:S(2)}) copy-start(bf16[4,2,256]{2,1,0:T(2,128)(2,1)S(1)} %constant_dynamic-update-slice_fusion.5.refs_3_.fresh_ref) | copy-start | bytes 12292
  120.8 0.6 copy-start.4
  121.4 0.6 copy-start.5
  124.2 4.7 %collective-permute-start.19 = (bf16[1,4,2,1024]{3,2,1,0:T(2,128)(2,1)S(1)}, bf16[1,4,2,1024]{3,2,1,0:T(2,128)(2,1)S(1)}, u32[]{:S(2)}, u32[]{:S(2)}) collective-permute-start(bf16[1,4,2,1024]{3,2,1,0:T(2,128)(2,1)S(1)} %broadcast_in_dim_reshape.4), channel_id=1, source_target_pairs={{0,8},{1,9},{2,10},{3,11},{4,12},{5,13},{6,14},{7,15},{8,0},{9,1},... | collective-permute-start | bytes 49160 | tf_op jit(solution)/shard_map/ppermute | solution.py:396
  128.9 4.0 %collective-permute-start.20 = (bf16[2,4,2,1024]{3,2,1,0:T(2,128)(2,1)S(1)}, bf16[2,4,2,1024]{3,2,1,0:T(2,128)(2,1)S(1)}, u32[]{:S(2)}, u32[]{:S(2)}) collective-permute-start(bf16[2,4,2,1024]{3,2,1,0:T(2,128)(2,1)S(1)} %pad_maximum_fusion.5), channel_id=1, source_target_pairs={{0,4},{1,5},{2,6},{3,7},{4,0},{5,1},{6,2},{7,3},{8,12},{9,13},{10,... | collective-permute-start | bytes 98312 | tf_op jit(solution)/shard_map/ppermute | solution.py:396
  133.0 4.3 %collective-permute-start.21 = (bf16[4,4,2,1024]{3,2,1,0:T(2,128)(2,1)S(1)}, bf16[4,4,2,1024]{3,2,1,0:T(2,128)(2,1)S(1)}, u32[]{:S(2)}, u32[]{:S(2)}) collective-permute-start(bf16[4,4,2,1024]{3,2,1,0:T(2,128)(2,1)S(1)} %pad_maximum_fusion.3), channel_id=1, source_target_pairs={{0,2},{1,3},{2,0},{3,1},{4,6},{5,7},{6,4},{7,5},{8,10},{9,11},{10,... | collective-permute-start | bytes 196616 | tf_op jit(solution)/shard_map/ppermute | solution.py:396
  137.6 1.4 collective-permute-start.22

commit v2 on v1

v2 whole, which is shorter than its diff:
```python
import functools
import math

import jax
import jax.numpy as jnp
from jax import lax
from jax.experimental import pallas as pl
from jax.experimental.pallas import tpu as pltpu
from jax.sharding import PartitionSpec as P

D = 8192
HEADS = 64
KVH = 8
HD = 128
U_DEV = 4
MAXCTX = 2048
PAGE = 128
GROUP = HEADS // KVH
QROWS = 2 * GROUP
PER_UNIT = MAXCTX // PAGE
VMEM_LIMIT = 32 * 1024 * 1024

rope_base = 10000.0


def rope_tables(positions):
    half_dim = HD // 2
    frequency = rope_base ** (-(jnp.arange(half_dim, dtype=jnp.float32) * 2.0 / HD))
    angles = positions.astype(jnp.float32)[..., None] * frequency
    cosine = jnp.concatenate([jnp.cos(angles), jnp.cos(angles)], axis=-1)
    sine = jnp.concatenate([-jnp.sin(angles), jnp.sin(angles)], axis=-1)
    return cosine, sine


def rotate(values, cosine, sine):
    half_dim = HD // 2
    turned = jnp.concatenate([values[..., half_dim:], values[..., :half_dim]], axis=-1)
    return values * cosine + turned * sine


def any_spec():
    return pl.BlockSpec(memory_space=pl.ANY)


def smem_spec():
    return pl.BlockSpec(memory_space=pltpu.SMEM)


def vmem_spec():
    return pl.BlockSpec(memory_space=pltpu.VMEM)


def load_order(devices, capacity, relative, units_ref, old_ref, order_ref, slots, count):
    device = lax.axis_index("tp")
    total_units = units_ref.shape[0]
    pages_dev = old_ref.shape[0] // devices

    def clear(t, carry):
        count[t] = 0
        return carry

    def empty(t, carry):
        order_ref[t] = 0
        return carry

    def invert(q, carry):
        slots[units_ref[q]] = q
        return carry

    def assign(i, carry):
        unit = old_ref[device * pages_dev + i] // PER_UNIT
        target = slots[unit] // U_DEV
        if relative:
            target = target ^ device
        rank = count[target]
        count[target] = rank + 1
        order_ref[target * capacity + rank] = i
        return carry

    lax.fori_loop(0, devices, clear, 0, unroll=8)
    if devices * capacity > pages_dev:
        lax.fori_loop(0, devices * capacity, empty, 0, unroll=8)
    lax.fori_loop(0, total_units, invert, 0, unroll=8)
    lax.fori_loop(0, pages_dev, assign, 0, unroll=8)


def move_pages(capacity, keys, order_ref, pages_ref, outs, stage, load_sem, store_sem):
    loads, stores = [], []
    for n, key in enumerate(keys):
        for r in range(capacity):
            copy = pltpu.make_async_copy(
                pages_ref.at[order_ref[key * capacity + r]],
                stage.at[n * capacity + r],
                load_sem.at[n * capacity + r],
            )
            copy.start()
            loads.append(copy)
    for n, key in enumerate(keys):
        for r in range(capacity):
            loads[n * capacity + r].wait()
        target = outs[n] if len(outs) > 1 else outs[0].at[pl.ds(n * capacity, capacity)]
        copy = pltpu.make_async_copy(
            stage.at[pl.ds(n * capacity, capacity)], target, store_sem.at[n]
        )
        copy.start()
        stores.append(copy)
    for copy in stores:
        copy.wait()


def first_pack_kernel(devices, capacity, keys, relative, units_ref, old_ref, pages_ref, *rest):
    outs = rest[:-6]
    order_ref, slots, count, stage, load_sem, store_sem = rest[-6:]
    load_order(devices, capacity, relative, units_ref, old_ref, order_ref, slots, count)
    move_pages(capacity, keys, order_ref, pages_ref, outs, stage, load_sem, store_sem)


def next_pack_kernel(capacity, keys, order_ref, pages_ref, after_ref, *rest):
    outs = rest[:-3]
    stage, load_sem, store_sem = rest[-3:]
    move_pages(capacity, keys, order_ref, pages_ref, outs, stage, load_sem, store_sem)


def pack_scratch(count, pages):
    return [
        pltpu.VMEM((count,) + pages.shape[1:], pages.dtype),
        pltpu.SemaphoreType.DMA((count,)),
        pltpu.SemaphoreType.DMA((count,)),
    ]


def first_pack(new_units, old_pages, pages, devices, capacity, keys, relative):
    chunk = (capacity,) + pages.shape[1:]
    if relative:
        outs = [jax.ShapeDtypeStruct(chunk, pages.dtype) for _ in keys]
    else:
        outs = [jax.ShapeDtypeStruct((len(keys) * capacity,) + chunk[1:], pages.dtype)]
    result = pl.pallas_call(
        functools.partial(first_pack_kernel, devices, capacity, keys, relative),
        out_shape=tuple(outs) + (jax.ShapeDtypeStruct((devices * capacity,), jnp.int32),),
        in_specs=[smem_spec(), smem_spec(), any_spec()],
        out_specs=tuple(any_spec() for _ in outs) + (smem_spec(),),
        scratch_shapes=[
            pltpu.SMEM(new_units.shape, jnp.int32),
            pltpu.SMEM((devices,), jnp.int32),
        ]
        + pack_scratch(len(keys) * capacity, pages),
        compiler_params=pltpu.CompilerParams(vmem_limit_bytes=VMEM_LIMIT),
        name="first_pack",
    )(new_units, old_pages, pages)
    return result[:-1], result[-1]


def next_pack(order, pages, after, capacity, keys):
    chunk = (capacity,) + pages.shape[1:]
    return pl.pallas_call(
        functools.partial(next_pack_kernel, capacity, keys),
        out_shape=tuple(jax.ShapeDtypeStruct(chunk, pages.dtype) for _ in keys),
        in_specs=[smem_spec(), any_spec(), any_spec()],
        out_specs=tuple(any_spec() for _ in keys),
        scratch_shapes=pack_scratch(len(keys) * capacity, pages),
        compiler_params=pltpu.CompilerParams(vmem_limit_bytes=VMEM_LIMIT),
        name="next_pack",
    )(order, pages, after)


def attend(query, keys, values, limit):
    scale = 1.0 / math.sqrt(HD)
    scores = (
        lax.dot_general(query, keys, (((1,), (1,)), ((), ())), preferred_element_type=jnp.float32)
        * scale
    )
    lane = lax.broadcasted_iota(jnp.int32, scores.shape, 1)
    weights = jnp.where(lane < limit, jnp.exp(scores), 0.0)
    total = jnp.sum(weights, axis=1, keepdims=True)
    weighted = jnp.dot(weights.astype(jnp.bfloat16), values, preferred_element_type=jnp.float32)
    return weighted, total


ALIGN = 16


def place_kernel(entries, started, finish, *refs):
    refs = list(refs)
    table_ref, order_ref, length_ref, fresh_ref = refs[:4]
    refs = refs[4:]
    queries_ref = refs.pop(0)
    if started:
        weighted_in, total_in = refs.pop(0), refs.pop(0)
    sources = 1 + max(source for source, _, _ in entries)
    source_refs, refs = refs[:sources], refs[sources:]
    if started:
        refs.pop(0)
    out_ref, weighted_ref, total_ref = refs[:3]
    refs = refs[3:]
    attended_ref = refs.pop(0) if finish else None
    stage, load_sem, store_sem = refs
    if started:
        weighted_ref[...] = weighted_in[...]
        total_ref[...] = total_in[...]
    else:
        own_terms(queries_ref, fresh_ref, weighted_ref, total_ref)
    loads = []
    for n, (source, index, _) in enumerate(entries):
        index = order_ref[index[0]] if isinstance(index, tuple) else index
        copy = pltpu.make_async_copy(
            source_refs[source].at[index], stage.at[n], load_sem.at[n]
        )
        copy.start()
        loads.append(copy)
    row = lax.broadcasted_iota(jnp.int32, (ALIGN, 2 * HD), 0)
    stores = []
    for n, (_, _, key) in enumerate(entries):
        w = table_ref[key[0]] if isinstance(key, tuple) else key
        unit, part = w // PER_UNIT, w % PER_UNIT
        length = length_ref[unit]
        loads[n].wait()
        for j in range(2):
            position = length + j

            @pl.when(position // PAGE == part)
            def _():
                inside = position % PAGE
                rows = pl.ds(pl.multiple_of(inside // ALIGN * ALIGN, ALIGN), ALIGN)
                block = stage[n, rows, :].astype(jnp.float32)
                token = fresh_ref[pl.ds(2 * unit + j, 1), :]
                block = jnp.where(row == inside % ALIGN, token, block)
                stage[n, rows, :] = block.astype(jnp.bfloat16)

        copy = pltpu.make_async_copy(stage.at[n], out_ref.at[w], store_sem.at[n])
        copy.start()
        stores.append(copy)
    group = 4
    for first in range(0, len(entries), group):
        found = []
        for n in range(first, min(first + group, len(entries))):
            key = entries[n][2]
            w = table_ref[key[0]] if isinstance(key, tuple) else key
            unit, part = w // PER_UNIT, w % PER_UNIT
            weighted, total = attend(
                queries_ref[unit].astype(jnp.bfloat16),
                stage[n, :, :HD],
                stage[n, :, HD:],
                length_ref[unit] - part * PAGE,
            )
            found.append((unit, weighted, total))
        for unit, weighted, total in found:
            weighted_ref[unit] += weighted
            total_ref[unit] += jnp.broadcast_to(total, (QROWS, HD))
    if finish:
        attended_ref[...] = (weighted_ref[...] / total_ref[...]).astype(jnp.bfloat16)
    for copy in stores:
        copy.wait()


def own_terms(queries_ref, fresh_ref, weighted_ref, total_ref):
    scale = 1.0 / math.sqrt(HD)
    row = lax.broadcasted_iota(jnp.int32, (QROWS, 1), 0)
    for unit in range(U_DEV):
        query = queries_ref[unit]
        weighted = jnp.zeros((QROWS, HD), jnp.float32)
        total = jnp.zeros((QROWS, 1), jnp.float32)
        for j in range(2):
            at = 2 * unit + j
            key = fresh_ref[at : at + 1, :HD]
            value = fresh_ref[at : at + 1, HD:]
            score = jnp.sum(query * key, axis=1, keepdims=True) * scale
            weight = jnp.where(row >= j * GROUP, jnp.exp(score), 0.0)
            total = total + weight
            weighted = weighted + weight.astype(jnp.bfloat16).astype(jnp.float32) * value
        weighted_ref[unit] = weighted
        total_ref[unit] = jnp.broadcast_to(total, (QROWS, HD))


def place_pages(table, order, lengths, fresh, queries, sums, sources, entries, cache, finish):
    started = cache is not None
    page_shape = sources[0].shape[1:]
    pages_dev = U_DEV * PER_UNIT
    args = [table, order, lengths, fresh, queries]
    specs = [smem_spec()] * 3 + [vmem_spec()] * 2
    if started:
        args += list(sums)
        specs += [vmem_spec()] * 2
    args += list(sources)
    specs += [any_spec()] * len(sources)
    aliases = {}
    if started:
        aliases = {len(args): 0}
        args.append(cache)
        specs.append(any_spec())
    outs = [jax.ShapeDtypeStruct((pages_dev,) + page_shape, jnp.bfloat16)]
    outs += [jax.ShapeDtypeStruct((U_DEV, QROWS, HD), jnp.float32)] * 2
    out_specs = [any_spec()] + [vmem_spec()] * 2
    if finish:
        outs.append(jax.ShapeDtypeStruct((U_DEV, QROWS, HD), jnp.bfloat16))
        out_specs.append(vmem_spec())
    count = len(entries)
    result = pl.pallas_call(
        functools.partial(place_kernel, entries, started, finish),
        out_shape=tuple(outs),
        in_specs=specs,
        out_specs=tuple(out_specs),
        input_output_aliases=aliases,
        scratch_shapes=[
            pltpu.VMEM((count,) + page_shape, jnp.bfloat16),
            pltpu.SemaphoreType.DMA((count,)),
            pltpu.SemaphoreType.DMA((count,)),
        ],
        compiler_params=pltpu.CompilerParams(vmem_limit_bytes=VMEM_LIMIT),
        name="place_pages",
    )(*args)
    return result[0], result[1:3], result[3] if finish else None


def own_rows_kernel(rows_ref, place_ref, request_ref, cosine_ref, sine_ref, queries_ref, fresh_ref):
    width = rows_ref.shape[2]
    pieces = place_ref.shape[0] // U_DEV
    row = lax.broadcasted_iota(jnp.int32, rows_ref.shape[1:], 0)
    half_dim = HD // 2
    for unit in range(U_DEV):
        found = []
        for piece in range(pieces):
            block = rows_ref[place_ref[unit * pieces + piece]].astype(jnp.float32)
            picked = [
                jnp.sum(
                    jnp.where(row == 2 * request_ref[unit] + j, block, 0.0), axis=0, keepdims=True
                )
                for j in range(2)
            ]
            for at in range(0, width, HD):
                found.append([line[:, at : at + HD] for line in picked])
        for j in range(2):
            heads = jnp.concatenate([head[j] for head in found[: GROUP + 1]], axis=0)
            turned = jnp.concatenate([heads[:, half_dim:], heads[:, :half_dim]], axis=1)
            cosine = cosine_ref[2 * unit + j : 2 * unit + j + 1, :]
            sine = sine_ref[2 * unit + j : 2 * unit + j + 1, :]
            heads = (heads * cosine + turned * sine).astype(jnp.bfloat16).astype(jnp.float32)
            queries_ref[unit, j * GROUP : (j + 1) * GROUP, :] = heads[:GROUP]
            fresh_ref[2 * unit + j : 2 * unit + j + 1, :HD] = heads[GROUP:]
            fresh_ref[2 * unit + j : 2 * unit + j + 1, HD:] = found[GROUP + 1][j]


def own_rows(rows, places, requests, cosine, sine):
    queries, fresh = pl.pallas_call(
        own_rows_kernel,
        out_shape=(
            jax.ShapeDtypeStruct((U_DEV, QROWS, HD), jnp.float32),
            jax.ShapeDtypeStruct((2 * U_DEV, 2 * HD), jnp.float32),
        ),
        in_specs=[vmem_spec(), smem_spec(), smem_spec(), vmem_spec(), vmem_spec()],
        out_specs=(vmem_spec(), vmem_spec()),
        name="own_rows",
    )(rows, places, requests, cosine, sine)
    return queries, fresh


def swap(values, key, devices):
    return lax.ppermute(values, "tp", [(i, i ^ key) for i in range(devices)])


def gather_swaps(values, devices, direct):
    values = values[None]
    step = devices // 2
    span = [0]
    if direct and devices >= 4:
        keys = [step, step // 2, step + step // 2]
        values = jnp.concatenate([values] + [swap(values, k, devices) for k in keys], axis=0)
        span = [0] + keys
        step //= 4
    while step:
        values = jnp.concatenate([values, swap(values, step, devices)], axis=0)
        span = span + [s ^ step for s in span]
        step //= 2
    return values, span


def exchange_plan(devices):
    half = devices // 2
    far = sorted(range(half, devices), key=lambda k: (k & 1, k & 2, k))
    across = [k for k in range(1, half) if k >= half // 2]
    beside = [k for k in range(1, half) if k < half // 2]
    if devices < 16:
        return [far + across + beside]
    return [
        far[:2] + beside[:1],
        far[2:4] + across[:2],
        far[4:6] + across[2:] + beside[1:2],
        far[6:] + beside[2:],
    ]


def body(hidden_states, qkv_weight, out_weight, cache_pages, context_lengths, new_units, old_pages):
    devices = lax.axis_size("tp")
    device = lax.axis_index("tp")
    requests = hidden_states.shape[0]
    pages_dev, page_rows, page_width = cache_pages.shape
    capacity = max(1, pages_dev // devices)
    total_units = new_units.shape[0]
    total_pages = old_pages.shape[0]
    pairwise = devices <= 16 and devices & (devices - 1) == 0

    if pairwise:
        plan = exchange_plan(devices)
        chunks, order = first_pack(
            new_units, old_pages, cache_pages, devices, capacity, plan[0], True
        )
        moved = [swap(c, k, devices) for c, k in zip(chunks, plan[0])]
    else:
        keys = list(range(devices))
        (packed,), order = first_pack(
            new_units, old_pages, cache_pages, devices, capacity, keys, False
        )
        arrived = lax.all_to_all(
            packed.reshape(devices, capacity, page_rows, page_width),
            "tp",
            split_axis=0,
            concat_axis=0,
            tiled=True,
        ).reshape(devices * capacity, page_rows, page_width)

    own_units = lax.dynamic_slice_in_dim(new_units, device * U_DEV, U_DEV)
    own_lengths = context_lengths[own_units // KVH]
    wanted = (
        own_units[:, None] * PER_UNIT + jnp.arange(PER_UNIT, dtype=jnp.int32)[None, :]
    ).reshape(pages_dev)
    source_pos = jnp.sum(
        jnp.where(
            wanted[:, None] == old_pages[None, :],
            jnp.arange(total_pages, dtype=jnp.int32)[None, :],
            0,
        ),
        axis=1,
    )
    source_dev = source_pos // pages_dev
    rank = jnp.sum(
        (
            (source_dev[:, None] == source_dev[None, :])
            & (source_pos[None, :] < source_pos[:, None])
        ).astype(jnp.int32),
        axis=1,
    )
    if pairwise:
        where = (source_dev ^ device) * capacity + rank
        spots = jnp.arange(devices * capacity, dtype=jnp.int32)
        slots = jnp.arange(pages_dev, dtype=jnp.int32)
        table = jnp.sum(jnp.where(where[None, :] == spots[:, None], slots[None, :], 0), axis=1)
    else:
        table = source_dev * capacity + rank

    flat_rows = hidden_states.reshape(requests * 2, D)
    flat_rows = flat_rows + jnp.minimum(order[0], 0).astype(jnp.bfloat16)
    own_part = lax.dot_general(
        flat_rows, qkv_weight, (((1,), (1,)), ((), ())), preferred_element_type=jnp.float32
    ).astype(jnp.bfloat16)
    own_requests, own_heads = own_units // KVH, own_units % KVH
    positions = own_lengths[:, None] + jnp.arange(2, dtype=jnp.int32)[None, :]
    cosine, sine = rope_tables(positions.reshape(2 * U_DEV))
    if pairwise:
        rows, span = gather_swaps(own_part, devices, True)
        turn = jnp.array([span.index(i) for i in range(devices)], jnp.int32)
        pieces = devices // KVH
        holders = own_heads[:, None] * pieces + jnp.arange(pieces, dtype=jnp.int32)[None, :]
        places = turn[(holders ^ device).reshape(U_DEV * pieces)]
        queries, fresh = own_rows(rows, places, own_requests, cosine, sine)
        new_cache, sums = None, None
        if len(plan) > 1:
            chunks = next_pack(order, cache_pages, own_part, capacity, plan[1])
            moved += [swap(c, k, devices) for c, k in zip(chunks, plan[1])]
            chunks = next_pack(order, cache_pages, queries, capacity, plan[2])
            moved += [swap(c, k, devices) for c, k in zip(chunks, plan[2])]
        at = 0
        keys = sum(plan, [])
        groups = [len(p) for p in plan[:-1]] + [len(plan[-1]) - 1, 1]
        for step, size in enumerate(groups):
            entries, sources = [], []
            for key, array in zip(keys[at : at + size], moved[at : at + size]):
                entries += [(len(sources), r, (key * capacity + r,)) for r in range(capacity)]
                sources.append(array)
            at += size
            if step == 0:
                entries = [(len(sources), (r,), (r,)) for r in range(capacity)] + entries
                sources.append(cache_pages)
            new_cache, sums, attended = place_pages(
                table,
                order,
                own_lengths,
                fresh,
                queries,
                sums,
                sources,
                entries,
                new_cache,
                step == len(groups) - 1,
            )
            if step == 0 and len(plan) > 1:
                chunks = next_pack(order, cache_pages, sums[0], capacity, plan[3])
                moved += [swap(c, k, devices) for c, k in zip(chunks, plan[3])]
    else:
        rows = lax.all_gather(own_part, "tp", axis=1, tiled=True)
        rows = rows.reshape(requests, 2, KVH, GROUP + 2, HD)
        rows = rows[own_requests, :, own_heads].astype(jnp.float32)
        turned = rotate(
            rows[:, :, : GROUP + 1],
            cosine.reshape(U_DEV, 2, 1, HD),
            sine.reshape(U_DEV, 2, 1, HD),
        )
        queries = turned[:, :, :GROUP].reshape(U_DEV, QROWS, HD)
        fresh = jnp.concatenate([turned[:, :, GROUP], rows[:, :, GROUP + 1]], axis=-1)
        fresh = fresh.reshape(2 * U_DEV, 2 * HD).astype(jnp.bfloat16).astype(jnp.float32)
        queries = queries.astype(jnp.bfloat16).astype(jnp.float32)
        entries = [(0, (w,), w) for w in range(pages_dev)]
        new_cache, sums, attended = place_pages(
            table, table, own_lengths, fresh, queries, None, [arrived], entries, None, True
        )

    slot_index = jnp.sum(
        jnp.where(
            new_units[None, :] == jnp.arange(total_units, dtype=jnp.int32)[:, None],
            jnp.arange(total_units, dtype=jnp.int32)[None, :],
            0,
        ),
        axis=1,
    )
    attended = attended.reshape(U_DEV, 2, GROUP * HD)
    if pairwise:
        heads, span = gather_swaps(attended, devices, False)
        turn = jnp.array([span.index(i) for i in range(devices)], jnp.int32)
        holder = turn[(slot_index // U_DEV) ^ device]
        heads = heads.reshape(total_units, 2, GROUP * HD)[holder * U_DEV + slot_index % U_DEV]
    else:
        heads = lax.all_gather(attended, "tp", axis=0, tiled=True)[slot_index]
    logical = (
        heads.reshape(requests, KVH, 2, GROUP * HD)
        .transpose(0, 2, 1, 3)
        .reshape(requests * 2, HEADS * HD)
    )
    mixed_rows = lax.dot_general(
        logical, out_weight, (((1,), (1,)), ((), ())), preferred_element_type=jnp.float32
    )
    mixed_rows = mixed_rows.astype(jnp.bfloat16).reshape(requests, 2, out_weight.shape[0])
    return (mixed_rows, new_cache)


def solution(mesh):
    in_specs = (
        P("group", None, None),
        P("tp", None),
        P("tp", None),
        P(("group", "tp"), None, None),
        P("group"),
        P("group"),
        P("group"),
    )
    out_specs = (P("group", None, "tp"), P(("group", "tp"), None, None))
    return jax.shard_map(body, mesh=mesh, in_specs=in_specs, out_specs=out_specs, check_vma=False)
```

time: 147 us -> 162 us (1.10)
  waiting for transfers between devices: 37.1 us -> 45.1 us
  starting transfers between devices: 34.6 us -> 41 us
  Pallas kernels: 34.8 us -> 38.6 us
  local copies, waits for them, and re-layouts: 21.6 us -> 18.7 us
    ppermute x23 -> x24, waiting for transfers between devices: 37.1 us -> 45.1 us  [swap(): return lax.ppermute(values, 'tp', [(i, i ^ key) for i in range(devices)])]
    unnamed x31 -> x36, local copies, waits for them, and re-layouts: 5.58 us -> 12.2 us
    ppermute x23 -> x24, starting transfers between devices: 34.6 us -> 41 us  [swap(): return lax.ppermute(values, 'tp', [(i, i ^ key) for i in range(devices)])]
    gather x5 -> x1, local copies, waits for them, and re-layouts: 4.89 us -> 1.18 us  [body(): places = turn[(holders ^ device).reshape(U_DEV * pieces)]]
    reshape x3 -> x0, local copies, waits for them, and re-layouts: 3.13 us -> none  [the longest x1 2.03 us: body(): rows = rows.reshape(requests, 2, KVH, GROUP + 2, HD)]
    pallas_call x5 -> x6, Pallas kernels: 24.3 us -> 26.6 us  [the longest x5 24.8 us: place_pages(): pl.pallas_call(functools.partial(place_kernel, entries, started, finish),...]
    slice x4 -> x0, local copies, waits for them, and re-layouts: 2.28 us -> none  [the longest x1 1.02 us: body(): rows[..., GROUP + 1, :].transpose(0, 2, 1, 3).reshape(total_units, 2, HD)]
    pallas_call x1 -> x3, Pallas kernels: 7 us -> 8.5 us  [next_pack(): pl.pallas_call(functools.partial(next_pack_kernel, capacity, keys), out_s...]
  transfers between devices with their start and end apart: 23 -> 24, of which waited for: 11 -> 9; matrix products, arithmetic and copies ran while one was open for 12% -> 5% of each run, Pallas kernels for 20% -> 20%
where the time goes in v2:
time: 162 us; the launch traced here: 161 us
  waiting for transfers between devices  45.1 us (28%)
  starting transfers between devices  41 us (25%)
  Pallas kernels  38.6 us (24%)
  local copies, waits for them, and re-layouts  18.7 us (12%)
  matrix products  13.1 us (8%)
  other arithmetic  3.73 us (2%)
    ppermute x24, waiting for transfers between devices, swap(): return lax.ppermute(values, 'tp', [(i, i ^ key) for i in range(devices)])  45.1 us
    ppermute x24, starting transfers between devices, swap(): return lax.ppermute(values, 'tp', [(i, i ^ key) for i in range(devices)])  41 us
    pallas_call x5, Pallas kernels, place_pages(): pl.pallas_call(functools.partial(place_kernel, entries, started, finish),...  24.8 us
    unnamed x36, local copies, waits for them, and re-layouts  12.2 us
    pallas_call x3, Pallas kernels, next_pack(): pl.pallas_call(functools.partial(next_pack_kernel, capacity, keys), out_s...  8.5 us
    dot_general x1, matrix products, body(): lax.dot_general(flat_rows, qkv_weight, (((1,), (1,)), ((), ())), preferre...  7.42 us
    dot_general x1, matrix products, body(): lax.dot_general(logical, out_weight, (((1,), (1,)), ((), ())), preferred_...  5.64 us
    pallas_call x1, Pallas kernels, first_pack(): pl.pallas_call(functools.partial(first_pack_kernel, devices, capacity, ke...  3.49 us
  transfers between devices with their start and end apart: 24, of which 9 were waited for; matrix products, arithmetic and copies ran while one was open for 5% of the time, Pallas kernels for 20%

profile of v2, /device:TPU:0, one launch (start us, length us, event | category | flops | bytes accessed | tf_op | source)
XLA Modules:
  0.0 161.2 jit_solution(11044076882516904377)
XLA Ops:
  0.7 2.2 %copy-done.1 = bf16[64,128,256]{2,1,0:T(8,128)(2,1)S(1)} copy-done((bf16[64,128,256]{2,1,0:T(8,128)(2,1)S(1)}, bf16[64,128,256]{2,1,0:T(8,128)(2,1)}, u32[]{:S(2)}) %copy-start.1) | copy-done | bytes 4194328
  2.8 0.7 copy-done.8
  3.5 0.7 copy-done.10
  4.2 3.5 %first_pack.1 = (bf16[4,128,256]{2,1,0:T(8,128)(2,1)S(1)}, bf16[4,128,256]{2,1,0:T(8,128)(2,1)S(1)}, bf16[4,128,256]{2,1,0:T(8,128)(2,1)S(1)}, s32[64]{0:T(128)S(1)}) custom-call(s32[64]{0:T(128)S(1)} %copy-done.10, s32[1024]{0:T(1024)S(1)} %copy-done.8, bf16[64,128,256]{2,1,0:T(8,128)(2,1)S(1)} %copy-done.1), custom_call_target="tpu_custom_call" | custom-call | tf_op jit(solution)/shard_map/first_pack/pallas_call | solution.py:138
  7.7 1.0 broadcast_add_fusion
  8.8 7.4 %constant_dynamic-update-slice_fusion.4 = (bf16[8,16,640]{2,1,0:T(8,128)(2,1)}, bf16[16,16,640]{2,1,0:T(8,128)(2,1)S(1)}, bf16[16,640]{1,0:T(8,128)(2,1)S(1)}) fusion(bf16[16,8192]{1,0:T(8,128)(2,1)S(1)} %add.176, bf16[640,8192]{1,0:T(8,128)(2,1)} %param.10), kind=kOutput, calls=%fused_computation.17 | convolution fusion | flops 167782400 | bytes 10809344 | tf_op jit(solution)/shard_map/dot_general | solution.py:452
  16.2 4.0 %collective-permute-start = (bf16[1,16,640]{2,1,0:T(8,128)(2,1)S(1)}, bf16[1,16,640]{2,1,0:T(8,128)(2,1)S(1)}, u32[]{:S(2)}, u32[]{:S(2)}) collective-permute-start(bf16[1,16,640]{2,1,0:T(8,128)(2,1)S(1)} %bitcast.47), channel_id=1, source_target_pairs={{0,8},{1,9},{2,10},{3,11},{4,12},{5,13},{6,14},{7,15},{8,0},{9,1},... | collective-permute-start | bytes 61448 | tf_op jit(solution)/shard_map/ppermute | solution.py:358
  20.3 1.6 collective-permute-start.1
  21.9 1.9 %collective-permute-start.5 = (bf16[4,128,256]{2,1,0:T(8,128)(2,1)S(1)}, bf16[4,128,256]{2,1,0:T(8,128)(2,1)S(1)}, u32[]{:S(2)}, u32[]{:S(2)}) collective-permute-start(bf16[4,128,256]{2,1,0:T(8,128)(2,1)S(1)} %get-tuple-element.37), channel_id=1, source_target_pairs={{0,8},{1,9},{2,10},{3,11},{4,12},{5,13},{6,14},{7,15},{8,0},{9,1},... | collective-permute-start | bytes 786440 | tf_op jit(solution)/shard_map/ppermute | solution.py:358
  23.8 1.9 %collective-permute-start.6 = (bf16[4,128,256]{2,1,0:T(8,128)(2,1)S(1)}, bf16[4,128,256]{2,1,0:T(8,128)(2,1)S(1)}, u32[]{:S(2)}, u32[]{:S(2)}) collective-permute-start(bf16[4,128,256]{2,1,0:T(8,128)(2,1)S(1)} %get-tuple-element.38), channel_id=1, source_target_pairs={{0,12},{1,13},{2,14},{3,15},{4,8},{5,9},{6,10},{7,11},{8,4},{9,5},... | collective-permute-start | bytes 786440 | tf_op jit(solution)/shard_map/ppermute | solution.py:358
  25.8 0.7 compare_select_fusion.3
  26.5 0.6 gather_fusion
  27.5 0.2 select_reduce_fusion
  27.7 0.2 convert_reduce_fusion
  27.9 0.1 fusion
  28.0 2.2 %copy-done.2 = bf16[64,128,256]{2,1,0:T(8,128)(2,1)S(1)} copy-done((bf16[64,128,256]{2,1,0:T(8,128)(2,1)S(1)}, bf16[64,128,256]{2,1,0:T(8,128)(2,1)}, u32[]{:S(2)}) %copy-start.2) | copy-done | bytes 4194328
  30.2 2.3 %next_pack.3 = (bf16[4,128,256]{2,1,0:T(8,128)(2,1)S(1)}, bf16[4,128,256]{2,1,0:T(8,128)(2,1)S(1)}, bf16[4,128,256]{2,1,0:T(8,128)(2,1)S(1)}, bf16[4,128,256]{2,1,0:T(8,128)(2,1)S(1)}) custom-call(s32[64]{0:T(128)S(1)} %get-tuple-element.34.refs_1_.order_ref, bf16[64,128,256]{2,1,0:T(8,128)(2,1)S(1)} %copy-done.2, ...), custom_call_target="tpu_custom_call" | custom-call | tf_op jit(solution)/shard_map/next_pack/pallas_call | solution.py:156
  32.7 0.6 collective-permute-start.10
  33.3 1.6 collective-permute-start.3
  34.9 0.6 constant_dynamic-update-slice_fusion.3
  35.5 0.6 constant_dynamic-update-slice_fusion.2
  36.1 0.6 constant_dynamic-update-slice_fusion.1
  36.7 1.2 collective-permute-done.3
  37.9 0.7 constant_dynamic-update-slice_fusion
  38.6 0.7 pad_maximum_fusion.4
  39.2 1.1 collective-permute-done.4
  40.3 4.3 %collective-permute-start.11 = (bf16[4,128,256]{2,1,0:T(8,128)(2,1)S(1)}, bf16[4,128,256]{2,1,0:T(8,128)(2,1)S(1)}, u32[]{:S(2)}, u32[]{:S(2)}) collective-permute-start(bf16[4,128,256]{2,1,0:T(8,128)(2,1)S(1)} %get-tuple-element.45), channel_id=1, source_target_pairs={{0,5},{1,4},{2,7},{3,6},{4,1},{5,0},{6,3},{7,2},{8,13},{9,12},{10,... | collective-permute-start | bytes 786440 | tf_op jit(solution)/shard_map/ppermute | solution.py:358
  44.6 1.2 gather_fusion.1
  45.8 0.1 select_reduce_fusion.1
  45.9 0.9 constant_dynamic-update-slice_fusion.5.rows_ref
  46.9 0.7 copy-done.13
  47.6 1.8 %own_rows.1 = (f32[4,16,128]{2,1,0:T(8,128)}, f32[8,256]{1,0:T(8,128)}) custom-call(bf16[16,16,640]{2,1,0:T(8,128)(2,1)} %copy-done.13, s32[8]{0:T(128)} %gather_fusion.1, s32[4]{0:T(128)} %get-tuple-element.69.request_ref, f32[8,128]{1,0:T(8,128)} %get-tuple-element.85.cosine_ref, f32[8,128]{1,0:T(8,128)} %get-tuple-element.86.sine_ref), custom_call_target="tpu_custom_call" | custom-call | tf_op jit(solution)/shard_map/own_rows/pallas_call | solution.py:344
  49.4 2.2 %copy-done.3 = bf16[64,128,256]{2,1,0:T(8,128)(2,1)S(1)} copy-done((bf16[64,128,256]{2,1,0:T(8,128)(2,1)S(1)}, bf16[64,128,256]{2,1,0:T(8,128)(2,1)}, u32[]{:S(2)}) %copy-start.3) | copy-done | bytes 4194328
  51.6 0.8 copy-done.4
  52.3 3.5 %next_pack.4 = (bf16[4,128,256]{2,1,0:T(8,128)(2,1)S(1)}, bf16[4,128,256]{2,1,0:T(8,128)(2,1)S(1)}, bf16[4,128,256]{2,1,0:T(8,128)(2,1)S(1)}, bf16[4,128,256]{2,1,0:T(8,128)(2,1)}, bf16[4,128,256]{2,1,0:T(8,128)(2,1)}) custom-call(s32[64]{0:T(128)S(1)} %get-tuple-element.34.refs_1_.order_ref, bf16[64,128,256]{2,1,0:T(8,128)(2,1)S(1)} %copy-done.3, ...), custom_call_target="tpu_custom_call" | custom-call | tf_op jit(solution)/shard_map/next_pack/pallas_call | solution.py:156
  56.0 3.5 %collective-permute-start.9 = (bf16[4,128,256]{2,1,0:T(8,128)(2,1)S(1)}, bf16[4,128,256]{2,1,0:T(8,128)(2,1)S(1)}, u32[]{:S(2)}, u32[]{:S(2)}) collective-permute-start(bf16[4,128,256]{2,1,0:T(8,128)(2,1)S(1)} %get-tuple-element.43), channel_id=1, source_target_pairs={{0,14},{1,15},{2,12},{3,13},{4,10},{5,11},{6,8},{7,9},{8,6},{9,7},... | collective-permute-start | bytes 786440 | tf_op jit(solution)/shard_map/ppermute | solution.py:358
  59.5 0.1 collective-permute-start.12
  59.6 2.8 %collective-permute-start.13 = (bf16[4,128,256]{2,1,0:T(8,128)(2,1)S(1)}, bf16[4,128,256]{2,1,0:T(8,128)(2,1)S(1)}, u32[]{:S(2)}, u32[]{:S(2)}) collective-permute-start(bf16[4,128,256]{2,1,0:T(8,128)(2,1)S(1)} %get-tuple-element.50), channel_id=1, source_target_pairs={{0,13},{1,12},{2,15},{3,14},{4,9},{5,8},{6,11},{7,10},{8,5},{9,4},... | collective-permute-start | bytes 786440 | tf_op jit(solution)/shard_map/ppermute | solution.py:358
  62.4 1.2 collective-permute-start.14
  63.6 0.1 select_reduce_fusion.2.refs_0_
  63.8 0.7 copy-done.6
  64.5 5.8 %place_pages.5 = (bf16[64,128,256]{2,1,0:T(8,128)(2,1)}, f32[4,16,128]{2,1,0:T(8,128)S(1)}, f32[4,16,128]{2,1,0:T(8,128)S(1)}) custom-call(s32[64]{0:T(128)S(1)} %select_reduce_fusion.2.refs_0_, s32[64]{0:T(128)S(1)} %get-tuple-element.34.refs_1_.order_ref, s32[4]{0:T(128)S(1)} %gather_fusion, f32[8,256]{1,0:T(8,128)S(1)} %copy-done.6, ...), custom_call_target="tpu_custom_call" | custom-call | tf_op jit(solution)/shard_map/place_pages/pallas_call | solution.py:298
  70.3 2.6 %next_pack.5 = (bf16[4,128,256]{2,1,0:T(8,128)(2,1)}, bf16[4,128,256]{2,1,0:T(8,128)(2,1)}, bf16[4,128,256]{2,1,0:T(8,128)(2,1)S(1)}) custom-call(s32[64]{0:T(128)S(1)} %get-tuple-element.34.refs_1_.order_ref, bf16[64,128,256]{2,1,0:T(8,128)(2,1)S(1)} %copy-done.3, f32[4,16,128]{2,1,0:T(8,128)S(1)} %get-tuple-element.40.refs_5_.after_ref), custom_call_target="tpu_custom_call" | custom-call | tf_op jit(solution)/shard_map/next_pack/pallas_call | solution.py:156
  73.0 15.4 %collective-permute-done.8.refs_7_ = bf16[4,128,256]{2,1,0:T(8,128)(2,1)S(1)} collective-permute-done((bf16[4,128,256]{2,1,0:T(8,128)(2,1)S(1)}, bf16[4,128,256]{2,1,0:T(8,128)(2,1)S(1)}, u32[]{:S(2)}, u32[]{:S(2)}) %collective-permute-start.8) | collective-permute-done | bytes 262176 | tf_op jit(solution)/shard_map/ppermute | solution.py:358
  88.4 1.5 collective-permute-start.16
  89.9 11.8 %collective-permute-done.12.refs_7_ = bf16[4,128,256]{2,1,0:T(8,128)(2,1)S(1)} collective-permute-done((bf16[4,128,256]{2,1,0:T(8,128)(2,1)S(1)}, bf16[4,128,256]{2,1,0:T(8,128)(2,1)S(1)}, u32[]{:S(2)}, u32[]{:S(2)}) %collective-permute-start.12) | collective-permute-done | bytes 262176 | tf_op jit(solution)/shard_map/ppermute | solution.py:358
  101.7 1.9 %collective-permute-start.18 = (bf16[4,128,256]{2,1,0:T(8,128)(2,1)}, bf16[4,128,256]{2,1,0:T(8,128)(2,1)S(1)}, u32[]{:S(2)}, u32[]{:S(2)}) collective-permute-start(bf16[4,128,256]{2,1,0:T(8,128)(2,1)} %get-tuple-element.58), channel_id=1, source_target_pairs={{0,15},{1,14},{2,13},{3,12},{4,11},{5,10},{6,9},{7,8},{8,7},{9,6},... | collective-permute-start | bytes 786440 | tf_op jit(solution)/shard_map/ppermute | solution.py:358
  103.6 0.8 gather_fusion.2
  104.4 5.8 %place_pages.6 = (bf16[64,128,256]{2,1,0:T(8,128)(2,1)}, f32[4,16,128]{2,1,0:T(8,128)S(1)}, f32[4,16,128]{2,1,0:T(8,128)S(1)}) custom-call(s32[64]{0:T(128)S(1)} %select_reduce_fusion.2.refs_0_, s32[64]{0:T(128)S(1)} %get-tuple-element.34.refs_1_.order_ref, s32[4]{0:T(128)S(1)} %gather_fusion, ...), custom_call_target="tpu_custom_call", output_to_operand_aliasing={{0}: (11, {})} | custom-call | tf_op jit(solution)/shard_map/place_pages/pallas_call | solution.py:298
  110.2 6.9 %place_pages.7 = (bf16[64,128,256]{2,1,0:T(8,128)(2,1)}, f32[4,16,128]{2,1,0:T(8,128)S(1)}, f32[4,16,128]{2,1,0:T(8,128)S(1)}) custom-call(s32[64]{0:T(128)S(1)} %select_reduce_fusion.2.refs_0_, s32[64]{0:T(128)S(1)} %get-tuple-element.34.refs_1_.order_ref, s32[4]{0:T(128)S(1)} %gather_fusion, ...), custom_call_target="tpu_custom_call", output_to_operand_aliasing={{0}: (12, {})} | custom-call | tf_op jit(solution)/shard_map/place_pages/pallas_call | solution.py:298
  117.1 5.9 %collective-permute-done.17.refs_7_ = bf16[4,128,256]{2,1,0:T(8,128)(2,1)S(1)} collective-permute-done((bf16[4,128,256]{2,1,0:T(8,128)(2,1)}, bf16[4,128,256]{2,1,0:T(8,128)(2,1)S(1)}, u32[]{:S(2)}, u32[]{:S(2)}) %collective-permute-start.17) | collective-permute-done | bytes 262176 | tf_op jit(solution)/shard_map/ppermute | solution.py:358
  123.0 3.6 %place_pages.8 = (bf16[64,128,256]{2,1,0:T(8,128)(2,1)}, f32[4,16,128]{2,1,0:T(8,128)S(1)}, f32[4,16,128]{2,1,0:T(8,128)S(1)}) custom-call(s32[64]{0:T(128)S(1)} %select_reduce_fusion.2.refs_0_, s32[64]{0:T(128)S(1)} %get-tuple-element.34.refs_1_.order_ref, s32[4]{0:T(128)S(1)} %gather_fusion, ...), custom_call_target="tpu_custom_call", output_to_operand_aliasing={{0}: (9, {})} | custom-call | tf_op jit(solution)/shard_map/place_pages/pallas_call | solution.py:298
  126.6 2.8 %place_pages.9 = (bf16[64,128,256]{2,1,0:T(8,128)(2,1)}, f32[4,16,128]{2,1,0:T(8,128)}, f32[4,16,128]{2,1,0:T(8,128)}, bf16[4,16,128]{2,1,0:T(8,128)(2,1)S(1)}) custom-call(s32[64]{0:T(128)S(1)} %select_reduce_fusion.2.refs_0_, s32[64]{0:T(128)S(1)} %get-tuple-element.34.refs_1_.order_ref, s32[4]{0:T(128)S(1)} %gather_fusion, ...), custom_call_target="tpu_custom_call", output_to_operand_aliasing={{0}: (8, {})} | custom-call | tf_op jit(solution)/shard_map/place_pages/pallas_call | solution.py:298
  129.4 12.3 %collective-permute-start.20 = (bf16[1,4,2,1024]{3,2,1,0:T(2,128)(2,1)S(1)}, bf16[1,4,2,1024]{3,2,1,0:T(2,128)(2,1)S(1)}, u32[]{:S(2)}, u32[]{:S(2)}) collective-permute-start(bf16[1,4,2,1024]{3,2,1,0:T(2,128)(2,1)S(1)} %broadcast_in_dim_reshape.4), channel_id=1, source_target_pairs={{0,8},{1,9},{2,10},{3,11},{4,12},{5,13},{6,14},{7,15},{8,0},{9,1},... | collective-permute-start | bytes 49160 | tf_op jit(solution)/shard_map/ppermute | solution.py:358
  141.7 1.7 %collective-permute-done.20 = bf16[1,4,2,1024]{3,2,1,0:T(2,128)(2,1)S(1)} collective-permute-done((bf16[1,4,2,1024]{3,2,1,0:T(2,128)(2,1)S(1)}, bf16[1,4,2,1024]{3,2,1,0:T(2,128)(2,1)S(1)}, u32[]{:S(2)}, u32[]{:S(2)}) %collective-permute-start.20) | collective-permute-done | bytes 16416 | tf_op jit(solution)/shard_map/ppermute | solution.py:358
  143.5 1.4 collective-permute-start.21
  144.9 2.6 %collective-permute-done.21 = bf16[2,4,2,1024]{3,2,1,0:T(2,128)(2,1)S(1)} collective-permute-done((bf16[2,4,2,1024]{3,2,1,0:T(2,128)(2,1)S(1)}, bf16[2,4,2,1024]{3,2,1,0:T(2,128)(2,1)S(1)}, u32[]{:S(2)}, u32[]{:S(2)}) %collective-permute-start.21) | collective-permute-done | bytes 32800 | tf_op jit(solution)/shard_map/ppermute | solution.py:358
  147.7 4.2 %collective-permute-done.22 = bf16[4,4,2,1024]{3,2,1,0:T(2,128)(2,1)S(1)} collective-permute-done((bf16[4,4,2,1024]{3,2,1,0:T(2,128)(2,1)S(1)}, bf16[4,4,2,1024]{3,2,1,0:T(2,128)(2,1)S(1)}, u32[]{:S(2)}, u32[]{:S(2)}) %collective-permute-start.22) | collective-permute-done | bytes 65568 | tf_op jit(solution)/shard_map/ppermute | solution.py:358
  151.9 0.2 pad_maximum_fusion
  152.3 1.2 collective-permute-done.23
  153.6 1.1 gather_fusion.3
  154.8 0.2 copy.20
  155.0 5.6 %convolution_convert_fusion.1 = bf16[16,512]{1,0:T(8,128)(2,1)S(1)} fusion(bf16[16,8192]{1,0:T(8,128)(2,1)S(1)} %bitcast.52, bf16[512,8192]{1,0:T(8,128)(2,1)} %param.11), kind=kOutput, calls=%fused_computation.5 | convolution fusion | flops 134225920 | bytes 8667136 | tf_op jit(solution)/shard_map/dot_general | solution.py:537
  160.6 0.6 reshape.250
  (73 shorter events, 1.5 us)
Async XLA Ops:
  0.6 25.8 %copy-start = (s32[8]{0:T(128)S(1)}, s32[8]{0:T(128)}, u32[]{:S(2)}) copy-start(s32[8]{0:T(128)} %param.13) | copy-start | bytes 100
  0.6 2.2 %copy-start.1 = (bf16[64,128,256]{2,1,0:T(8,128)(2,1)S(1)}, bf16[64,128,256]{2,1,0:T(8,128)(2,1)}, u32[]{:S(2)}) copy-start(bf16[64,128,256]{2,1,0:T(8,128)(2,1)} %pages_ref.7) | copy-start | bytes 12582916
  2.8 0.7 copy-start.8
  3.5 0.7 copy-start.10
  4.2 21.5 %copy-start.11 = (s32[64]{0:T(128)S(1)}, s32[64]{0:T(128)}, u32[]{:S(2)}) copy-start(s32[64]{0:T(128)} %units_ref.1) | copy-start | bytes 772
  4.2 23.3 %copy-start.9 = (s32[1024]{0:T(1024)S(1)}, s32[1024]{0:T(1024)}, u32[]{:S(2)}) copy-start(s32[1024]{0:T(1024)} %old_ref.1) | copy-start | bytes 12292
  8.7 35.9 %copy-start.12 = (s32[16]{0:T(128)S(1)}, s32[16]{0:T(128)}, u32[]{:S(2)}) copy-start(s32[16]{0:T(128)} %constant.93.clone) | copy-start | bytes 196
  16.2 16.4 %collective-permute-start = (bf16[1,16,640]{2,1,0:T(8,128)(2,1)S(1)}, bf16[1,16,640]{2,1,0:T(8,128)(2,1)S(1)}, u32[]{:S(2)}, u32[]{:S(2)}) collective-permute-start(bf16[1,16,640]{2,1,0:T(8,128)(2,1)S(1)} %bitcast.47), channel_id=1, source_target_pairs={{0,8},{1,9},{2,10},{3,11},{4,12},{5,13},{6,14},{7,15},{8,0},{9,1},... | collective-permute-start | bytes 61448 | tf_op jit(solution)/shard_map/ppermute | solution.py:358
  20.3 12.4 %collective-permute-start.1 = (bf16[1,16,640]{2,1,0:T(8,128)(2,1)S(1)}, bf16[1,16,640]{2,1,0:T(8,128)(2,1)S(1)}, u32[]{:S(2)}, u32[]{:S(2)}) collective-permute-start(bf16[1,16,640]{2,1,0:T(8,128)(2,1)S(1)} %bitcast.48), channel_id=1, source_target_pairs={{0,4},{1,5},{2,6},{3,7},{4,0},{5,1},{6,2},{7,3},{8,12},{9,13},{10,... | collective-permute-start | bytes 61448 | tf_op jit(solution)/shard_map/ppermute | solution.py:358
  21.9 11.4 %collective-permute-start.2 = (bf16[1,16,640]{2,1,0:T(8,128)(2,1)S(1)}, bf16[1,16,640]{2,1,0:T(8,128)(2,1)S(1)}, u32[]{:S(2)}, u32[]{:S(2)}) collective-permute-start(bf16[1,16,640]{2,1,0:T(8,128)(2,1)S(1)} %bitcast.49), channel_id=1, source_target_pairs={{0,12},{1,13},{2,14},{3,15},{4,8},{5,9},{6,10},{7,11},{8,4},{9,5},... | collective-permute-start | bytes 61448 | tf_op jit(solution)/shard_map/ppermute | solution.py:358
  21.9 34.0 %collective-permute-start.5 = (bf16[4,128,256]{2,1,0:T(8,128)(2,1)S(1)}, bf16[4,128,256]{2,1,0:T(8,128)(2,1)S(1)}, u32[]{:S(2)}, u32[]{:S(2)}) collective-permute-start(bf16[4,128,256]{2,1,0:T(8,128)(2,1)S(1)} %get-tuple-element.37), channel_id=1, source_target_pairs={{0,8},{1,9},{2,10},{3,11},{4,12},{5,13},{6,14},{7,15},{8,0},{9,1},... | collective-permute-start | bytes 786440 | tf_op jit(solution)/shard_map/ppermute | solution.py:358
  23.8 32.2 %collective-permute-start.6 = (bf16[4,128,256]{2,1,0:T(8,128)(2,1)S(1)}, bf16[4,128,256]{2,1,0:T(8,128)(2,1)S(1)}, u32[]{:S(2)}, u32[]{:S(2)}) collective-permute-start(bf16[4,128,256]{2,1,0:T(8,128)(2,1)S(1)} %get-tuple-element.38), channel_id=1, source_target_pairs={{0,12},{1,13},{2,14},{3,15},{4,8},{5,9},{6,10},{7,11},{8,4},{9,5},... | collective-permute-start | bytes 786440 | tf_op jit(solution)/shard_map/ppermute | solution.py:358
  28.0 2.2 %copy-start.2 = (bf16[64,128,256]{2,1,0:T(8,128)(2,1)S(1)}, bf16[64,128,256]{2,1,0:T(8,128)(2,1)}, u32[]{:S(2)}) copy-start(bf16[64,128,256]{2,1,0:T(8,128)(2,1)} %pages_ref.7) | copy-start | bytes 12582916
  32.6 26.8 %collective-permute-start.7 = (bf16[4,128,256]{2,1,0:T(8,128)(2,1)S(1)}, bf16[4,128,256]{2,1,0:T(8,128)(2,1)S(1)}, u32[]{:S(2)}, u32[]{:S(2)}) collective-permute-start(bf16[4,128,256]{2,1,0:T(8,128)(2,1)S(1)} %get-tuple-element.39), channel_id=1, source_target_pairs={{0,1},{1,0},{2,3},{3,2},{4,5},{5,4},{6,7},{7,6},{8,9},{9,8},{10,11... | collective-permute-start | bytes 786440 | tf_op jit(solution)/shard_map/ppermute | solution.py:358
  32.7 26.9 %collective-permute-start.10 = (bf16[4,128,256]{2,1,0:T(8,128)(2,1)S(1)}, bf16[4,128,256]{2,1,0:T(8,128)(2,1)S(1)}, u32[]{:S(2)}, u32[]{:S(2)}) collective-permute-start(bf16[4,128,256]{2,1,0:T(8,128)(2,1)S(1)} %get-tuple-element.44), channel_id=1, source_target_pairs={{0,4},{1,5},{2,6},{3,7},{4,0},{5,1},{6,2},{7,3},{8,12},{9,13},{10,... | collective-permute-start | bytes 786440 | tf_op jit(solution)/shard_map/ppermute | solution.py:358
  33.3 4.6 %collective-permute-start.3 = (bf16[4,16,640]{2,1,0:T(8,128)(2,1)S(1)}, bf16[4,16,640]{2,1,0:T(8,128)(2,1)S(1)}, u32[]{:S(2)}, u32[]{:S(2)}) collective-permute-start(bf16[4,16,640]{2,1,0:T(8,128)(2,1)S(1)} %pad_maximum_fusion.1), channel_id=1, source_target_pairs={{0,2},{1,3},{2,0},{3,1},{4,6},{5,7},{6,4},{7,5},{8,10},{9,11},{10,... | collective-permute-start | bytes 245768 | tf_op jit(solution)/shard_map/ppermute | solution.py:358
  38.6 1.7 %collective-permute-start.4 = (bf16[8,16,640]{2,1,0:T(8,128)(2,1)}, bf16[8,16,640]{2,1,0:T(8,128)(2,1)}, u32[]{:S(2)}, u32[]{:S(2)}) collective-permute-start(bf16[8,16,640]{2,1,0:T(8,128)(2,1)} %get-tuple-element.70), channel_id=1, source_target_pairs={{0,1},{1,0},{2,3},{3,2},{4,5},{5,4},{6,7},{7,6},{8,9},{9,8},{10,11... | collective-permute-start | bytes 491528 | tf_op jit(solution)/shard_map/ppermute | solution.py:358
  40.3 22.1 %collective-permute-start.11 = (bf16[4,128,256]{2,1,0:T(8,128)(2,1)S(1)}, bf16[4,128,256]{2,1,0:T(8,128)(2,1)S(1)}, u32[]{:S(2)}, u32[]{:S(2)}) collective-permute-start(bf16[4,128,256]{2,1,0:T(8,128)(2,1)S(1)} %get-tuple-element.45), channel_id=1, source_target_pairs={{0,5},{1,4},{2,7},{3,6},{4,1},{5,0},{6,3},{7,2},{8,13},{9,12},{10,... | collective-permute-start | bytes 786440 | tf_op jit(solution)/shard_map/ppermute | solution.py:358
  46.9 0.7 copy-start.13
  49.4 2.2 %copy-start.3 = (bf16[64,128,256]{2,1,0:T(8,128)(2,1)S(1)}, bf16[64,128,256]{2,1,0:T(8,128)(2,1)}, u32[]{:S(2)}) copy-start(bf16[64,128,256]{2,1,0:T(8,128)(2,1)} %pages_ref.7) | copy-start | bytes 12582916
  51.6 0.8 copy-start.4
  52.3 52.0 %copy-start.5 = (f32[4,16,128]{2,1,0:T(8,128)S(1)}, f32[4,16,128]{2,1,0:T(8,128)}, u32[]{:S(2)}) copy-start(f32[4,16,128]{2,1,0:T(8,128)} %get-tuple-element.36.refs_4_.after_ref) | copy-start | bytes 98308
  52.3 52.0 %copy-start.7 = (f32[8,256]{1,0:T(8,128)S(1)}, f32[8,256]{1,0:T(8,128)}, u32[]{:S(2)}) copy-start(f32[8,256]{1,0:T(8,128)} %get-tuple-element.35.refs_3_) | copy-start | bytes 24580
  55.9 32.5 %collective-permute-start.8 = (bf16[4,128,256]{2,1,0:T(8,128)(2,1)S(1)}, bf16[4,128,256]{2,1,0:T(8,128)(2,1)S(1)}, u32[]{:S(2)}, u32[]{:S(2)}) collective-permute-start(bf16[4,128,256]{2,1,0:T(8,128)(2,1)S(1)} %get-tuple-element.42), channel_id=1, source_target_pairs={{0,10},{1,11},{2,8},{3,9},{4,14},{5,15},{6,12},{7,13},{8,2},{9,3},... | collective-permute-start | bytes 786440 | tf_op jit(solution)/shard_map/ppermute | solution.py:358
  56.0 32.4 %collective-permute-start.9 = (bf16[4,128,256]{2,1,0:T(8,128)(2,1)S(1)}, bf16[4,128,256]{2,1,0:T(8,128)(2,1)S(1)}, u32[]{:S(2)}, u32[]{:S(2)}) collective-permute-start(bf16[4,128,256]{2,1,0:T(8,128)(2,1)S(1)} %get-tuple-element.43), channel_id=1, source_target_pairs={{0,14},{1,15},{2,12},{3,13},{4,10},{5,11},{6,8},{7,9},{8,6},{9,7},... | collective-permute-start | bytes 786440 | tf_op jit(solution)/shard_map/ppermute | solution.py:358
  59.5 42.2 %collective-permute-start.12 = (bf16[4,128,256]{2,1,0:T(8,128)(2,1)S(1)}, bf16[4,128,256]{2,1,0:T(8,128)(2,1)S(1)}, u32[]{:S(2)}, u32[]{:S(2)}) collective-permute-start(bf16[4,128,256]{2,1,0:T(8,128)(2,1)S(1)} %get-tuple-element.49), channel_id=1, source_target_pairs={{0,9},{1,8},{2,11},{3,10},{4,13},{5,12},{6,15},{7,14},{8,1},{9,0},... | collective-permute-start | bytes 786440 | tf_op jit(solution)/shard_map/ppermute | solution.py:358
  59.6 42.1 %collective-permute-start.13 = (bf16[4,128,256]{2,1,0:T(8,128)(2,1)S(1)}, bf16[4,128,256]{2,1,0:T(8,128)(2,1)S(1)}, u32[]{:S(2)}, u32[]{:S(2)}) collective-permute-start(bf16[4,128,256]{2,1,0:T(8,128)(2,1)S(1)} %get-tuple-element.50), channel_id=1, source_target_pairs={{0,13},{1,12},{2,15},{3,14},{4,9},{5,8},{6,11},{7,10},{8,5},{9,4},... | collective-permute-start | bytes 786440 | tf_op jit(solution)/shard_map/ppermute | solution.py:358
  62.4 41.1 %collective-permute-start.14 = (bf16[4,128,256]{2,1,0:T(8,128)(2,1)S(1)}, bf16[4,128,256]{2,1,0:T(8,128)(2,1)S(1)}, u32[]{:S(2)}, u32[]{:S(2)}) collective-permute-start(bf16[4,128,256]{2,1,0:T(8,128)(2,1)S(1)} %get-tuple-element.51), channel_id=1, source_target_pairs={{0,6},{1,7},{2,4},{3,5},{4,2},{5,3},{6,0},{7,1},{8,14},{9,15},{10,... | collective-permute-start | bytes 786440 | tf_op jit(solution)/shard_map/ppermute | solution.py:358
  63.8 0.7 copy-start.6
  88.4 21.8 %collective-permute-start.15 = (bf16[4,128,256]{2,1,0:T(8,128)(2,1)}, bf16[4,128,256]{2,1,0:T(8,128)(2,1)S(1)}, u32[]{:S(2)}, u32[]{:S(2)}) collective-permute-start(bf16[4,128,256]{2,1,0:T(8,128)(2,1)} %get-tuple-element.52), channel_id=1, source_target_pairs={{0,7},{1,6},{2,5},{3,4},{4,3},{5,2},{6,1},{7,0},{8,15},{9,14},{10,... | collective-permute-start | bytes 786440 | tf_op jit(solution)/shard_map/ppermute | solution.py:358
  88.4 21.8 %collective-permute-start.16 = (bf16[4,128,256]{2,1,0:T(8,128)(2,1)}, bf16[4,128,256]{2,1,0:T(8,128)(2,1)S(1)}, u32[]{:S(2)}, u32[]{:S(2)}) collective-permute-start(bf16[4,128,256]{2,1,0:T(8,128)(2,1)} %get-tuple-element.53), channel_id=1, source_target_pairs={{0,2},{1,3},{2,0},{3,1},{4,6},{5,7},{6,4},{7,5},{8,10},{9,11},{10,... | collective-permute-start | bytes 786440 | tf_op jit(solution)/shard_map/ppermute | solution.py:358
  101.7 21.3 %collective-permute-start.17 = (bf16[4,128,256]{2,1,0:T(8,128)(2,1)}, bf16[4,128,256]{2,1,0:T(8,128)(2,1)S(1)}, u32[]{:S(2)}, u32[]{:S(2)}) collective-permute-start(bf16[4,128,256]{2,1,0:T(8,128)(2,1)} %get-tuple-element.57), channel_id=1, source_target_pairs={{0,11},{1,10},{2,9},{3,8},{4,15},{5,14},{6,13},{7,12},{8,3},{9,2},... | collective-permute-start | bytes 786440 | tf_op jit(solution)/shard_map/ppermute | solution.py:358
  101.7 21.3 %collective-permute-start.18 = (bf16[4,128,256]{2,1,0:T(8,128)(2,1)}, bf16[4,128,256]{2,1,0:T(8,128)(2,1)S(1)}, u32[]{:S(2)}, u32[]{:S(2)}) collective-permute-start(bf16[4,128,256]{2,1,0:T(8,128)(2,1)} %get-tuple-element.58), channel_id=1, source_target_pairs={{0,15},{1,14},{2,13},{3,12},{4,11},{5,10},{6,9},{7,8},{8,7},{9,6},... | collective-permute-start | bytes 786440 | tf_op jit(solution)/shard_map/ppermute | solution.py:358
  103.6 23.0 %collective-permute-start.19 = (bf16[4,128,256]{2,1,0:T(8,128)(2,1)S(1)}, bf16[4,128,256]{2,1,0:T(8,128)(2,1)S(1)}, u32[]{:S(2)}, u32[]{:S(2)}) collective-permute-start(bf16[4,128,256]{2,1,0:T(8,128)(2,1)S(1)} %get-tuple-element.62), channel_id=1, source_target_pairs={{0,3},{1,2},{2,1},{3,0},{4,7},{5,6},{6,5},{7,4},{8,11},{9,10},{10,... | collective-permute-start | bytes 786440 | tf_op jit(solution)/shard_map/ppermute | solution.py:358
  129.4 14.1 %collective-permute-start.20 = (bf16[1,4,2,1024]{3,2,1,0:T(2,128)(2,1)S(1)}, bf16[1,4,2,1024]{3,2,1,0:T(2,128)(2,1)S(1)}, u32[]{:S(2)}, u32[]{:S(2)}) collective-permute-start(bf16[1,4,2,1024]{3,2,1,0:T(2,128)(2,1)S(1)} %broadcast_in_dim_reshape.4), channel_id=1, source_target_pairs={{0,8},{1,9},{2,10},{3,11},{4,12},{5,13},{6,14},{7,15},{8,0},{9,1},... | collective-permute-start | bytes 49160 | tf_op jit(solution)/shard_map/ppermute | solution.py:358
  143.5 4.0 %collective-permute-start.21 = (bf16[2,4,2,1024]{3,2,1,0:T(2,128)(2,1)S(1)}, bf16[2,4,2,1024]{3,2,1,0:T(2,128)(2,1)S(1)}, u32[]{:S(2)}, u32[]{:S(2)}) collective-permute-start(bf16[2,4,2,1024]{3,2,1,0:T(2,128)(2,1)S(1)} %pad_maximum_fusion.3), channel_id=1, source_target_pairs={{0,4},{1,5},{2,6},{3,7},{4,0},{5,1},{6,2},{7,3},{8,12},{9,13},{10,... | collective-permute-start | bytes 98312 | tf_op jit(solution)/shard_map/ppermute | solution.py:358
  147.6 4.3 %collective-permute-start.22 = (bf16[4,4,2,1024]{3,2,1,0:T(2,128)(2,1)S(1)}, bf16[4,4,2,1024]{3,2,1,0:T(2,128)(2,1)S(1)}, u32[]{:S(2)}, u32[]{:S(2)}) collective-permute-start(bf16[4,4,2,1024]{3,2,1,0:T(2,128)(2,1)S(1)} %pad_maximum_fusion.2), channel_id=1, source_target_pairs={{0,2},{1,3},{2,0},{3,1},{4,6},{5,7},{6,4},{7,5},{8,10},{9,11},{10,... | collective-permute-start | bytes 196616 | tf_op jit(solution)/shard_map/ppermute | solution.py:358
  152.1 1.4 collective-permute-start.23

commit v3 on v2

--- a/solution.py
+++ b/solution.py
@@ -18,7 +18,7 @@
 GROUP = HEADS // KVH
 QROWS = 2 * GROUP
 PER_UNIT = MAXCTX // PAGE
-VMEM_LIMIT = 32 * 1024 * 1024
+VMEM_LIMIT = 56 * 1024 * 1024
 
 rope_base = 10000.0
 
@@ -84,26 +84,25 @@
     lax.fori_loop(0, pages_dev, assign, 0, unroll=8)
 
 
-def move_pages(capacity, keys, order_ref, pages_ref, outs, stage, load_sem, store_sem):
-    loads, stores = [], []
-    for n, key in enumerate(keys):
-        for r in range(capacity):
+def move_pages(capacity, items, order_ref, pages_ref, outs, stage, load_sem, store_sem):
+    loads, stores, slot = [], [], 0
+    for key, first, count in items:
+        for r in range(first, first + count):
             copy = pltpu.make_async_copy(
-                pages_ref.at[order_ref[key * capacity + r]],
-                stage.at[n * capacity + r],
-                load_sem.at[n * capacity + r],
+                pages_ref.at[order_ref[key * capacity + r]], stage.at[slot], load_sem.at[slot]
             )
             copy.start()
             loads.append(copy)
-    for n, key in enumerate(keys):
-        for r in range(capacity):
-            loads[n * capacity + r].wait()
-        target = outs[n] if len(outs) > 1 else outs[0].at[pl.ds(n * capacity, capacity)]
-        copy = pltpu.make_async_copy(
-            stage.at[pl.ds(n * capacity, capacity)], target, store_sem.at[n]
-        )
+            slot += 1
+    slot = 0
+    for n, (key, first, count) in enumerate(items):
+        for copy in loads[slot : slot + count]:
+            copy.wait()
+        target = outs[n] if len(outs) > 1 else outs[0].at[pl.ds(slot, count)]
+        copy = pltpu.make_async_copy(stage.at[pl.ds(slot, count)], target, store_sem.at[n])
         copy.start()
         stores.append(copy)
+        slot += count
     for copy in stores:
         copy.wait()
 
@@ -130,11 +129,12 @@
 
 
 def first_pack(new_units, old_pages, pages, devices, capacity, keys, relative):
-    chunk = (capacity,) + pages.shape[1:]
+    shape = pages.shape[1:]
+    total = sum(count for _, _, count in keys)
     if relative:
-        outs = [jax.ShapeDtypeStruct(chunk, pages.dtype) for _ in keys]
+        outs = [jax.ShapeDtypeStruct((count,) + shape, pages.dtype) for _, _, count in keys]
     else:
-        outs = [jax.ShapeDtypeStruct((len(keys) * capacity,) + chunk[1:], pages.dtype)]
+        outs = [jax.ShapeDtypeStruct((total,) + shape, pages.dtype)]
     result = pl.pallas_call(
         functools.partial(first_pack_kernel, devices, capacity, keys, relative),
         out_shape=tuple(outs) + (jax.ShapeDtypeStruct((devices * capacity,), jnp.int32),),
@@ -144,7 +144,7 @@
             pltpu.SMEM(new_units.shape, jnp.int32),
             pltpu.SMEM((devices,), jnp.int32),
         ]
-        + pack_scratch(len(keys) * capacity, pages),
+        + pack_scratch(total, pages),
         compiler_params=pltpu.CompilerParams(vmem_limit_bytes=VMEM_LIMIT),
         name="first_pack",
     )(new_units, old_pages, pages)
@@ -152,13 +152,16 @@
 
 
 def next_pack(order, pages, after, capacity, keys):
-    chunk = (capacity,) + pages.shape[1:]
+    shape = pages.shape[1:]
+    total = sum(count for _, _, count in keys)
     return pl.pallas_call(
         functools.partial(next_pack_kernel, capacity, keys),
-        out_shape=tuple(jax.ShapeDtypeStruct(chunk, pages.dtype) for _ in keys),
+        out_shape=tuple(
+            jax.ShapeDtypeStruct((count,) + shape, pages.dtype) for _, _, count in keys
+        ),
         in_specs=[smem_spec(), any_spec(), any_spec()],
         out_specs=tuple(any_spec() for _ in keys),
-        scratch_shapes=pack_scratch(len(keys) * capacity, pages),
+        scratch_shapes=pack_scratch(total, pages),
         compiler_params=pltpu.CompilerParams(vmem_limit_bytes=VMEM_LIMIT),
         name="next_pack",
     )(order, pages, after)
@@ -374,18 +377,21 @@
     return values, span
 
 
-def exchange_plan(devices):
+def exchange_plan(devices, capacity):
     half = devices // 2
     far = sorted(range(half, devices), key=lambda k: (k & 1, k & 2, k))
     across = [k for k in range(1, half) if k >= half // 2]
     beside = [k for k in range(1, half) if k < half // 2]
+    whole = lambda keys: [(k, 0, capacity) for k in keys]
     if devices < 16:
-        return [far + across + beside]
+        return [whole(far + across + beside)]
+    cut = max(1, capacity // 2)
+    head = [(far[0], 0, cut)] + [(far[0], cut, capacity - cut)] * (capacity > cut)
     return [
-        far[:2] + beside[:1],
-        far[2:4] + across[:2],
-        far[4:6] + across[2:] + beside[1:2],
-        far[6:] + beside[2:],
+        head + whole(far[1:2] + beside[:1]),
+        whole(far[2:4] + across[:2]),
+        whole(far[4:6] + across[2:] + beside[1:2]),
+        whole(beside[2:] + far[6:]),
     ]
 
 
@@ -400,13 +406,13 @@
     pairwise = devices <= 16 and devices & (devices - 1) == 0
 
     if pairwise:
-        plan = exchange_plan(devices)
+        plan = exchange_plan(devices, capacity)
         chunks, order = first_pack(
             new_units, old_pages, cache_pages, devices, capacity, plan[0], True
         )
-        moved = [swap(c, k, devices) for c, k in zip(chunks, plan[0])]
+        moved = [swap(c, k[0], devices) for c, k in zip(chunks, plan[0])]
     else:
-        keys = list(range(devices))
+        keys = [(k, 0, capacity) for k in range(devices)]
         (packed,), order = first_pack(
             new_units, old_pages, cache_pages, devices, capacity, keys, False
         )
@@ -448,7 +454,8 @@
         table = source_dev * capacity + rank
 
     flat_rows = hidden_states.reshape(requests * 2, D)
-    flat_rows = flat_rows + jnp.minimum(order[0], 0).astype(jnp.bfloat16)
+    if pairwise:
+        flat_rows, _ = lax.optimization_barrier((flat_rows, moved[0]))
     own_part = lax.dot_general(
         flat_rows, qkv_weight, (((1,), (1,)), ((), ())), preferred_element_type=jnp.float32
     ).astype(jnp.bfloat16)
@@ -465,16 +472,18 @@
         new_cache, sums = None, None
         if len(plan) > 1:
             chunks = next_pack(order, cache_pages, own_part, capacity, plan[1])
-            moved += [swap(c, k, devices) for c, k in zip(chunks, plan[1])]
-            chunks = next_pack(order, cache_pages, queries, capacity, plan[2])
-            moved += [swap(c, k, devices) for c, k in zip(chunks, plan[2])]
+            moved += [swap(c, k[0], devices) for c, k in zip(chunks, plan[1])]
+            chunks = next_pack(order, cache_pages, moved[2], capacity, plan[2])
+            moved += [swap(c, k[0], devices) for c, k in zip(chunks, plan[2])]
         at = 0
         keys = sum(plan, [])
         groups = [len(p) for p in plan[:-1]] + [len(plan[-1]) - 1, 1]
         for step, size in enumerate(groups):
             entries, sources = [], []
-            for key, array in zip(keys[at : at + size], moved[at : at + size]):
-                entries += [(len(sources), r, (key * capacity + r,)) for r in range(capacity)]
+            for (key, low, count), array in zip(keys[at : at + size], moved[at : at + size]):
+                entries += [
+                    (len(sources), r, (key * capacity + low + r,)) for r in range(count)
+                ]
                 sources.append(array)
             at += size
             if step == 0:
@@ -494,7 +503,7 @@
             )
             if step == 0 and len(plan) > 1:
                 chunks = next_pack(order, cache_pages, sums[0], capacity, plan[3])
-                moved += [swap(c, k, devices) for c, k in zip(chunks, plan[3])]
+                moved += [swap(c, k[0], devices) for c, k in zip(chunks, plan[3])]
     else:
         rows = lax.all_gather(own_part, "tp", axis=1, tiled=True)
         rows = rows.reshape(requests, 2, KVH, GROUP + 2, HD)

time: 162 us -> 147 us (0.907)
  local copies, waits for them, and re-layouts: 18.7 us -> 9.82 us
  waiting for transfers between devices: 45.1 us -> 37.6 us
  starting transfers between devices: 41 us -> 36.9 us
  Pallas kernels: 38.6 us -> 41.1 us
  other arithmetic: 3.73 us -> 6.07 us
    unnamed x36 -> x56, local copies, waits for them, and re-layouts: 12.2 us -> 3.25 us
    ppermute x24 -> x25, waiting for transfers between devices: 45.1 us -> 37.6 us  [swap(): return lax.ppermute(values, 'tp', [(i, i ^ key) for i in range(devices)])]
    ppermute x24 -> x25, starting transfers between devices: 41 us -> 36.9 us  [swap(): return lax.ppermute(values, 'tp', [(i, i ^ key) for i in range(devices)])]
  transfers between devices with their start and end apart: 24 -> 25, of which waited for: 9 -> 9; matrix products, arithmetic and copies ran while one was open for 5% -> 11% of each run, Pallas kernels for 20% -> 23%
where the time goes in v3:
time: 147 us; the launch traced here: 145 us
  Pallas kernels  41.1 us (28%)
  waiting for transfers between devices  37.6 us (26%)
  starting transfers between devices  36.9 us (25%)
  matrix products  12.5 us (9%)
  local copies, waits for them, and re-layouts  9.82 us (7%)
  other arithmetic  6.07 us (4%)
    ppermute x25, waiting for transfers between devices, swap(): return lax.ppermute(values, 'tp', [(i, i ^ key) for i in range(devices)])  37.6 us
    ppermute x25, starting transfers between devices, swap(): return lax.ppermute(values, 'tp', [(i, i ^ key) for i in range(devices)])  36.9 us
    pallas_call x5, Pallas kernels, place_pages(): pl.pallas_call(functools.partial(place_kernel, entries, started, finish),...  26.2 us
    pallas_call x3, Pallas kernels, next_pack(): pl.pallas_call(functools.partial(next_pack_kernel, capacity, keys), out_s...  8.7 us
    dot_general x1, matrix products, body(): lax.dot_general(flat_rows, qkv_weight, (((1,), (1,)), ((), ())), preferre...  6.83 us
    dot_general x1, matrix products, body(): lax.dot_general(logical, out_weight, (((1,), (1,)), ((), ())), preferred_...  5.64 us
    pallas_call x1, Pallas kernels, first_pack(): pl.pallas_call(functools.partial(first_pack_kernel, devices, capacity, ke...  4.4 us
    unnamed x56, local copies, waits for them, and re-layouts  3.25 us
  transfers between devices with their start and end apart: 25, of which 9 were waited for; matrix products, arithmetic and copies ran while one was open for 11% of the time, Pallas kernels for 23%

profile of v3, /device:TPU:0, one launch (start us, length us, event | category | flops | bytes accessed | tf_op | source)
XLA Modules:
  0.0 145.1 jit_solution(2795577928175781752)
XLA Ops:
  0.7 4.4 %first_pack.1 = (bf16[2,128,256]{2,1,0:T(8,128)(2,1)}, bf16[2,128,256]{2,1,0:T(8,128)(2,1)}, bf16[4,128,256]{2,1,0:T(8,128)(2,1)}, bf16[4,128,256]{2,1,0:T(8,128)(2,1)}, s32[64]{0:T(128)}) custom-call(s32[64]{0:T(128)} %units_ref.1, s32[1024]{0:T(1024)} %old_ref.1, bf16[64,128,256]{2,1,0:T(8,128)(2,1)} %pages_ref.7), custom_call_target="tpu_custom_call" | custom-call | tf_op jit(solution)/shard_map/first_pack/pallas_call | solution.py:138
  5.1 4.1 %collective-permute-start = (bf16[2,128,256]{2,1,0:T(8,128)(2,1)}, bf16[2,128,256]{2,1,0:T(8,128)(2,1)S(1)}, u32[]{:S(2)}, u32[]{:S(2)}) collective-permute-start(bf16[2,128,256]{2,1,0:T(8,128)(2,1)} %get-tuple-element.37), channel_id=1, source_target_pairs={{0,8},{1,9},{2,10},{3,11},{4,12},{5,13},{6,14},{7,15},{8,0},{9,1},... | collective-permute-start | bytes 393224 | tf_op jit(solution)/shard_map/ppermute | solution.py:361
  9.2 1.3 collective-permute-start.7
  10.5 1.1 reshape.244
  11.6 0.7 fusion.2
  12.3 1.3 compare_select_fusion.3
  13.7 0.6 gather_fusion
  14.8 0.9 select_reduce_fusion
  15.7 0.2 convert_reduce_fusion
  15.9 0.1 fusion
  16.0 6.1 %collective-permute-done.refs_5_ = bf16[2,128,256]{2,1,0:T(8,128)(2,1)S(1)} collective-permute-done((bf16[2,128,256]{2,1,0:T(8,128)(2,1)}, bf16[2,128,256]{2,1,0:T(8,128)(2,1)S(1)}, u32[]{:S(2)}, u32[]{:S(2)}) %collective-permute-start) | collective-permute-done | bytes 131104 | tf_op jit(solution)/shard_map/ppermute | solution.py:361
  22.1 6.8 %constant_dynamic-update-slice_fusion.4 = (bf16[8,16,640]{2,1,0:T(8,128)(2,1)S(1)}, bf16[16,16,640]{2,1,0:T(8,128)(2,1)S(1)}, bf16[16,640]{1,0:T(8,128)(2,1)S(1)}) fusion(bf16[16,8192]{1,0:T(8,128)(2,1)S(1)} %reshape.244, bf16[640,8192]{1,0:T(8,128)(2,1)} %param.10), kind=kOutput, calls=%fused_computation.16 | convolution fusion | flops 167782400 | bytes 10809344 | tf_op jit(solution)/shard_map/dot_general | solution.py:459
  29.0 3.4 %collective-permute-start.2 = (bf16[1,16,640]{2,1,0:T(8,128)(2,1)S(1)}, bf16[1,16,640]{2,1,0:T(8,128)(2,1)S(1)}, u32[]{:S(2)}, u32[]{:S(2)}) collective-permute-start(bf16[1,16,640]{2,1,0:T(8,128)(2,1)S(1)} %bitcast.48), channel_id=1, source_target_pairs={{0,4},{1,5},{2,6},{3,7},{4,0},{5,1},{6,2},{7,3},{8,12},{9,13},{10,... | collective-permute-start | bytes 61448 | tf_op jit(solution)/shard_map/ppermute | solution.py:361
  32.4 1.0 collective-permute-start.3
  33.4 0.1 select_reduce_fusion.1
  33.5 2.9 %next_pack.3 = (bf16[4,128,256]{2,1,0:T(8,128)(2,1)}, bf16[4,128,256]{2,1,0:T(8,128)(2,1)}, bf16[4,128,256]{2,1,0:T(8,128)(2,1)}, bf16[4,128,256]{2,1,0:T(8,128)(2,1)}) custom-call(s32[64]{0:T(128)} %get-tuple-element.36.refs_1_.order_ref, bf16[64,128,256]{2,1,0:T(8,128)(2,1)} %pages_ref.7, bf16[16,640]{1,0:T(8,128)(2,1)} %copy-done.17), custom_call_target="tpu_custom_call" | custom-call | tf_op jit(solution)/shard_map/next_pack/pallas_call | solution.py:157
  36.4 0.5 collective-permute-start.6
  36.9 3.4 %collective-permute-start.10 = (bf16[4,128,256]{2,1,0:T(8,128)(2,1)}, bf16[4,128,256]{2,1,0:T(8,128)(2,1)S(1)}, u32[]{:S(2)}, u32[]{:S(2)}) collective-permute-start(bf16[4,128,256]{2,1,0:T(8,128)(2,1)} %get-tuple-element.47), channel_id=1, source_target_pairs={{0,14},{1,15},{2,12},{3,13},{4,10},{5,11},{6,8},{7,9},{8,6},{9,7},... | collective-permute-start | bytes 786440 | tf_op jit(solution)/shard_map/ppermute | solution.py:361
  40.3 0.7 pad_maximum_fusion.1
  41.1 0.6 collective-permute-start.4
  41.7 7.3 %collective-permute-done.4 = bf16[4,16,640]{2,1,0:T(8,128)(2,1)S(1)} collective-permute-done((bf16[4,16,640]{2,1,0:T(8,128)(2,1)S(1)}, bf16[4,16,640]{2,1,0:T(8,128)(2,1)S(1)}, u32[]{:S(2)}, u32[]{:S(2)}) %collective-permute-start.4) | collective-permute-done | bytes 81952 | tf_op jit(solution)/shard_map/ppermute | solution.py:361
  49.2 0.7 pad_maximum_fusion.4
  49.8 3.1 %next_pack.4 = (bf16[4,128,256]{2,1,0:T(8,128)(2,1)}, bf16[4,128,256]{2,1,0:T(8,128)(2,1)}, bf16[4,128,256]{2,1,0:T(8,128)(2,1)}, bf16[4,128,256]{2,1,0:T(8,128)(2,1)}, bf16[4,128,256]{2,1,0:T(8,128)(2,1)}) custom-call(s32[64]{0:T(128)} %get-tuple-element.36.refs_1_.order_ref, bf16[64,128,256]{2,1,0:T(8,128)(2,1)} %pages_ref.7, bf16[4,128,256]{2,1,0:T(8,128)(2,1)} %copy-done.2), custom_call_target="tpu_custom_call" | custom-call | tf_op jit(solution)/shard_map/next_pack/pallas_call | solution.py:157
  52.9 2.2 %collective-permute-start.12 = (bf16[4,128,256]{2,1,0:T(8,128)(2,1)}, bf16[4,128,256]{2,1,0:T(8,128)(2,1)S(1)}, u32[]{:S(2)}, u32[]{:S(2)}) collective-permute-start(bf16[4,128,256]{2,1,0:T(8,128)(2,1)} %get-tuple-element.49), channel_id=1, source_target_pairs={{0,5},{1,4},{2,7},{3,6},{4,1},{5,0},{6,3},{7,2},{8,13},{9,12},{10,... | collective-permute-start | bytes 786440 | tf_op jit(solution)/shard_map/ppermute | solution.py:361
  55.1 0.9 collective-permute-start.9
  56.1 2.2 %collective-permute-start.13 = (bf16[4,128,256]{2,1,0:T(8,128)(2,1)}, bf16[4,128,256]{2,1,0:T(8,128)(2,1)S(1)}, u32[]{:S(2)}, u32[]{:S(2)}) collective-permute-start(bf16[4,128,256]{2,1,0:T(8,128)(2,1)} %get-tuple-element.53), channel_id=1, source_target_pairs={{0,9},{1,8},{2,11},{3,10},{4,13},{5,12},{6,15},{7,14},{8,1},{9,0},... | collective-permute-start | bytes 786440 | tf_op jit(solution)/shard_map/ppermute | solution.py:361
  58.3 1.9 %collective-permute-start.14 = (bf16[4,128,256]{2,1,0:T(8,128)(2,1)}, bf16[4,128,256]{2,1,0:T(8,128)(2,1)S(1)}, u32[]{:S(2)}, u32[]{:S(2)}) collective-permute-start(bf16[4,128,256]{2,1,0:T(8,128)(2,1)} %get-tuple-element.54), channel_id=1, source_target_pairs={{0,13},{1,12},{2,15},{3,14},{4,9},{5,8},{6,11},{7,10},{8,5},{9,4},... | collective-permute-start | bytes 786440 | tf_op jit(solution)/shard_map/ppermute | solution.py:361
  60.2 1.2 gather_fusion.1
  61.4 0.7 select_reduce_fusion.2.refs_0_
  62.1 0.7 copy-done.3
  62.8 1.8 %own_rows.1 = (f32[4,16,128]{2,1,0:T(8,128)}, f32[8,256]{1,0:T(8,128)}) custom-call(bf16[16,16,640]{2,1,0:T(8,128)(2,1)} %copy-done.3, s32[8]{0:T(128)} %gather_fusion.1, s32[4]{0:T(128)} %get-tuple-element.73.request_ref, f32[8,128]{1,0:T(8,128)} %get-tuple-element.89.cosine_ref, f32[8,128]{1,0:T(8,128)} %get-tuple-element.90.sine_ref), custom_call_target="tpu_custom_call" | custom-call | tf_op jit(solution)/shard_map/own_rows/pallas_call | solution.py:347
  64.7 5.9 %place_pages.5 = (bf16[64,128,256]{2,1,0:T(8,128)(2,1)}, f32[4,16,128]{2,1,0:T(8,128)}, f32[4,16,128]{2,1,0:T(8,128)}) custom-call(s32[64]{0:T(128)} %select_reduce_fusion.2.refs_0_, s32[64]{0:T(128)} %get-tuple-element.36.refs_1_.order_ref, s32[4]{0:T(128)} %copy-done.20, f32[8,256]{1,0:T(8,128)} %get-tuple-element.39.refs_3_, ...), custom_call_target="tpu_custom_call" | custom-call | tf_op jit(solution)/shard_map/place_pages/pallas_call | solution.py:301
  70.6 2.7 %next_pack.5 = (bf16[4,128,256]{2,1,0:T(8,128)(2,1)}, bf16[4,128,256]{2,1,0:T(8,128)(2,1)}, bf16[4,128,256]{2,1,0:T(8,128)(2,1)}) custom-call(s32[64]{0:T(128)} %get-tuple-element.36.refs_1_.order_ref, bf16[64,128,256]{2,1,0:T(8,128)(2,1)} %pages_ref.7, f32[4,16,128]{2,1,0:T(8,128)} %get-tuple-element.44.refs_5_.after_ref), custom_call_target="tpu_custom_call" | custom-call | tf_op jit(solution)/shard_map/next_pack/pallas_call | solution.py:157
  73.3 2.2 %collective-permute-start.16 = (bf16[4,128,256]{2,1,0:T(8,128)(2,1)}, bf16[4,128,256]{2,1,0:T(8,128)(2,1)S(1)}, u32[]{:S(2)}, u32[]{:S(2)}) collective-permute-start(bf16[4,128,256]{2,1,0:T(8,128)(2,1)} %get-tuple-element.56), channel_id=1, source_target_pairs={{0,7},{1,6},{2,5},{3,4},{4,3},{5,2},{6,1},{7,0},{8,15},{9,14},{10,... | collective-permute-start | bytes 786440 | tf_op jit(solution)/shard_map/ppermute | solution.py:361
  75.5 7.8 %collective-permute-done.9.refs_7_ = bf16[4,128,256]{2,1,0:T(8,128)(2,1)S(1)} collective-permute-done((bf16[4,128,256]{2,1,0:T(8,128)(2,1)}, bf16[4,128,256]{2,1,0:T(8,128)(2,1)S(1)}, u32[]{:S(2)}, u32[]{:S(2)}) %collective-permute-start.9) | collective-permute-done | bytes 262176 | tf_op jit(solution)/shard_map/ppermute | solution.py:361
  83.3 1.4 collective-permute-start.17
  84.7 2.3 %collective-permute-done.13.refs_7_ = bf16[4,128,256]{2,1,0:T(8,128)(2,1)S(1)} collective-permute-done((bf16[4,128,256]{2,1,0:T(8,128)(2,1)}, bf16[4,128,256]{2,1,0:T(8,128)(2,1)S(1)}, u32[]{:S(2)}, u32[]{:S(2)}) %collective-permute-start.13) | collective-permute-done | bytes 262176 | tf_op jit(solution)/shard_map/ppermute | solution.py:361
  87.0 2.2 %collective-permute-start.18 = (bf16[4,128,256]{2,1,0:T(8,128)(2,1)}, bf16[4,128,256]{2,1,0:T(8,128)(2,1)S(1)}, u32[]{:S(2)}, u32[]{:S(2)}) collective-permute-start(bf16[4,128,256]{2,1,0:T(8,128)(2,1)} %get-tuple-element.61), channel_id=1, source_target_pairs={{0,3},{1,2},{2,1},{3,0},{4,7},{5,6},{6,5},{7,4},{8,11},{9,10},{10,... | collective-permute-start | bytes 786440 | tf_op jit(solution)/shard_map/ppermute | solution.py:361
  89.2 5.5 %collective-permute-start.19 = (bf16[4,128,256]{2,1,0:T(8,128)(2,1)}, bf16[4,128,256]{2,1,0:T(8,128)(2,1)S(1)}, u32[]{:S(2)}, u32[]{:S(2)}) collective-permute-start(bf16[4,128,256]{2,1,0:T(8,128)(2,1)} %get-tuple-element.62), channel_id=1, source_target_pairs={{0,11},{1,10},{2,9},{3,8},{4,15},{5,14},{6,13},{7,12},{8,3},{9,2},... | collective-permute-start | bytes 786440 | tf_op jit(solution)/shard_map/ppermute | solution.py:361
  94.7 1.4 collective-permute-start.20
  96.1 0.8 gather_fusion.2
  96.9 6.0 %place_pages.6 = (bf16[64,128,256]{2,1,0:T(8,128)(2,1)}, f32[4,16,128]{2,1,0:T(8,128)}, f32[4,16,128]{2,1,0:T(8,128)}) custom-call(s32[64]{0:T(128)} %select_reduce_fusion.2.refs_0_, s32[64]{0:T(128)} %get-tuple-element.36.refs_1_.order_ref, s32[4]{0:T(128)} %copy-done.20, f32[8,256]{1,0:T(8,128)} %get-tuple-element.39.refs_3_, ...), custom_call_target="tpu_custom_call", output_to_operand_aliasing={{0}: (11, {})} | custom-call | tf_op jit(solution)/shard_map/place_pages/pallas_call | solution.py:301
  103.0 0.6 copy-done.13
  103.6 0.1 copy-done.15
  103.7 6.7 %place_pages.7 = (bf16[64,128,256]{2,1,0:T(8,128)(2,1)}, f32[4,16,128]{2,1,0:T(8,128)}, f32[4,16,128]{2,1,0:T(8,128)}) custom-call(s32[64]{0:T(128)} %select_reduce_fusion.2.refs_0_, s32[64]{0:T(128)} %get-tuple-element.36.refs_1_.order_ref, s32[4]{0:T(128)} %copy-done.20, f32[8,256]{1,0:T(8,128)} %get-tuple-element.39.refs_3_, ...), custom_call_target="tpu_custom_call", output_to_operand_aliasing={{0}: (12, {})} | custom-call | tf_op jit(solution)/shard_map/place_pages/pallas_call | solution.py:301
  110.5 2.4 %collective-permute-done.19.refs_8_ = bf16[4,128,256]{2,1,0:T(8,128)(2,1)S(1)} collective-permute-done((bf16[4,128,256]{2,1,0:T(8,128)(2,1)}, bf16[4,128,256]{2,1,0:T(8,128)(2,1)S(1)}, u32[]{:S(2)}, u32[]{:S(2)}) %collective-permute-start.19) | collective-permute-done | bytes 262176 | tf_op jit(solution)/shard_map/ppermute | solution.py:361
  112.9 0.7 copy-done.14
  113.6 4.4 %place_pages.8 = (bf16[64,128,256]{2,1,0:T(8,128)(2,1)}, f32[4,16,128]{2,1,0:T(8,128)}, f32[4,16,128]{2,1,0:T(8,128)}) custom-call(s32[64]{0:T(128)} %select_reduce_fusion.2.refs_0_, s32[64]{0:T(128)} %get-tuple-element.36.refs_1_.order_ref, s32[4]{0:T(128)} %copy-done.20, f32[8,256]{1,0:T(8,128)} %get-tuple-element.39.refs_3_, ...), custom_call_target="tpu_custom_call", output_to_operand_aliasing={{0}: (9, {})} | custom-call | tf_op jit(solution)/shard_map/place_pages/pallas_call | solution.py:301
  118.0 0.7 copy-done.16
  118.7 3.2 %place_pages.9 = (bf16[64,128,256]{2,1,0:T(8,128)(2,1)}, f32[4,16,128]{2,1,0:T(8,128)}, f32[4,16,128]{2,1,0:T(8,128)}, bf16[4,16,128]{2,1,0:T(8,128)(2,1)}) custom-call(s32[64]{0:T(128)} %select_reduce_fusion.2.refs_0_, s32[64]{0:T(128)} %get-tuple-element.36.refs_1_.order_ref, s32[4]{0:T(128)} %copy-done.20, ...), custom_call_target="tpu_custom_call", output_to_operand_aliasing={{0}: (8, {})} | custom-call | tf_op jit(solution)/shard_map/place_pages/pallas_call | solution.py:301
  121.9 0.7 broadcast_in_dim_reshape.4
  122.6 0.9 collective-permute-start.21
  123.6 3.7 %collective-permute-done.21 = bf16[1,4,2,1024]{3,2,1,0:T(2,128)(2,1)S(1)} collective-permute-done((bf16[1,4,2,1024]{3,2,1,0:T(2,128)(2,1)S(1)}, bf16[1,4,2,1024]{3,2,1,0:T(2,128)(2,1)S(1)}, u32[]{:S(2)}, u32[]{:S(2)}) %collective-permute-start.21) | collective-permute-done | bytes 16416 | tf_op jit(solution)/shard_map/ppermute | solution.py:361
  127.3 0.9 collective-permute-start.22
  128.2 3.1 %collective-permute-done.22 = bf16[2,4,2,1024]{3,2,1,0:T(2,128)(2,1)S(1)} collective-permute-done((bf16[2,4,2,1024]{3,2,1,0:T(2,128)(2,1)S(1)}, bf16[2,4,2,1024]{3,2,1,0:T(2,128)(2,1)S(1)}, u32[]{:S(2)}, u32[]{:S(2)}) %collective-permute-start.22) | collective-permute-done | bytes 32800 | tf_op jit(solution)/shard_map/ppermute | solution.py:361
  131.4 0.7 collective-permute-start.23
  132.2 3.6 %collective-permute-done.23 = bf16[4,4,2,1024]{3,2,1,0:T(2,128)(2,1)S(1)} collective-permute-done((bf16[4,4,2,1024]{3,2,1,0:T(2,128)(2,1)S(1)}, bf16[4,4,2,1024]{3,2,1,0:T(2,128)(2,1)S(1)}, u32[]{:S(2)}, u32[]{:S(2)}) %collective-permute-start.23) | collective-permute-done | bytes 65568 | tf_op jit(solution)/shard_map/ppermute | solution.py:361
  135.7 0.2 pad_maximum_fusion
  136.1 1.2 collective-permute-done.24
  137.3 0.1 constant_dynamic-update-slice_fusion.11
  137.4 1.1 gather_fusion.3
  138.6 0.2 copy.20
  138.8 5.6 %convolution_convert_fusion.1 = bf16[16,512]{1,0:T(8,128)(2,1)S(1)} fusion(bf16[16,8192]{1,0:T(8,128)(2,1)S(1)} %bitcast.43, bf16[512,8192]{1,0:T(8,128)(2,1)} %param.11), kind=kOutput, calls=%fused_computation.5 | convolution fusion | flops 134225920 | bytes 8667136 | tf_op jit(solution)/shard_map/dot_general | solution.py:546
  144.4 0.6 reshape.248
  (94 shorter events, 1.3 us)
Async XLA Ops:
  0.6 13.0 %copy-start = (s32[8]{0:T(128)S(1)}, s32[8]{0:T(128)}, u32[]{:S(2)}) copy-start(s32[8]{0:T(128)} %param.13) | copy-start | bytes 100
  0.6 32.7 %copy-start.21 = (s32[64]{0:T(128)S(1)}, s32[64]{0:T(128)}, u32[]{:S(2)}) copy-start(s32[64]{0:T(128)} %units_ref.1) | copy-start | bytes 772
  5.1 31.3 %copy-start.23 = (bf16[2,128,256]{2,1,0:T(8,128)(2,1)S(1)}, bf16[2,128,256]{2,1,0:T(8,128)(2,1)}, u32[]{:S(2)}) copy-start(bf16[2,128,256]{2,1,0:T(8,128)(2,1)} %get-tuple-element.41) | copy-start | bytes 393220
  5.1 17.1 %collective-permute-start = (bf16[2,128,256]{2,1,0:T(8,128)(2,1)}, bf16[2,128,256]{2,1,0:T(8,128)(2,1)S(1)}, u32[]{:S(2)}, u32[]{:S(2)}) collective-permute-start(bf16[2,128,256]{2,1,0:T(8,128)(2,1)} %get-tuple-element.37), channel_id=1, source_target_pairs={{0,8},{1,9},{2,10},{3,11},{4,12},{5,13},{6,14},{7,15},{8,0},{9,1},... | collective-permute-start | bytes 393224 | tf_op jit(solution)/shard_map/ppermute | solution.py:361
  9.2 39.9 %collective-permute-start.7 = (bf16[4,128,256]{2,1,0:T(8,128)(2,1)}, bf16[4,128,256]{2,1,0:T(8,128)(2,1)S(1)}, u32[]{:S(2)}, u32[]{:S(2)}) collective-permute-start(bf16[4,128,256]{2,1,0:T(8,128)(2,1)} %get-tuple-element.42), channel_id=1, source_target_pairs={{0,12},{1,13},{2,14},{3,15},{4,8},{5,9},{6,10},{7,11},{8,4},{9,5},... | collective-permute-start | bytes 786440 | tf_op jit(solution)/shard_map/ppermute | solution.py:361
  10.5 44.6 %collective-permute-start.8 = (bf16[4,128,256]{2,1,0:T(8,128)(2,1)}, bf16[4,128,256]{2,1,0:T(8,128)(2,1)S(1)}, u32[]{:S(2)}, u32[]{:S(2)}) collective-permute-start(bf16[4,128,256]{2,1,0:T(8,128)(2,1)} %get-tuple-element.43), channel_id=1, source_target_pairs={{0,1},{1,0},{2,3},{3,2},{4,5},{5,4},{6,7},{7,6},{8,9},{9,8},{10,11... | collective-permute-start | bytes 786440 | tf_op jit(solution)/shard_map/ppermute | solution.py:361
  14.3 38.6 %copy-start.20 = (s32[4]{0:T(128)}, s32[4]{0:T(128)S(1)}, u32[]{:S(2)}) copy-start(s32[4]{0:T(128)S(1)} %gather_fusion) | copy-start | bytes 52
  16.0 44.2 %copy-start.1 = (s32[16]{0:T(128)S(1)}, s32[16]{0:T(128)}, u32[]{:S(2)}) copy-start(s32[16]{0:T(128)} %constant.91.clone) | copy-start | bytes 196
  22.1 30.8 %copy-start.18 = (bf16[2,128,256]{2,1,0:T(8,128)(2,1)}, bf16[2,128,256]{2,1,0:T(8,128)(2,1)S(1)}, u32[]{:S(2)}) copy-start(bf16[2,128,256]{2,1,0:T(8,128)(2,1)S(1)} %collective-permute-done.refs_5_) | copy-start | bytes 393220
  29.0 4.5 %copy-start.17 = (bf16[16,640]{1,0:T(8,128)(2,1)}, bf16[16,640]{1,0:T(8,128)(2,1)S(1)}, u32[]{:S(2)}) copy-start(bf16[16,640]{1,0:T(8,128)(2,1)S(1)} %get-tuple-element.88.after_ref) | copy-start | bytes 61444
  29.0 7.4 %collective-permute-start.1 = (bf16[1,16,640]{2,1,0:T(8,128)(2,1)S(1)}, bf16[1,16,640]{2,1,0:T(8,128)(2,1)S(1)}, u32[]{:S(2)}, u32[]{:S(2)}) collective-permute-start(bf16[1,16,640]{2,1,0:T(8,128)(2,1)S(1)} %bitcast.47), channel_id=1, source_target_pairs={{0,8},{1,9},{2,10},{3,11},{4,12},{5,13},{6,14},{7,15},{8,0},{9,1},... | collective-permute-start | bytes 61448 | tf_op jit(solution)/shard_map/ppermute | solution.py:361
  29.0 7.9 %collective-permute-start.2 = (bf16[1,16,640]{2,1,0:T(8,128)(2,1)S(1)}, bf16[1,16,640]{2,1,0:T(8,128)(2,1)S(1)}, u32[]{:S(2)}, u32[]{:S(2)}) collective-permute-start(bf16[1,16,640]{2,1,0:T(8,128)(2,1)S(1)} %bitcast.48), channel_id=1, source_target_pairs={{0,4},{1,5},{2,6},{3,7},{4,0},{5,1},{6,2},{7,3},{8,12},{9,13},{10,... | collective-permute-start | bytes 61448 | tf_op jit(solution)/shard_map/ppermute | solution.py:361
  32.4 8.0 %collective-permute-start.3 = (bf16[1,16,640]{2,1,0:T(8,128)(2,1)S(1)}, bf16[1,16,640]{2,1,0:T(8,128)(2,1)S(1)}, u32[]{:S(2)}, u32[]{:S(2)}) collective-permute-start(bf16[1,16,640]{2,1,0:T(8,128)(2,1)S(1)} %bitcast.49), channel_id=1, source_target_pairs={{0,12},{1,13},{2,14},{3,15},{4,8},{5,9},{6,10},{7,11},{8,4},{9,5},... | collective-permute-start | bytes 61448 | tf_op jit(solution)/shard_map/ppermute | solution.py:361
  36.4 16.5 %collective-permute-start.6 = (bf16[2,128,256]{2,1,0:T(8,128)(2,1)S(1)}, bf16[2,128,256]{2,1,0:T(8,128)(2,1)S(1)}, u32[]{:S(2)}, u32[]{:S(2)}) collective-permute-start(bf16[2,128,256]{2,1,0:T(8,128)(2,1)S(1)} %copy-done.23), channel_id=1, source_target_pairs={{0,8},{1,9},{2,10},{3,11},{4,12},{5,13},{6,14},{7,15},{8,0},{9,1},... | collective-permute-start | bytes 393224 | tf_op jit(solution)/shard_map/ppermute | solution.py:361
  36.9 19.1 %collective-permute-start.10 = (bf16[4,128,256]{2,1,0:T(8,128)(2,1)}, bf16[4,128,256]{2,1,0:T(8,128)(2,1)S(1)}, u32[]{:S(2)}, u32[]{:S(2)}) collective-permute-start(bf16[4,128,256]{2,1,0:T(8,128)(2,1)} %get-tuple-element.47), channel_id=1, source_target_pairs={{0,14},{1,15},{2,12},{3,13},{4,10},{5,11},{6,8},{7,9},{8,6},{9,7},... | collective-permute-start | bytes 786440 | tf_op jit(solution)/shard_map/ppermute | solution.py:361
  41.1 7.9 %collective-permute-start.4 = (bf16[4,16,640]{2,1,0:T(8,128)(2,1)S(1)}, bf16[4,16,640]{2,1,0:T(8,128)(2,1)S(1)}, u32[]{:S(2)}, u32[]{:S(2)}) collective-permute-start(bf16[4,16,640]{2,1,0:T(8,128)(2,1)S(1)} %pad_maximum_fusion.1), channel_id=1, source_target_pairs={{0,2},{1,3},{2,0},{3,1},{4,6},{5,7},{6,4},{7,5},{8,10},{9,11},{10,... | collective-permute-start | bytes 245768 | tf_op jit(solution)/shard_map/ppermute | solution.py:361
  49.0 9.2 %collective-permute-start.11 = (bf16[4,128,256]{2,1,0:T(8,128)(2,1)}, bf16[4,128,256]{2,1,0:T(8,128)(2,1)S(1)}, u32[]{:S(2)}, u32[]{:S(2)}) collective-permute-start(bf16[4,128,256]{2,1,0:T(8,128)(2,1)} %get-tuple-element.48), channel_id=1, source_target_pairs={{0,4},{1,5},{2,6},{3,7},{4,0},{5,1},{6,2},{7,3},{8,12},{9,13},{10,... | collective-permute-start | bytes 786440 | tf_op jit(solution)/shard_map/ppermute | solution.py:361
  49.0 0.8 copy-start.2
  49.1 11.1 %collective-permute-start.5 = (bf16[8,16,640]{2,1,0:T(8,128)(2,1)S(1)}, bf16[8,16,640]{2,1,0:T(8,128)(2,1)S(1)}, u32[]{:S(2)}, u32[]{:S(2)}) collective-permute-start(bf16[8,16,640]{2,1,0:T(8,128)(2,1)S(1)} %get-tuple-element.74), channel_id=1, source_target_pairs={{0,1},{1,0},{2,3},{3,2},{4,5},{5,4},{6,7},{7,6},{8,9},{9,8},{10,11... | collective-permute-start | bytes 491528 | tf_op jit(solution)/shard_map/ppermute | solution.py:361
  52.9 30.4 %copy-start.22 = (bf16[4,128,256]{2,1,0:T(8,128)(2,1)S(1)}, bf16[4,128,256]{2,1,0:T(8,128)(2,1)}, u32[]{:S(2)}) copy-start(bf16[4,128,256]{2,1,0:T(8,128)(2,1)} %get-tuple-element.57) | copy-start | bytes 786436
  52.9 11.7 %copy-start.19 = (bf16[2,128,256]{2,1,0:T(8,128)(2,1)}, bf16[2,128,256]{2,1,0:T(8,128)(2,1)S(1)}, u32[]{:S(2)}) copy-start(bf16[2,128,256]{2,1,0:T(8,128)(2,1)S(1)} %collective-permute-done.6.refs_6_) | copy-start | bytes 393220
  52.9 20.4 %collective-permute-start.12 = (bf16[4,128,256]{2,1,0:T(8,128)(2,1)}, bf16[4,128,256]{2,1,0:T(8,128)(2,1)S(1)}, u32[]{:S(2)}, u32[]{:S(2)}) collective-permute-start(bf16[4,128,256]{2,1,0:T(8,128)(2,1)} %get-tuple-element.49), channel_id=1, source_target_pairs={{0,5},{1,4},{2,7},{3,6},{4,1},{5,0},{6,3},{7,2},{8,13},{9,12},{10,... | collective-permute-start | bytes 786440 | tf_op jit(solution)/shard_map/ppermute | solution.py:361
  55.1 9.5 %copy-start.4 = (bf16[4,128,256]{2,1,0:T(8,128)(2,1)}, bf16[4,128,256]{2,1,0:T(8,128)(2,1)S(1)}, u32[]{:S(2)}) copy-start(bf16[4,128,256]{2,1,0:T(8,128)(2,1)S(1)} %collective-permute-done.8.refs_8_) | copy-start | bytes 786436
  55.1 28.2 %collective-permute-start.9 = (bf16[4,128,256]{2,1,0:T(8,128)(2,1)}, bf16[4,128,256]{2,1,0:T(8,128)(2,1)S(1)}, u32[]{:S(2)}, u32[]{:S(2)}) collective-permute-start(bf16[4,128,256]{2,1,0:T(8,128)(2,1)} %get-tuple-element.46), channel_id=1, source_target_pairs={{0,10},{1,11},{2,8},{3,9},{4,14},{5,15},{6,12},{7,13},{8,2},{9,3},... | collective-permute-start | bytes 786440 | tf_op jit(solution)/shard_map/ppermute | solution.py:361
  56.1 40.8 %copy-start.5 = (bf16[4,128,256]{2,1,0:T(8,128)(2,1)}, bf16[4,128,256]{2,1,0:T(8,128)(2,1)S(1)}, u32[]{:S(2)}) copy-start(bf16[4,128,256]{2,1,0:T(8,128)(2,1)S(1)} %collective-permute-done.10.refs_8_) | copy-start | bytes 786436
  56.1 30.9 %collective-permute-start.13 = (bf16[4,128,256]{2,1,0:T(8,128)(2,1)}, bf16[4,128,256]{2,1,0:T(8,128)(2,1)S(1)}, u32[]{:S(2)}, u32[]{:S(2)}) collective-permute-start(bf16[4,128,256]{2,1,0:T(8,128)(2,1)} %get-tuple-element.53), channel_id=1, source_target_pairs={{0,9},{1,8},{2,11},{3,10},{4,13},{5,12},{6,15},{7,14},{8,1},{9,0},... | collective-permute-start | bytes 786440 | tf_op jit(solution)/shard_map/ppermute | solution.py:361
  58.3 38.7 %copy-start.6 = (bf16[4,128,256]{2,1,0:T(8,128)(2,1)}, bf16[4,128,256]{2,1,0:T(8,128)(2,1)S(1)}, u32[]{:S(2)}) copy-start(bf16[4,128,256]{2,1,0:T(8,128)(2,1)S(1)} %collective-permute-done.11.refs_9_) | copy-start | bytes 786436
  58.3 30.9 %collective-permute-start.14 = (bf16[4,128,256]{2,1,0:T(8,128)(2,1)}, bf16[4,128,256]{2,1,0:T(8,128)(2,1)S(1)}, u32[]{:S(2)}, u32[]{:S(2)}) collective-permute-start(bf16[4,128,256]{2,1,0:T(8,128)(2,1)} %get-tuple-element.54), channel_id=1, source_target_pairs={{0,13},{1,12},{2,15},{3,14},{4,9},{5,8},{6,11},{7,10},{8,5},{9,4},... | collective-permute-start | bytes 786440 | tf_op jit(solution)/shard_map/ppermute | solution.py:361
  60.2 34.5 %collective-permute-start.15 = (bf16[4,128,256]{2,1,0:T(8,128)(2,1)}, bf16[4,128,256]{2,1,0:T(8,128)(2,1)S(1)}, u32[]{:S(2)}, u32[]{:S(2)}) collective-permute-start(bf16[4,128,256]{2,1,0:T(8,128)(2,1)} %get-tuple-element.55), channel_id=1, source_target_pairs={{0,6},{1,7},{2,4},{3,5},{4,2},{5,3},{6,0},{7,1},{8,14},{9,15},{10,... | collective-permute-start | bytes 786440 | tf_op jit(solution)/shard_map/ppermute | solution.py:361
  62.1 0.7 copy-start.3
  73.3 23.6 %copy-start.8 = (bf16[4,128,256]{2,1,0:T(8,128)(2,1)}, bf16[4,128,256]{2,1,0:T(8,128)(2,1)S(1)}, u32[]{:S(2)}) copy-start(bf16[4,128,256]{2,1,0:T(8,128)(2,1)S(1)} %collective-permute-done.12.refs_10_) | copy-start | bytes 786436
  73.3 29.6 %collective-permute-start.16 = (bf16[4,128,256]{2,1,0:T(8,128)(2,1)}, bf16[4,128,256]{2,1,0:T(8,128)(2,1)S(1)}, u32[]{:S(2)}, u32[]{:S(2)}) collective-permute-start(bf16[4,128,256]{2,1,0:T(8,128)(2,1)} %get-tuple-element.56), channel_id=1, source_target_pairs={{0,7},{1,6},{2,5},{3,4},{4,3},{5,2},{6,1},{7,0},{8,15},{9,14},{10,... | collective-permute-start | bytes 786440 | tf_op jit(solution)/shard_map/ppermute | solution.py:361
  83.3 13.6 %copy-start.10 = (bf16[4,128,256]{2,1,0:T(8,128)(2,1)}, bf16[4,128,256]{2,1,0:T(8,128)(2,1)S(1)}, u32[]{:S(2)}) copy-start(bf16[4,128,256]{2,1,0:T(8,128)(2,1)S(1)} %collective-permute-done.9.refs_7_) | copy-start | bytes 786436
  83.3 19.6 %collective-permute-start.17 = (bf16[4,128,256]{2,1,0:T(8,128)(2,1)S(1)}, bf16[4,128,256]{2,1,0:T(8,128)(2,1)S(1)}, u32[]{:S(2)}, u32[]{:S(2)}) collective-permute-start(bf16[4,128,256]{2,1,0:T(8,128)(2,1)S(1)} %copy-done.22), channel_id=1, source_target_pairs={{0,2},{1,3},{2,0},{3,1},{4,6},{5,7},{6,4},{7,5},{8,10},{9,11},{10,... | collective-permute-start | bytes 786440 | tf_op jit(solution)/shard_map/ppermute | solution.py:361
  87.0 16.0 %copy-start.7 = (bf16[4,128,256]{2,1,0:T(8,128)(2,1)}, bf16[4,128,256]{2,1,0:T(8,128)(2,1)S(1)}, u32[]{:S(2)}) copy-start(bf16[4,128,256]{2,1,0:T(8,128)(2,1)S(1)} %collective-permute-done.13.refs_7_) | copy-start | bytes 786436
  87.0 23.5 %collective-permute-start.18 = (bf16[4,128,256]{2,1,0:T(8,128)(2,1)}, bf16[4,128,256]{2,1,0:T(8,128)(2,1)S(1)}, u32[]{:S(2)}, u32[]{:S(2)}) collective-permute-start(bf16[4,128,256]{2,1,0:T(8,128)(2,1)} %get-tuple-element.61), channel_id=1, source_target_pairs={{0,3},{1,2},{2,1},{3,0},{4,7},{5,6},{6,5},{7,4},{8,11},{9,10},{10,... | collective-permute-start | bytes 786440 | tf_op jit(solution)/shard_map/ppermute | solution.py:361
  89.2 13.8 %copy-start.9 = (bf16[4,128,256]{2,1,0:T(8,128)(2,1)}, bf16[4,128,256]{2,1,0:T(8,128)(2,1)S(1)}, u32[]{:S(2)}) copy-start(bf16[4,128,256]{2,1,0:T(8,128)(2,1)S(1)} %collective-permute-done.14.refs_8_) | copy-start | bytes 786436
  89.2 23.7 %collective-permute-start.19 = (bf16[4,128,256]{2,1,0:T(8,128)(2,1)}, bf16[4,128,256]{2,1,0:T(8,128)(2,1)S(1)}, u32[]{:S(2)}, u32[]{:S(2)}) collective-permute-start(bf16[4,128,256]{2,1,0:T(8,128)(2,1)} %get-tuple-element.62), channel_id=1, source_target_pairs={{0,11},{1,10},{2,9},{3,8},{4,15},{5,14},{6,13},{7,12},{8,3},{9,2},... | collective-permute-start | bytes 786440 | tf_op jit(solution)/shard_map/ppermute | solution.py:361
  94.7 8.3 %copy-start.11 = (bf16[4,128,256]{2,1,0:T(8,128)(2,1)}, bf16[4,128,256]{2,1,0:T(8,128)(2,1)S(1)}, u32[]{:S(2)}) copy-start(bf16[4,128,256]{2,1,0:T(8,128)(2,1)S(1)} %collective-permute-done.15.refs_9_) | copy-start | bytes 786436
  94.7 23.3 %collective-permute-start.20 = (bf16[4,128,256]{2,1,0:T(8,128)(2,1)}, bf16[4,128,256]{2,1,0:T(8,128)(2,1)S(1)}, u32[]{:S(2)}, u32[]{:S(2)}) collective-permute-start(bf16[4,128,256]{2,1,0:T(8,128)(2,1)} %get-tuple-element.66), channel_id=1, source_target_pairs={{0,15},{1,14},{2,13},{3,12},{4,11},{5,10},{6,9},{7,8},{8,7},{9,6},... | collective-permute-start | bytes 786440 | tf_op jit(solution)/shard_map/ppermute | solution.py:361
  102.9 0.7 copy-start.13
  103.0 0.8 copy-start.15
  110.5 2.4 %copy-start.12 = (bf16[4,128,256]{2,1,0:T(8,128)(2,1)}, bf16[4,128,256]{2,1,0:T(8,128)(2,1)S(1)}, u32[]{:S(2)}) copy-start(bf16[4,128,256]{2,1,0:T(8,128)(2,1)S(1)} %collective-permute-done.18.refs_7_) | copy-start | bytes 786436
  112.9 0.7 copy-start.14
  118.0 0.7 copy-start.16
  122.6 4.6 %collective-permute-start.21 = (bf16[1,4,2,1024]{3,2,1,0:T(2,128)(2,1)S(1)}, bf16[1,4,2,1024]{3,2,1,0:T(2,128)(2,1)S(1)}, u32[]{:S(2)}, u32[]{:S(2)}) collective-permute-start(bf16[1,4,2,1024]{3,2,1,0:T(2,128)(2,1)S(1)} %broadcast_in_dim_reshape.4), channel_id=1, source_target_pairs={{0,8},{1,9},{2,10},{3,11},{4,12},{5,13},{6,14},{7,15},{8,0},{9,1},... | collective-permute-start | bytes 49160 | tf_op jit(solution)/shard_map/ppermute | solution.py:361
  127.3 4.0 %collective-permute-start.22 = (bf16[2,4,2,1024]{3,2,1,0:T(2,128)(2,1)S(1)}, bf16[2,4,2,1024]{3,2,1,0:T(2,128)(2,1)S(1)}, u32[]{:S(2)}, u32[]{:S(2)}) collective-permute-start(bf16[2,4,2,1024]{3,2,1,0:T(2,128)(2,1)S(1)} %pad_maximum_fusion.3), channel_id=1, source_target_pairs={{0,4},{1,5},{2,6},{3,7},{4,0},{5,1},{6,2},{7,3},{8,12},{9,13},{10,... | collective-permute-start | bytes 98312 | tf_op jit(solution)/shard_map/ppermute | solution.py:361
  131.4 4.3 %collective-permute-start.23 = (bf16[4,4,2,1024]{3,2,1,0:T(2,128)(2,1)S(1)}, bf16[4,4,2,1024]{3,2,1,0:T(2,128)(2,1)S(1)}, u32[]{:S(2)}, u32[]{:S(2)}) collective-permute-start(bf16[4,4,2,1024]{3,2,1,0:T(2,128)(2,1)S(1)} %pad_maximum_fusion.2), channel_id=1, source_target_pairs={{0,2},{1,3},{2,0},{3,1},{4,6},{5,7},{6,4},{7,5},{8,10},{9,11},{10,... | collective-permute-start | bytes 196616 | tf_op jit(solution)/shard_map/ppermute | solution.py:361
  135.9 1.4 collective-permute-start.24

commit v4 on v2

--- a/solution.py
+++ b/solution.py
@@ -18,7 +18,7 @@
 GROUP = HEADS // KVH
 QROWS = 2 * GROUP
 PER_UNIT = MAXCTX // PAGE
-VMEM_LIMIT = 32 * 1024 * 1024
+VMEM_LIMIT = 56 * 1024 * 1024
 
 rope_base = 10000.0
 
@@ -84,59 +84,63 @@
     lax.fori_loop(0, pages_dev, assign, 0, unroll=8)
 
 
-def move_pages(capacity, keys, order_ref, pages_ref, outs, stage, load_sem, store_sem):
+def move_pages(outs_pages, capacity, order_ref, sources, outs, stage, load_sem, store_sem):
     loads, stores = [], []
-    for n, key in enumerate(keys):
-        for r in range(capacity):
-            copy = pltpu.make_async_copy(
-                pages_ref.at[order_ref[key * capacity + r]],
-                stage.at[n * capacity + r],
-                load_sem.at[n * capacity + r],
-            )
-            copy.start()
-            loads.append(copy)
-    for n, key in enumerate(keys):
-        for r in range(capacity):
-            loads[n * capacity + r].wait()
-        target = outs[n] if len(outs) > 1 else outs[0].at[pl.ds(n * capacity, capacity)]
+    for source, key, r in sum(outs_pages, []):
+        slot = len(loads)
+        index = order_ref[key * capacity + r] if source == 0 else r
         copy = pltpu.make_async_copy(
-            stage.at[pl.ds(n * capacity, capacity)], target, store_sem.at[n]
-        )
+            sources[source].at[index], stage.at[slot], load_sem.at[slot]
+        )
+        copy.start()
+        loads.append(copy)
+    slot = 0
+    for n, pages in enumerate(outs_pages):
+        count = len(pages)
+        for copy in loads[slot : slot + count]:
+            copy.wait()
+        copy = pltpu.make_async_copy(stage.at[pl.ds(slot, count)], outs[n], store_sem.at[n])
         copy.start()
         stores.append(copy)
+        slot += count
     for copy in stores:
         copy.wait()
 
 
-def first_pack_kernel(devices, capacity, keys, relative, units_ref, old_ref, pages_ref, *rest):
+def first_pack_kernel(
+    devices, capacity, outs_pages, relative, units_ref, old_ref, pages_ref, *rest
+):
     outs = rest[:-6]
     order_ref, slots, count, stage, load_sem, store_sem = rest[-6:]
     load_order(devices, capacity, relative, units_ref, old_ref, order_ref, slots, count)
-    move_pages(capacity, keys, order_ref, pages_ref, outs, stage, load_sem, store_sem)
-
-
-def next_pack_kernel(capacity, keys, order_ref, pages_ref, after_ref, *rest):
-    outs = rest[:-3]
+    move_pages(
+        outs_pages, capacity, order_ref, [pages_ref], outs, stage, load_sem, store_sem
+    )
+
+
+def next_pack_kernel(capacity, outs_pages, sources, order_ref, *rest):
+    source_refs, outs = rest[:sources], rest[sources:-3]
     stage, load_sem, store_sem = rest[-3:]
-    move_pages(capacity, keys, order_ref, pages_ref, outs, stage, load_sem, store_sem)
-
-
-def pack_scratch(count, pages):
-    return [
-        pltpu.VMEM((count,) + pages.shape[1:], pages.dtype),
-        pltpu.SemaphoreType.DMA((count,)),
-        pltpu.SemaphoreType.DMA((count,)),
+    move_pages(
+        outs_pages, capacity, order_ref, source_refs, outs, stage, load_sem, store_sem
+    )
+
+
+def pack_shapes(outs_pages, pages):
+    total = sum(len(p) for p in outs_pages)
+    shapes = [jax.ShapeDtypeStruct((len(p),) + pages.shape[1:], pages.dtype) for p in outs_pages]
+    scratch = [
+        pltpu.VMEM((total,) + pages.shape[1:], pages.dtype),
+        pltpu.SemaphoreType.DMA((total,)),
+        pltpu.SemaphoreType.DMA((len(outs_pages),)),
     ]
-
-
-def first_pack(new_units, old_pages, pages, devices, capacity, keys, relative):
-    chunk = (capacity,) + pages.shape[1:]
-    if relative:
-        outs = [jax.ShapeDtypeStruct(chunk, pages.dtype) for _ in keys]
-    else:
-        outs = [jax.ShapeDtypeStruct((len(keys) * capacity,) + chunk[1:], pages.dtype)]
+    return shapes, scratch
+
+
+def first_pack(new_units, old_pages, pages, devices, capacity, outs_pages, relative):
+    outs, scratch = pack_shapes(outs_pages, pages)
     result = pl.pallas_call(
-        functools.partial(first_pack_kernel, devices, capacity, keys, relative),
+        functools.partial(first_pack_kernel, devices, capacity, outs_pages, relative),
         out_shape=tuple(outs) + (jax.ShapeDtypeStruct((devices * capacity,), jnp.int32),),
         in_specs=[smem_spec(), smem_spec(), any_spec()],
         out_specs=tuple(any_spec() for _ in outs) + (smem_spec(),),
@@ -144,24 +148,24 @@
             pltpu.SMEM(new_units.shape, jnp.int32),
             pltpu.SMEM((devices,), jnp.int32),
         ]
-        + pack_scratch(len(keys) * capacity, pages),
+        + scratch,
         compiler_params=pltpu.CompilerParams(vmem_limit_bytes=VMEM_LIMIT),
         name="first_pack",
     )(new_units, old_pages, pages)
     return result[:-1], result[-1]
 
 
-def next_pack(order, pages, after, capacity, keys):
-    chunk = (capacity,) + pages.shape[1:]
+def next_pack(order, sources, capacity, outs_pages):
+    outs, scratch = pack_shapes(outs_pages, sources[0])
     return pl.pallas_call(
-        functools.partial(next_pack_kernel, capacity, keys),
-        out_shape=tuple(jax.ShapeDtypeStruct(chunk, pages.dtype) for _ in keys),
-        in_specs=[smem_spec(), any_spec(), any_spec()],
-        out_specs=tuple(any_spec() for _ in keys),
-        scratch_shapes=pack_scratch(len(keys) * capacity, pages),
+        functools.partial(next_pack_kernel, capacity, outs_pages, len(sources)),
+        out_shape=tuple(outs),
+        in_specs=[smem_spec()] + [any_spec()] * len(sources),
+        out_specs=tuple(any_spec() for _ in outs),
+        scratch_shapes=scratch,
         compiler_params=pltpu.CompilerParams(vmem_limit_bytes=VMEM_LIMIT),
         name="next_pack",
-    )(order, pages, after)
+    )(order, *sources)
 
 
 def attend(query, keys, values, limit):
@@ -374,19 +378,8 @@
     return values, span
 
 
-def exchange_plan(devices):
-    half = devices // 2
-    far = sorted(range(half, devices), key=lambda k: (k & 1, k & 2, k))
-    across = [k for k in range(1, half) if k >= half // 2]
-    beside = [k for k in range(1, half) if k < half // 2]
-    if devices < 16:
-        return [far + across + beside]
-    return [
-        far[:2] + beside[:1],
-        far[2:4] + across[:2],
-        far[4:6] + across[2:] + beside[1:2],
-        far[6:] + beside[2:],
-    ]
+def after(value, *others):
+    return lax.optimization_barrier((value,) + others)[0]
 
 
 def body(hidden_states, qkv_weight, out_weight, cache_pages, context_lengths, new_units, old_pages):
@@ -397,18 +390,42 @@
     capacity = max(1, pages_dev // devices)
     total_units = new_units.shape[0]
     total_pages = old_pages.shape[0]
-    pairwise = devices <= 16 and devices & (devices - 1) == 0
+    pairwise = devices == 2 * KVH
+
+    def own(*keys):
+        return [(0, key, r) for key in keys for r in range(capacity)]
+
+    def passed(source, piece):
+        return [(source, 0, piece * capacity + r) for r in range(capacity)]
+
+    def piece(chunk, n):
+        return chunk[n * capacity : (n + 1) * capacity]
+
+    def send(chunk, key):
+        return swap(chunk, key, devices)
 
     if pairwise:
-        plan = exchange_plan(devices)
-        chunks, order = first_pack(
-            new_units, old_pages, cache_pages, devices, capacity, plan[0], True
-        )
-        moved = [swap(c, k, devices) for c, k in zip(chunks, plan[0])]
+        half, quarter = devices // 2, devices // 4
+        a, b = half, half + quarter
+        c, d = a + 2, b + 2
+        (chunk_a, cross_far), order = first_pack(
+            new_units,
+            old_pages,
+            cache_pages,
+            devices,
+            capacity,
+            [own(a), own(a + 1, b + 1, c + 1, d + 1)],
+            True,
+        )
+        moved_a, cross_far = send(chunk_a, a), send(cross_far, 1)
+        near = list(range(2, half, 2))
+        chunk_b, cross_near = next_pack(
+            order, [cache_pages], capacity, [own(b), own(1, *[k + 1 for k in near])]
+        )
+        moved_b, cross_near = send(chunk_b, b), send(cross_near, 1)
     else:
-        keys = list(range(devices))
         (packed,), order = first_pack(
-            new_units, old_pages, cache_pages, devices, capacity, keys, False
+            new_units, old_pages, cache_pages, devices, capacity, [own(*range(devices))], False
         )
         arrived = lax.all_to_all(
             packed.reshape(devices, capacity, page_rows, page_width),
@@ -448,7 +465,8 @@
         table = source_dev * capacity + rank
 
     flat_rows = hidden_states.reshape(requests * 2, D)
-    flat_rows = flat_rows + jnp.minimum(order[0], 0).astype(jnp.bfloat16)
+    if pairwise:
+        flat_rows = after(flat_rows, cross_near)
     own_part = lax.dot_general(
         flat_rows, qkv_weight, (((1,), (1,)), ((), ())), preferred_element_type=jnp.float32
     ).astype(jnp.bfloat16)
@@ -462,39 +480,56 @@
         holders = own_heads[:, None] * pieces + jnp.arange(pieces, dtype=jnp.int32)[None, :]
         places = turn[(holders ^ device).reshape(U_DEV * pieces)]
         queries, fresh = own_rows(rows, places, own_requests, cosine, sine)
-        new_cache, sums = None, None
-        if len(plan) > 1:
-            chunks = next_pack(order, cache_pages, own_part, capacity, plan[1])
-            moved += [swap(c, k, devices) for c, k in zip(chunks, plan[1])]
-            chunks = next_pack(order, cache_pages, queries, capacity, plan[2])
-            moved += [swap(c, k, devices) for c, k in zip(chunks, plan[2])]
-        at = 0
-        keys = sum(plan, [])
-        groups = [len(p) for p in plan[:-1]] + [len(plan[-1]) - 1, 1]
-        for step, size in enumerate(groups):
+        moved_a2 = send(after(piece(cross_far, 0), own_part), a + 0)
+        moved_b2 = send(after(piece(cross_far, 1), own_part), b + 0)
+        near_chunks = next_pack(
+            order,
+            [cache_pages, after(cross_near, own_part)],
+            capacity,
+            [own(k) + passed(1, n + 1) for n, k in enumerate(near)],
+        )
+        moved_near = [send(chunk, k) for chunk, k in zip(near_chunks, near)]
+        chunk_c, chunk_d = next_pack(
+            order,
+            [cache_pages, after(cross_far, moved_a)],
+            capacity,
+            [own(c) + passed(1, 2), own(d)],
+        )
+        moved_c = send(after(chunk_c, moved_b), c)
+
+        def place(groups, sums, cache, finish):
             entries, sources = [], []
-            for key, array in zip(keys[at : at + size], moved[at : at + size]):
-                entries += [(len(sources), r, (key * capacity + r,)) for r in range(capacity)]
+            for array, keys, first in groups:
+                for n, key in enumerate(keys):
+                    for r in range(capacity):
+                        at = (r,) if array is cache_pages else first + n * capacity + r
+                        entries.append((len(sources), at, (key * capacity + r,)))
                 sources.append(array)
-            at += size
-            if step == 0:
-                entries = [(len(sources), (r,), (r,)) for r in range(capacity)] + entries
-                sources.append(cache_pages)
-            new_cache, sums, attended = place_pages(
-                table,
-                order,
-                own_lengths,
-                fresh,
-                queries,
-                sums,
-                sources,
-                entries,
-                new_cache,
-                step == len(groups) - 1,
+            return place_pages(
+                table, order, own_lengths, fresh, queries, sums, sources, entries, cache, finish
             )
-            if step == 0 and len(plan) > 1:
-                chunks = next_pack(order, cache_pages, sums[0], capacity, plan[3])
-                moved += [swap(c, k, devices) for c, k in zip(chunks, plan[3])]
+
+        new_cache, sums, _ = place(
+            [(cache_pages, [0], 0), (cross_near, [1], 0), (moved_a, [a], 0), (moved_b, [b], 0)],
+            None,
+            None,
+            False,
+        )
+        moved_d = send(after(chunk_d, moved_a2, sums[0]), d)
+        new_cache, sums, _ = place(
+            [(moved_a2, [a + 1], 0), (moved_b2, [b + 1], 0), (moved_near[0], [2, 3], 0)],
+            sums,
+            new_cache,
+            False,
+        )
+        moved_d2 = send(after(piece(cross_far, 3), moved_b2, sums[0]), d)
+        new_cache, sums, _ = place(
+            [(m, [k, k + 1], 0) for m, k in zip(moved_near[1:], near[1:])], sums, new_cache, False
+        )
+        new_cache, sums, _ = place(
+            [(moved_c, [c, c + 1], 0), (moved_d, [d], 0)], sums, new_cache, False
+        )
+        new_cache, sums, attended = place([(moved_d2, [d + 1], 0)], sums, new_cache, True)
     else:
         rows = lax.all_gather(own_part, "tp", axis=1, tiled=True)
         rows = rows.reshape(requests, 2, KVH, GROUP + 2, HD)

time: 162 us -> 147 us (0.907)
  starting transfers between devices: 41 us -> 32.1 us
  waiting for transfers between devices: 45.1 us -> 39.8 us
  local copies, waits for them, and re-layouts: 18.7 us -> 14 us
  Pallas kernels: 38.6 us -> 41.8 us
    ppermute x24 -> x21, starting transfers between devices: 41 us -> 32.1 us  [swap(): return lax.ppermute(values, 'tp', [(i, i ^ key) for i in range(devices)])]
    unnamed x36 -> x46, local copies, waits for them, and re-layouts: 12.2 us -> 5.88 us
    ppermute x24 -> x21, waiting for transfers between devices: 45.1 us -> 39.8 us  [swap(): return lax.ppermute(values, 'tp', [(i, i ^ key) for i in range(devices)])]
    pallas_call x4, Pallas kernels: 12 us -> 13.9 us  [the longest x3 9.06 us: next_pack(): pl.pallas_call(functools.partial(next_pack_kernel, capacity, outs_pages,...]
  transfers between devices with their start and end apart: 24 -> 21, of which waited for: 9 -> 7; matrix products, arithmetic and copies ran while one was open for 5% -> 12% of each run, Pallas kernels for 20% -> 23%
where the time goes in v4:
time: 147 us; the launch traced here: 145 us
  Pallas kernels  41.8 us (28%)
  waiting for transfers between devices  39.8 us (27%)
  starting transfers between devices  32.1 us (22%)
  local copies, waits for them, and re-layouts  14 us (10%)
  matrix products  13.4 us (9%)
  other arithmetic  3.2 us (2%)
    ppermute x21, waiting for transfers between devices, swap(): return lax.ppermute(values, 'tp', [(i, i ^ key) for i in range(devices)])  39.8 us
    ppermute x21, starting transfers between devices, swap(): return lax.ppermute(values, 'tp', [(i, i ^ key) for i in range(devices)])  32.1 us
    pallas_call x5, Pallas kernels, place_pages(): pl.pallas_call(functools.partial(place_kernel, entries, started, finish),...  26.1 us
    pallas_call x3, Pallas kernels, next_pack(): pl.pallas_call(functools.partial(next_pack_kernel, capacity, outs_pages,...  9.06 us
    dot_general x1, matrix products, body(): lax.dot_general(flat_rows, qkv_weight, (((1,), (1,)), ((), ())), preferre...  7.77 us
    unnamed x46, local copies, waits for them, and re-layouts  5.88 us
    dot_general x1, matrix products, body(): lax.dot_general(logical, out_weight, (((1,), (1,)), ((), ())), preferred_...  5.64 us
    pallas_call x1, Pallas kernels, first_pack(): pl.pallas_call(functools.partial(first_pack_kernel, devices, capacity, ou...  4.82 us
  transfers between devices with their start and end apart: 21, of which 7 were waited for; matrix products, arithmetic and copies ran while one was open for 12% of the time, Pallas kernels for 23%

profile of v4, /device:TPU:0, one launch (start us, length us, event | category | flops | bytes accessed | tf_op | source)
XLA Modules:
  0.0 145.3 jit_solution(17451459468496776620)
XLA Ops:
  0.7 4.8 %first_pack.1 = (bf16[4,128,256]{2,1,0:T(8,128)(2,1)}, bf16[16,128,256]{2,1,0:T(8,128)(2,1)}, s32[64]{0:T(128)}) custom-call(s32[64]{0:T(128)} %units_ref.1, s32[1024]{0:T(1024)} %old_ref.1, bf16[64,128,256]{2,1,0:T(8,128)(2,1)} %rest_0_.5), custom_call_target="tpu_custom_call" | custom-call | tf_op jit(solution)/shard_map/first_pack/pallas_call | solution.py:142
  5.5 4.1 %collective-permute-start.6 = (bf16[4,128,256]{2,1,0:T(8,128)(2,1)}, bf16[4,128,256]{2,1,0:T(8,128)(2,1)S(1)}, u32[]{:S(2)}, u32[]{:S(2)}) collective-permute-start(bf16[4,128,256]{2,1,0:T(8,128)(2,1)} %get-tuple-element.41), channel_id=1, source_target_pairs={{0,8},{1,9},{2,10},{3,11},{4,12},{5,13},{6,14},{7,15},{8,0},{9,1},... | collective-permute-start | bytes 786440 | tf_op jit(solution)/shard_map/ppermute | solution.py:362
  9.6 3.2 %next_pack.3 = (bf16[4,128,256]{2,1,0:T(8,128)(2,1)}, bf16[16,128,256]{2,1,0:T(8,128)(2,1)}) custom-call(s32[64]{0:T(128)} %get-tuple-element.36.order_ref.refs_1_, bf16[64,128,256]{2,1,0:T(8,128)(2,1)} %rest_0_.5), custom_call_target="tpu_custom_call" | custom-call | tf_op jit(solution)/shard_map/next_pack/pallas_call | solution.py:160
  12.8 1.4 collective-permute-start.7
  14.2 0.2 collective-permute-start
  14.4 0.1 select_reduce_fusion.1
  14.6 0.6 compare_select_fusion.3
  15.4 0.2 select_reduce_fusion
  15.7 0.6 gather_fusion
  16.6 0.1 reshape.244
  16.7 0.2 convert_reduce_fusion
  16.9 0.1 fusion
  17.1 7.8 %constant_dynamic-update-slice_fusion.4 = (bf16[8,16,640]{2,1,0:T(8,128)(2,1)}, bf16[16,16,640]{2,1,0:T(8,128)(2,1)S(1)}, bf16[16,640]{1,0:T(8,128)(2,1)S(1)}) fusion(bf16[16,8192]{1,0:T(8,128)(2,1)S(1)} %reshape.244, bf16[640,8192]{1,0:T(8,128)(2,1)} %param.10), kind=kOutput, calls=%fused_computation.16 | convolution fusion | flops 167782400 | bytes 10809344 | tf_op jit(solution)/shard_map/dot_general | solution.py:470
  24.9 2.5 %collective-permute-start.3 = (bf16[1,16,640]{2,1,0:T(8,128)(2,1)S(1)}, bf16[1,16,640]{2,1,0:T(8,128)(2,1)S(1)}, u32[]{:S(2)}, u32[]{:S(2)}) collective-permute-start(bf16[1,16,640]{2,1,0:T(8,128)(2,1)S(1)} %bitcast.47), channel_id=1, source_target_pairs={{0,12},{1,13},{2,14},{3,15},{4,8},{5,9},{6,10},{7,11},{8,4},{9,5},... | collective-permute-start | bytes 61448 | tf_op jit(solution)/shard_map/ppermute | solution.py:362
  27.3 1.9 %collective-permute-start.1 = (bf16[1,16,640]{2,1,0:T(8,128)(2,1)S(1)}, bf16[1,16,640]{2,1,0:T(8,128)(2,1)S(1)}, u32[]{:S(2)}, u32[]{:S(2)}) collective-permute-start(bf16[1,16,640]{2,1,0:T(8,128)(2,1)S(1)} %bitcast.49), channel_id=1, source_target_pairs={{0,8},{1,9},{2,10},{3,11},{4,12},{5,13},{6,14},{7,15},{8,0},{9,1},... | collective-permute-start | bytes 61448 | tf_op jit(solution)/shard_map/ppermute | solution.py:362
  29.2 0.9 fusion.6
  30.2 3.1 %next_pack.4 = (bf16[8,128,256]{2,1,0:T(8,128)(2,1)}, bf16[8,128,256]{2,1,0:T(8,128)(2,1)}, bf16[8,128,256]{2,1,0:T(8,128)(2,1)}) custom-call(s32[64]{0:T(128)} %get-tuple-element.36.order_ref.refs_1_, bf16[64,128,256]{2,1,0:T(8,128)(2,1)} %rest_0_.5, bf16[16,128,256]{2,1,0:T(8,128)(2,1)} %copy-done.2), custom_call_target="tpu_custom_call" | custom-call | tf_op jit(solution)/shard_map/next_pack/pallas_call | solution.py:160
  33.3 3.7 %collective-permute-start.9 = (bf16[4,128,256]{2,1,0:T(8,128)(2,1)}, bf16[4,128,256]{2,1,0:T(8,128)(2,1)S(1)}, u32[]{:S(2)}, u32[]{:S(2)}) collective-permute-start(bf16[4,128,256]{2,1,0:T(8,128)(2,1)} %get-tuple-element.46), channel_id=1, source_target_pairs={{0,8},{1,9},{2,10},{3,11},{4,12},{5,13},{6,14},{7,15},{8,0},{9,1},... | collective-permute-start | bytes 786440 | tf_op jit(solution)/shard_map/ppermute | solution.py:362
  37.0 1.5 %collective-permute-start.11 = (bf16[8,128,256]{2,1,0:T(8,128)(2,1)}, bf16[8,128,256]{2,1,0:T(8,128)(2,1)S(1)}, u32[]{:S(2)}, u32[]{:S(2)}) collective-permute-start(bf16[8,128,256]{2,1,0:T(8,128)(2,1)} %get-tuple-element.49), channel_id=1, source_target_pairs={{0,2},{1,3},{2,0},{3,1},{4,6},{5,7},{6,4},{7,5},{8,10},{9,11},{10,... | collective-permute-start | bytes 1572872 | tf_op jit(solution)/shard_map/ppermute | solution.py:362
  38.6 0.6 collective-permute-start.4
  39.1 0.6 constant_dynamic-update-slice_fusion.3
  39.7 0.6 constant_dynamic-update-slice_fusion.2
  40.4 0.6 constant_dynamic-update-slice_fusion.1
  41.0 11.5 %collective-permute-done.4 = bf16[4,16,640]{2,1,0:T(8,128)(2,1)S(1)} collective-permute-done((bf16[4,16,640]{2,1,0:T(8,128)(2,1)S(1)}, bf16[4,16,640]{2,1,0:T(8,128)(2,1)S(1)}, u32[]{:S(2)}, u32[]{:S(2)}) %collective-permute-start.4) | collective-permute-done | bytes 81952 | tf_op jit(solution)/shard_map/ppermute | solution.py:362
  52.5 0.7 constant_dynamic-update-slice_fusion
  53.1 0.6 select_reduce_fusion.2.refs_0_
  53.8 0.4 collective-permute-start.10
  54.2 1.2 gather_fusion.1
  55.4 2.8 %next_pack.5 = (bf16[8,128,256]{2,1,0:T(8,128)(2,1)}, bf16[4,128,256]{2,1,0:T(8,128)(2,1)}) custom-call(s32[64]{0:T(128)} %get-tuple-element.36.order_ref.refs_1_, bf16[64,128,256]{2,1,0:T(8,128)(2,1)} %rest_0_.5, bf16[16,128,256]{2,1,0:T(8,128)(2,1)} %copy-done.3), custom_call_target="tpu_custom_call" | custom-call | tf_op jit(solution)/shard_map/next_pack/pallas_call | solution.py:160
  58.2 1.0 collective-permute-start.14
  59.1 4.0 %collective-permute-start.12 = (bf16[8,128,256]{2,1,0:T(8,128)(2,1)}, bf16[8,128,256]{2,1,0:T(8,128)(2,1)S(1)}, u32[]{:S(2)}, u32[]{:S(2)}) collective-permute-start(bf16[8,128,256]{2,1,0:T(8,128)(2,1)} %get-tuple-element.53), channel_id=1, source_target_pairs={{0,4},{1,5},{2,6},{3,7},{4,0},{5,1},{6,2},{7,3},{8,12},{9,13},{10,... | collective-permute-start | bytes 1572872 | tf_op jit(solution)/shard_map/ppermute | solution.py:362
  63.2 0.7 pad_maximum_fusion.4
  63.8 0.9 constant_dynamic-update-slice_fusion.5.rows_ref
  64.8 0.7 copy-done.8
  65.5 1.8 %own_rows.1 = (f32[4,16,128]{2,1,0:T(8,128)}, f32[8,256]{1,0:T(8,128)}) custom-call(bf16[16,16,640]{2,1,0:T(8,128)(2,1)} %copy-done.8, s32[8]{0:T(128)} %gather_fusion.1, s32[4]{0:T(128)} %get-tuple-element.73.request_ref, f32[8,128]{1,0:T(8,128)} %get-tuple-element.92.cosine_ref, f32[8,128]{1,0:T(8,128)} %get-tuple-element.93.sine_ref), custom_call_target="tpu_custom_call" | custom-call | tf_op jit(solution)/shard_map/own_rows/pallas_call | solution.py:348
  67.3 6.0 %place_pages.5 = (bf16[64,128,256]{2,1,0:T(8,128)(2,1)}, f32[4,16,128]{2,1,0:T(8,128)}, f32[4,16,128]{2,1,0:T(8,128)}) custom-call(s32[64]{0:T(128)} %select_reduce_fusion.2.refs_0_, s32[64]{0:T(128)} %get-tuple-element.36.order_ref.refs_1_, s32[4]{0:T(128)} %copy-done.16, f32[8,256]{1,0:T(8,128)} %get-tuple-element.39.refs_3_, ...), custom_call_target="tpu_custom_call" | custom-call | tf_op jit(solution)/shard_map/place_pages/pallas_call | solution.py:302
  73.3 1.8 %collective-permute-start.15 = (bf16[4,128,256]{2,1,0:T(8,128)(2,1)}, bf16[4,128,256]{2,1,0:T(8,128)(2,1)S(1)}, u32[]{:S(2)}, u32[]{:S(2)}) collective-permute-start(bf16[4,128,256]{2,1,0:T(8,128)(2,1)} %get-tuple-element.62), channel_id=1, source_target_pairs={{0,14},{1,15},{2,12},{3,13},{4,10},{5,11},{6,8},{7,9},{8,6},{9,7},... | collective-permute-start | bytes 786440 | tf_op jit(solution)/shard_map/ppermute | solution.py:362
  75.1 0.8 copy-done.4
  75.9 5.9 %place_pages.6 = (bf16[64,128,256]{2,1,0:T(8,128)(2,1)}, f32[4,16,128]{2,1,0:T(8,128)}, f32[4,16,128]{2,1,0:T(8,128)}) custom-call(s32[64]{0:T(128)} %select_reduce_fusion.2.refs_0_, s32[64]{0:T(128)} %get-tuple-element.36.order_ref.refs_1_, s32[4]{0:T(128)} %copy-done.16, f32[8,256]{1,0:T(8,128)} %get-tuple-element.39.refs_3_, ...), custom_call_target="tpu_custom_call", output_to_operand_aliasing={{0}: (10, {})} | custom-call | tf_op jit(solution)/shard_map/place_pages/pallas_call | solution.py:302
  81.8 3.3 %collective-permute-start.16 = (bf16[4,128,256]{2,1,0:T(8,128)(2,1)}, bf16[4,128,256]{2,1,0:T(8,128)(2,1)S(1)}, u32[]{:S(2)}, u32[]{:S(2)}) collective-permute-start(bf16[4,128,256]{2,1,0:T(8,128)(2,1)} %get-tuple-element.66), channel_id=1, source_target_pairs={{0,14},{1,15},{2,12},{3,13},{4,10},{5,11},{6,8},{7,9},{8,6},{9,7},... | collective-permute-start | bytes 786440 | tf_op jit(solution)/shard_map/ppermute | solution.py:362
  85.0 0.8 gather_fusion.2
  85.9 14.7 %collective-permute-done.13.refs_8_ = bf16[8,128,256]{2,1,0:T(8,128)(2,1)S(1)} collective-permute-done((bf16[8,128,256]{2,1,0:T(8,128)(2,1)}, bf16[8,128,256]{2,1,0:T(8,128)(2,1)S(1)}, u32[]{:S(2)}, u32[]{:S(2)}) %collective-permute-start.13) | collective-permute-done | bytes 524320 | tf_op jit(solution)/shard_map/ppermute | solution.py:362
  100.6 0.8 copy-done.7
  101.4 5.9 %place_pages.7 = (bf16[64,128,256]{2,1,0:T(8,128)(2,1)}, f32[4,16,128]{2,1,0:T(8,128)}, f32[4,16,128]{2,1,0:T(8,128)}) custom-call(s32[64]{0:T(128)} %select_reduce_fusion.2.refs_0_, s32[64]{0:T(128)} %get-tuple-element.36.order_ref.refs_1_, s32[4]{0:T(128)} %copy-done.16, f32[8,256]{1,0:T(8,128)} %get-tuple-element.39.refs_3_, ...), custom_call_target="tpu_custom_call", output_to_operand_aliasing={{0}: (9, {})} | custom-call | tf_op jit(solution)/shard_map/place_pages/pallas_call | solution.py:302
  107.3 4.4 %collective-permute-done.15.refs_8_ = bf16[4,128,256]{2,1,0:T(8,128)(2,1)S(1)} collective-permute-done((bf16[4,128,256]{2,1,0:T(8,128)(2,1)}, bf16[4,128,256]{2,1,0:T(8,128)(2,1)S(1)}, u32[]{:S(2)}, u32[]{:S(2)}) %collective-permute-start.15) | collective-permute-done | bytes 262176 | tf_op jit(solution)/shard_map/ppermute | solution.py:362
  111.7 0.7 copy-done.13
  112.4 5.1 %place_pages.8 = (bf16[64,128,256]{2,1,0:T(8,128)(2,1)}, f32[4,16,128]{2,1,0:T(8,128)}, f32[4,16,128]{2,1,0:T(8,128)}) custom-call(s32[64]{0:T(128)} %select_reduce_fusion.2.refs_0_, s32[64]{0:T(128)} %get-tuple-element.36.order_ref.refs_1_, s32[4]{0:T(128)} %copy-done.16, f32[8,256]{1,0:T(8,128)} %get-tuple-element.39.refs_3_, ...), custom_call_target="tpu_custom_call", output_to_operand_aliasing={{0}: (9, {})} | custom-call | tf_op jit(solution)/shard_map/place_pages/pallas_call | solution.py:302
  117.6 0.7 copy-done.15
  118.3 3.2 %place_pages.9 = (bf16[64,128,256]{2,1,0:T(8,128)(2,1)}, f32[4,16,128]{2,1,0:T(8,128)}, f32[4,16,128]{2,1,0:T(8,128)}, bf16[4,16,128]{2,1,0:T(8,128)(2,1)}) custom-call(s32[64]{0:T(128)} %select_reduce_fusion.2.refs_0_, s32[64]{0:T(128)} %get-tuple-element.36.order_ref.refs_1_, s32[4]{0:T(128)} %copy-done.16, ...), custom_call_target="tpu_custom_call", output_to_operand_aliasing={{0}: (8, {})} | custom-call | tf_op jit(solution)/shard_map/place_pages/pallas_call | solution.py:302
  121.5 0.7 broadcast_in_dim_reshape.4
  122.2 2.4 %collective-permute-start.17 = (bf16[1,4,2,1024]{3,2,1,0:T(2,128)(2,1)S(1)}, bf16[1,4,2,1024]{3,2,1,0:T(2,128)(2,1)S(1)}, u32[]{:S(2)}, u32[]{:S(2)}) collective-permute-start(bf16[1,4,2,1024]{3,2,1,0:T(2,128)(2,1)S(1)} %broadcast_in_dim_reshape.4), channel_id=1, source_target_pairs={{0,8},{1,9},{2,10},{3,11},{4,12},{5,13},{6,14},{7,15},{8,0},{9,1},... | collective-permute-start | bytes 49160 | tf_op jit(solution)/shard_map/ppermute | solution.py:362
  124.6 2.2 %collective-permute-done.17 = bf16[1,4,2,1024]{3,2,1,0:T(2,128)(2,1)S(1)} collective-permute-done((bf16[1,4,2,1024]{3,2,1,0:T(2,128)(2,1)S(1)}, bf16[1,4,2,1024]{3,2,1,0:T(2,128)(2,1)S(1)}, u32[]{:S(2)}, u32[]{:S(2)}) %collective-permute-start.17) | collective-permute-done | bytes 16416 | tf_op jit(solution)/shard_map/ppermute | solution.py:362
  126.9 2.7 %collective-permute-start.18 = (bf16[2,4,2,1024]{3,2,1,0:T(2,128)(2,1)S(1)}, bf16[2,4,2,1024]{3,2,1,0:T(2,128)(2,1)S(1)}, u32[]{:S(2)}, u32[]{:S(2)}) collective-permute-start(bf16[2,4,2,1024]{3,2,1,0:T(2,128)(2,1)S(1)} %pad_maximum_fusion.3), channel_id=1, source_target_pairs={{0,4},{1,5},{2,6},{3,7},{4,0},{5,1},{6,2},{7,3},{8,12},{9,13},{10,... | collective-permute-start | bytes 98312 | tf_op jit(solution)/shard_map/ppermute | solution.py:362
  129.7 1.9 %collective-permute-done.18 = bf16[2,4,2,1024]{3,2,1,0:T(2,128)(2,1)S(1)} collective-permute-done((bf16[2,4,2,1024]{3,2,1,0:T(2,128)(2,1)S(1)}, bf16[2,4,2,1024]{3,2,1,0:T(2,128)(2,1)S(1)}, u32[]{:S(2)}, u32[]{:S(2)}) %collective-permute-start.18) | collective-permute-done | bytes 32800 | tf_op jit(solution)/shard_map/ppermute | solution.py:362
  131.5 0.1 pad_maximum_fusion.2
  131.6 0.6 collective-permute-start.19
  132.2 3.7 %collective-permute-done.19 = bf16[4,4,2,1024]{3,2,1,0:T(2,128)(2,1)S(1)} collective-permute-done((bf16[4,4,2,1024]{3,2,1,0:T(2,128)(2,1)S(1)}, bf16[4,4,2,1024]{3,2,1,0:T(2,128)(2,1)S(1)}, u32[]{:S(2)}, u32[]{:S(2)}) %collective-permute-start.19) | collective-permute-done | bytes 65568 | tf_op jit(solution)/shard_map/ppermute | solution.py:362
  136.0 0.2 pad_maximum_fusion
  136.3 1.2 collective-permute-done.20
  137.6 0.1 constant_dynamic-update-slice_fusion.11
  137.7 1.1 gather_fusion.3
  138.8 0.2 copy.20
  139.0 5.6 %convolution_convert_fusion.1 = bf16[16,512]{1,0:T(8,128)(2,1)S(1)} fusion(bf16[16,8192]{1,0:T(8,128)(2,1)S(1)} %bitcast.43, bf16[512,8192]{1,0:T(8,128)(2,1)} %param.11), kind=kOutput, calls=%fused_computation.5 | convolution fusion | flops 134225920 | bytes 8667136 | tf_op jit(solution)/shard_map/dot_general | solution.py:572
  144.6 0.6 reshape.248
  (77 shorter events, 1.1 us)
Async XLA Ops:
  0.6 15.0 %copy-start = (s32[8]{0:T(128)S(1)}, s32[8]{0:T(128)}, u32[]{:S(2)}) copy-start(s32[8]{0:T(128)} %param.13) | copy-start | bytes 100
  0.6 13.8 %copy-start.18 = (s32[64]{0:T(128)S(1)}, s32[64]{0:T(128)}, u32[]{:S(2)}) copy-start(s32[64]{0:T(128)} %units_ref.1) | copy-start | bytes 772
  0.7 14.8 %copy-start.17 = (s32[1024]{0:T(1024)S(1)}, s32[1024]{0:T(1024)}, u32[]{:S(2)}) copy-start(s32[1024]{0:T(1024)} %old_ref.1) | copy-start | bytes 12292
  0.7 15.9 %copy-start.14 = (bf16[8,2,8192]{2,1,0:T(2,128)(2,1)S(1)}, bf16[8,2,8192]{2,1,0:T(2,128)(2,1)}, u32[]{:S(2)}) copy-start(bf16[8,2,8192]{2,1,0:T(2,128)(2,1)} %param.9) | copy-start | bytes 786436
  5.5 48.2 %collective-permute-start.6 = (bf16[4,128,256]{2,1,0:T(8,128)(2,1)}, bf16[4,128,256]{2,1,0:T(8,128)(2,1)S(1)}, u32[]{:S(2)}, u32[]{:S(2)}) collective-permute-start(bf16[4,128,256]{2,1,0:T(8,128)(2,1)} %get-tuple-element.41), channel_id=1, source_target_pairs={{0,8},{1,9},{2,10},{3,11},{4,12},{5,13},{6,14},{7,15},{8,0},{9,1},... | collective-permute-start | bytes 786440 | tf_op jit(solution)/shard_map/ppermute | solution.py:362
  9.6 17.7 %collective-permute-start.8 = (bf16[16,128,256]{2,1,0:T(8,128)(2,1)}, bf16[16,128,256]{2,1,0:T(8,128)(2,1)S(1)}, u32[]{:S(2)}, u32[]{:S(2)}) collective-permute-start(bf16[16,128,256]{2,1,0:T(8,128)(2,1)} %get-tuple-element.45), channel_id=1, source_target_pairs={{0,1},{1,0},{2,3},{3,2},{4,5},{5,4},{6,7},{7,6},{8,9},{9,8},{10,11... | collective-permute-start | bytes 3145736 | tf_op jit(solution)/shard_map/ppermute | solution.py:362
  12.8 45.4 %collective-permute-start.7 = (bf16[4,128,256]{2,1,0:T(8,128)(2,1)}, bf16[4,128,256]{2,1,0:T(8,128)(2,1)S(1)}, u32[]{:S(2)}, u32[]{:S(2)}) collective-permute-start(bf16[4,128,256]{2,1,0:T(8,128)(2,1)} %get-tuple-element.42), channel_id=1, source_target_pairs={{0,12},{1,13},{2,14},{3,15},{4,8},{5,9},{6,10},{7,11},{8,4},{9,5},... | collective-permute-start | bytes 786440 | tf_op jit(solution)/shard_map/ppermute | solution.py:362
  14.2 2.9 %collective-permute-start = (bf16[16,128,256]{2,1,0:T(8,128)(2,1)}, bf16[16,128,256]{2,1,0:T(8,128)(2,1)S(1)}, u32[]{:S(2)}, u32[]{:S(2)}) collective-permute-start(bf16[16,128,256]{2,1,0:T(8,128)(2,1)} %get-tuple-element.37), channel_id=1, source_target_pairs={{0,1},{1,0},{2,3},{3,2},{4,5},{5,4},{6,7},{7,6},{8,9},{9,8},{10,11... | collective-permute-start | bytes 3145736 | tf_op jit(solution)/shard_map/ppermute | solution.py:362
  16.3 17.0 %copy-start.16 = (s32[4]{0:T(128)}, s32[4]{0:T(128)S(1)}, u32[]{:S(2)}) copy-start(s32[4]{0:T(128)S(1)} %gather_fusion) | copy-start | bytes 52
  17.0 37.2 %copy-start.1 = (s32[16]{0:T(128)S(1)}, s32[16]{0:T(128)}, u32[]{:S(2)}) copy-start(s32[16]{0:T(128)} %constant.91.clone) | copy-start | bytes 196
  17.1 13.1 %copy-start.2 = (bf16[16,128,256]{2,1,0:T(8,128)(2,1)}, bf16[16,128,256]{2,1,0:T(8,128)(2,1)S(1)}, u32[]{:S(2)}) copy-start(bf16[16,128,256]{2,1,0:T(8,128)(2,1)S(1)} %collective-permute-done.refs_6_.rest_1_) | copy-start | bytes 3145732
  24.9 8.5 %collective-permute-start.3 = (bf16[1,16,640]{2,1,0:T(8,128)(2,1)S(1)}, bf16[1,16,640]{2,1,0:T(8,128)(2,1)S(1)}, u32[]{:S(2)}, u32[]{:S(2)}) collective-permute-start(bf16[1,16,640]{2,1,0:T(8,128)(2,1)S(1)} %bitcast.47), channel_id=1, source_target_pairs={{0,12},{1,13},{2,14},{3,15},{4,8},{5,9},{6,10},{7,11},{8,4},{9,5},... | collective-permute-start | bytes 61448 | tf_op jit(solution)/shard_map/ppermute | solution.py:362
  27.3 9.7 %collective-permute-start.2 = (bf16[1,16,640]{2,1,0:T(8,128)(2,1)S(1)}, bf16[1,16,640]{2,1,0:T(8,128)(2,1)S(1)}, u32[]{:S(2)}, u32[]{:S(2)}) collective-permute-start(bf16[1,16,640]{2,1,0:T(8,128)(2,1)S(1)} %bitcast.48), channel_id=1, source_target_pairs={{0,4},{1,5},{2,6},{3,7},{4,0},{5,1},{6,2},{7,3},{8,12},{9,13},{10,... | collective-permute-start | bytes 61448 | tf_op jit(solution)/shard_map/ppermute | solution.py:362
  27.3 28.0 %copy-start.3 = (bf16[16,128,256]{2,1,0:T(8,128)(2,1)}, bf16[16,128,256]{2,1,0:T(8,128)(2,1)S(1)}, u32[]{:S(2)}) copy-start(bf16[16,128,256]{2,1,0:T(8,128)(2,1)S(1)} %collective-permute-done.8.rest_1_) | copy-start | bytes 3145732
  27.3 11.2 %collective-permute-start.1 = (bf16[1,16,640]{2,1,0:T(8,128)(2,1)S(1)}, bf16[1,16,640]{2,1,0:T(8,128)(2,1)S(1)}, u32[]{:S(2)}, u32[]{:S(2)}) collective-permute-start(bf16[1,16,640]{2,1,0:T(8,128)(2,1)S(1)} %bitcast.49), channel_id=1, source_target_pairs={{0,8},{1,9},{2,10},{3,11},{4,12},{5,13},{6,14},{7,15},{8,0},{9,1},... | collective-permute-start | bytes 61448 | tf_op jit(solution)/shard_map/ppermute | solution.py:362
  33.3 25.8 %collective-permute-start.9 = (bf16[4,128,256]{2,1,0:T(8,128)(2,1)}, bf16[4,128,256]{2,1,0:T(8,128)(2,1)S(1)}, u32[]{:S(2)}, u32[]{:S(2)}) collective-permute-start(bf16[4,128,256]{2,1,0:T(8,128)(2,1)} %get-tuple-element.46), channel_id=1, source_target_pairs={{0,8},{1,9},{2,10},{3,11},{4,12},{5,13},{6,14},{7,15},{8,0},{9,1},... | collective-permute-start | bytes 786440 | tf_op jit(solution)/shard_map/ppermute | solution.py:362
  37.0 38.1 %collective-permute-start.11 = (bf16[8,128,256]{2,1,0:T(8,128)(2,1)}, bf16[8,128,256]{2,1,0:T(8,128)(2,1)S(1)}, u32[]{:S(2)}, u32[]{:S(2)}) collective-permute-start(bf16[8,128,256]{2,1,0:T(8,128)(2,1)} %get-tuple-element.49), channel_id=1, source_target_pairs={{0,2},{1,3},{2,0},{3,1},{4,6},{5,7},{6,4},{7,5},{8,10},{9,11},{10,... | collective-permute-start | bytes 1572872 | tf_op jit(solution)/shard_map/ppermute | solution.py:362
  38.6 13.9 %collective-permute-start.4 = (bf16[4,16,640]{2,1,0:T(8,128)(2,1)S(1)}, bf16[4,16,640]{2,1,0:T(8,128)(2,1)S(1)}, u32[]{:S(2)}, u32[]{:S(2)}) collective-permute-start(bf16[4,16,640]{2,1,0:T(8,128)(2,1)S(1)} %pad_maximum_fusion.1), channel_id=1, source_target_pairs={{0,2},{1,3},{2,0},{3,1},{4,6},{5,7},{6,4},{7,5},{8,10},{9,11},{10,... | collective-permute-start | bytes 245768 | tf_op jit(solution)/shard_map/ppermute | solution.py:362
  53.1 10.0 %collective-permute-start.5 = (bf16[8,16,640]{2,1,0:T(8,128)(2,1)}, bf16[8,16,640]{2,1,0:T(8,128)(2,1)}, u32[]{:S(2)}, u32[]{:S(2)}) collective-permute-start(bf16[8,16,640]{2,1,0:T(8,128)(2,1)} %get-tuple-element.77), channel_id=1, source_target_pairs={{0,1},{1,0},{2,3},{3,2},{4,5},{5,4},{6,7},{7,6},{8,9},{9,8},{10,11... | collective-permute-start | bytes 491528 | tf_op jit(solution)/shard_map/ppermute | solution.py:362
  53.8 13.6 %copy-start.9 = (bf16[4,128,256]{2,1,0:T(8,128)(2,1)}, bf16[4,128,256]{2,1,0:T(8,128)(2,1)S(1)}, u32[]{:S(2)}) copy-start(bf16[4,128,256]{2,1,0:T(8,128)(2,1)S(1)} %collective-permute-done.6.refs_7_) | copy-start | bytes 786436
  53.8 19.6 %collective-permute-start.10 = (bf16[4,128,256]{2,1,0:T(8,128)(2,1)}, bf16[4,128,256]{2,1,0:T(8,128)(2,1)S(1)}, u32[]{:S(2)}, u32[]{:S(2)}) collective-permute-start(bf16[4,128,256]{2,1,0:T(8,128)(2,1)} %get-tuple-element.47), channel_id=1, source_target_pairs={{0,12},{1,13},{2,14},{3,15},{4,8},{5,9},{6,10},{7,11},{8,4},{9,5},... | collective-permute-start | bytes 786440 | tf_op jit(solution)/shard_map/ppermute | solution.py:362
  58.2 9.2 %copy-start.10 = (bf16[4,128,256]{2,1,0:T(8,128)(2,1)}, bf16[4,128,256]{2,1,0:T(8,128)(2,1)S(1)}, u32[]{:S(2)}) copy-start(bf16[4,128,256]{2,1,0:T(8,128)(2,1)S(1)} %collective-permute-done.7.refs_8_) | copy-start | bytes 786436
  58.2 49.1 %collective-permute-start.14 = (bf16[8,128,256]{2,1,0:T(8,128)(2,1)}, bf16[8,128,256]{2,1,0:T(8,128)(2,1)S(1)}, u32[]{:S(2)}, u32[]{:S(2)}) collective-permute-start(bf16[8,128,256]{2,1,0:T(8,128)(2,1)} %get-tuple-element.60), channel_id=1, source_target_pairs={{0,10},{1,11},{2,8},{3,9},{4,14},{5,15},{6,12},{7,13},{8,2},{9,3},... | collective-permute-start | bytes 1572872 | tf_op jit(solution)/shard_map/ppermute | solution.py:362
  59.1 16.0 %copy-start.11 = (bf16[4,128,256]{2,1,0:T(8,128)(2,1)}, bf16[4,128,256]{2,1,0:T(8,128)(2,1)S(1)}, u32[]{:S(2)}) copy-start(bf16[4,128,256]{2,1,0:T(8,128)(2,1)S(1)} %collective-permute-done.9.refs_7_) | copy-start | bytes 786436
  59.1 26.7 %collective-permute-start.12 = (bf16[8,128,256]{2,1,0:T(8,128)(2,1)}, bf16[8,128,256]{2,1,0:T(8,128)(2,1)S(1)}, u32[]{:S(2)}, u32[]{:S(2)}) collective-permute-start(bf16[8,128,256]{2,1,0:T(8,128)(2,1)} %get-tuple-element.53), channel_id=1, source_target_pairs={{0,4},{1,5},{2,6},{3,7},{4,0},{5,1},{6,2},{7,3},{8,12},{9,13},{10,... | collective-permute-start | bytes 1572872 | tf_op jit(solution)/shard_map/ppermute | solution.py:362
  63.1 37.4 %collective-permute-start.13 = (bf16[8,128,256]{2,1,0:T(8,128)(2,1)}, bf16[8,128,256]{2,1,0:T(8,128)(2,1)S(1)}, u32[]{:S(2)}, u32[]{:S(2)}) collective-permute-start(bf16[8,128,256]{2,1,0:T(8,128)(2,1)} %get-tuple-element.54), channel_id=1, source_target_pairs={{0,6},{1,7},{2,4},{3,5},{4,2},{5,3},{6,0},{7,1},{8,14},{9,15},{10,... | collective-permute-start | bytes 1572872 | tf_op jit(solution)/shard_map/ppermute | solution.py:362
  64.8 0.7 copy-start.8
  73.3 1.8 %copy-start.12 = (bf16[4,128,256]{2,1,0:T(8,128)(2,1)}, bf16[4,128,256]{2,1,0:T(8,128)(2,1)S(1)}, u32[]{:S(2)}) copy-start(bf16[4,128,256]{2,1,0:T(8,128)(2,1)S(1)} %collective-permute-done.10.refs_8_) | copy-start | bytes 786436
  73.3 38.4 %collective-permute-start.15 = (bf16[4,128,256]{2,1,0:T(8,128)(2,1)}, bf16[4,128,256]{2,1,0:T(8,128)(2,1)S(1)}, u32[]{:S(2)}, u32[]{:S(2)}) collective-permute-start(bf16[4,128,256]{2,1,0:T(8,128)(2,1)} %get-tuple-element.62), channel_id=1, source_target_pairs={{0,14},{1,15},{2,12},{3,13},{4,10},{5,11},{6,8},{7,9},{8,6},{9,7},... | collective-permute-start | bytes 786440 | tf_op jit(solution)/shard_map/ppermute | solution.py:362
  75.1 0.8 copy-start.4
  81.8 35.8 %collective-permute-start.16 = (bf16[4,128,256]{2,1,0:T(8,128)(2,1)}, bf16[4,128,256]{2,1,0:T(8,128)(2,1)S(1)}, u32[]{:S(2)}, u32[]{:S(2)}) collective-permute-start(bf16[4,128,256]{2,1,0:T(8,128)(2,1)} %get-tuple-element.66), channel_id=1, source_target_pairs={{0,14},{1,15},{2,12},{3,13},{4,10},{5,11},{6,8},{7,9},{8,6},{9,7},... | collective-permute-start | bytes 786440 | tf_op jit(solution)/shard_map/ppermute | solution.py:362
  85.8 14.7 %copy-start.6 = (bf16[8,128,256]{2,1,0:T(8,128)(2,1)}, bf16[8,128,256]{2,1,0:T(8,128)(2,1)S(1)}, u32[]{:S(2)}) copy-start(bf16[8,128,256]{2,1,0:T(8,128)(2,1)S(1)} %collective-permute-done.12.refs_7_) | copy-start | bytes 1572868
  100.6 0.8 copy-start.7
  107.3 4.4 %copy-start.5 = (bf16[8,128,256]{2,1,0:T(8,128)(2,1)}, bf16[8,128,256]{2,1,0:T(8,128)(2,1)S(1)}, u32[]{:S(2)}) copy-start(bf16[8,128,256]{2,1,0:T(8,128)(2,1)S(1)} %collective-permute-done.14.refs_7_) | copy-start | bytes 1572868
  111.7 0.7 copy-start.13
  117.6 0.7 copy-start.15
  122.2 4.6 %collective-permute-start.17 = (bf16[1,4,2,1024]{3,2,1,0:T(2,128)(2,1)S(1)}, bf16[1,4,2,1024]{3,2,1,0:T(2,128)(2,1)S(1)}, u32[]{:S(2)}, u32[]{:S(2)}) collective-permute-start(bf16[1,4,2,1024]{3,2,1,0:T(2,128)(2,1)S(1)} %broadcast_in_dim_reshape.4), channel_id=1, source_target_pairs={{0,8},{1,9},{2,10},{3,11},{4,12},{5,13},{6,14},{7,15},{8,0},{9,1},... | collective-permute-start | bytes 49160 | tf_op jit(solution)/shard_map/ppermute | solution.py:362
  126.9 4.6 %collective-permute-start.18 = (bf16[2,4,2,1024]{3,2,1,0:T(2,128)(2,1)S(1)}, bf16[2,4,2,1024]{3,2,1,0:T(2,128)(2,1)S(1)}, u32[]{:S(2)}, u32[]{:S(2)}) collective-permute-start(bf16[2,4,2,1024]{3,2,1,0:T(2,128)(2,1)S(1)} %pad_maximum_fusion.3), channel_id=1, source_target_pairs={{0,4},{1,5},{2,6},{3,7},{4,0},{5,1},{6,2},{7,3},{8,12},{9,13},{10,... | collective-permute-start | bytes 98312 | tf_op jit(solution)/shard_map/ppermute | solution.py:362
  131.6 4.3 %collective-permute-start.19 = (bf16[4,4,2,1024]{3,2,1,0:T(2,128)(2,1)S(1)}, bf16[4,4,2,1024]{3,2,1,0:T(2,128)(2,1)S(1)}, u32[]{:S(2)}, u32[]{:S(2)}) collective-permute-start(bf16[4,4,2,1024]{3,2,1,0:T(2,128)(2,1)S(1)} %pad_maximum_fusion.2), channel_id=1, source_target_pairs={{0,2},{1,3},{2,0},{3,1},{4,6},{5,7},{6,4},{7,5},{8,10},{9,11},{10,... | collective-permute-start | bytes 196616 | tf_op jit(solution)/shard_map/ppermute | solution.py:362
  136.2 1.4 collective-permute-start.20

commit v5 on v4

--- a/solution.py
+++ b/solution.py
@@ -184,26 +184,27 @@
 ALIGN = 16
 
 
-def place_kernel(entries, started, finish, *refs):
+def place_kernel(entries, started, attends, finish, late, *refs):
     refs = list(refs)
     table_ref, order_ref, length_ref, fresh_ref = refs[:4]
     refs = refs[4:]
-    queries_ref = refs.pop(0)
-    if started:
-        weighted_in, total_in = refs.pop(0), refs.pop(0)
+    if attends:
+        queries_ref = refs.pop(0)
+        if started:
+            weighted_in, total_in = refs.pop(0), refs.pop(0)
+        part_ref = refs.pop(0) if late else None
     sources = 1 + max(source for source, _, _ in entries)
     source_refs, refs = refs[:sources], refs[sources:]
     if started:
         refs.pop(0)
-    out_ref, weighted_ref, total_ref = refs[:3]
-    refs = refs[3:]
+    out_ref = refs.pop(0)
+    if attends:
+        weighted_ref, total_ref = refs.pop(0), refs.pop(0)
     attended_ref = refs.pop(0) if finish else None
     stage, load_sem, store_sem = refs
-    if started:
+    if attends and started:
         weighted_ref[...] = weighted_in[...]
         total_ref[...] = total_in[...]
-    else:
-        own_terms(queries_ref, fresh_ref, weighted_ref, total_ref)
     loads = []
     for n, (source, index, _) in enumerate(entries):
         index = order_ref[index[0]] if isinstance(index, tuple) else index
@@ -234,8 +235,19 @@
         copy = pltpu.make_async_copy(stage.at[n], out_ref.at[w], store_sem.at[n])
         copy.start()
         stores.append(copy)
+    if attends and not started:
+        own_terms(queries_ref, fresh_ref, weighted_ref, total_ref)
+    lane = lax.broadcasted_iota(jnp.int32, (QROWS, HD), 1)
+    if late:
+        sums = part_ref[len(late) * QROWS :, :].astype(jnp.float32)
+    for n, at in enumerate(late):
+        unit = table_ref[at] // PER_UNIT
+        mine = (lane == 2 * n) | (lane == 2 * n + 1)
+        total = jnp.sum(jnp.where(mine, sums, 0.0), axis=1, keepdims=True)
+        weighted_ref[unit] += part_ref[n * QROWS : (n + 1) * QROWS, :].astype(jnp.float32)
+        total_ref[unit] += jnp.broadcast_to(total, (QROWS, HD))
     group = 4
-    for first in range(0, len(entries), group):
+    for first in range(0, len(entries) if attends else 0, group):
         found = []
         for n in range(first, min(first + group, len(entries))):
             key = entries[n][2]
@@ -276,15 +288,18 @@
         total_ref[unit] = jnp.broadcast_to(total, (QROWS, HD))
 
 
-def place_pages(table, order, lengths, fresh, queries, sums, sources, entries, cache, finish):
-    started = cache is not None
+def place_pages(
+    table, order, lengths, fresh, queries, sums, parts, late, sources, entries, cache, finish
+):
+    started, attends = cache is not None, queries is not None
     page_shape = sources[0].shape[1:]
     pages_dev = U_DEV * PER_UNIT
-    args = [table, order, lengths, fresh, queries]
-    specs = [smem_spec()] * 3 + [vmem_spec()] * 2
-    if started:
-        args += list(sums)
-        specs += [vmem_spec()] * 2
+    args = [table, order, lengths, fresh]
+    specs = [smem_spec()] * 3 + [vmem_spec()]
+    if attends:
+        vmem_args = [queries] + (list(sums) if started else []) + list(parts)
+        args += vmem_args
+        specs += [vmem_spec()] * len(vmem_args)
     args += list(sources)
     specs += [any_spec()] * len(sources)
     aliases = {}
@@ -293,14 +308,16 @@
         args.append(cache)
         specs.append(any_spec())
     outs = [jax.ShapeDtypeStruct((pages_dev,) + page_shape, jnp.bfloat16)]
-    outs += [jax.ShapeDtypeStruct((U_DEV, QROWS, HD), jnp.float32)] * 2
-    out_specs = [any_spec()] + [vmem_spec()] * 2
+    out_specs = [any_spec()]
+    if attends:
+        outs += [jax.ShapeDtypeStruct((U_DEV, QROWS, HD), jnp.float32)] * 2
+        out_specs += [vmem_spec()] * 2
     if finish:
         outs.append(jax.ShapeDtypeStruct((U_DEV, QROWS, HD), jnp.bfloat16))
         out_specs.append(vmem_spec())
     count = len(entries)
     result = pl.pallas_call(
-        functools.partial(place_kernel, entries, started, finish),
+        functools.partial(place_kernel, entries, started, attends, finish, late),
         out_shape=tuple(outs),
         in_specs=specs,
         out_specs=tuple(out_specs),
@@ -316,66 +333,118 @@
     return result[0], result[1:3], result[3] if finish else None
 
 
-def own_rows_kernel(rows_ref, place_ref, request_ref, cosine_ref, sine_ref, queries_ref, fresh_ref):
-    width = rows_ref.shape[2]
-    pieces = place_ref.shape[0] // U_DEV
+def rows_kernel(
+    late,
+    units_ref,
+    turn_ref,
+    order_ref,
+    ids_ref,
+    lengths_ref,
+    rows_ref,
+    cosine_ref,
+    sine_ref,
+    pages_ref,
+    passed_ref,
+    queries_ref,
+    fresh_ref,
+    part_ref,
+    stage,
+    load_sem,
+):
+    device = lax.axis_index("tp")
+    devices, _, width = rows_ref.shape
+    pieces = (GROUP + 2) * HD // width
+    half_dim = HD // 2
     row = lax.broadcasted_iota(jnp.int32, rows_ref.shape[1:], 0)
-    half_dim = HD // 2
-    for unit in range(U_DEV):
+    lane = lax.broadcasted_iota(jnp.int32, (QROWS, HD), 1)
+
+    def unit_rows(unit):
+        request, head = unit // KVH, unit % KVH
         found = []
         for piece in range(pieces):
-            block = rows_ref[place_ref[unit * pieces + piece]].astype(jnp.float32)
+            place = turn_ref[(head * pieces + piece) ^ device]
+            block = rows_ref[place].astype(jnp.float32)
             picked = [
-                jnp.sum(
-                    jnp.where(row == 2 * request_ref[unit] + j, block, 0.0), axis=0, keepdims=True
-                )
+                jnp.sum(jnp.where(row == 2 * request + j, block, 0.0), axis=0, keepdims=True)
                 for j in range(2)
             ]
             for at in range(0, width, HD):
                 found.append([line[:, at : at + HD] for line in picked])
+        turned = []
         for j in range(2):
             heads = jnp.concatenate([head[j] for head in found[: GROUP + 1]], axis=0)
-            turned = jnp.concatenate([heads[:, half_dim:], heads[:, :half_dim]], axis=1)
-            cosine = cosine_ref[2 * unit + j : 2 * unit + j + 1, :]
-            sine = sine_ref[2 * unit + j : 2 * unit + j + 1, :]
-            heads = (heads * cosine + turned * sine).astype(jnp.bfloat16).astype(jnp.float32)
-            queries_ref[unit, j * GROUP : (j + 1) * GROUP, :] = heads[:GROUP]
-            fresh_ref[2 * unit + j : 2 * unit + j + 1, :HD] = heads[GROUP:]
-            fresh_ref[2 * unit + j : 2 * unit + j + 1, HD:] = found[GROUP + 1][j]
-
-
-def own_rows(rows, places, requests, cosine, sine):
-    queries, fresh = pl.pallas_call(
-        own_rows_kernel,
+            swapped = jnp.concatenate([heads[:, half_dim:], heads[:, :half_dim]], axis=1)
+            cosine = cosine_ref[pl.ds(2 * request + j, 1), :]
+            sine = sine_ref[pl.ds(2 * request + j, 1), :]
+            heads = heads * cosine + swapped * sine
+            turned.append(heads.astype(jnp.bfloat16).astype(jnp.float32))
+        return turned, [found[GROUP + 1][j] for j in range(2)]
+
+    loads = []
+    for slot, (source, at) in enumerate(late):
+        page = pages_ref.at[order_ref[at]] if source == 0 else passed_ref.at[at]
+        copy = pltpu.make_async_copy(page, stage.at[slot], load_sem.at[slot])
+        copy.start()
+        loads.append(copy)
+    sums = jnp.zeros((QROWS, HD), jnp.float32)
+    for slot in range(len(late)):
+        page = ids_ref[slot]
+        unit = page // PER_UNIT
+        limit = lengths_ref[unit // KVH] - (page % PER_UNIT) * PAGE
+        turned, _ = unit_rows(unit)
+        query = jnp.concatenate([turned[0][:GROUP], turned[1][:GROUP]], axis=0)
+        loads[slot].wait()
+        weighted, total = attend(
+            query.astype(jnp.bfloat16), stage[slot, :, :HD], stage[slot, :, HD:], limit
+        )
+        part_ref[slot * QROWS : (slot + 1) * QROWS, :] = weighted.astype(jnp.bfloat16)
+        high = total.astype(jnp.bfloat16).astype(jnp.float32)
+        sums = jnp.where(lane == 2 * slot, high, sums)
+        sums = jnp.where(lane == 2 * slot + 1, total - high, sums)
+    part_ref[len(late) * QROWS :, :] = sums.astype(jnp.bfloat16)
+    for slot in range(U_DEV):
+        turned, values = unit_rows(units_ref[slot])
+        for j in range(2):
+            at = 2 * slot + j
+            queries_ref[slot, j * GROUP : (j + 1) * GROUP, :] = turned[j][:GROUP]
+            fresh_ref[at : at + 1, :HD] = turned[j][GROUP:]
+            fresh_ref[at : at + 1, HD:] = values[j]
+
+
+def rows_and_parts(units, turn, order, ids, lengths, rows, cosine, sine, pages, passed, late):
+    return pl.pallas_call(
+        functools.partial(rows_kernel, late),
         out_shape=(
             jax.ShapeDtypeStruct((U_DEV, QROWS, HD), jnp.float32),
             jax.ShapeDtypeStruct((2 * U_DEV, 2 * HD), jnp.float32),
+            jax.ShapeDtypeStruct(((len(late) + 1) * QROWS, HD), jnp.bfloat16),
         ),
-        in_specs=[vmem_spec(), smem_spec(), smem_spec(), vmem_spec(), vmem_spec()],
-        out_specs=(vmem_spec(), vmem_spec()),
-        name="own_rows",
-    )(rows, places, requests, cosine, sine)
-    return queries, fresh
+        in_specs=[smem_spec()] * 5 + [vmem_spec()] * 3 + [any_spec()] * 2,
+        out_specs=(vmem_spec(),) * 3,
+        scratch_shapes=[
+            pltpu.VMEM((len(late),) + pages.shape[1:], pages.dtype),
+            pltpu.SemaphoreType.DMA((len(late),)),
+        ],
+        compiler_params=pltpu.CompilerParams(vmem_limit_bytes=VMEM_LIMIT),
+        name="rows_and_parts",
+    )(units, turn, order, ids, lengths, rows, cosine, sine, pages, passed)
 
 
 def swap(values, key, devices):
     return lax.ppermute(values, "tp", [(i, i ^ key) for i in range(devices)])
 
 
-def gather_swaps(values, devices, direct):
+def gather_line(values, devices):
     values = values[None]
     step = devices // 2
-    span = [0]
-    if direct and devices >= 4:
-        keys = [step, step // 2, step + step // 2]
-        values = jnp.concatenate([values] + [swap(values, k, devices) for k in keys], axis=0)
-        span = [0] + keys
-        step //= 4
-    while step:
-        values = jnp.concatenate([values, swap(values, step, devices)], axis=0)
-        span = span + [s ^ step for s in span]
-        step //= 2
-    return values, span
+    keys = [step // 2, step, step + step // 2]
+    found = [swap(values, k, devices) for k in keys]
+    return jnp.concatenate([values] + found, axis=0), [0] + keys
+
+
+def gather_more(values, span, step, devices):
+    values = jnp.concatenate([values, swap(values, step, devices)], axis=0)
+    return values, span + [s ^ step for s in span]
 
 
 def after(value, *others):
@@ -464,40 +533,82 @@
     else:
         table = source_dev * capacity + rank
 
+    slot_index = jnp.sum(
+        jnp.where(
+            new_units[None, :] == jnp.arange(total_units, dtype=jnp.int32)[:, None],
+            jnp.arange(total_units, dtype=jnp.int32)[None, :],
+            0,
+        ),
+        axis=1,
+    )
+    if pairwise:
+        ids = old_pages.reshape(devices, 1, pages_dev)
+        ids = jnp.concatenate([ids[device], ids[device ^ 1]], axis=0)
+        reached = jnp.sum(
+            jnp.where(
+                (ids // PER_UNIT)[..., None] == new_units, jnp.arange(total_units) // U_DEV, 0
+            ),
+            axis=-1,
+        )
+        chosen = reached == (device ^ d)
+        earlier = jnp.arange(pages_dev)[None, :] < jnp.arange(pages_dev)[:, None]
+        ranks = jnp.sum((chosen[:, None, :] & earlier[None]).astype(jnp.int32), axis=-1)
+        wants = jnp.arange(capacity, dtype=jnp.int32)[None, :, None]
+        picked = chosen[:, None, :] & (ranks[:, None, :] == wants)
+        late_ids = jnp.sum(jnp.where(picked, ids[:, None, :], 0), axis=-1)
+        late_ids = late_ids.reshape(2 * capacity).astype(jnp.int32)
     flat_rows = hidden_states.reshape(requests * 2, D)
     if pairwise:
-        flat_rows = after(flat_rows, cross_near)
+        flat_rows = after(flat_rows, cross_near, cross_far)
     own_part = lax.dot_general(
         flat_rows, qkv_weight, (((1,), (1,)), ((), ())), preferred_element_type=jnp.float32
     ).astype(jnp.bfloat16)
-    own_requests, own_heads = own_units // KVH, own_units % KVH
-    positions = own_lengths[:, None] + jnp.arange(2, dtype=jnp.int32)[None, :]
-    cosine, sine = rope_tables(positions.reshape(2 * U_DEV))
     if pairwise:
-        rows, span = gather_swaps(own_part, devices, True)
-        turn = jnp.array([span.index(i) for i in range(devices)], jnp.int32)
-        pieces = devices // KVH
-        holders = own_heads[:, None] * pieces + jnp.arange(pieces, dtype=jnp.int32)[None, :]
-        places = turn[(holders ^ device).reshape(U_DEV * pieces)]
-        queries, fresh = own_rows(rows, places, own_requests, cosine, sine)
-        moved_a2 = send(after(piece(cross_far, 0), own_part), a + 0)
-        moved_b2 = send(after(piece(cross_far, 1), own_part), b + 0)
+        positions = context_lengths[:, None] + jnp.arange(2, dtype=jnp.int32)[None, :]
+        cosine, sine = rope_tables(positions.reshape(2 * requests))
+        rows, span = gather_line(own_part, devices)
+        moved_a2 = send(after(piece(cross_far, 0), own_part, moved_a), a)
+        moved_b2 = send(after(piece(cross_far, 1), own_part), b)
         near_chunks = next_pack(
             order,
-            [cache_pages, after(cross_near, own_part)],
+            [cache_pages, after(cross_near, rows)],
             capacity,
             [own(k) + passed(1, n + 1) for n, k in enumerate(near)],
         )
-        moved_near = [send(chunk, k) for chunk, k in zip(near_chunks, near)]
+        rows, span = gather_more(after(rows, moved_a, moved_b), span, 2, devices)
+        rows, span = gather_more(rows, span, 1, devices)
+        moved_near = [
+            send(after(near_chunks[0], rows), near[0]),
+            send(near_chunks[1], near[1]),
+            send(after(near_chunks[2], rows), near[2]),
+        ]
+        turn = jnp.array([span.index(i) for i in range(devices)], jnp.int32)
+        late = [(0, d * capacity + r) for r in range(capacity)]
+        late += [(1, 3 * capacity + r) for r in range(capacity)]
+        places = [key * capacity + r for key in (d, d + 1) for r in range(capacity)]
+        queries, fresh, sent = rows_and_parts(
+            own_units,
+            turn,
+            order,
+            late_ids,
+            context_lengths,
+            rows,
+            cosine,
+            sine,
+            cache_pages,
+            cross_far,
+            late,
+        )
+        parts = [send(sent, d)]
         chunk_c, chunk_d = next_pack(
             order,
-            [cache_pages, after(cross_far, moved_a)],
+            [cache_pages, after(cross_far, rows)],
             capacity,
             [own(c) + passed(1, 2), own(d)],
         )
-        moved_c = send(after(chunk_c, moved_b), c)
-
-        def place(groups, sums, cache, finish):
+        moved_c = send(after(chunk_c, moved_a2, parts[0]), c)
+
+        def place(groups, sums, cache, attends, parts, finish):
             entries, sources = [], []
             for array, keys, first in groups:
                 for n, key in enumerate(keys):
@@ -506,31 +617,57 @@
                         entries.append((len(sources), at, (key * capacity + r,)))
                 sources.append(array)
             return place_pages(
-                table, order, own_lengths, fresh, queries, sums, sources, entries, cache, finish
+                table,
+                order,
+                own_lengths,
+                fresh,
+                queries if attends else None,
+                sums,
+                parts,
+                places if parts else [],
+                sources,
+                entries,
+                cache,
+                finish,
             )
 
         new_cache, sums, _ = place(
             [(cache_pages, [0], 0), (cross_near, [1], 0), (moved_a, [a], 0), (moved_b, [b], 0)],
             None,
             None,
+            True,
+            [],
             False,
         )
-        moved_d = send(after(chunk_d, moved_a2, sums[0]), d)
+        moved_d = send(after(chunk_d, moved_b2, sums[0]), d)
         new_cache, sums, _ = place(
             [(moved_a2, [a + 1], 0), (moved_b2, [b + 1], 0), (moved_near[0], [2, 3], 0)],
             sums,
             new_cache,
+            True,
+            [],
             False,
         )
-        moved_d2 = send(after(piece(cross_far, 3), moved_b2, sums[0]), d)
         new_cache, sums, _ = place(
-            [(m, [k, k + 1], 0) for m, k in zip(moved_near[1:], near[1:])], sums, new_cache, False
-        )
-        new_cache, sums, _ = place(
-            [(moved_c, [c, c + 1], 0), (moved_d, [d], 0)], sums, new_cache, False
-        )
-        new_cache, sums, attended = place([(moved_d2, [d + 1], 0)], sums, new_cache, True)
+            [(m, [k, k + 1], 0) for m, k in zip(moved_near[1:], near[1:])],
+            sums,
+            new_cache,
+            True,
+            [],
+            False,
+        )
+        new_cache, sums, attended = place(
+            [(moved_c, [c, c + 1], 0)], sums, new_cache, True, parts, True
+        )
+        attended = after(attended, moved_d)
+        moved_d2 = send(after(piece(cross_far, 3), attended), d)
+        new_cache, _, _ = place(
+            [(moved_d, [d], 0), (moved_d2, [d + 1], 0)], None, new_cache, False, [], False
+        )
     else:
+        own_requests, own_heads = own_units // KVH, own_units % KVH
+        positions = own_lengths[:, None] + jnp.arange(2, dtype=jnp.int32)[None, :]
+        cosine, sine = rope_tables(positions.reshape(2 * U_DEV))
         rows = lax.all_gather(own_part, "tp", axis=1, tiled=True)
         rows = rows.reshape(requests, 2, KVH, GROUP + 2, HD)
         rows = rows[own_requests, :, own_heads].astype(jnp.float32)
@@ -545,21 +682,25 @@
         queries = queries.astype(jnp.bfloat16).astype(jnp.float32)
         entries = [(0, (w,), w) for w in range(pages_dev)]
         new_cache, sums, attended = place_pages(
-            table, table, own_lengths, fresh, queries, None, [arrived], entries, None, True
-        )
-
-    slot_index = jnp.sum(
-        jnp.where(
-            new_units[None, :] == jnp.arange(total_units, dtype=jnp.int32)[:, None],
-            jnp.arange(total_units, dtype=jnp.int32)[None, :],
-            0,
-        ),
-        axis=1,
-    )
+            table,
+            table,
+            own_lengths,
+            fresh,
+            queries,
+            None,
+            [],
+            [],
+            [arrived],
+            entries,
+            None,
+            True,
+        )
+
     attended = attended.reshape(U_DEV, 2, GROUP * HD)
     if pairwise:
-        heads, span = gather_swaps(attended, devices, False)
-        turn = jnp.array([span.index(i) for i in range(devices)], jnp.int32)
+        heads, span = gather_line(attended, devices)
+        heads, span = gather_more(heads, span, 2, devices)
+        heads, span = gather_more(heads, span, 1, devices)
         holder = turn[(slot_index // U_DEV) ^ device]
         heads = heads.reshape(total_units, 2, GROUP * HD)[holder * U_DEV + slot_index % U_DEV]
     else:

time: 147 us -> 156 us (1.061)
  waiting for transfers between devices: 39.8 us -> 53 us
  local copies, waits for them, and re-layouts: 14 us -> 10.9 us
  starting transfers between devices: 32.1 us -> 29.8 us
  Pallas kernels: 41.8 us -> 43.4 us
    ppermute x21 -> x23, waiting for transfers between devices: 39.8 us -> 53 us  [swap(): return lax.ppermute(values, 'tp', [(i, i ^ key) for i in range(devices)])]
    ppermute x21 -> x23, starting transfers between devices: 32.1 us -> 29.8 us  [swap(): return lax.ppermute(values, 'tp', [(i, i ^ key) for i in range(devices)])]
    pallas_call x6, Pallas kernels: 27.9 us -> 29.5 us  [the longest x5 24.8 us: place_pages(): pl.pallas_call(functools.partial(place_kernel, entries, started, attends,...]
    unnamed x46 -> x51, local copies, waits for them, and re-layouts: 5.88 us -> 4.31 us
  transfers between devices with their start and end apart: 21 -> 23, of which waited for: 7 -> 8; matrix products, arithmetic and copies ran while one was open for 12% -> 14% of each run, Pallas kernels for 23% -> 21%
where the time goes in v5:
time: 156 us; the launch traced here: 154 us
  waiting for transfers between devices  53 us (34%)
  Pallas kernels  43.4 us (28%)
  starting transfers between devices  29.8 us (19%)
  matrix products  13.2 us (8%)
  local copies, waits for them, and re-layouts  10.9 us (7%)
  other arithmetic  2.94 us (2%)
    ppermute x23, waiting for transfers between devices, swap(): return lax.ppermute(values, 'tp', [(i, i ^ key) for i in range(devices)])  53 us
    ppermute x23, starting transfers between devices, swap(): return lax.ppermute(values, 'tp', [(i, i ^ key) for i in range(devices)])  29.8 us
    pallas_call x5, Pallas kernels, place_pages(): pl.pallas_call(functools.partial(place_kernel, entries, started, attends,...  24.8 us
    pallas_call x3, Pallas kernels, next_pack(): pl.pallas_call(functools.partial(next_pack_kernel, capacity, outs_pages,...  9.02 us
    dot_general x1, matrix products, body(): lax.dot_general(flat_rows, qkv_weight, (((1,), (1,)), ((), ())), preferre...  7.52 us
    dot_general x1, matrix products, body(): lax.dot_general(logical, out_weight, (((1,), (1,)), ((), ())), preferred_...  5.64 us
    pallas_call x1, Pallas kernels, first_pack(): pl.pallas_call(functools.partial(first_pack_kernel, devices, capacity, ou...  4.82 us
    pallas_call x1, Pallas kernels, rows_and_parts(): pl.pallas_call(functools.partial(rows_kernel, late), out_shape=(jax.Shape...  4.74 us
  transfers between devices with their start and end apart: 23, of which 8 were waited for; matrix products, arithmetic and copies ran while one was open for 14% of the time, Pallas kernels for 21%

profile of v5, /device:TPU:0, one launch (start us, length us, event | category | flops | bytes accessed | tf_op | source)
XLA Modules:
  0.0 154.5 jit_solution(4571913207893779612)
XLA Ops:
  0.7 4.8 %first_pack.1 = (bf16[4,128,256]{2,1,0:T(8,128)(2,1)}, bf16[16,128,256]{2,1,0:T(8,128)(2,1)}, s32[64]{0:T(128)}) custom-call(s32[64]{0:T(128)} %units_ref.1, s32[1024]{0:T(1024)} %old_ref.1, bf16[64,128,256]{2,1,0:T(8,128)(2,1)} %rest_0_.5), custom_call_target="tpu_custom_call" | custom-call | tf_op jit(solution)/shard_map/first_pack/pallas_call | solution.py:142
  5.5 3.2 %next_pack.3 = (bf16[4,128,256]{2,1,0:T(8,128)(2,1)}, bf16[16,128,256]{2,1,0:T(8,128)(2,1)}) custom-call(s32[64]{0:T(128)} %get-tuple-element.38.order_ref.refs_1_, bf16[64,128,256]{2,1,0:T(8,128)(2,1)} %rest_0_.5), custom_call_target="tpu_custom_call" | custom-call | tf_op jit(solution)/shard_map/next_pack/pallas_call | solution.py:160
  8.7 0.5 collective-permute-start
  9.3 5.0 %collective-permute-start.6 = (bf16[4,128,256]{2,1,0:T(8,128)(2,1)}, bf16[4,128,256]{2,1,0:T(8,128)(2,1)S(1)}, u32[]{:S(2)}, u32[]{:S(2)}) collective-permute-start(bf16[4,128,256]{2,1,0:T(8,128)(2,1)} %get-tuple-element.43), channel_id=1, source_target_pairs={{0,12},{1,13},{2,14},{3,15},{4,8},{5,9},{6,10},{7,11},{8,4},{9,5},... | collective-permute-start | bytes 786440 | tf_op jit(solution)/shard_map/ppermute | solution.py:434
  14.4 0.1 compare_select_fusion.2
  14.8 0.2 select_reduce_fusion.1
  14.9 0.1 fusion.1
  15.1 0.7 pad_maximum_fusion.3
  15.8 0.1 reshape.300
  16.0 0.1 convert_reduce_fusion
  16.1 0.2 select_reduce_fusion
  16.3 0.2 convert_reduce_fusion.1
  16.6 7.5 %convolution_convert_fusion = bf16[16,640]{1,0:T(8,128)(2,1)S(1)} fusion(bf16[16,8192]{1,0:T(8,128)(2,1)S(1)} %reshape.300, bf16[640,8192]{1,0:T(8,128)(2,1)} %param.9), kind=kOutput, calls=%fused_computation.3 | convolution fusion | flops 167782400 | bytes 10768384 | tf_op jit(solution)/shard_map/dot_general | solution.py:563
  24.1 0.6 collective-permute-start.2
  24.7 2.4 %collective-permute-start.3 = (bf16[1,16,640]{2,1,0:T(8,128)(2,1)S(1)}, bf16[1,16,640]{2,1,0:T(8,128)(2,1)S(1)}, u32[]{:S(2)}, u32[]{:S(2)}) collective-permute-start(bf16[1,16,640]{2,1,0:T(8,128)(2,1)S(1)} %bitcast.48), channel_id=1, source_target_pairs={{0,8},{1,9},{2,10},{3,11},{4,12},{5,13},{6,14},{7,15},{8,0},{9,1},... | collective-permute-start | bytes 61448 | tf_op jit(solution)/shard_map/ppermute | solution.py:434
  27.1 1.4 collective-permute-start.4
  28.5 0.1 select_reduce_fusion.4
  28.6 0.6 reshape.299.ids_ref
  29.3 9.3 %collective-permute-done.3 = bf16[1,16,640]{2,1,0:T(8,128)(2,1)S(1)} collective-permute-done((bf16[1,16,640]{2,1,0:T(8,128)(2,1)S(1)}, bf16[1,16,640]{2,1,0:T(8,128)(2,1)S(1)}, u32[]{:S(2)}, u32[]{:S(2)}) %collective-permute-start.3) | collective-permute-done | bytes 20512 | tf_op jit(solution)/shard_map/ppermute | solution.py:434
  38.7 1.6 %collective-permute-start.7 = (bf16[4,16,640]{2,1,0:T(8,128)(2,1)S(1)}, bf16[4,16,640]{2,1,0:T(8,128)(2,1)S(1)}, u32[]{:S(2)}, u32[]{:S(2)}) collective-permute-start(bf16[4,16,640]{2,1,0:T(8,128)(2,1)S(1)} %pad_maximum_fusion.1), channel_id=1, source_target_pairs={{0,2},{1,3},{2,0},{3,1},{4,6},{5,7},{6,4},{7,5},{8,10},{9,11},{10,... | collective-permute-start | bytes 245768 | tf_op jit(solution)/shard_map/ppermute | solution.py:434
  40.2 0.9 fusion.5
  41.1 2.5 %collective-permute-start.10 = (bf16[4,128,256]{2,1,0:T(8,128)(2,1)S(1)}, bf16[4,128,256]{2,1,0:T(8,128)(2,1)S(1)}, u32[]{:S(2)}, u32[]{:S(2)}) collective-permute-start(bf16[4,128,256]{2,1,0:T(8,128)(2,1)S(1)} %get-tuple-element.50), channel_id=1, source_target_pairs={{0,12},{1,13},{2,14},{3,15},{4,8},{5,9},{6,10},{7,11},{8,4},{9,5},... | collective-permute-start | bytes 786440 | tf_op jit(solution)/shard_map/ppermute | solution.py:434
  43.7 1.3 collective-permute-done.8
  45.1 0.7 copy-done.9
  45.8 4.7 %rows_and_parts.1 = (f32[4,16,128]{2,1,0:T(8,128)}, f32[8,256]{1,0:T(8,128)}, bf16[144,128]{1,0:T(8,128)(2,1)}) custom-call(s32[4]{0:T(128)} %copy-done.21, s32[16]{0:T(128)} %constant.99.clone.turn_ref, s32[64]{0:T(128)} %get-tuple-element.38.order_ref.refs_1_, s32[8]{0:T(128)} %reshape.299.ids_ref, s32[8]{0:T(128)} %lengths_ref.1, ...), custom_call_target="tpu_custom_call" | custom-call | tf_op jit(solution)/shard_map/rows_and_parts/pallas_call | solution.py:415
  50.6 3.1 %collective-permute-start.14 = (bf16[144,128]{1,0:T(8,128)(2,1)}, bf16[144,128]{1,0:T(8,128)(2,1)S(1)}, u32[]{:S(2)}, u32[]{:S(2)}) collective-permute-start(bf16[144,128]{1,0:T(8,128)(2,1)} %get-tuple-element.63), channel_id=1, source_target_pairs={{0,14},{1,15},{2,12},{3,13},{4,10},{5,11},{6,8},{7,9},{8,6},{9,7},... | collective-permute-start | bytes 110600 | tf_op jit(solution)/shard_map/ppermute | solution.py:434
  53.7 1.2 gather_fusion
  54.8 3.1 %next_pack.4 = (bf16[8,128,256]{2,1,0:T(8,128)(2,1)}, bf16[8,128,256]{2,1,0:T(8,128)(2,1)}, bf16[8,128,256]{2,1,0:T(8,128)(2,1)}) custom-call(s32[64]{0:T(128)} %get-tuple-element.38.order_ref.refs_1_, bf16[64,128,256]{2,1,0:T(8,128)(2,1)} %rest_0_.5, bf16[16,128,256]{2,1,0:T(8,128)(2,1)} %copy-done.4), custom_call_target="tpu_custom_call" | custom-call | tf_op jit(solution)/shard_map/next_pack/pallas_call | solution.py:160
  58.0 0.5 collective-permute-start.12
  58.5 2.7 %next_pack.5 = (bf16[8,128,256]{2,1,0:T(8,128)(2,1)}, bf16[4,128,256]{2,1,0:T(8,128)(2,1)}) custom-call(s32[64]{0:T(128)} %get-tuple-element.38.order_ref.refs_1_, bf16[64,128,256]{2,1,0:T(8,128)(2,1)} %rest_0_.5, bf16[16,128,256]{2,1,0:T(8,128)(2,1)} %copy-done.3), custom_call_target="tpu_custom_call" | custom-call | tf_op jit(solution)/shard_map/next_pack/pallas_call | solution.py:160
  61.2 1.8 %collective-permute-start.13 = (bf16[8,128,256]{2,1,0:T(8,128)(2,1)}, bf16[8,128,256]{2,1,0:T(8,128)(2,1)S(1)}, u32[]{:S(2)}, u32[]{:S(2)}) collective-permute-start(bf16[8,128,256]{2,1,0:T(8,128)(2,1)} %get-tuple-element.59), channel_id=1, source_target_pairs={{0,6},{1,7},{2,4},{3,5},{4,2},{5,3},{6,0},{7,1},{8,14},{9,15},{10,... | collective-permute-start | bytes 1572872 | tf_op jit(solution)/shard_map/ppermute | solution.py:434
  63.0 3.3 %collective-permute-done.9.refs_7_ = bf16[4,128,256]{2,1,0:T(8,128)(2,1)S(1)} collective-permute-done((bf16[4,128,256]{2,1,0:T(8,128)(2,1)}, bf16[4,128,256]{2,1,0:T(8,128)(2,1)S(1)}, u32[]{:S(2)}, u32[]{:S(2)}) %collective-permute-start.9) | collective-permute-done | bytes 262176 | tf_op jit(solution)/shard_map/ppermute | solution.py:434
  66.4 0.5 collective-permute-start.11
  66.9 2.4 %collective-permute-start.15 = (bf16[8,128,256]{2,1,0:T(8,128)(2,1)}, bf16[8,128,256]{2,1,0:T(8,128)(2,1)S(1)}, u32[]{:S(2)}, u32[]{:S(2)}) collective-permute-start(bf16[8,128,256]{2,1,0:T(8,128)(2,1)} %get-tuple-element.66), channel_id=1, source_target_pairs={{0,10},{1,11},{2,8},{3,9},{4,14},{5,15},{6,12},{7,13},{8,2},{9,3},... | collective-permute-start | bytes 1572872 | tf_op jit(solution)/shard_map/ppermute | solution.py:434
  69.3 0.1 select_reduce_fusion.2
  69.4 0.7 select_reduce_fusion.3.refs_0_
  70.1 5.8 %place_pages.5 = (bf16[64,128,256]{2,1,0:T(8,128)(2,1)}, f32[4,16,128]{2,1,0:T(8,128)}, f32[4,16,128]{2,1,0:T(8,128)}) custom-call(s32[64]{0:T(128)} %select_reduce_fusion.3.refs_0_, s32[64]{0:T(128)} %get-tuple-element.38.order_ref.refs_1_, s32[4]{0:T(128)} %gather_fusion, f32[8,256]{1,0:T(8,128)} %get-tuple-element.45.refs_3_, ...), custom_call_target="tpu_custom_call" | custom-call | tf_op jit(solution)/shard_map/place_pages/pallas_call | solution.py:319
  76.0 1.5 collective-permute-start.16
  77.5 0.8 gather_fusion.1
  78.3 28.1 %collective-permute-done.11.refs_9_ = bf16[8,128,256]{2,1,0:T(8,128)(2,1)S(1)} collective-permute-done((bf16[8,128,256]{2,1,0:T(8,128)(2,1)}, bf16[8,128,256]{2,1,0:T(8,128)(2,1)S(1)}, u32[]{:S(2)}, u32[]{:S(2)}) %collective-permute-start.11) | collective-permute-done | bytes 524320 | tf_op jit(solution)/shard_map/ppermute | solution.py:434
  106.3 0.8 copy-done.8
  107.1 6.0 %place_pages.6 = (bf16[64,128,256]{2,1,0:T(8,128)(2,1)}, f32[4,16,128]{2,1,0:T(8,128)}, f32[4,16,128]{2,1,0:T(8,128)}) custom-call(s32[64]{0:T(128)} %select_reduce_fusion.3.refs_0_, s32[64]{0:T(128)} %get-tuple-element.38.order_ref.refs_1_, s32[4]{0:T(128)} %gather_fusion, f32[8,256]{1,0:T(8,128)} %get-tuple-element.45.refs_3_, ...), custom_call_target="tpu_custom_call", output_to_operand_aliasing={{0}: (10, {})} | custom-call | tf_op jit(solution)/shard_map/place_pages/pallas_call | solution.py:319
  113.2 0.8 copy-done.5
  113.9 0.2 copy-done.6
  114.1 5.9 %place_pages.7 = (bf16[64,128,256]{2,1,0:T(8,128)(2,1)}, f32[4,16,128]{2,1,0:T(8,128)}, f32[4,16,128]{2,1,0:T(8,128)}) custom-call(s32[64]{0:T(128)} %select_reduce_fusion.3.refs_0_, s32[64]{0:T(128)} %get-tuple-element.38.order_ref.refs_1_, s32[4]{0:T(128)} %gather_fusion, f32[8,256]{1,0:T(8,128)} %get-tuple-element.45.refs_3_, ...), custom_call_target="tpu_custom_call", output_to_operand_aliasing={{0}: (9, {})} | custom-call | tf_op jit(solution)/shard_map/place_pages/pallas_call | solution.py:319
  120.0 0.8 copy-done.7
  120.8 4.6 %place_pages.8 = (bf16[64,128,256]{2,1,0:T(8,128)(2,1)}, f32[4,16,128]{2,1,0:T(8,128)}, f32[4,16,128]{2,1,0:T(8,128)}, bf16[4,16,128]{2,1,0:T(8,128)(2,1)}) custom-call(s32[64]{0:T(128)} %select_reduce_fusion.3.refs_0_, s32[64]{0:T(128)} %get-tuple-element.38.order_ref.refs_1_, s32[4]{0:T(128)} %gather_fusion, ...), custom_call_target="tpu_custom_call", output_to_operand_aliasing={{0}: (9, {})} | custom-call | tf_op jit(solution)/shard_map/place_pages/pallas_call | solution.py:319
  125.4 0.8 broadcast_in_dim_reshape.4
  126.2 3.1 %collective-permute-start.18 = (bf16[1,4,2,1024]{3,2,1,0:T(2,128)(2,1)S(1)}, bf16[1,4,2,1024]{3,2,1,0:T(2,128)(2,1)S(1)}, u32[]{:S(2)}, u32[]{:S(2)}) collective-permute-start(bf16[1,4,2,1024]{3,2,1,0:T(2,128)(2,1)S(1)} %broadcast_in_dim_reshape.4), channel_id=1, source_target_pairs={{0,8},{1,9},{2,10},{3,11},{4,12},{5,13},{6,14},{7,15},{8,0},{9,1},... | collective-permute-start | bytes 49160 | tf_op jit(solution)/shard_map/ppermute | solution.py:434
  129.3 1.2 collective-permute-start.19
  130.6 0.4 collective-permute-done.18
  131.0 3.8 %collective-permute-done.19 = bf16[1,4,2,1024]{3,2,1,0:T(2,128)(2,1)S(1)} collective-permute-done((bf16[1,4,2,1024]{3,2,1,0:T(2,128)(2,1)S(1)}, bf16[1,4,2,1024]{3,2,1,0:T(2,128)(2,1)S(1)}, u32[]{:S(2)}, u32[]{:S(2)}) %collective-permute-start.19) | collective-permute-done | bytes 16416 | tf_op jit(solution)/shard_map/ppermute | solution.py:434
  134.8 0.1 pad_maximum_fusion.2
  135.0 0.2 collective-permute-start.20
  135.2 4.0 %collective-permute-done.20 = bf16[4,4,2,1024]{3,2,1,0:T(2,128)(2,1)S(1)} collective-permute-done((bf16[4,4,2,1024]{3,2,1,0:T(2,128)(2,1)S(1)}, bf16[4,4,2,1024]{3,2,1,0:T(2,128)(2,1)S(1)}, u32[]{:S(2)}, u32[]{:S(2)}) %collective-permute-start.20) | collective-permute-done | bytes 65568 | tf_op jit(solution)/shard_map/ppermute | solution.py:434
  139.5 1.2 collective-permute-start.22
  140.8 0.1 constant_dynamic-update-slice_fusion.8
  140.9 1.1 gather_fusion.2
  142.1 0.2 copy.19
  142.2 5.6 %convolution_convert_fusion.1 = bf16[16,512]{1,0:T(8,128)(2,1)S(1)} fusion(bf16[16,8192]{1,0:T(8,128)(2,1)S(1)} %bitcast.43, bf16[512,8192]{1,0:T(8,128)(2,1)} %param.10), kind=kOutput, calls=%fused_computation.4 | convolution fusion | flops 134225920 | bytes 8667136 | tf_op jit(solution)/shard_map/dot_general | solution.py:713
  147.9 0.6 reshape.304
  148.5 2.6 %collective-permute-done.22.refs_5_ = bf16[4,128,256]{2,1,0:T(8,128)(2,1)S(1)} collective-permute-done((bf16[4,128,256]{2,1,0:T(8,128)(2,1)S(1)}, bf16[4,128,256]{2,1,0:T(8,128)(2,1)S(1)}, u32[]{:S(2)}, u32[]{:S(2)}) %collective-permute-start.22) | collective-permute-done | bytes 262176 | tf_op jit(solution)/shard_map/ppermute | solution.py:434
  151.1 0.7 copy-done.15
  151.8 2.5 %place_pages.9 = bf16[64,128,256]{2,1,0:T(8,128)(2,1)} custom-call(s32[64]{0:T(128)} %select_reduce_fusion.3.refs_0_, s32[64]{0:T(128)} %get-tuple-element.38.order_ref.refs_1_, s32[4]{0:T(128)} %gather_fusion, f32[8,256]{1,0:T(8,128)} %get-tuple-element.45.refs_3_, bf16[4,128,256]{2,1,0:T(8,128)(2,1)} %copy-done.12, ...), custom_call_target="tpu_custom_call", output_to_operand_aliasing={{}: (6, {})} | custom-call | tf_op jit(solution)/shard_map/place_pages/pallas_call | solution.py:319
  (90 shorter events, 1.2 us)
Async XLA Ops:
  0.6 13.8 %copy-start.20 = (s32[64]{0:T(128)S(1)}, s32[64]{0:T(128)}, u32[]{:S(2)}) copy-start(s32[64]{0:T(128)} %units_ref.1) | copy-start | bytes 772
  0.6 13.7 %copy-start.19 = (s32[1024]{0:T(1024)S(1)}, s32[1024]{0:T(1024)}, u32[]{:S(2)}) copy-start(s32[1024]{0:T(1024)} %old_ref.1) | copy-start | bytes 12292
  0.6 13.8 %copy-start = (s32[8]{0:T(128)S(1)}, s32[8]{0:T(128)}, u32[]{:S(2)}) copy-start(s32[8]{0:T(128)} %lengths_ref.1) | copy-start | bytes 100
  0.7 15.1 %copy-start.16 = (bf16[8,2,8192]{2,1,0:T(2,128)(2,1)S(1)}, bf16[8,2,8192]{2,1,0:T(2,128)(2,1)}, u32[]{:S(2)}) copy-start(bf16[8,2,8192]{2,1,0:T(2,128)(2,1)} %param.8) | copy-start | bytes 786436
  8.7 7.8 %collective-permute-start = (bf16[16,128,256]{2,1,0:T(8,128)(2,1)}, bf16[16,128,256]{2,1,0:T(8,128)(2,1)S(1)}, u32[]{:S(2)}, u32[]{:S(2)}) collective-permute-start(bf16[16,128,256]{2,1,0:T(8,128)(2,1)} %get-tuple-element.39), channel_id=1, source_target_pairs={{0,1},{1,0},{2,3},{3,2},{4,5},{5,4},{6,7},{7,6},{8,9},{9,8},{10,11... | collective-permute-start | bytes 3145736 | tf_op jit(solution)/shard_map/ppermute | solution.py:434
  9.2 7.3 %collective-permute-start.1 = (bf16[16,128,256]{2,1,0:T(8,128)(2,1)}, bf16[16,128,256]{2,1,0:T(8,128)(2,1)S(1)}, u32[]{:S(2)}, u32[]{:S(2)}) collective-permute-start(bf16[16,128,256]{2,1,0:T(8,128)(2,1)} %get-tuple-element.40), channel_id=1, source_target_pairs={{0,1},{1,0},{2,3},{3,2},{4,5},{5,4},{6,7},{7,6},{8,9},{9,8},{10,11... | collective-permute-start | bytes 3145736 | tf_op jit(solution)/shard_map/ppermute | solution.py:434
  9.3 29.4 %collective-permute-start.6 = (bf16[4,128,256]{2,1,0:T(8,128)(2,1)}, bf16[4,128,256]{2,1,0:T(8,128)(2,1)S(1)}, u32[]{:S(2)}, u32[]{:S(2)}) collective-permute-start(bf16[4,128,256]{2,1,0:T(8,128)(2,1)} %get-tuple-element.43), channel_id=1, source_target_pairs={{0,12},{1,13},{2,14},{3,15},{4,8},{5,9},{6,10},{7,11},{8,4},{9,5},... | collective-permute-start | bytes 786440 | tf_op jit(solution)/shard_map/ppermute | solution.py:434
  14.3 24.3 %collective-permute-start.5 = (bf16[4,128,256]{2,1,0:T(8,128)(2,1)}, bf16[4,128,256]{2,1,0:T(8,128)(2,1)S(1)}, u32[]{:S(2)}, u32[]{:S(2)}) collective-permute-start(bf16[4,128,256]{2,1,0:T(8,128)(2,1)} %get-tuple-element.42), channel_id=1, source_target_pairs={{0,8},{1,9},{2,10},{3,11},{4,12},{5,13},{6,14},{7,15},{8,0},{9,1},... | collective-permute-start | bytes 786440 | tf_op jit(solution)/shard_map/ppermute | solution.py:434
  14.5 30.6 %copy-start.21 = (s32[4]{0:T(128)}, s32[4]{0:T(128)S(1)}, u32[]{:S(2)}) copy-start(s32[4]{0:T(128)S(1)} %get-tuple-element.75.units_ref) | copy-start | bytes 52
  16.5 37.2 %copy-start.1 = (s32[8]{0:T(128)S(1)}, s32[8]{0:T(128)}, u32[]{:S(2)}) copy-start(s32[8]{0:T(128)} %lengths_ref.1) | copy-start | bytes 100
  16.5 34.1 %copy-start.4 = (bf16[16,128,256]{2,1,0:T(8,128)(2,1)}, bf16[16,128,256]{2,1,0:T(8,128)(2,1)S(1)}, u32[]{:S(2)}) copy-start(bf16[16,128,256]{2,1,0:T(8,128)(2,1)S(1)} %collective-permute-done.refs_6_.rest_1_) | copy-start | bytes 3145732
  16.5 28.6 %copy-start.3 = (bf16[16,128,256]{2,1,0:T(8,128)(2,1)}, bf16[16,128,256]{2,1,0:T(8,128)(2,1)S(1)}, u32[]{:S(2)}) copy-start(bf16[16,128,256]{2,1,0:T(8,128)(2,1)S(1)} %collective-permute-done.1.passed_ref.rest_1_) | copy-start | bytes 3145732
  24.1 5.2 %collective-permute-start.2 = (bf16[1,16,640]{2,1,0:T(8,128)(2,1)S(1)}, bf16[1,16,640]{2,1,0:T(8,128)(2,1)S(1)}, u32[]{:S(2)}, u32[]{:S(2)}) collective-permute-start(bf16[1,16,640]{2,1,0:T(8,128)(2,1)S(1)} %bitcast.47), channel_id=1, source_target_pairs={{0,4},{1,5},{2,6},{3,7},{4,0},{5,1},{6,2},{7,3},{8,12},{9,13},{10,... | collective-permute-start | bytes 61448 | tf_op jit(solution)/shard_map/ppermute | solution.py:434
  24.7 13.9 %collective-permute-start.3 = (bf16[1,16,640]{2,1,0:T(8,128)(2,1)S(1)}, bf16[1,16,640]{2,1,0:T(8,128)(2,1)S(1)}, u32[]{:S(2)}, u32[]{:S(2)}) collective-permute-start(bf16[1,16,640]{2,1,0:T(8,128)(2,1)S(1)} %bitcast.48), channel_id=1, source_target_pairs={{0,8},{1,9},{2,10},{3,11},{4,12},{5,13},{6,14},{7,15},{8,0},{9,1},... | collective-permute-start | bytes 61448 | tf_op jit(solution)/shard_map/ppermute | solution.py:434
  27.1 11.5 %collective-permute-start.4 = (bf16[1,16,640]{2,1,0:T(8,128)(2,1)S(1)}, bf16[1,16,640]{2,1,0:T(8,128)(2,1)S(1)}, u32[]{:S(2)}, u32[]{:S(2)}) collective-permute-start(bf16[1,16,640]{2,1,0:T(8,128)(2,1)S(1)} %bitcast.49), channel_id=1, source_target_pairs={{0,12},{1,13},{2,14},{3,15},{4,8},{5,9},{6,10},{7,11},{8,4},{9,5},... | collective-permute-start | bytes 61448 | tf_op jit(solution)/shard_map/ppermute | solution.py:434
  38.6 22.6 %copy-start.10 = (bf16[4,128,256]{2,1,0:T(8,128)(2,1)}, bf16[4,128,256]{2,1,0:T(8,128)(2,1)S(1)}, u32[]{:S(2)}) copy-start(bf16[4,128,256]{2,1,0:T(8,128)(2,1)S(1)} %collective-permute-done.6.refs_8_) | copy-start | bytes 786436
  38.6 22.6 %copy-start.11 = (bf16[4,128,256]{2,1,0:T(8,128)(2,1)}, bf16[4,128,256]{2,1,0:T(8,128)(2,1)S(1)}, u32[]{:S(2)}) copy-start(bf16[4,128,256]{2,1,0:T(8,128)(2,1)S(1)} %collective-permute-done.5.refs_7_) | copy-start | bytes 786436
  38.7 4.9 %collective-permute-start.7 = (bf16[4,16,640]{2,1,0:T(8,128)(2,1)S(1)}, bf16[4,16,640]{2,1,0:T(8,128)(2,1)S(1)}, u32[]{:S(2)}, u32[]{:S(2)}) collective-permute-start(bf16[4,16,640]{2,1,0:T(8,128)(2,1)S(1)} %pad_maximum_fusion.1), channel_id=1, source_target_pairs={{0,2},{1,3},{2,0},{3,1},{4,6},{5,7},{6,4},{7,5},{8,10},{9,11},{10,... | collective-permute-start | bytes 245768 | tf_op jit(solution)/shard_map/ppermute | solution.py:434
  41.1 34.8 %collective-permute-start.10 = (bf16[4,128,256]{2,1,0:T(8,128)(2,1)S(1)}, bf16[4,128,256]{2,1,0:T(8,128)(2,1)S(1)}, u32[]{:S(2)}, u32[]{:S(2)}) collective-permute-start(bf16[4,128,256]{2,1,0:T(8,128)(2,1)S(1)} %get-tuple-element.50), channel_id=1, source_target_pairs={{0,12},{1,13},{2,14},{3,15},{4,8},{5,9},{6,10},{7,11},{8,4},{9,5},... | collective-permute-start | bytes 786440 | tf_op jit(solution)/shard_map/ppermute | solution.py:434
  43.6 22.8 %collective-permute-start.9 = (bf16[4,128,256]{2,1,0:T(8,128)(2,1)}, bf16[4,128,256]{2,1,0:T(8,128)(2,1)S(1)}, u32[]{:S(2)}, u32[]{:S(2)}) collective-permute-start(bf16[4,128,256]{2,1,0:T(8,128)(2,1)} %get-tuple-element.49), channel_id=1, source_target_pairs={{0,8},{1,9},{2,10},{3,11},{4,12},{5,13},{6,14},{7,15},{8,0},{9,1},... | collective-permute-start | bytes 786440 | tf_op jit(solution)/shard_map/ppermute | solution.py:434
  43.6 1.5 collective-permute-start.8
  45.1 0.7 copy-start.9
  50.6 16.3 %collective-permute-start.14 = (bf16[144,128]{1,0:T(8,128)(2,1)}, bf16[144,128]{1,0:T(8,128)(2,1)S(1)}, u32[]{:S(2)}, u32[]{:S(2)}) collective-permute-start(bf16[144,128]{1,0:T(8,128)(2,1)} %get-tuple-element.63), channel_id=1, source_target_pairs={{0,14},{1,15},{2,12},{3,13},{4,10},{5,11},{6,8},{7,9},{8,6},{9,7},... | collective-permute-start | bytes 110600 | tf_op jit(solution)/shard_map/ppermute | solution.py:434
  53.7 23.8 %copy-start.2 = (s32[16]{0:T(128)S(1)}, s32[16]{0:T(128)}, u32[]{:S(2)}) copy-start(s32[16]{0:T(128)} %constant.99.clone.turn_ref) | copy-start | bytes 196
  58.0 55.1 %collective-permute-start.12 = (bf16[8,128,256]{2,1,0:T(8,128)(2,1)}, bf16[8,128,256]{2,1,0:T(8,128)(2,1)S(1)}, u32[]{:S(2)}, u32[]{:S(2)}) collective-permute-start(bf16[8,128,256]{2,1,0:T(8,128)(2,1)} %get-tuple-element.57), channel_id=1, source_target_pairs={{0,4},{1,5},{2,6},{3,7},{4,0},{5,1},{6,2},{7,3},{8,12},{9,13},{10,... | collective-permute-start | bytes 1572872 | tf_op jit(solution)/shard_map/ppermute | solution.py:434
  61.2 51.9 %collective-permute-start.13 = (bf16[8,128,256]{2,1,0:T(8,128)(2,1)}, bf16[8,128,256]{2,1,0:T(8,128)(2,1)S(1)}, u32[]{:S(2)}, u32[]{:S(2)}) collective-permute-start(bf16[8,128,256]{2,1,0:T(8,128)(2,1)} %get-tuple-element.59), channel_id=1, source_target_pairs={{0,6},{1,7},{2,4},{3,5},{4,2},{5,3},{6,0},{7,1},{8,14},{9,15},{10,... | collective-permute-start | bytes 1572872 | tf_op jit(solution)/shard_map/ppermute | solution.py:434
  66.4 40.0 %copy-start.14 = (bf16[4,128,256]{2,1,0:T(8,128)(2,1)}, bf16[4,128,256]{2,1,0:T(8,128)(2,1)S(1)}, u32[]{:S(2)}) copy-start(bf16[4,128,256]{2,1,0:T(8,128)(2,1)S(1)} %collective-permute-done.9.refs_7_) | copy-start | bytes 786436
  66.4 40.0 %collective-permute-start.11 = (bf16[8,128,256]{2,1,0:T(8,128)(2,1)}, bf16[8,128,256]{2,1,0:T(8,128)(2,1)S(1)}, u32[]{:S(2)}, u32[]{:S(2)}) collective-permute-start(bf16[8,128,256]{2,1,0:T(8,128)(2,1)} %get-tuple-element.53), channel_id=1, source_target_pairs={{0,2},{1,3},{2,0},{3,1},{4,6},{5,7},{6,4},{7,5},{8,10},{9,11},{10,... | collective-permute-start | bytes 1572872 | tf_op jit(solution)/shard_map/ppermute | solution.py:434
  66.9 53.1 %copy-start.18 = (bf16[144,128]{1,0:T(8,128)(2,1)}, bf16[144,128]{1,0:T(8,128)(2,1)S(1)}, u32[]{:S(2)}) copy-start(bf16[144,128]{1,0:T(8,128)(2,1)S(1)} %collective-permute-done.14.refs_7_) | copy-start | bytes 110596
  66.9 53.1 %collective-permute-start.15 = (bf16[8,128,256]{2,1,0:T(8,128)(2,1)}, bf16[8,128,256]{2,1,0:T(8,128)(2,1)S(1)}, u32[]{:S(2)}, u32[]{:S(2)}) collective-permute-start(bf16[8,128,256]{2,1,0:T(8,128)(2,1)} %get-tuple-element.66), channel_id=1, source_target_pairs={{0,10},{1,11},{2,8},{3,9},{4,14},{5,15},{6,12},{7,13},{8,2},{9,3},... | collective-permute-start | bytes 1572872 | tf_op jit(solution)/shard_map/ppermute | solution.py:434
  75.9 63.6 %copy-start.17 = (bf16[4,128,256]{2,1,0:T(8,128)(2,1)S(1)}, bf16[4,128,256]{2,1,0:T(8,128)(2,1)}, u32[]{:S(2)}) copy-start(bf16[4,128,256]{2,1,0:T(8,128)(2,1)} %get-tuple-element.72) | copy-start | bytes 786436
  76.0 30.4 %copy-start.13 = (bf16[4,128,256]{2,1,0:T(8,128)(2,1)}, bf16[4,128,256]{2,1,0:T(8,128)(2,1)S(1)}, u32[]{:S(2)}) copy-start(bf16[4,128,256]{2,1,0:T(8,128)(2,1)S(1)} %collective-permute-done.10.refs_8_) | copy-start | bytes 786436
  76.0 49.4 %collective-permute-start.16 = (bf16[4,128,256]{2,1,0:T(8,128)(2,1)}, bf16[4,128,256]{2,1,0:T(8,128)(2,1)S(1)}, u32[]{:S(2)}, u32[]{:S(2)}) collective-permute-start(bf16[4,128,256]{2,1,0:T(8,128)(2,1)} %get-tuple-element.70), channel_id=1, source_target_pairs={{0,14},{1,15},{2,12},{3,13},{4,10},{5,11},{6,8},{7,9},{8,6},{9,7},... | collective-permute-start | bytes 786440 | tf_op jit(solution)/shard_map/ppermute | solution.py:434
  106.3 0.8 copy-start.8
  113.1 0.8 copy-start.5
  113.1 1.0 copy-start.6
  120.0 0.8 copy-start.7
  125.4 25.7 %copy-start.12 = (bf16[4,128,256]{2,1,0:T(8,128)(2,1)}, bf16[4,128,256]{2,1,0:T(8,128)(2,1)S(1)}, u32[]{:S(2)}) copy-start(bf16[4,128,256]{2,1,0:T(8,128)(2,1)S(1)} %collective-permute-done.16.refs_4_) | copy-start | bytes 786436
  126.2 4.4 %collective-permute-start.17 = (bf16[1,4,2,1024]{3,2,1,0:T(2,128)(2,1)S(1)}, bf16[1,4,2,1024]{3,2,1,0:T(2,128)(2,1)S(1)}, u32[]{:S(2)}, u32[]{:S(2)}) collective-permute-start(bf16[1,4,2,1024]{3,2,1,0:T(2,128)(2,1)S(1)} %broadcast_in_dim_reshape.4), channel_id=1, source_target_pairs={{0,4},{1,5},{2,6},{3,7},{4,0},{5,1},{6,2},{7,3},{8,12},{9,13},{10,... | collective-permute-start | bytes 49160 | tf_op jit(solution)/shard_map/ppermute | solution.py:434
  126.2 4.9 %collective-permute-start.18 = (bf16[1,4,2,1024]{3,2,1,0:T(2,128)(2,1)S(1)}, bf16[1,4,2,1024]{3,2,1,0:T(2,128)(2,1)S(1)}, u32[]{:S(2)}, u32[]{:S(2)}) collective-permute-start(bf16[1,4,2,1024]{3,2,1,0:T(2,128)(2,1)S(1)} %broadcast_in_dim_reshape.4), channel_id=1, source_target_pairs={{0,8},{1,9},{2,10},{3,11},{4,12},{5,13},{6,14},{7,15},{8,0},{9,1},... | collective-permute-start | bytes 49160 | tf_op jit(solution)/shard_map/ppermute | solution.py:434
  129.3 5.5 %collective-permute-start.19 = (bf16[1,4,2,1024]{3,2,1,0:T(2,128)(2,1)S(1)}, bf16[1,4,2,1024]{3,2,1,0:T(2,128)(2,1)S(1)}, u32[]{:S(2)}, u32[]{:S(2)}) collective-permute-start(bf16[1,4,2,1024]{3,2,1,0:T(2,128)(2,1)S(1)} %broadcast_in_dim_reshape.4), channel_id=1, source_target_pairs={{0,12},{1,13},{2,14},{3,15},{4,8},{5,9},{6,10},{7,11},{8,4},{9,5},... | collective-permute-start | bytes 49160 | tf_op jit(solution)/shard_map/ppermute | solution.py:434
  135.0 4.3 %collective-permute-start.20 = (bf16[4,4,2,1024]{3,2,1,0:T(2,128)(2,1)S(1)}, bf16[4,4,2,1024]{3,2,1,0:T(2,128)(2,1)S(1)}, u32[]{:S(2)}, u32[]{:S(2)}) collective-permute-start(bf16[4,4,2,1024]{3,2,1,0:T(2,128)(2,1)S(1)} %pad_maximum_fusion.2), channel_id=1, source_target_pairs={{0,2},{1,3},{2,0},{3,1},{4,6},{5,7},{6,4},{7,5},{8,10},{9,11},{10,... | collective-permute-start | bytes 196616 | tf_op jit(solution)/shard_map/ppermute | solution.py:434
  139.4 1.4 collective-permute-start.21
  139.5 11.6 %collective-permute-start.22 = (bf16[4,128,256]{2,1,0:T(8,128)(2,1)S(1)}, bf16[4,128,256]{2,1,0:T(8,128)(2,1)S(1)}, u32[]{:S(2)}, u32[]{:S(2)}) collective-permute-start(bf16[4,128,256]{2,1,0:T(8,128)(2,1)S(1)} %copy-done.17), channel_id=1, source_target_pairs={{0,14},{1,15},{2,12},{3,13},{4,10},{5,11},{6,8},{7,9},{8,6},{9,7},... | collective-permute-start | bytes 786440 | tf_op jit(solution)/shard_map/ppermute | solution.py:434
  151.1 0.7 copy-start.15

commit v6 on v5

--- a/solution.py
+++ b/solution.py
@@ -489,7 +489,7 @@
         moved_a, cross_far = send(chunk_a, a), send(cross_far, 1)
         near = list(range(2, half, 2))
         chunk_b, cross_near = next_pack(
-            order, [cache_pages], capacity, [own(b), own(1, *[k + 1 for k in near])]
+            after(order, cross_far), [cache_pages], capacity, [own(b), own(1, *[k + 1 for k in near])]
         )
         moved_b, cross_near = send(chunk_b, b), send(cross_near, 1)
     else:
@@ -559,7 +559,7 @@
         late_ids = late_ids.reshape(2 * capacity).astype(jnp.int32)
     flat_rows = hidden_states.reshape(requests * 2, D)
     if pairwise:
-        flat_rows = after(flat_rows, cross_near, cross_far)
+        flat_rows = after(flat_rows, chunk_b)
     own_part = lax.dot_general(
         flat_rows, qkv_weight, (((1,), (1,)), ((), ())), preferred_element_type=jnp.float32
     ).astype(jnp.bfloat16)
@@ -576,9 +576,10 @@
             [own(k) + passed(1, n + 1) for n, k in enumerate(near)],
         )
         rows, span = gather_more(after(rows, moved_a, moved_b), span, 2, devices)
+        rows_y = rows
         rows, span = gather_more(rows, span, 1, devices)
         moved_near = [
-            send(after(near_chunks[0], rows), near[0]),
+            send(after(near_chunks[0], rows_y), near[0]),
             send(near_chunks[1], near[1]),
             send(after(near_chunks[2], rows), near[2]),
         ]
@@ -606,7 +607,7 @@
             capacity,
             [own(c) + passed(1, 2), own(d)],
         )
-        moved_c = send(after(chunk_c, moved_a2, parts[0]), c)
+        moved_c = send(after(chunk_c, moved_a2), c)
 
         def place(groups, sums, cache, attends, parts, finish):
             entries, sources = [], []
@@ -639,25 +640,15 @@
             [],
             False,
         )
+        new_cache, sums, _ = place(
+            [(m, [k, k + 1], 0) for m, k in zip(moved_near, near)], sums, new_cache, True, [], False
+        )
         moved_d = send(after(chunk_d, moved_b2, sums[0]), d)
         new_cache, sums, _ = place(
-            [(moved_a2, [a + 1], 0), (moved_b2, [b + 1], 0), (moved_near[0], [2, 3], 0)],
-            sums,
-            new_cache,
-            True,
-            [],
-            False,
-        )
-        new_cache, sums, _ = place(
-            [(m, [k, k + 1], 0) for m, k in zip(moved_near[1:], near[1:])],
-            sums,
-            new_cache,
-            True,
-            [],
-            False,
+            [(moved_a2, [a + 1], 0), (moved_b2, [b + 1], 0)], sums, new_cache, True, parts, False
         )
         new_cache, sums, attended = place(
-            [(moved_c, [c, c + 1], 0)], sums, new_cache, True, parts, True
+            [(moved_c, [c, c + 1], 0)], sums, new_cache, True, [], True
         )
         attended = after(attended, moved_d)
         moved_d2 = send(after(piece(cross_far, 3), attended), d)

time: 156 us -> 161 us (1.032)
  starting transfers between devices: 29.8 us -> 34.3 us
  waiting for transfers between devices: 53 us -> 49 us
  other arithmetic: 2.94 us -> 5.48 us
  local copies, waits for them, and re-layouts: 10.9 us -> 12.6 us
    ppermute x23, starting transfers between devices: 29.8 us -> 34.3 us  [swap(): return lax.ppermute(values, 'tp', [(i, i ^ key) for i in range(devices)])]
    ppermute x23, waiting for transfers between devices: 53 us -> 49 us  [swap(): return lax.ppermute(values, 'tp', [(i, i ^ key) for i in range(devices)])]
    unnamed x51 -> x46, local copies, waits for them, and re-layouts: 4.31 us -> 4.25 us
  transfers between devices with their start and end apart: 23 -> 23, of which waited for: 8 -> 12; matrix products, arithmetic and copies ran while one was open for 14% -> 16% of each run, Pallas kernels for 21% -> 23%
where the time goes in v6:
time: 161 us; the launch traced here: 159 us
  waiting for transfers between devices  49 us (30%)
  Pallas kernels  43.5 us (27%)
  starting transfers between devices  34.3 us (21%)
  local copies, waits for them, and re-layouts  12.6 us (8%)
  matrix products  12.4 us (8%)
  other arithmetic  5.48 us (3%)
    ppermute x23, waiting for transfers between devices, swap(): return lax.ppermute(values, 'tp', [(i, i ^ key) for i in range(devices)])  49 us
    ppermute x23, starting transfers between devices, swap(): return lax.ppermute(values, 'tp', [(i, i ^ key) for i in range(devices)])  34.3 us
    pallas_call x5, Pallas kernels, place_pages(): pl.pallas_call(functools.partial(place_kernel, entries, started, attends,...  25 us
    pallas_call x3, Pallas kernels, next_pack(): pl.pallas_call(functools.partial(next_pack_kernel, capacity, outs_pages,...  9.05 us
    dot_general x1, matrix products, body(): lax.dot_general(flat_rows, qkv_weight, (((1,), (1,)), ((), ())), preferre...  6.8 us
    dot_general x1, matrix products, body(): lax.dot_general(logical, out_weight, (((1,), (1,)), ((), ())), preferred_...  5.64 us
    pallas_call x1, Pallas kernels, rows_and_parts(): pl.pallas_call(functools.partial(rows_kernel, late), out_shape=(jax.Shape...  4.75 us
    pallas_call x1, Pallas kernels, first_pack(): pl.pallas_call(functools.partial(first_pack_kernel, devices, capacity, ou...  4.69 us
  transfers between devices with their start and end apart: 23, of which 12 were waited for; matrix products, arithmetic and copies ran while one was open for 16% of the time, Pallas kernels for 23%

profile of v6, /device:TPU:0, one launch (start us, length us, event | category | flops | bytes accessed | tf_op | source)
XLA Modules:
  0.0 158.5 jit_solution(3020376398731974950)
XLA Ops:
  0.6 4.7 %first_pack.1 = (bf16[4,128,256]{2,1,0:T(8,128)(2,1)}, bf16[16,128,256]{2,1,0:T(8,128)(2,1)}, s32[64]{0:T(128)}) custom-call(s32[64]{0:T(128)} %units_ref.1, s32[1024]{0:T(1024)} %old_ref.1, bf16[64,128,256]{2,1,0:T(8,128)(2,1)} %rest_0_.5), custom_call_target="tpu_custom_call" | custom-call | tf_op jit(solution)/shard_map/first_pack/pallas_call | solution.py:142
  5.3 4.1 %collective-permute-start.4 = (bf16[4,128,256]{2,1,0:T(8,128)(2,1)}, bf16[4,128,256]{2,1,0:T(8,128)(2,1)S(1)}, u32[]{:S(2)}, u32[]{:S(2)}) collective-permute-start(bf16[4,128,256]{2,1,0:T(8,128)(2,1)} %get-tuple-element.44), channel_id=1, source_target_pairs={{0,8},{1,9},{2,10},{3,11},{4,12},{5,13},{6,14},{7,15},{8,0},{9,1},... | collective-permute-start | bytes 786440 | tf_op jit(solution)/shard_map/ppermute | solution.py:434
  9.4 0.8 reshape.298
  10.2 0.7 compare_select_fusion.2
  11.1 0.9 select_reduce_fusion
  12.0 0.7 add_convert_fusion
  12.7 0.8 select_reduce_fusion.1
  13.7 1.1 reshape.300
  14.8 0.2 convert_reduce_fusion.1
  15.1 3.2 %next_pack.3 = (bf16[4,128,256]{2,1,0:T(8,128)(2,1)}, bf16[16,128,256]{2,1,0:T(8,128)(2,1)}) custom-call(s32[64]{0:T(128)} %get-tuple-element.41.order_ref.refs_1_, bf16[64,128,256]{2,1,0:T(8,128)(2,1)} %rest_0_.5), custom_call_target="tpu_custom_call" | custom-call | tf_op jit(solution)/shard_map/next_pack/pallas_call | solution.py:160
  18.3 1.4 collective-permute-start.5
  19.7 0.2 collective-permute-start.8
  19.9 6.8 %convolution_convert_fusion = bf16[16,640]{1,0:T(8,128)(2,1)S(1)} fusion(bf16[16,8192]{1,0:T(8,128)(2,1)S(1)} %reshape.300, bf16[640,8192]{1,0:T(8,128)(2,1)} %param.9), kind=kOutput, calls=%fused_computation.3 | convolution fusion | flops 167782400 | bytes 10768384 | tf_op jit(solution)/shard_map/dot_general | solution.py:563
  26.7 2.5 %collective-permute-start.3 = (bf16[1,16,640]{2,1,0:T(8,128)(2,1)S(1)}, bf16[1,16,640]{2,1,0:T(8,128)(2,1)S(1)}, u32[]{:S(2)}, u32[]{:S(2)}) collective-permute-start(bf16[1,16,640]{2,1,0:T(8,128)(2,1)S(1)} %bitcast.47), channel_id=1, source_target_pairs={{0,12},{1,13},{2,14},{3,15},{4,8},{5,9},{6,10},{7,11},{8,4},{9,5},... | collective-permute-start | bytes 61448 | tf_op jit(solution)/shard_map/ppermute | solution.py:434
  29.3 3.2 %collective-permute-done.3 = bf16[1,16,640]{2,1,0:T(8,128)(2,1)S(1)} collective-permute-done((bf16[1,16,640]{2,1,0:T(8,128)(2,1)S(1)}, bf16[1,16,640]{2,1,0:T(8,128)(2,1)S(1)}, u32[]{:S(2)}, u32[]{:S(2)}) %collective-permute-start.3) | collective-permute-done | bytes 20512 | tf_op jit(solution)/shard_map/ppermute | solution.py:434
  32.5 3.5 %collective-permute-start.1 = (bf16[1,16,640]{2,1,0:T(8,128)(2,1)S(1)}, bf16[1,16,640]{2,1,0:T(8,128)(2,1)S(1)}, u32[]{:S(2)}, u32[]{:S(2)}) collective-permute-start(bf16[1,16,640]{2,1,0:T(8,128)(2,1)S(1)} %bitcast.49), channel_id=1, source_target_pairs={{0,4},{1,5},{2,6},{3,7},{4,0},{5,1},{6,2},{7,3},{8,12},{9,13},{10,... | collective-permute-start | bytes 61448 | tf_op jit(solution)/shard_map/ppermute | solution.py:434
  36.1 1.6 %collective-permute-done.1 = bf16[1,16,640]{2,1,0:T(8,128)(2,1)S(1)} collective-permute-done((bf16[1,16,640]{2,1,0:T(8,128)(2,1)S(1)}, bf16[1,16,640]{2,1,0:T(8,128)(2,1)S(1)}, u32[]{:S(2)}, u32[]{:S(2)}) %collective-permute-start.1) | collective-permute-done | bytes 20512 | tf_op jit(solution)/shard_map/ppermute | solution.py:434
  37.8 1.6 collective-permute-start.6
  39.4 2.9 %collective-permute-done.6 = bf16[4,16,640]{2,1,0:T(8,128)(2,1)S(1)} collective-permute-done((bf16[4,16,640]{2,1,0:T(8,128)(2,1)S(1)}, bf16[4,16,640]{2,1,0:T(8,128)(2,1)S(1)}, u32[]{:S(2)}, u32[]{:S(2)}) %collective-permute-start.6) | collective-permute-done | bytes 81952 | tf_op jit(solution)/shard_map/ppermute | solution.py:434
  42.4 0.9 fusion.5
  43.4 2.9 %collective-permute-start.13 = (bf16[4,128,256]{2,1,0:T(8,128)(2,1)}, bf16[4,128,256]{2,1,0:T(8,128)(2,1)S(1)}, u32[]{:S(2)}, u32[]{:S(2)}) collective-permute-start(bf16[4,128,256]{2,1,0:T(8,128)(2,1)} %get-tuple-element.61), channel_id=1, source_target_pairs={{0,8},{1,9},{2,10},{3,11},{4,12},{5,13},{6,14},{7,15},{8,0},{9,1},... | collective-permute-start | bytes 786440 | tf_op jit(solution)/shard_map/ppermute | solution.py:434
  46.3 1.0 copy-done.3
  47.3 3.1 %next_pack.4 = (bf16[8,128,256]{2,1,0:T(8,128)(2,1)}, bf16[8,128,256]{2,1,0:T(8,128)(2,1)}, bf16[8,128,256]{2,1,0:T(8,128)(2,1)}) custom-call(s32[64]{0:T(128)} %get-tuple-element.41.order_ref.refs_1_, bf16[64,128,256]{2,1,0:T(8,128)(2,1)} %rest_0_.5, bf16[16,128,256]{2,1,0:T(8,128)(2,1)} %copy-done.3), custom_call_target="tpu_custom_call" | custom-call | tf_op jit(solution)/shard_map/next_pack/pallas_call | solution.py:160
  50.4 1.0 collective-permute-start.11
  51.4 0.6 collective-permute-start.9
  52.1 1.9 %collective-permute-start.10 = (bf16[8,128,256]{2,1,0:T(8,128)(2,1)}, bf16[8,128,256]{2,1,0:T(8,128)(2,1)S(1)}, u32[]{:S(2)}, u32[]{:S(2)}) collective-permute-start(bf16[8,128,256]{2,1,0:T(8,128)(2,1)} %get-tuple-element.54), channel_id=1, source_target_pairs={{0,4},{1,5},{2,6},{3,7},{4,0},{5,1},{6,2},{7,3},{8,12},{9,13},{10,... | collective-permute-start | bytes 1572872 | tf_op jit(solution)/shard_map/ppermute | solution.py:434
  54.2 1.6 %collective-permute-start.14 = (bf16[4,128,256]{2,1,0:T(8,128)(2,1)}, bf16[4,128,256]{2,1,0:T(8,128)(2,1)S(1)}, u32[]{:S(2)}, u32[]{:S(2)}) collective-permute-start(bf16[4,128,256]{2,1,0:T(8,128)(2,1)} %get-tuple-element.62), channel_id=1, source_target_pairs={{0,12},{1,13},{2,14},{3,15},{4,8},{5,9},{6,10},{7,11},{8,4},{9,5},... | collective-permute-start | bytes 786440 | tf_op jit(solution)/shard_map/ppermute | solution.py:434
  55.8 1.2 gather_fusion
  57.0 0.7 reshape.299.ids_ref
  57.7 2.8 %next_pack.5 = (bf16[8,128,256]{2,1,0:T(8,128)(2,1)}, bf16[4,128,256]{2,1,0:T(8,128)(2,1)}) custom-call(s32[64]{0:T(128)} %get-tuple-element.41.order_ref.refs_1_, bf16[64,128,256]{2,1,0:T(8,128)(2,1)} %rest_0_.5, bf16[16,128,256]{2,1,0:T(8,128)(2,1)} %copy-done.2), custom_call_target="tpu_custom_call" | custom-call | tf_op jit(solution)/shard_map/next_pack/pallas_call | solution.py:160
  60.5 1.0 collective-permute-start.15
  61.4 0.7 pad_maximum_fusion.2
  62.1 0.6 select_reduce_fusion.3.refs_0_
  62.7 4.8 %rows_and_parts.1 = (f32[4,16,128]{2,1,0:T(8,128)}, f32[8,256]{1,0:T(8,128)}, bf16[144,128]{1,0:T(8,128)(2,1)}) custom-call(s32[4]{0:T(128)} %copy-done.18, s32[16]{0:T(128)} %constant.99.clone.turn_ref, s32[64]{0:T(128)} %get-tuple-element.41.order_ref.refs_1_, s32[8]{0:T(128)} %reshape.299.ids_ref, s32[8]{0:T(128)} %lengths_ref.1, ...), custom_call_target="tpu_custom_call" | custom-call | tf_op jit(solution)/shard_map/rows_and_parts/pallas_call | solution.py:415
  67.5 5.9 %place_pages.5 = (bf16[64,128,256]{2,1,0:T(8,128)(2,1)}, f32[4,16,128]{2,1,0:T(8,128)}, f32[4,16,128]{2,1,0:T(8,128)}) custom-call(s32[64]{0:T(128)} %select_reduce_fusion.3.refs_0_, s32[64]{0:T(128)} %get-tuple-element.41.order_ref.refs_1_, s32[4]{0:T(128)} %gather_fusion, f32[8,256]{1,0:T(8,128)} %get-tuple-element.46.refs_3_, ...), custom_call_target="tpu_custom_call" | custom-call | tf_op jit(solution)/shard_map/place_pages/pallas_call | solution.py:319
  73.4 14.2 %collective-permute-done.11.refs_9_ = bf16[8,128,256]{2,1,0:T(8,128)(2,1)S(1)} collective-permute-done((bf16[8,128,256]{2,1,0:T(8,128)(2,1)}, bf16[8,128,256]{2,1,0:T(8,128)(2,1)S(1)}, u32[]{:S(2)}, u32[]{:S(2)}) %collective-permute-start.11) | collective-permute-done | bytes 524320 | tf_op jit(solution)/shard_map/ppermute | solution.py:434
  87.6 0.3 collective-permute-done.9.refs_7_
  87.9 10.2 %collective-permute-done.10.refs_8_ = bf16[8,128,256]{2,1,0:T(8,128)(2,1)S(1)} collective-permute-done((bf16[8,128,256]{2,1,0:T(8,128)(2,1)}, bf16[8,128,256]{2,1,0:T(8,128)(2,1)S(1)}, u32[]{:S(2)}, u32[]{:S(2)}) %collective-permute-start.10) | collective-permute-done | bytes 524320 | tf_op jit(solution)/shard_map/ppermute | solution.py:434
  98.1 0.8 copy-done.6
  98.9 7.7 %place_pages.6 = (bf16[64,128,256]{2,1,0:T(8,128)(2,1)}, f32[4,16,128]{2,1,0:T(8,128)}, f32[4,16,128]{2,1,0:T(8,128)}) custom-call(s32[64]{0:T(128)} %select_reduce_fusion.3.refs_0_, s32[64]{0:T(128)} %get-tuple-element.41.order_ref.refs_1_, s32[4]{0:T(128)} %gather_fusion, f32[8,256]{1,0:T(8,128)} %get-tuple-element.46.refs_3_, ...), custom_call_target="tpu_custom_call", output_to_operand_aliasing={{0}: (10, {})} | custom-call | tf_op jit(solution)/shard_map/place_pages/pallas_call | solution.py:319
  106.7 1.3 collective-permute-start.16
  108.0 3.5 %collective-permute-start.12 = (bf16[144,128]{1,0:T(8,128)(2,1)S(1)}, bf16[144,128]{1,0:T(8,128)(2,1)S(1)}, u32[]{:S(2)}, u32[]{:S(2)}) collective-permute-start(bf16[144,128]{1,0:T(8,128)(2,1)S(1)} %copy-done.19), channel_id=1, source_target_pairs={{0,14},{1,15},{2,12},{3,13},{4,10},{5,11},{6,8},{7,9},{8,6},{9,7},... | collective-permute-start | bytes 110600 | tf_op jit(solution)/shard_map/ppermute | solution.py:434
  111.5 0.8 gather_fusion.1
  112.3 6.2 %collective-permute-done.12.refs_7_ = bf16[144,128]{1,0:T(8,128)(2,1)S(1)} collective-permute-done((bf16[144,128]{1,0:T(8,128)(2,1)S(1)}, bf16[144,128]{1,0:T(8,128)(2,1)S(1)}, u32[]{:S(2)}, u32[]{:S(2)}) %collective-permute-start.12) | collective-permute-done | bytes 36896 | tf_op jit(solution)/shard_map/ppermute | solution.py:434
  118.5 0.6 copy-done.16
  119.1 4.4 %place_pages.7 = (bf16[64,128,256]{2,1,0:T(8,128)(2,1)}, f32[4,16,128]{2,1,0:T(8,128)}, f32[4,16,128]{2,1,0:T(8,128)}) custom-call(s32[64]{0:T(128)} %select_reduce_fusion.3.refs_0_, s32[64]{0:T(128)} %get-tuple-element.41.order_ref.refs_1_, s32[4]{0:T(128)} %gather_fusion, f32[8,256]{1,0:T(8,128)} %get-tuple-element.46.refs_3_, ...), custom_call_target="tpu_custom_call", output_to_operand_aliasing={{0}: (10, {})} | custom-call | tf_op jit(solution)/shard_map/place_pages/pallas_call | solution.py:319
  123.5 0.8 copy-done.7
  124.3 4.5 %place_pages.8 = (bf16[64,128,256]{2,1,0:T(8,128)(2,1)}, f32[4,16,128]{2,1,0:T(8,128)}, f32[4,16,128]{2,1,0:T(8,128)}, bf16[4,16,128]{2,1,0:T(8,128)(2,1)}) custom-call(s32[64]{0:T(128)} %select_reduce_fusion.3.refs_0_, s32[64]{0:T(128)} %get-tuple-element.41.order_ref.refs_1_, s32[4]{0:T(128)} %gather_fusion, ...), custom_call_target="tpu_custom_call", output_to_operand_aliasing={{0}: (8, {})} | custom-call | tf_op jit(solution)/shard_map/place_pages/pallas_call | solution.py:319
  128.8 0.8 broadcast_in_dim_reshape.4
  129.6 0.9 collective-permute-start.19
  130.5 4.7 %collective-permute-start.18 = (bf16[1,4,2,1024]{3,2,1,0:T(2,128)(2,1)S(1)}, bf16[1,4,2,1024]{3,2,1,0:T(2,128)(2,1)S(1)}, u32[]{:S(2)}, u32[]{:S(2)}) collective-permute-start(bf16[1,4,2,1024]{3,2,1,0:T(2,128)(2,1)S(1)} %broadcast_in_dim_reshape.4), channel_id=1, source_target_pairs={{0,8},{1,9},{2,10},{3,11},{4,12},{5,13},{6,14},{7,15},{8,0},{9,1},... | collective-permute-start | bytes 49160 | tf_op jit(solution)/shard_map/ppermute | solution.py:434
  135.2 1.9 %collective-permute-done.18 = bf16[1,4,2,1024]{3,2,1,0:T(2,128)(2,1)S(1)} collective-permute-done((bf16[1,4,2,1024]{3,2,1,0:T(2,128)(2,1)S(1)}, bf16[1,4,2,1024]{3,2,1,0:T(2,128)(2,1)S(1)}, u32[]{:S(2)}, u32[]{:S(2)}) %collective-permute-start.18) | collective-permute-done | bytes 16416 | tf_op jit(solution)/shard_map/ppermute | solution.py:434
  137.0 1.9 %collective-permute-done.17 = bf16[1,4,2,1024]{3,2,1,0:T(2,128)(2,1)S(1)} collective-permute-done((bf16[1,4,2,1024]{3,2,1,0:T(2,128)(2,1)S(1)}, bf16[1,4,2,1024]{3,2,1,0:T(2,128)(2,1)S(1)}, u32[]{:S(2)}, u32[]{:S(2)}) %collective-permute-start.17) | collective-permute-done | bytes 16416 | tf_op jit(solution)/shard_map/ppermute | solution.py:434
  139.0 0.3 collective-permute-start.20
  139.4 3.9 %collective-permute-done.20 = bf16[4,4,2,1024]{3,2,1,0:T(2,128)(2,1)S(1)} collective-permute-done((bf16[4,4,2,1024]{3,2,1,0:T(2,128)(2,1)S(1)}, bf16[4,4,2,1024]{3,2,1,0:T(2,128)(2,1)S(1)}, u32[]{:S(2)}, u32[]{:S(2)}) %collective-permute-start.20) | collective-permute-done | bytes 65568 | tf_op jit(solution)/shard_map/ppermute | solution.py:434
  143.5 1.1 collective-permute-start.22
  144.6 0.2 collective-permute-done.21
  144.9 1.1 gather_fusion.2
  146.1 0.2 copy.19
  146.3 5.6 %convolution_convert_fusion.1 = bf16[16,512]{1,0:T(8,128)(2,1)S(1)} fusion(bf16[16,8192]{1,0:T(8,128)(2,1)S(1)} %bitcast.43, bf16[512,8192]{1,0:T(8,128)(2,1)} %param.10), kind=kOutput, calls=%fused_computation.4 | convolution fusion | flops 134225920 | bytes 8667136 | tf_op jit(solution)/shard_map/dot_general | solution.py:704
  151.9 0.6 reshape.304
  152.5 2.6 %collective-permute-done.22.refs_5_ = bf16[4,128,256]{2,1,0:T(8,128)(2,1)S(1)} collective-permute-done((bf16[4,128,256]{2,1,0:T(8,128)(2,1)S(1)}, bf16[4,128,256]{2,1,0:T(8,128)(2,1)S(1)}, u32[]{:S(2)}, u32[]{:S(2)}) %collective-permute-start.22) | collective-permute-done | bytes 262176 | tf_op jit(solution)/shard_map/ppermute | solution.py:434
  155.1 0.7 copy-done.14
  155.8 2.5 %place_pages.9 = bf16[64,128,256]{2,1,0:T(8,128)(2,1)} custom-call(s32[64]{0:T(128)} %select_reduce_fusion.3.refs_0_, s32[64]{0:T(128)} %get-tuple-element.41.order_ref.refs_1_, s32[4]{0:T(128)} %gather_fusion, f32[8,256]{1,0:T(8,128)} %get-tuple-element.46.refs_3_, bf16[4,128,256]{2,1,0:T(8,128)(2,1)} %copy-done.10, ...), custom_call_target="tpu_custom_call", output_to_operand_aliasing={{}: (6, {})} | custom-call | tf_op jit(solution)/shard_map/place_pages/pallas_call | solution.py:319
  (85 shorter events, 1.7 us)
Async XLA Ops:
  5.3 32.5 %collective-permute-start.4 = (bf16[4,128,256]{2,1,0:T(8,128)(2,1)}, bf16[4,128,256]{2,1,0:T(8,128)(2,1)S(1)}, u32[]{:S(2)}, u32[]{:S(2)}) collective-permute-start(bf16[4,128,256]{2,1,0:T(8,128)(2,1)} %get-tuple-element.44), channel_id=1, source_target_pairs={{0,8},{1,9},{2,10},{3,11},{4,12},{5,13},{6,14},{7,15},{8,0},{9,1},... | collective-permute-start | bytes 786440 | tf_op jit(solution)/shard_map/ppermute | solution.py:434
  9.4 5.7 %collective-permute-start = (bf16[16,128,256]{2,1,0:T(8,128)(2,1)}, bf16[16,128,256]{2,1,0:T(8,128)(2,1)S(1)}, u32[]{:S(2)}, u32[]{:S(2)}) collective-permute-start(bf16[16,128,256]{2,1,0:T(8,128)(2,1)} %get-tuple-element.40), channel_id=1, source_target_pairs={{0,1},{1,0},{2,3},{3,2},{4,5},{5,4},{6,7},{7,6},{8,9},{9,8},{10,11... | collective-permute-start | bytes 3145736 | tf_op jit(solution)/shard_map/ppermute | solution.py:434
  10.9 32.4 %copy-start.18 = (s32[4]{0:T(128)}, s32[4]{0:T(128)S(1)}, u32[]{:S(2)}) copy-start(s32[4]{0:T(128)S(1)} %get-tuple-element.77.units_ref) | copy-start | bytes 52
  15.1 28.3 %copy-start.2 = (bf16[16,128,256]{2,1,0:T(8,128)(2,1)}, bf16[16,128,256]{2,1,0:T(8,128)(2,1)S(1)}, u32[]{:S(2)}) copy-start(bf16[16,128,256]{2,1,0:T(8,128)(2,1)S(1)} %collective-permute-done.passed_ref.rest_1_) | copy-start | bytes 3145732
  18.3 19.5 %collective-permute-start.5 = (bf16[4,128,256]{2,1,0:T(8,128)(2,1)}, bf16[4,128,256]{2,1,0:T(8,128)(2,1)S(1)}, u32[]{:S(2)}, u32[]{:S(2)}) collective-permute-start(bf16[4,128,256]{2,1,0:T(8,128)(2,1)} %get-tuple-element.42), channel_id=1, source_target_pairs={{0,12},{1,13},{2,14},{3,15},{4,8},{5,9},{6,10},{7,11},{8,4},{9,5},... | collective-permute-start | bytes 786440 | tf_op jit(solution)/shard_map/ppermute | solution.py:434
  19.7 34.4 %copy-start.17 = (s32[64]{0:T(128)S(1)}, s32[64]{0:T(128)}, u32[]{:S(2)}) copy-start(s32[64]{0:T(128)} %units_ref.1) | copy-start | bytes 772
  19.7 36.1 %copy-start = (s32[8]{0:T(128)S(1)}, s32[8]{0:T(128)}, u32[]{:S(2)}) copy-start(s32[8]{0:T(128)} %lengths_ref.1) | copy-start | bytes 100
  19.7 26.6 %collective-permute-start.8 = (bf16[16,128,256]{2,1,0:T(8,128)(2,1)}, bf16[16,128,256]{2,1,0:T(8,128)(2,1)S(1)}, u32[]{:S(2)}, u32[]{:S(2)}) collective-permute-start(bf16[16,128,256]{2,1,0:T(8,128)(2,1)} %get-tuple-element.48), channel_id=1, source_target_pairs={{0,1},{1,0},{2,3},{3,2},{4,5},{5,4},{6,7},{7,6},{8,9},{9,8},{10,11... | collective-permute-start | bytes 3145736 | tf_op jit(solution)/shard_map/ppermute | solution.py:434
  26.7 5.8 %collective-permute-start.3 = (bf16[1,16,640]{2,1,0:T(8,128)(2,1)S(1)}, bf16[1,16,640]{2,1,0:T(8,128)(2,1)S(1)}, u32[]{:S(2)}, u32[]{:S(2)}) collective-permute-start(bf16[1,16,640]{2,1,0:T(8,128)(2,1)S(1)} %bitcast.47), channel_id=1, source_target_pairs={{0,12},{1,13},{2,14},{3,15},{4,8},{5,9},{6,10},{7,11},{8,4},{9,5},... | collective-permute-start | bytes 61448 | tf_op jit(solution)/shard_map/ppermute | solution.py:434
  29.2 6.9 %collective-permute-start.2 = (bf16[1,16,640]{2,1,0:T(8,128)(2,1)S(1)}, bf16[1,16,640]{2,1,0:T(8,128)(2,1)S(1)}, u32[]{:S(2)}, u32[]{:S(2)}) collective-permute-start(bf16[1,16,640]{2,1,0:T(8,128)(2,1)S(1)} %bitcast.48), channel_id=1, source_target_pairs={{0,8},{1,9},{2,10},{3,11},{4,12},{5,13},{6,14},{7,15},{8,0},{9,1},... | collective-permute-start | bytes 61448 | tf_op jit(solution)/shard_map/ppermute | solution.py:434
  32.5 5.3 %collective-permute-start.1 = (bf16[1,16,640]{2,1,0:T(8,128)(2,1)S(1)}, bf16[1,16,640]{2,1,0:T(8,128)(2,1)S(1)}, u32[]{:S(2)}, u32[]{:S(2)}) collective-permute-start(bf16[1,16,640]{2,1,0:T(8,128)(2,1)S(1)} %bitcast.49), channel_id=1, source_target_pairs={{0,4},{1,5},{2,6},{3,7},{4,0},{5,1},{6,2},{7,3},{8,12},{9,13},{10,... | collective-permute-start | bytes 61448 | tf_op jit(solution)/shard_map/ppermute | solution.py:434
  37.8 29.7 %copy-start.9 = (bf16[4,128,256]{2,1,0:T(8,128)(2,1)}, bf16[4,128,256]{2,1,0:T(8,128)(2,1)S(1)}, u32[]{:S(2)}) copy-start(bf16[4,128,256]{2,1,0:T(8,128)(2,1)S(1)} %collective-permute-done.4.refs_7_) | copy-start | bytes 786436
  37.8 29.7 %copy-start.11 = (bf16[4,128,256]{2,1,0:T(8,128)(2,1)}, bf16[4,128,256]{2,1,0:T(8,128)(2,1)S(1)}, u32[]{:S(2)}) copy-start(bf16[4,128,256]{2,1,0:T(8,128)(2,1)S(1)} %collective-permute-done.5.refs_8_) | copy-start | bytes 786436
  37.8 4.5 %collective-permute-start.6 = (bf16[4,16,640]{2,1,0:T(8,128)(2,1)S(1)}, bf16[4,16,640]{2,1,0:T(8,128)(2,1)S(1)}, u32[]{:S(2)}, u32[]{:S(2)}) collective-permute-start(bf16[4,16,640]{2,1,0:T(8,128)(2,1)S(1)} %pad_maximum_fusion), channel_id=1, source_target_pairs={{0,2},{1,3},{2,0},{3,1},{4,6},{5,7},{6,4},{7,5},{8,10},{9,11},{10,... | collective-permute-start | bytes 245768 | tf_op jit(solution)/shard_map/ppermute | solution.py:434
  42.4 3.9 %collective-permute-start.7 = (bf16[8,16,640]{2,1,0:T(8,128)(2,1)S(1)}, bf16[8,16,640]{2,1,0:T(8,128)(2,1)S(1)}, u32[]{:S(2)}, u32[]{:S(2)}) collective-permute-start(bf16[8,16,640]{2,1,0:T(8,128)(2,1)S(1)} %get-tuple-element.81), channel_id=1, source_target_pairs={{0,1},{1,0},{2,3},{3,2},{4,5},{5,4},{6,7},{7,6},{8,9},{9,8},{10,11... | collective-permute-start | bytes 491528 | tf_op jit(solution)/shard_map/ppermute | solution.py:434
  43.4 17.1 %collective-permute-start.13 = (bf16[4,128,256]{2,1,0:T(8,128)(2,1)}, bf16[4,128,256]{2,1,0:T(8,128)(2,1)S(1)}, u32[]{:S(2)}, u32[]{:S(2)}) collective-permute-start(bf16[4,128,256]{2,1,0:T(8,128)(2,1)} %get-tuple-element.61), channel_id=1, source_target_pairs={{0,8},{1,9},{2,10},{3,11},{4,12},{5,13},{6,14},{7,15},{8,0},{9,1},... | collective-permute-start | bytes 786440 | tf_op jit(solution)/shard_map/ppermute | solution.py:434
  46.3 16.5 %copy-start.8 = (bf16[16,16,640]{2,1,0:T(8,128)(2,1)}, bf16[16,16,640]{2,1,0:T(8,128)(2,1)S(1)}, u32[]{:S(2)}) copy-start(bf16[16,16,640]{2,1,0:T(8,128)(2,1)S(1)} %constant_dynamic-update-slice_fusion.2.rows_ref) | copy-start | bytes 983044
  46.3 1.0 copy-start.3
  50.4 37.2 %collective-permute-start.11 = (bf16[8,128,256]{2,1,0:T(8,128)(2,1)}, bf16[8,128,256]{2,1,0:T(8,128)(2,1)S(1)}, u32[]{:S(2)}, u32[]{:S(2)}) collective-permute-start(bf16[8,128,256]{2,1,0:T(8,128)(2,1)} %get-tuple-element.56), channel_id=1, source_target_pairs={{0,6},{1,7},{2,4},{3,5},{4,2},{5,3},{6,0},{7,1},{8,14},{9,15},{10,... | collective-permute-start | bytes 1572872 | tf_op jit(solution)/shard_map/ppermute | solution.py:434
  51.4 36.4 %collective-permute-start.9 = (bf16[8,128,256]{2,1,0:T(8,128)(2,1)}, bf16[8,128,256]{2,1,0:T(8,128)(2,1)S(1)}, u32[]{:S(2)}, u32[]{:S(2)}) collective-permute-start(bf16[8,128,256]{2,1,0:T(8,128)(2,1)} %get-tuple-element.53), channel_id=1, source_target_pairs={{0,2},{1,3},{2,0},{3,1},{4,6},{5,7},{6,4},{7,5},{8,10},{9,11},{10,... | collective-permute-start | bytes 1572872 | tf_op jit(solution)/shard_map/ppermute | solution.py:434
  52.1 46.0 %collective-permute-start.10 = (bf16[8,128,256]{2,1,0:T(8,128)(2,1)}, bf16[8,128,256]{2,1,0:T(8,128)(2,1)S(1)}, u32[]{:S(2)}, u32[]{:S(2)}) collective-permute-start(bf16[8,128,256]{2,1,0:T(8,128)(2,1)} %get-tuple-element.54), channel_id=1, source_target_pairs={{0,4},{1,5},{2,6},{3,7},{4,0},{5,1},{6,2},{7,3},{8,12},{9,13},{10,... | collective-permute-start | bytes 1572872 | tf_op jit(solution)/shard_map/ppermute | solution.py:434
  54.2 52.4 %collective-permute-start.14 = (bf16[4,128,256]{2,1,0:T(8,128)(2,1)}, bf16[4,128,256]{2,1,0:T(8,128)(2,1)S(1)}, u32[]{:S(2)}, u32[]{:S(2)}) collective-permute-start(bf16[4,128,256]{2,1,0:T(8,128)(2,1)} %get-tuple-element.62), channel_id=1, source_target_pairs={{0,12},{1,13},{2,14},{3,15},{4,8},{5,9},{6,10},{7,11},{8,4},{9,5},... | collective-permute-start | bytes 786440 | tf_op jit(solution)/shard_map/ppermute | solution.py:434
  60.5 46.2 %copy-start.12 = (bf16[4,128,256]{2,1,0:T(8,128)(2,1)}, bf16[4,128,256]{2,1,0:T(8,128)(2,1)S(1)}, u32[]{:S(2)}) copy-start(bf16[4,128,256]{2,1,0:T(8,128)(2,1)S(1)} %collective-permute-done.13.refs_8_) | copy-start | bytes 786436
  60.5 63.0 %collective-permute-start.15 = (bf16[8,128,256]{2,1,0:T(8,128)(2,1)}, bf16[8,128,256]{2,1,0:T(8,128)(2,1)S(1)}, u32[]{:S(2)}, u32[]{:S(2)}) collective-permute-start(bf16[8,128,256]{2,1,0:T(8,128)(2,1)} %get-tuple-element.68), channel_id=1, source_target_pairs={{0,10},{1,11},{2,8},{3,9},{4,14},{5,15},{6,12},{7,13},{8,2},{9,3},... | collective-permute-start | bytes 1572872 | tf_op jit(solution)/shard_map/ppermute | solution.py:434
  62.7 48.8 %copy-start.1 = (s32[16]{0:T(128)S(1)}, s32[16]{0:T(128)}, u32[]{:S(2)}) copy-start(s32[16]{0:T(128)} %constant.99.clone.turn_ref) | copy-start | bytes 196
  67.5 40.5 %copy-start.19 = (bf16[144,128]{1,0:T(8,128)(2,1)S(1)}, bf16[144,128]{1,0:T(8,128)(2,1)}, u32[]{:S(2)}) copy-start(bf16[144,128]{1,0:T(8,128)(2,1)} %get-tuple-element.60) | copy-start | bytes 110596
  73.4 70.1 %copy-start.15 = (bf16[4,128,256]{2,1,0:T(8,128)(2,1)S(1)}, bf16[4,128,256]{2,1,0:T(8,128)(2,1)}, u32[]{:S(2)}) copy-start(bf16[4,128,256]{2,1,0:T(8,128)(2,1)} %get-tuple-element.74) | copy-start | bytes 786436
  87.6 10.5 %copy-start.4 = (bf16[8,128,256]{2,1,0:T(8,128)(2,1)}, bf16[8,128,256]{2,1,0:T(8,128)(2,1)S(1)}, u32[]{:S(2)}) copy-start(bf16[8,128,256]{2,1,0:T(8,128)(2,1)S(1)} %collective-permute-done.11.refs_9_) | copy-start | bytes 1572868
  87.9 10.2 %copy-start.5 = (bf16[8,128,256]{2,1,0:T(8,128)(2,1)}, bf16[8,128,256]{2,1,0:T(8,128)(2,1)S(1)}, u32[]{:S(2)}) copy-start(bf16[8,128,256]{2,1,0:T(8,128)(2,1)S(1)} %collective-permute-done.9.refs_7_) | copy-start | bytes 1572868
  98.1 0.8 copy-start.6
  106.6 11.8 %copy-start.13 = (bf16[4,128,256]{2,1,0:T(8,128)(2,1)}, bf16[4,128,256]{2,1,0:T(8,128)(2,1)S(1)}, u32[]{:S(2)}) copy-start(bf16[4,128,256]{2,1,0:T(8,128)(2,1)S(1)} %collective-permute-done.14.refs_9_) | copy-start | bytes 786436
  106.7 22.2 %collective-permute-start.16 = (bf16[4,128,256]{2,1,0:T(8,128)(2,1)}, bf16[4,128,256]{2,1,0:T(8,128)(2,1)S(1)}, u32[]{:S(2)}, u32[]{:S(2)}) collective-permute-start(bf16[4,128,256]{2,1,0:T(8,128)(2,1)} %get-tuple-element.72), channel_id=1, source_target_pairs={{0,14},{1,15},{2,12},{3,13},{4,10},{5,11},{6,8},{7,9},{8,6},{9,7},... | collective-permute-start | bytes 786440 | tf_op jit(solution)/shard_map/ppermute | solution.py:434
  108.0 10.5 %collective-permute-start.12 = (bf16[144,128]{1,0:T(8,128)(2,1)S(1)}, bf16[144,128]{1,0:T(8,128)(2,1)S(1)}, u32[]{:S(2)}, u32[]{:S(2)}) collective-permute-start(bf16[144,128]{1,0:T(8,128)(2,1)S(1)} %copy-done.19), channel_id=1, source_target_pairs={{0,14},{1,15},{2,12},{3,13},{4,10},{5,11},{6,8},{7,9},{8,6},{9,7},... | collective-permute-start | bytes 110600 | tf_op jit(solution)/shard_map/ppermute | solution.py:434
  118.5 0.6 copy-start.16
  123.5 0.8 copy-start.7
  128.8 26.3 %copy-start.10 = (bf16[4,128,256]{2,1,0:T(8,128)(2,1)}, bf16[4,128,256]{2,1,0:T(8,128)(2,1)S(1)}, u32[]{:S(2)}) copy-start(bf16[4,128,256]{2,1,0:T(8,128)(2,1)S(1)} %collective-permute-done.16.refs_4_) | copy-start | bytes 786436
  129.6 5.6 %collective-permute-start.19 = (bf16[1,4,2,1024]{3,2,1,0:T(2,128)(2,1)S(1)}, bf16[1,4,2,1024]{3,2,1,0:T(2,128)(2,1)S(1)}, u32[]{:S(2)}, u32[]{:S(2)}) collective-permute-start(bf16[1,4,2,1024]{3,2,1,0:T(2,128)(2,1)S(1)} %broadcast_in_dim_reshape.4), channel_id=1, source_target_pairs={{0,12},{1,13},{2,14},{3,15},{4,8},{5,9},{6,10},{7,11},{8,4},{9,5},... | collective-permute-start | bytes 49160 | tf_op jit(solution)/shard_map/ppermute | solution.py:434
  130.5 6.6 %collective-permute-start.18 = (bf16[1,4,2,1024]{3,2,1,0:T(2,128)(2,1)S(1)}, bf16[1,4,2,1024]{3,2,1,0:T(2,128)(2,1)S(1)}, u32[]{:S(2)}, u32[]{:S(2)}) collective-permute-start(bf16[1,4,2,1024]{3,2,1,0:T(2,128)(2,1)S(1)} %broadcast_in_dim_reshape.4), channel_id=1, source_target_pairs={{0,8},{1,9},{2,10},{3,11},{4,12},{5,13},{6,14},{7,15},{8,0},{9,1},... | collective-permute-start | bytes 49160 | tf_op jit(solution)/shard_map/ppermute | solution.py:434
  135.1 3.7 %collective-permute-start.17 = (bf16[1,4,2,1024]{3,2,1,0:T(2,128)(2,1)S(1)}, bf16[1,4,2,1024]{3,2,1,0:T(2,128)(2,1)S(1)}, u32[]{:S(2)}, u32[]{:S(2)}) collective-permute-start(bf16[1,4,2,1024]{3,2,1,0:T(2,128)(2,1)S(1)} %broadcast_in_dim_reshape.4), channel_id=1, source_target_pairs={{0,4},{1,5},{2,6},{3,7},{4,0},{5,1},{6,2},{7,3},{8,12},{9,13},{10,... | collective-permute-start | bytes 49160 | tf_op jit(solution)/shard_map/ppermute | solution.py:434
  139.0 4.3 %collective-permute-start.20 = (bf16[4,4,2,1024]{3,2,1,0:T(2,128)(2,1)S(1)}, bf16[4,4,2,1024]{3,2,1,0:T(2,128)(2,1)S(1)}, u32[]{:S(2)}, u32[]{:S(2)}) collective-permute-start(bf16[4,4,2,1024]{3,2,1,0:T(2,128)(2,1)S(1)} %pad_maximum_fusion.1), channel_id=1, source_target_pairs={{0,2},{1,3},{2,0},{3,1},{4,6},{5,7},{6,4},{7,5},{8,10},{9,11},{10,... | collective-permute-start | bytes 196616 | tf_op jit(solution)/shard_map/ppermute | solution.py:434
  143.4 1.4 collective-permute-start.21
  143.5 11.6 %collective-permute-start.22 = (bf16[4,128,256]{2,1,0:T(8,128)(2,1)S(1)}, bf16[4,128,256]{2,1,0:T(8,128)(2,1)S(1)}, u32[]{:S(2)}, u32[]{:S(2)}) collective-permute-start(bf16[4,128,256]{2,1,0:T(8,128)(2,1)S(1)} %copy-done.15), channel_id=1, source_target_pairs={{0,14},{1,15},{2,12},{3,13},{4,10},{5,11},{6,8},{7,9},{8,6},{9,7},... | collective-permute-start | bytes 786440 | tf_op jit(solution)/shard_map/ppermute | solution.py:434
  155.1 0.7 copy-start.14

commit v7 on v5

--- a/solution.py
+++ b/solution.py
@@ -477,21 +477,30 @@
         half, quarter = devices // 2, devices // 4
         a, b = half, half + quarter
         c, d = a + 2, b + 2
-        (chunk_a, cross_far), order = first_pack(
+        near = list(range(2, half, 2))
+        (chunk_a, cross_near), order = first_pack(
             new_units,
             old_pages,
             cache_pages,
             devices,
             capacity,
-            [own(a), own(a + 1, b + 1, c + 1, d + 1)],
+            [own(a), own(1, *[k + 1 for k in near])],
             True,
         )
-        moved_a, cross_far = send(chunk_a, a), send(cross_far, 1)
-        near = list(range(2, half, 2))
-        chunk_b, cross_near = next_pack(
-            order, [cache_pages], capacity, [own(b), own(1, *[k + 1 for k in near])]
-        )
-        moved_b, cross_near = send(chunk_b, b), send(cross_near, 1)
+        moved_a, cross_near = send(chunk_a, a), send(cross_near, 1)
+        chunk_4, chunk_6, chunk_b, cross_far = next_pack(
+            order,
+            [cache_pages, cross_near],
+            capacity,
+            [
+                own(near[1]) + passed(1, 2),
+                own(near[2]) + passed(1, 3),
+                own(b),
+                own(a + 1, b + 1, c + 1, d + 1),
+            ],
+        )
+        moved_4, moved_6 = send(chunk_4, near[1]), send(chunk_6, near[2])
+        moved_b, cross_far = send(chunk_b, b), send(cross_far, 1)
     else:
         (packed,), order = first_pack(
             new_units, old_pages, cache_pages, devices, capacity, [own(*range(devices))], False
@@ -559,7 +568,7 @@
         late_ids = late_ids.reshape(2 * capacity).astype(jnp.int32)
     flat_rows = hidden_states.reshape(requests * 2, D)
     if pairwise:
-        flat_rows = after(flat_rows, cross_near, cross_far)
+        flat_rows = after(flat_rows, cross_far)
     own_part = lax.dot_general(
         flat_rows, qkv_weight, (((1,), (1,)), ((), ())), preferred_element_type=jnp.float32
     ).astype(jnp.bfloat16)
@@ -569,19 +578,8 @@
         rows, span = gather_line(own_part, devices)
         moved_a2 = send(after(piece(cross_far, 0), own_part, moved_a), a)
         moved_b2 = send(after(piece(cross_far, 1), own_part), b)
-        near_chunks = next_pack(
-            order,
-            [cache_pages, after(cross_near, rows)],
-            capacity,
-            [own(k) + passed(1, n + 1) for n, k in enumerate(near)],
-        )
         rows, span = gather_more(after(rows, moved_a, moved_b), span, 2, devices)
         rows, span = gather_more(rows, span, 1, devices)
-        moved_near = [
-            send(after(near_chunks[0], rows), near[0]),
-            send(near_chunks[1], near[1]),
-            send(after(near_chunks[2], rows), near[2]),
-        ]
         turn = jnp.array([span.index(i) for i in range(devices)], jnp.int32)
         late = [(0, d * capacity + r) for r in range(capacity)]
         late += [(1, 3 * capacity + r) for r in range(capacity)]
@@ -600,13 +598,14 @@
             late,
         )
         parts = [send(sent, d)]
-        chunk_c, chunk_d = next_pack(
+        chunk_c, chunk_d, chunk_2 = next_pack(
             order,
-            [cache_pages, after(cross_far, rows)],
+            [cache_pages, after(cross_far, rows), cross_near],
             capacity,
-            [own(c) + passed(1, 2), own(d)],
-        )
-        moved_c = send(after(chunk_c, moved_a2, parts[0]), c)
+            [own(c) + passed(1, 2), own(d), own(near[0]) + passed(2, 1)],
+        )
+        moved_2 = send(chunk_2, near[0])
+        moved_c = send(after(chunk_c, moved_a2, sent), c)
 
         def place(groups, sums, cache, attends, parts, finish):
             entries, sources = [], []
@@ -639,9 +638,8 @@
             [],
             False,
         )
-        moved_d = send(after(chunk_d, moved_b2, sums[0]), d)
         new_cache, sums, _ = place(
-            [(moved_a2, [a + 1], 0), (moved_b2, [b + 1], 0), (moved_near[0], [2, 3], 0)],
+            [(moved_4, [near[1], near[1] + 1], 0), (moved_6, [near[2], near[2] + 1], 0)],
             sums,
             new_cache,
             True,
@@ -649,13 +647,14 @@
             False,
         )
         new_cache, sums, _ = place(
-            [(m, [k, k + 1], 0) for m, k in zip(moved_near[1:], near[1:])],
+            [(moved_a2, [a + 1], 0), (moved_b2, [b + 1], 0), (moved_2, [near[0], near[0] + 1], 0)],
             sums,
             new_cache,
             True,
             [],
             False,
         )
+        moved_d = send(after(chunk_d, moved_b2, sums[0], parts[0]), d)
         new_cache, sums, attended = place(
             [(moved_c, [c, c + 1], 0)], sums, new_cache, True, parts, True
         )

time: 156 us -> 138 us (0.88)
  the two profiles are of different devices: /device:TPU:0 before, /device:TPU:8 now
where the time goes in v7:
time: 138 us; the launch traced here: 137 us
  waiting for transfers between devices  41.8 us (30%)
  Pallas kernels  41 us (30%)
  starting transfers between devices  22.5 us (16%)
  matrix products  12.8 us (9%)
  local copies, waits for them, and re-layouts  11.6 us (8%)
  other arithmetic  6.23 us (5%)
    ppermute x23, waiting for transfers between devices, swap(): return lax.ppermute(values, 'tp', [(i, i ^ key) for i in range(devices)])  41.8 us
    pallas_call x5, Pallas kernels, place_pages(): pl.pallas_call(functools.partial(place_kernel, entries, started, attends,...  24.8 us
    ppermute x23, starting transfers between devices, swap(): return lax.ppermute(values, 'tp', [(i, i ^ key) for i in range(devices)])  22.5 us
    dot_general x1, matrix products, body(): lax.dot_general(flat_rows, qkv_weight, (((1,), (1,)), ((), ())), preferre...  7.16 us
    pallas_call x2, Pallas kernels, next_pack(): pl.pallas_call(functools.partial(next_pack_kernel, capacity, outs_pages,...  6.61 us
    dot_general x1, matrix products, body(): lax.dot_general(logical, out_weight, (((1,), (1,)), ((), ())), preferred_...  5.64 us
    pallas_call x1, Pallas kernels, first_pack(): pl.pallas_call(functools.partial(first_pack_kernel, devices, capacity, ou...  4.82 us
    pallas_call x1, Pallas kernels, rows_and_parts(): pl.pallas_call(functools.partial(rows_kernel, late), out_shape=(jax.Shape...  4.73 us
  transfers between devices with their start and end apart: 23, of which 11 were waited for; matrix products, arithmetic and copies ran while one was open for 19% of the time, Pallas kernels for 24%

profile of v7, /device:TPU:8, one launch (start us, length us, event | category | flops | bytes accessed | tf_op | source)
XLA Modules:
  0.0 137.2 jit_solution(7741911403037877734)
XLA Ops:
  0.6 4.8 %first_pack.1 = (bf16[4,128,256]{2,1,0:T(8,128)(2,1)}, bf16[16,128,256]{2,1,0:T(8,128)(2,1)}, s32[64]{0:T(128)}) custom-call(s32[64]{0:T(128)} %units_ref.1, s32[1024]{0:T(1024)} %old_ref.1, bf16[64,128,256]{2,1,0:T(8,128)(2,1)} %rest_0_.3), custom_call_target="tpu_custom_call" | custom-call | tf_op jit(solution)/shard_map/first_pack/pallas_call | solution.py:142
  5.5 2.7 %collective-permute-start.5 = (bf16[4,128,256]{2,1,0:T(8,128)(2,1)}, bf16[4,128,256]{2,1,0:T(8,128)(2,1)S(1)}, u32[]{:S(2)}, u32[]{:S(2)}) collective-permute-start(bf16[4,128,256]{2,1,0:T(8,128)(2,1)} %get-tuple-element.39), channel_id=1, source_target_pairs={{0,8},{1,9},{2,10},{3,11},{4,12},{5,13},{6,14},{7,15},{8,0},{9,1},... | collective-permute-start | bytes 786440 | tf_op jit(solution)/shard_map/ppermute | solution.py:434
  8.1 0.8 reshape.298
  8.9 0.7 compare_select_fusion.2
  9.8 0.8 select_reduce_fusion.2
  10.6 0.8 select_reduce_fusion.1
  11.4 0.9 select_reduce_fusion
  12.3 0.7 add_convert_fusion
  13.1 1.0 copy-done.2
  14.1 3.6 %next_pack.2 = (bf16[8,128,256]{2,1,0:T(8,128)(2,1)}, bf16[8,128,256]{2,1,0:T(8,128)(2,1)}, bf16[4,128,256]{2,1,0:T(8,128)(2,1)}, bf16[16,128,256]{2,1,0:T(8,128)(2,1)}) custom-call(s32[64]{0:T(128)} %get-tuple-element.35.order_ref.refs_1_, bf16[64,128,256]{2,1,0:T(8,128)(2,1)} %rest_0_.3, bf16[16,128,256]{2,1,0:T(8,128)(2,1)} %copy-done.2), custom_call_target="tpu_custom_call" | custom-call | tf_op jit(solution)/shard_map/next_pack/pallas_call | solution.py:160
  17.7 0.6 collective-permute-start.1
  18.5 0.2 convert_reduce_fusion.1
  18.7 0.1 fusion.1
  18.9 1.9 %collective-permute-done.1.passed_ref.rest_1_ = bf16[16,128,256]{2,1,0:T(8,128)(2,1)S(1)} collective-permute-done((bf16[16,128,256]{2,1,0:T(8,128)(2,1)}, bf16[16,128,256]{2,1,0:T(8,128)(2,1)S(1)}, u32[]{:S(2)}, u32[]{:S(2)}) %collective-permute-start.1) | collective-permute-done | bytes 1048608 | tf_op jit(solution)/shard_map/ppermute | solution.py:434
  20.8 7.2 %convolution_convert_fusion = bf16[16,640]{1,0:T(8,128)(2,1)S(1)} fusion(bf16[16,8192]{1,0:T(8,128)(2,1)S(1)} %reshape.300, bf16[640,8192]{1,0:T(8,128)(2,1)} %param.9), kind=kOutput, calls=%fused_computation.3 | convolution fusion | flops 167782400 | bytes 10768384 | tf_op jit(solution)/shard_map/dot_general | solution.py:572
  27.9 0.2 collective-permute-start.4
  28.1 2.7 %collective-permute-start.3 = (bf16[1,16,640]{2,1,0:T(8,128)(2,1)S(1)}, bf16[1,16,640]{2,1,0:T(8,128)(2,1)S(1)}, u32[]{:S(2)}, u32[]{:S(2)}) collective-permute-start(bf16[1,16,640]{2,1,0:T(8,128)(2,1)S(1)} %bitcast.48), channel_id=1, source_target_pairs={{0,8},{1,9},{2,10},{3,11},{4,12},{5,13},{6,14},{7,15},{8,0},{9,1},... | collective-permute-start | bytes 61448 | tf_op jit(solution)/shard_map/ppermute | solution.py:434
  30.8 0.7 collective-permute-start.2
  31.4 0.7 pad_maximum_fusion.3
  32.1 2.4 %collective-permute-done.4 = bf16[1,16,640]{2,1,0:T(8,128)(2,1)S(1)} collective-permute-done((bf16[1,16,640]{2,1,0:T(8,128)(2,1)S(1)}, bf16[1,16,640]{2,1,0:T(8,128)(2,1)S(1)}, u32[]{:S(2)}, u32[]{:S(2)}) %collective-permute-start.4) | collective-permute-done | bytes 20512 | tf_op jit(solution)/shard_map/ppermute | solution.py:434
  34.5 3.0 %collective-permute-start.10 = (bf16[8,128,256]{2,1,0:T(8,128)(2,1)}, bf16[8,128,256]{2,1,0:T(8,128)(2,1)S(1)}, u32[]{:S(2)}, u32[]{:S(2)}) collective-permute-start(bf16[8,128,256]{2,1,0:T(8,128)(2,1)} %get-tuple-element.47), channel_id=1, source_target_pairs={{0,6},{1,7},{2,4},{3,5},{4,2},{5,3},{6,0},{7,1},{8,14},{9,15},{10,... | collective-permute-start | bytes 1572872 | tf_op jit(solution)/shard_map/ppermute | solution.py:434
  37.5 0.6 collective-permute-start.7
  38.1 0.9 fusion.5
  39.1 2.9 %collective-permute-done.7 = bf16[4,16,640]{2,1,0:T(8,128)(2,1)S(1)} collective-permute-done((bf16[4,16,640]{2,1,0:T(8,128)(2,1)S(1)}, bf16[4,16,640]{2,1,0:T(8,128)(2,1)S(1)}, u32[]{:S(2)}, u32[]{:S(2)}) %collective-permute-start.7) | collective-permute-done | bytes 81952 | tf_op jit(solution)/shard_map/ppermute | solution.py:434
  42.2 1.3 collective-permute-done.8
  43.6 3.0 %next_pack.3 = (bf16[8,128,256]{2,1,0:T(8,128)(2,1)}, bf16[4,128,256]{2,1,0:T(8,128)(2,1)}, bf16[8,128,256]{2,1,0:T(8,128)(2,1)}) custom-call(s32[64]{0:T(128)} %get-tuple-element.35.order_ref.refs_1_, bf16[64,128,256]{2,1,0:T(8,128)(2,1)} %rest_0_.3, bf16[16,128,256]{2,1,0:T(8,128)(2,1)} %copy-done.3, bf16[16,128,256]{2,1,0:T(8,128)(2,1)} %copy-done.2), custom_call_target="tpu_custom_call" | custom-call | tf_op jit(solution)/shard_map/next_pack/pallas_call | solution.py:160
  46.6 0.6 collective-permute-start.13
  47.1 0.1 convert_reduce_fusion
  47.3 0.1 collective-permute-start.12
  47.4 0.1 select_reduce_fusion.4
  47.5 0.6 reshape.299.ids_ref
  48.1 4.7 %rows_and_parts.1 = (f32[4,16,128]{2,1,0:T(8,128)}, f32[8,256]{1,0:T(8,128)}, bf16[144,128]{1,0:T(8,128)(2,1)}) custom-call(s32[4]{0:T(128)} %copy-done.18, s32[16]{0:T(128)} %constant.99.clone.turn_ref, s32[64]{0:T(128)} %get-tuple-element.35.order_ref.refs_1_, s32[8]{0:T(128)} %reshape.299.ids_ref, s32[8]{0:T(128)} %lengths_ref.1, ...), custom_call_target="tpu_custom_call" | custom-call | tf_op jit(solution)/shard_map/rows_and_parts/pallas_call | solution.py:415
  52.9 13.1 %collective-permute-done.11.refs_7_ = bf16[4,128,256]{2,1,0:T(8,128)(2,1)S(1)} collective-permute-done((bf16[4,128,256]{2,1,0:T(8,128)(2,1)}, bf16[4,128,256]{2,1,0:T(8,128)(2,1)S(1)}, u32[]{:S(2)}, u32[]{:S(2)}) %collective-permute-start.11) | collective-permute-done | bytes 262176 | tf_op jit(solution)/shard_map/ppermute | solution.py:434
  66.0 0.5 collective-permute-start.15
  66.6 0.7 select_reduce_fusion.3.refs_0_
  67.3 2.4 %collective-permute-start.14 = (bf16[144,128]{1,0:T(8,128)(2,1)}, bf16[144,128]{1,0:T(8,128)(2,1)S(1)}, u32[]{:S(2)}, u32[]{:S(2)}) collective-permute-start(bf16[144,128]{1,0:T(8,128)(2,1)} %get-tuple-element.58), channel_id=1, source_target_pairs={{0,14},{1,15},{2,12},{3,13},{4,10},{5,11},{6,8},{7,9},{8,6},{9,7},... | collective-permute-start | bytes 110600 | tf_op jit(solution)/shard_map/ppermute | solution.py:434
  69.7 1.2 gather_fusion
  70.9 5.9 %place_pages.5 = (bf16[64,128,256]{2,1,0:T(8,128)(2,1)}, f32[4,16,128]{2,1,0:T(8,128)}, f32[4,16,128]{2,1,0:T(8,128)}) custom-call(s32[64]{0:T(128)} %select_reduce_fusion.3.refs_0_, s32[64]{0:T(128)} %get-tuple-element.35.order_ref.refs_1_, s32[4]{0:T(128)} %gather_fusion, f32[8,256]{1,0:T(8,128)} %get-tuple-element.42.refs_3_, ...), custom_call_target="tpu_custom_call" | custom-call | tf_op jit(solution)/shard_map/place_pages/pallas_call | solution.py:319
  76.8 0.8 copy-done.5
  77.6 6.0 %place_pages.6 = (bf16[64,128,256]{2,1,0:T(8,128)(2,1)}, f32[4,16,128]{2,1,0:T(8,128)}, f32[4,16,128]{2,1,0:T(8,128)}) custom-call(s32[64]{0:T(128)} %select_reduce_fusion.3.refs_0_, s32[64]{0:T(128)} %get-tuple-element.35.order_ref.refs_1_, s32[4]{0:T(128)} %gather_fusion, f32[8,256]{1,0:T(8,128)} %get-tuple-element.42.refs_3_, ...), custom_call_target="tpu_custom_call", output_to_operand_aliasing={{0}: (9, {})} | custom-call | tf_op jit(solution)/shard_map/place_pages/pallas_call | solution.py:319
  83.6 0.7 copy-done.13
  84.3 0.2 copy-done.6
  84.5 6.0 %place_pages.7 = (bf16[64,128,256]{2,1,0:T(8,128)(2,1)}, f32[4,16,128]{2,1,0:T(8,128)}, f32[4,16,128]{2,1,0:T(8,128)}) custom-call(s32[64]{0:T(128)} %select_reduce_fusion.3.refs_0_, s32[64]{0:T(128)} %get-tuple-element.35.order_ref.refs_1_, s32[4]{0:T(128)} %gather_fusion, f32[8,256]{1,0:T(8,128)} %get-tuple-element.42.refs_3_, ...), custom_call_target="tpu_custom_call", output_to_operand_aliasing={{0}: (10, {})} | custom-call | tf_op jit(solution)/shard_map/place_pages/pallas_call | solution.py:319
  90.4 6.7 %collective-permute-done.14.refs_7_ = bf16[144,128]{1,0:T(8,128)(2,1)S(1)} collective-permute-done((bf16[144,128]{1,0:T(8,128)(2,1)}, bf16[144,128]{1,0:T(8,128)(2,1)S(1)}, u32[]{:S(2)}, u32[]{:S(2)}) %collective-permute-start.14) | collective-permute-done | bytes 36896 | tf_op jit(solution)/shard_map/ppermute | solution.py:434
  97.2 2.1 %collective-permute-start.16 = (bf16[4,128,256]{2,1,0:T(8,128)(2,1)S(1)}, bf16[4,128,256]{2,1,0:T(8,128)(2,1)S(1)}, u32[]{:S(2)}, u32[]{:S(2)}) collective-permute-start(bf16[4,128,256]{2,1,0:T(8,128)(2,1)S(1)} %copy-done.19), channel_id=1, source_target_pairs={{0,14},{1,15},{2,12},{3,13},{4,10},{5,11},{6,8},{7,9},{8,6},{9,7},... | collective-permute-start | bytes 786440 | tf_op jit(solution)/shard_map/ppermute | solution.py:434
  99.3 0.8 gather_fusion.1
  100.1 0.8 copy-done.7
  100.9 4.4 %place_pages.8 = (bf16[64,128,256]{2,1,0:T(8,128)(2,1)}, f32[4,16,128]{2,1,0:T(8,128)}, f32[4,16,128]{2,1,0:T(8,128)}, bf16[4,16,128]{2,1,0:T(8,128)(2,1)}) custom-call(s32[64]{0:T(128)} %select_reduce_fusion.3.refs_0_, s32[64]{0:T(128)} %get-tuple-element.35.order_ref.refs_1_, s32[4]{0:T(128)} %gather_fusion, ...), custom_call_target="tpu_custom_call", output_to_operand_aliasing={{0}: (9, {})} | custom-call | tf_op jit(solution)/shard_map/place_pages/pallas_call | solution.py:319
  105.3 1.0 collective-permute-done.16.refs_4_
  106.3 0.7 broadcast_in_dim_reshape.4
  107.0 2.2 %collective-permute-start.19 = (bf16[1,4,2,1024]{3,2,1,0:T(2,128)(2,1)S(1)}, bf16[1,4,2,1024]{3,2,1,0:T(2,128)(2,1)S(1)}, u32[]{:S(2)}, u32[]{:S(2)}) collective-permute-start(bf16[1,4,2,1024]{3,2,1,0:T(2,128)(2,1)S(1)} %broadcast_in_dim_reshape.4), channel_id=1, source_target_pairs={{0,12},{1,13},{2,14},{3,15},{4,8},{5,9},{6,10},{7,11},{8,4},{9,5},... | collective-permute-start | bytes 49160 | tf_op jit(solution)/shard_map/ppermute | solution.py:434
  109.2 1.5 %collective-permute-start.17 = (bf16[1,4,2,1024]{3,2,1,0:T(2,128)(2,1)S(1)}, bf16[1,4,2,1024]{3,2,1,0:T(2,128)(2,1)S(1)}, u32[]{:S(2)}, u32[]{:S(2)}) collective-permute-start(bf16[1,4,2,1024]{3,2,1,0:T(2,128)(2,1)S(1)} %broadcast_in_dim_reshape.4), channel_id=1, source_target_pairs={{0,4},{1,5},{2,6},{3,7},{4,0},{5,1},{6,2},{7,3},{8,12},{9,13},{10,... | collective-permute-start | bytes 49160 | tf_op jit(solution)/shard_map/ppermute | solution.py:434
  110.7 0.2 collective-permute-done.19
  110.9 2.9 %collective-permute-done.18 = bf16[1,4,2,1024]{3,2,1,0:T(2,128)(2,1)S(1)} collective-permute-done((bf16[1,4,2,1024]{3,2,1,0:T(2,128)(2,1)S(1)}, bf16[1,4,2,1024]{3,2,1,0:T(2,128)(2,1)S(1)}, u32[]{:S(2)}, u32[]{:S(2)}) %collective-permute-start.18) | collective-permute-done | bytes 16416 | tf_op jit(solution)/shard_map/ppermute | solution.py:434
  113.9 1.2 collective-permute-start.20
  115.2 3.1 %collective-permute-done.20 = bf16[4,4,2,1024]{3,2,1,0:T(2,128)(2,1)S(1)} collective-permute-done((bf16[4,4,2,1024]{3,2,1,0:T(2,128)(2,1)S(1)}, bf16[4,4,2,1024]{3,2,1,0:T(2,128)(2,1)S(1)}, u32[]{:S(2)}, u32[]{:S(2)}) %collective-permute-start.20) | collective-permute-done | bytes 65568 | tf_op jit(solution)/shard_map/ppermute | solution.py:434
  118.5 1.3 collective-permute-start.22
  119.9 1.1 gather_fusion.2
  121.1 0.2 copy.19
  121.3 5.6 %convolution_convert_fusion.1 = bf16[16,512]{1,0:T(8,128)(2,1)S(1)} fusion(bf16[16,8192]{1,0:T(8,128)(2,1)S(1)} %bitcast.43, bf16[512,8192]{1,0:T(8,128)(2,1)} %param.10), kind=kOutput, calls=%fused_computation.4 | convolution fusion | flops 134225920 | bytes 8667136 | tf_op jit(solution)/shard_map/dot_general | solution.py:712
  126.9 0.6 reshape.304
  127.5 6.2 %collective-permute-done.22.refs_5_ = bf16[4,128,256]{2,1,0:T(8,128)(2,1)S(1)} collective-permute-done((bf16[4,128,256]{2,1,0:T(8,128)(2,1)S(1)}, bf16[4,128,256]{2,1,0:T(8,128)(2,1)S(1)}, u32[]{:S(2)}, u32[]{:S(2)}) %collective-permute-start.22) | collective-permute-done | bytes 262176 | tf_op jit(solution)/shard_map/ppermute | solution.py:434
  133.8 0.7 copy-done.14
  134.5 2.5 %place_pages.9 = bf16[64,128,256]{2,1,0:T(8,128)(2,1)} custom-call(s32[64]{0:T(128)} %select_reduce_fusion.3.refs_0_, s32[64]{0:T(128)} %get-tuple-element.35.order_ref.refs_1_, s32[4]{0:T(128)} %gather_fusion, f32[8,256]{1,0:T(8,128)} %get-tuple-element.42.refs_3_, bf16[4,128,256]{2,1,0:T(8,128)(2,1)} %copy-done.11, ...), custom_call_target="tpu_custom_call", output_to_operand_aliasing={{}: (6, {})} | custom-call | tf_op jit(solution)/shard_map/place_pages/pallas_call | solution.py:319
  (85 shorter events, 1.4 us)
Async XLA Ops:
  0.6 17.7 %copy-start.15 = (bf16[8,2,8192]{2,1,0:T(2,128)(2,1)S(1)}, bf16[8,2,8192]{2,1,0:T(2,128)(2,1)}, u32[]{:S(2)}) copy-start(bf16[8,2,8192]{2,1,0:T(2,128)(2,1)} %param.8) | copy-start | bytes 786436
  5.5 32.0 %collective-permute-start.5 = (bf16[4,128,256]{2,1,0:T(8,128)(2,1)}, bf16[4,128,256]{2,1,0:T(8,128)(2,1)S(1)}, u32[]{:S(2)}, u32[]{:S(2)}) collective-permute-start(bf16[4,128,256]{2,1,0:T(8,128)(2,1)} %get-tuple-element.39), channel_id=1, source_target_pairs={{0,8},{1,9},{2,10},{3,11},{4,12},{5,13},{6,14},{7,15},{8,0},{9,1},... | collective-permute-start | bytes 786440 | tf_op jit(solution)/shard_map/ppermute | solution.py:434
  8.1 4.9 %collective-permute-start = (bf16[16,128,256]{2,1,0:T(8,128)(2,1)}, bf16[16,128,256]{2,1,0:T(8,128)(2,1)S(1)}, u32[]{:S(2)}, u32[]{:S(2)}) collective-permute-start(bf16[16,128,256]{2,1,0:T(8,128)(2,1)} %get-tuple-element.36), channel_id=1, source_target_pairs={{0,1},{1,0},{2,3},{3,2},{4,5},{5,4},{6,7},{7,6},{8,9},{9,8},{10,11... | collective-permute-start | bytes 3145736 | tf_op jit(solution)/shard_map/ppermute | solution.py:434
  9.6 27.9 %copy-start.18 = (s32[4]{0:T(128)}, s32[4]{0:T(128)S(1)}, u32[]{:S(2)}) copy-start(s32[4]{0:T(128)S(1)} %get-tuple-element.69.units_ref) | copy-start | bytes 52
  13.1 1.0 copy-start.2
  17.7 3.1 %collective-permute-start.1 = (bf16[16,128,256]{2,1,0:T(8,128)(2,1)}, bf16[16,128,256]{2,1,0:T(8,128)(2,1)S(1)}, u32[]{:S(2)}, u32[]{:S(2)}) collective-permute-start(bf16[16,128,256]{2,1,0:T(8,128)(2,1)} %get-tuple-element.37), channel_id=1, source_target_pairs={{0,1},{1,0},{2,3},{3,2},{4,5},{5,4},{6,7},{7,6},{8,9},{9,8},{10,11... | collective-permute-start | bytes 3145736 | tf_op jit(solution)/shard_map/ppermute | solution.py:434
  18.8 18.7 %collective-permute-start.6 = (bf16[4,128,256]{2,1,0:T(8,128)(2,1)}, bf16[4,128,256]{2,1,0:T(8,128)(2,1)S(1)}, u32[]{:S(2)}, u32[]{:S(2)}) collective-permute-start(bf16[4,128,256]{2,1,0:T(8,128)(2,1)} %get-tuple-element.40), channel_id=1, source_target_pairs={{0,12},{1,13},{2,14},{3,15},{4,8},{5,9},{6,10},{7,11},{8,4},{9,5},... | collective-permute-start | bytes 786440 | tf_op jit(solution)/shard_map/ppermute | solution.py:434
  20.8 22.8 %copy-start.3 = (bf16[16,128,256]{2,1,0:T(8,128)(2,1)}, bf16[16,128,256]{2,1,0:T(8,128)(2,1)S(1)}, u32[]{:S(2)}) copy-start(bf16[16,128,256]{2,1,0:T(8,128)(2,1)S(1)} %collective-permute-done.1.passed_ref.rest_1_) | copy-start | bytes 3145732
  27.9 41.8 %copy-start = (s32[8]{0:T(128)S(1)}, s32[8]{0:T(128)}, u32[]{:S(2)}) copy-start(s32[8]{0:T(128)} %lengths_ref.1) | copy-start | bytes 100
  27.9 6.6 %collective-permute-start.4 = (bf16[1,16,640]{2,1,0:T(8,128)(2,1)S(1)}, bf16[1,16,640]{2,1,0:T(8,128)(2,1)S(1)}, u32[]{:S(2)}, u32[]{:S(2)}) collective-permute-start(bf16[1,16,640]{2,1,0:T(8,128)(2,1)S(1)} %bitcast.47), channel_id=1, source_target_pairs={{0,12},{1,13},{2,14},{3,15},{4,8},{5,9},{6,10},{7,11},{8,4},{9,5},... | collective-permute-start | bytes 61448 | tf_op jit(solution)/shard_map/ppermute | solution.py:434
  28.1 6.4 %collective-permute-start.3 = (bf16[1,16,640]{2,1,0:T(8,128)(2,1)S(1)}, bf16[1,16,640]{2,1,0:T(8,128)(2,1)S(1)}, u32[]{:S(2)}, u32[]{:S(2)}) collective-permute-start(bf16[1,16,640]{2,1,0:T(8,128)(2,1)S(1)} %bitcast.48), channel_id=1, source_target_pairs={{0,8},{1,9},{2,10},{3,11},{4,12},{5,13},{6,14},{7,15},{8,0},{9,1},... | collective-permute-start | bytes 61448 | tf_op jit(solution)/shard_map/ppermute | solution.py:434
  30.8 6.7 %collective-permute-start.2 = (bf16[1,16,640]{2,1,0:T(8,128)(2,1)S(1)}, bf16[1,16,640]{2,1,0:T(8,128)(2,1)S(1)}, u32[]{:S(2)}, u32[]{:S(2)}) collective-permute-start(bf16[1,16,640]{2,1,0:T(8,128)(2,1)S(1)} %bitcast.49), channel_id=1, source_target_pairs={{0,4},{1,5},{2,6},{3,7},{4,0},{5,1},{6,2},{7,3},{8,12},{9,13},{10,... | collective-permute-start | bytes 61448 | tf_op jit(solution)/shard_map/ppermute | solution.py:434
  34.5 32.8 %collective-permute-start.9 = (bf16[8,128,256]{2,1,0:T(8,128)(2,1)}, bf16[8,128,256]{2,1,0:T(8,128)(2,1)S(1)}, u32[]{:S(2)}, u32[]{:S(2)}) collective-permute-start(bf16[8,128,256]{2,1,0:T(8,128)(2,1)} %get-tuple-element.46), channel_id=1, source_target_pairs={{0,4},{1,5},{2,6},{3,7},{4,0},{5,1},{6,2},{7,3},{8,12},{9,13},{10,... | collective-permute-start | bytes 1572872 | tf_op jit(solution)/shard_map/ppermute | solution.py:434
  34.5 42.3 %collective-permute-start.10 = (bf16[8,128,256]{2,1,0:T(8,128)(2,1)}, bf16[8,128,256]{2,1,0:T(8,128)(2,1)S(1)}, u32[]{:S(2)}, u32[]{:S(2)}) collective-permute-start(bf16[8,128,256]{2,1,0:T(8,128)(2,1)} %get-tuple-element.47), channel_id=1, source_target_pairs={{0,6},{1,7},{2,4},{3,5},{4,2},{5,3},{6,0},{7,1},{8,14},{9,15},{10,... | collective-permute-start | bytes 1572872 | tf_op jit(solution)/shard_map/ppermute | solution.py:434
  37.5 33.3 %copy-start.9 = (bf16[4,128,256]{2,1,0:T(8,128)(2,1)}, bf16[4,128,256]{2,1,0:T(8,128)(2,1)S(1)}, u32[]{:S(2)}) copy-start(bf16[4,128,256]{2,1,0:T(8,128)(2,1)S(1)} %collective-permute-done.5.refs_7_) | copy-start | bytes 786436
  37.5 33.3 %copy-start.10 = (bf16[4,128,256]{2,1,0:T(8,128)(2,1)}, bf16[4,128,256]{2,1,0:T(8,128)(2,1)S(1)}, u32[]{:S(2)}) copy-start(bf16[4,128,256]{2,1,0:T(8,128)(2,1)S(1)} %collective-permute-done.6.refs_8_) | copy-start | bytes 786436
  37.5 4.5 %collective-permute-start.7 = (bf16[4,16,640]{2,1,0:T(8,128)(2,1)S(1)}, bf16[4,16,640]{2,1,0:T(8,128)(2,1)S(1)}, u32[]{:S(2)}, u32[]{:S(2)}) collective-permute-start(bf16[4,16,640]{2,1,0:T(8,128)(2,1)S(1)} %pad_maximum_fusion.1), channel_id=1, source_target_pairs={{0,2},{1,3},{2,0},{3,1},{4,6},{5,7},{6,4},{7,5},{8,10},{9,11},{10,... | collective-permute-start | bytes 245768 | tf_op jit(solution)/shard_map/ppermute | solution.py:434
  39.0 27.0 %collective-permute-start.11 = (bf16[4,128,256]{2,1,0:T(8,128)(2,1)}, bf16[4,128,256]{2,1,0:T(8,128)(2,1)S(1)}, u32[]{:S(2)}, u32[]{:S(2)}) collective-permute-start(bf16[4,128,256]{2,1,0:T(8,128)(2,1)} %get-tuple-element.51), channel_id=1, source_target_pairs={{0,8},{1,9},{2,10},{3,11},{4,12},{5,13},{6,14},{7,15},{8,0},{9,1},... | collective-permute-start | bytes 786440 | tf_op jit(solution)/shard_map/ppermute | solution.py:434
  42.1 1.5 %collective-permute-start.8 = (bf16[8,16,640]{2,1,0:T(8,128)(2,1)S(1)}, bf16[8,16,640]{2,1,0:T(8,128)(2,1)S(1)}, u32[]{:S(2)}, u32[]{:S(2)}) collective-permute-start(bf16[8,16,640]{2,1,0:T(8,128)(2,1)S(1)} %pad_maximum_fusion), channel_id=1, source_target_pairs={{0,1},{1,0},{2,3},{3,2},{4,5},{5,4},{6,7},{7,6},{8,9},{9,8},{10,11... | collective-permute-start | bytes 491528 | tf_op jit(solution)/shard_map/ppermute | solution.py:434
  43.6 4.6 %copy-start.8 = (bf16[16,16,640]{2,1,0:T(8,128)(2,1)}, bf16[16,16,640]{2,1,0:T(8,128)(2,1)S(1)}, u32[]{:S(2)}) copy-start(bf16[16,16,640]{2,1,0:T(8,128)(2,1)S(1)} %constant_dynamic-update-slice_fusion.rows_ref) | copy-start | bytes 983044
  46.6 37.0 %collective-permute-start.13 = (bf16[8,128,256]{2,1,0:T(8,128)(2,1)}, bf16[8,128,256]{2,1,0:T(8,128)(2,1)S(1)}, u32[]{:S(2)}, u32[]{:S(2)}) collective-permute-start(bf16[8,128,256]{2,1,0:T(8,128)(2,1)} %get-tuple-element.54), channel_id=1, source_target_pairs={{0,2},{1,3},{2,0},{3,1},{4,6},{5,7},{6,4},{7,5},{8,10},{9,11},{10,... | collective-permute-start | bytes 1572872 | tf_op jit(solution)/shard_map/ppermute | solution.py:434
  47.3 36.3 %collective-permute-start.12 = (bf16[4,128,256]{2,1,0:T(8,128)(2,1)}, bf16[4,128,256]{2,1,0:T(8,128)(2,1)S(1)}, u32[]{:S(2)}, u32[]{:S(2)}) collective-permute-start(bf16[4,128,256]{2,1,0:T(8,128)(2,1)} %get-tuple-element.52), channel_id=1, source_target_pairs={{0,12},{1,13},{2,14},{3,15},{4,8},{5,9},{6,10},{7,11},{8,4},{9,5},... | collective-permute-start | bytes 786440 | tf_op jit(solution)/shard_map/ppermute | solution.py:434
  66.0 17.6 %copy-start.12 = (bf16[4,128,256]{2,1,0:T(8,128)(2,1)}, bf16[4,128,256]{2,1,0:T(8,128)(2,1)S(1)}, u32[]{:S(2)}) copy-start(bf16[4,128,256]{2,1,0:T(8,128)(2,1)S(1)} %collective-permute-done.11.refs_7_) | copy-start | bytes 786436
  66.0 34.1 %collective-permute-start.15 = (bf16[8,128,256]{2,1,0:T(8,128)(2,1)}, bf16[8,128,256]{2,1,0:T(8,128)(2,1)S(1)}, u32[]{:S(2)}, u32[]{:S(2)}) collective-permute-start(bf16[8,128,256]{2,1,0:T(8,128)(2,1)} %get-tuple-element.60), channel_id=1, source_target_pairs={{0,10},{1,11},{2,8},{3,9},{4,14},{5,15},{6,12},{7,13},{8,2},{9,3},... | collective-permute-start | bytes 1572872 | tf_op jit(solution)/shard_map/ppermute | solution.py:434
  67.3 9.6 %copy-start.4 = (bf16[8,128,256]{2,1,0:T(8,128)(2,1)}, bf16[8,128,256]{2,1,0:T(8,128)(2,1)S(1)}, u32[]{:S(2)}) copy-start(bf16[8,128,256]{2,1,0:T(8,128)(2,1)S(1)} %collective-permute-done.9.refs_7_) | copy-start | bytes 1572868
  67.3 29.9 %collective-permute-start.14 = (bf16[144,128]{1,0:T(8,128)(2,1)}, bf16[144,128]{1,0:T(8,128)(2,1)S(1)}, u32[]{:S(2)}, u32[]{:S(2)}) collective-permute-start(bf16[144,128]{1,0:T(8,128)(2,1)} %get-tuple-element.58), channel_id=1, source_target_pairs={{0,14},{1,15},{2,12},{3,13},{4,10},{5,11},{6,8},{7,9},{8,6},{9,7},... | collective-permute-start | bytes 110600 | tf_op jit(solution)/shard_map/ppermute | solution.py:434
  70.8 26.3 %copy-start.19 = (bf16[4,128,256]{2,1,0:T(8,128)(2,1)S(1)}, bf16[4,128,256]{2,1,0:T(8,128)(2,1)}, u32[]{:S(2)}) copy-start(bf16[4,128,256]{2,1,0:T(8,128)(2,1)} %get-tuple-element.64) | copy-start | bytes 786436
  70.8 28.5 %copy-start.1 = (s32[16]{0:T(128)S(1)}, s32[16]{0:T(128)}, u32[]{:S(2)}) copy-start(s32[16]{0:T(128)} %constant.99.clone.turn_ref) | copy-start | bytes 196
  76.8 41.7 %copy-start.16 = (bf16[4,128,256]{2,1,0:T(8,128)(2,1)S(1)}, bf16[4,128,256]{2,1,0:T(8,128)(2,1)}, u32[]{:S(2)}) copy-start(bf16[4,128,256]{2,1,0:T(8,128)(2,1)} %get-tuple-element.66) | copy-start | bytes 786436
  76.8 0.8 copy-start.5
  83.6 0.7 copy-start.13
  83.6 0.9 copy-start.6
  97.2 2.9 %copy-start.17 = (bf16[144,128]{1,0:T(8,128)(2,1)}, bf16[144,128]{1,0:T(8,128)(2,1)S(1)}, u32[]{:S(2)}) copy-start(bf16[144,128]{1,0:T(8,128)(2,1)S(1)} %collective-permute-done.14.refs_7_) | copy-start | bytes 110596
  97.2 9.1 %collective-permute-start.16 = (bf16[4,128,256]{2,1,0:T(8,128)(2,1)S(1)}, bf16[4,128,256]{2,1,0:T(8,128)(2,1)S(1)}, u32[]{:S(2)}, u32[]{:S(2)}) collective-permute-start(bf16[4,128,256]{2,1,0:T(8,128)(2,1)S(1)} %copy-done.19), channel_id=1, source_target_pairs={{0,14},{1,15},{2,12},{3,13},{4,10},{5,11},{6,8},{7,9},{8,6},{9,7},... | collective-permute-start | bytes 786440 | tf_op jit(solution)/shard_map/ppermute | solution.py:434
  100.1 0.8 copy-start.7
  106.3 27.5 %copy-start.11 = (bf16[4,128,256]{2,1,0:T(8,128)(2,1)}, bf16[4,128,256]{2,1,0:T(8,128)(2,1)S(1)}, u32[]{:S(2)}) copy-start(bf16[4,128,256]{2,1,0:T(8,128)(2,1)S(1)} %collective-permute-done.16.refs_4_) | copy-start | bytes 786436
  107.0 3.9 %collective-permute-start.19 = (bf16[1,4,2,1024]{3,2,1,0:T(2,128)(2,1)S(1)}, bf16[1,4,2,1024]{3,2,1,0:T(2,128)(2,1)S(1)}, u32[]{:S(2)}, u32[]{:S(2)}) collective-permute-start(bf16[1,4,2,1024]{3,2,1,0:T(2,128)(2,1)S(1)} %broadcast_in_dim_reshape.4), channel_id=1, source_target_pairs={{0,12},{1,13},{2,14},{3,15},{4,8},{5,9},{6,10},{7,11},{8,4},{9,5},... | collective-permute-start | bytes 49160 | tf_op jit(solution)/shard_map/ppermute | solution.py:434
  109.2 4.6 %collective-permute-start.18 = (bf16[1,4,2,1024]{3,2,1,0:T(2,128)(2,1)S(1)}, bf16[1,4,2,1024]{3,2,1,0:T(2,128)(2,1)S(1)}, u32[]{:S(2)}, u32[]{:S(2)}) collective-permute-start(bf16[1,4,2,1024]{3,2,1,0:T(2,128)(2,1)S(1)} %broadcast_in_dim_reshape.4), channel_id=1, source_target_pairs={{0,8},{1,9},{2,10},{3,11},{4,12},{5,13},{6,14},{7,15},{8,0},{9,1},... | collective-permute-start | bytes 49160 | tf_op jit(solution)/shard_map/ppermute | solution.py:434
  109.2 4.6 %collective-permute-start.17 = (bf16[1,4,2,1024]{3,2,1,0:T(2,128)(2,1)S(1)}, bf16[1,4,2,1024]{3,2,1,0:T(2,128)(2,1)S(1)}, u32[]{:S(2)}, u32[]{:S(2)}) collective-permute-start(bf16[1,4,2,1024]{3,2,1,0:T(2,128)(2,1)S(1)} %broadcast_in_dim_reshape.4), channel_id=1, source_target_pairs={{0,4},{1,5},{2,6},{3,7},{4,0},{5,1},{6,2},{7,3},{8,12},{9,13},{10,... | collective-permute-start | bytes 49160 | tf_op jit(solution)/shard_map/ppermute | solution.py:434
  113.9 4.3 %collective-permute-start.20 = (bf16[4,4,2,1024]{3,2,1,0:T(2,128)(2,1)S(1)}, bf16[4,4,2,1024]{3,2,1,0:T(2,128)(2,1)S(1)}, u32[]{:S(2)}, u32[]{:S(2)}) collective-permute-start(bf16[4,4,2,1024]{3,2,1,0:T(2,128)(2,1)S(1)} %pad_maximum_fusion.2), channel_id=1, source_target_pairs={{0,2},{1,3},{2,0},{3,1},{4,6},{5,7},{6,4},{7,5},{8,10},{9,11},{10,... | collective-permute-start | bytes 196616 | tf_op jit(solution)/shard_map/ppermute | solution.py:434
  118.4 1.5 %collective-permute-start.21 = (bf16[8,4,2,1024]{3,2,1,0:T(2,128)(2,1)S(1)}, bf16[8,4,2,1024]{3,2,1,0:T(2,128)(2,1)S(1)}, u32[]{:S(2)}, u32[]{:S(2)}) collective-permute-start(bf16[8,4,2,1024]{3,2,1,0:T(2,128)(2,1)S(1)} %get-tuple-element.73), channel_id=1, source_target_pairs={{0,1},{1,0},{2,3},{3,2},{4,5},{5,4},{6,7},{7,6},{8,9},{9,8},{10,11... | collective-permute-start | bytes 393224 | tf_op jit(solution)/shard_map/ppermute | solution.py:434
  118.5 15.3 %collective-permute-start.22 = (bf16[4,128,256]{2,1,0:T(8,128)(2,1)S(1)}, bf16[4,128,256]{2,1,0:T(8,128)(2,1)S(1)}, u32[]{:S(2)}, u32[]{:S(2)}) collective-permute-start(bf16[4,128,256]{2,1,0:T(8,128)(2,1)S(1)} %copy-done.16), channel_id=1, source_target_pairs={{0,14},{1,15},{2,12},{3,13},{4,10},{5,11},{6,8},{7,9},{8,6},{9,7},... | collective-permute-start | bytes 786440 | tf_op jit(solution)/shard_map/ppermute | solution.py:434
  133.8 0.7 copy-start.14

commit v8 on v7

--- a/solution.py
+++ b/solution.py
@@ -499,7 +499,6 @@
                 own(a + 1, b + 1, c + 1, d + 1),
             ],
         )
-        moved_4, moved_6 = send(chunk_4, near[1]), send(chunk_6, near[2])
         moved_b, cross_far = send(chunk_b, b), send(cross_far, 1)
     else:
         (packed,), order = first_pack(
@@ -512,35 +511,6 @@
             concat_axis=0,
             tiled=True,
         ).reshape(devices * capacity, page_rows, page_width)
-
-    own_units = lax.dynamic_slice_in_dim(new_units, device * U_DEV, U_DEV)
-    own_lengths = context_lengths[own_units // KVH]
-    wanted = (
-        own_units[:, None] * PER_UNIT + jnp.arange(PER_UNIT, dtype=jnp.int32)[None, :]
-    ).reshape(pages_dev)
-    source_pos = jnp.sum(
-        jnp.where(
-            wanted[:, None] == old_pages[None, :],
-            jnp.arange(total_pages, dtype=jnp.int32)[None, :],
-            0,
-        ),
-        axis=1,
-    )
-    source_dev = source_pos // pages_dev
-    rank = jnp.sum(
-        (
-            (source_dev[:, None] == source_dev[None, :])
-            & (source_pos[None, :] < source_pos[:, None])
-        ).astype(jnp.int32),
-        axis=1,
-    )
-    if pairwise:
-        where = (source_dev ^ device) * capacity + rank
-        spots = jnp.arange(devices * capacity, dtype=jnp.int32)
-        slots = jnp.arange(pages_dev, dtype=jnp.int32)
-        table = jnp.sum(jnp.where(where[None, :] == spots[:, None], slots[None, :], 0), axis=1)
-    else:
-        table = source_dev * capacity + rank
 
     slot_index = jnp.sum(
         jnp.where(
@@ -573,10 +543,43 @@
         flat_rows, qkv_weight, (((1,), (1,)), ((), ())), preferred_element_type=jnp.float32
     ).astype(jnp.bfloat16)
     if pairwise:
+        new_units, old_pages, _ = lax.optimization_barrier((new_units, old_pages, own_part))
+    own_units = lax.dynamic_slice_in_dim(new_units, device * U_DEV, U_DEV)
+    own_lengths = context_lengths[own_units // KVH]
+    wanted = (
+        own_units[:, None] * PER_UNIT + jnp.arange(PER_UNIT, dtype=jnp.int32)[None, :]
+    ).reshape(pages_dev)
+    source_pos = jnp.sum(
+        jnp.where(
+            wanted[:, None] == old_pages[None, :],
+            jnp.arange(total_pages, dtype=jnp.int32)[None, :],
+            0,
+        ),
+        axis=1,
+    )
+    source_dev = source_pos // pages_dev
+    rank = jnp.sum(
+        (
+            (source_dev[:, None] == source_dev[None, :])
+            & (source_pos[None, :] < source_pos[:, None])
+        ).astype(jnp.int32),
+        axis=1,
+    )
+    if pairwise:
+        where = (source_dev ^ device) * capacity + rank
+        spots = jnp.arange(devices * capacity, dtype=jnp.int32)
+        slots = jnp.arange(pages_dev, dtype=jnp.int32)
+        table = jnp.sum(jnp.where(where[None, :] == spots[:, None], slots[None, :], 0), axis=1)
+    else:
+        table = source_dev * capacity + rank
+
+    if pairwise:
         positions = context_lengths[:, None] + jnp.arange(2, dtype=jnp.int32)[None, :]
         cosine, sine = rope_tables(positions.reshape(2 * requests))
         rows, span = gather_line(own_part, devices)
         moved_a2 = send(after(piece(cross_far, 0), own_part, moved_a), a)
+        moved_4 = send(after(chunk_4, rows), near[1])
+        moved_6 = send(after(chunk_6, rows), near[2])
         moved_b2 = send(after(piece(cross_far, 1), own_part), b)
         rows, span = gather_more(after(rows, moved_a, moved_b), span, 2, devices)
         rows, span = gather_more(rows, span, 1, devices)
@@ -604,8 +607,8 @@
             capacity,
             [own(c) + passed(1, 2), own(d), own(near[0]) + passed(2, 1)],
         )
-        moved_2 = send(chunk_2, near[0])
-        moved_c = send(after(chunk_c, moved_a2, sent), c)
+        moved_2 = send(after(chunk_2, sent), near[0])
+        moved_c = send(after(chunk_c, sent, moved_a2), c)
 
         def place(groups, sums, cache, attends, parts, finish):
             entries, sources = [], []
@@ -709,6 +712,8 @@
         .transpose(0, 2, 1, 3)
         .reshape(requests * 2, HEADS * HD)
     )
+    if pairwise:
+        logical = after(logical, moved_d2)
     mixed_rows = lax.dot_general(
         logical, out_weight, (((1,), (1,)), ((), ())), preferred_element_type=jnp.float32
     )

time: 138 us -> 142 us (1.029)
  the two profiles are of different devices: /device:TPU:8 before, /device:TPU:0 now
where the time goes in v8:
time: 142 us; the launch traced here: 140 us
  starting transfers between devices  59.3 us (42%)
  Pallas kernels  41 us (29%)
  matrix products  12.9 us (9%)
  waiting for transfers between devices  12.2 us (9%)
  local copies, waits for them, and re-layouts  10.9 us (8%)
  other arithmetic  2.87 us (2%)
    ppermute x23, starting transfers between devices, swap(): return lax.ppermute(values, 'tp', [(i, i ^ key) for i in range(devices)])  59.3 us
    pallas_call x5, Pallas kernels, place_pages(): pl.pallas_call(functools.partial(place_kernel, entries, started, attends,...  24.8 us
    ppermute x23, waiting for transfers between devices, swap(): return lax.ppermute(values, 'tp', [(i, i ^ key) for i in range(devices)])  12.2 us
    dot_general x1, matrix products, body(): lax.dot_general(flat_rows, qkv_weight, (((1,), (1,)), ((), ())), preferre...  7.16 us
    pallas_call x2, Pallas kernels, next_pack(): pl.pallas_call(functools.partial(next_pack_kernel, capacity, outs_pages,...  6.62 us
    dot_general x1, matrix products, body(): lax.dot_general(logical, out_weight, (((1,), (1,)), ((), ())), preferred_...  5.74 us
    pallas_call x1, Pallas kernels, first_pack(): pl.pallas_call(functools.partial(first_pack_kernel, devices, capacity, ou...  4.82 us
    pallas_call x1, Pallas kernels, rows_and_parts(): pl.pallas_call(functools.partial(rows_kernel, late), out_shape=(jax.Shape...  4.73 us
  transfers between devices with their start and end apart: 23, of which 5 were waited for; matrix products, arithmetic and copies ran while one was open for 11% of the time, Pallas kernels for 24%

profile of v8, /device:TPU:0, one launch (start us, length us, event | category | flops | bytes accessed | tf_op | source)
XLA Modules:
  0.0 140.5 jit_solution(16494840611613238355)
XLA Ops:
  0.7 4.8 %first_pack.1 = (bf16[4,128,256]{2,1,0:T(8,128)(2,1)}, bf16[16,128,256]{2,1,0:T(8,128)(2,1)}, s32[64]{0:T(128)}) custom-call(s32[64]{0:T(128)} %units_ref.1, s32[1024]{0:T(1024)} %old_ref.1, bf16[64,128,256]{2,1,0:T(8,128)(2,1)} %rest_0_.3), custom_call_target="tpu_custom_call" | custom-call | tf_op jit(solution)/shard_map/first_pack/pallas_call | solution.py:142
  5.5 0.5 collective-permute-start
  6.0 3.7 %collective-permute-start.5 = (bf16[4,128,256]{2,1,0:T(8,128)(2,1)}, bf16[4,128,256]{2,1,0:T(8,128)(2,1)S(1)}, u32[]{:S(2)}, u32[]{:S(2)}) collective-permute-start(bf16[4,128,256]{2,1,0:T(8,128)(2,1)} %get-tuple-element.47), channel_id=1, source_target_pairs={{0,8},{1,9},{2,10},{3,11},{4,12},{5,13},{6,14},{7,15},{8,0},{9,1},... | collective-permute-start | bytes 786440 | tf_op jit(solution)/shard_map/ppermute | solution.py:434
  9.7 0.8 reshape.299
  10.4 1.0 copy-done.3
  11.4 3.6 %next_pack.2 = (bf16[8,128,256]{2,1,0:T(8,128)(2,1)}, bf16[8,128,256]{2,1,0:T(8,128)(2,1)}, bf16[4,128,256]{2,1,0:T(8,128)(2,1)}, bf16[16,128,256]{2,1,0:T(8,128)(2,1)}) custom-call(s32[64]{0:T(128)} %get-tuple-element.41.order_ref.refs_1_, bf16[64,128,256]{2,1,0:T(8,128)(2,1)} %rest_0_.3, bf16[16,128,256]{2,1,0:T(8,128)(2,1)} %copy-done.3), custom_call_target="tpu_custom_call" | custom-call | tf_op jit(solution)/shard_map/next_pack/pallas_call | solution.py:160
  15.1 0.2 collective-permute-start.1
  15.5 0.1 reshape.298
  15.6 0.1 fusion.1
  15.8 0.7 pad_maximum_fusion.3
  16.4 0.1 select_reduce_fusion.2
  16.6 3.1 %collective-permute-start.6 = (bf16[4,128,256]{2,1,0:T(8,128)(2,1)}, bf16[4,128,256]{2,1,0:T(8,128)(2,1)S(1)}, u32[]{:S(2)}, u32[]{:S(2)}) collective-permute-start(bf16[4,128,256]{2,1,0:T(8,128)(2,1)} %get-tuple-element.48), channel_id=1, source_target_pairs={{0,12},{1,13},{2,14},{3,15},{4,8},{5,9},{6,10},{7,11},{8,4},{9,5},... | collective-permute-start | bytes 786440 | tf_op jit(solution)/shard_map/ppermute | solution.py:434
  19.6 7.2 %convolution_convert_fusion = bf16[16,640]{1,0:T(8,128)(2,1)S(1)} fusion(bf16[16,8192]{1,0:T(8,128)(2,1)S(1)} %reshape.298, bf16[640,8192]{1,0:T(8,128)(2,1)} %param.9), kind=kOutput, calls=%fused_computation.3 | convolution fusion | flops 167782400 | bytes 10768384 | tf_op jit(solution)/shard_map/dot_general | solution.py:542
  26.8 1.4 %collective-permute-start.4 = (bf16[1,16,640]{2,1,0:T(8,128)(2,1)S(1)}, bf16[1,16,640]{2,1,0:T(8,128)(2,1)S(1)}, u32[]{:S(2)}, u32[]{:S(2)}) collective-permute-start(bf16[1,16,640]{2,1,0:T(8,128)(2,1)S(1)} %bitcast.47), channel_id=1, source_target_pairs={{0,12},{1,13},{2,14},{3,15},{4,8},{5,9},{6,10},{7,11},{8,4},{9,5},... | collective-permute-start | bytes 61448 | tf_op jit(solution)/shard_map/ppermute | solution.py:434
  28.2 3.0 %collective-permute-start.2 = (bf16[1,16,640]{2,1,0:T(8,128)(2,1)S(1)}, bf16[1,16,640]{2,1,0:T(8,128)(2,1)S(1)}, u32[]{:S(2)}, u32[]{:S(2)}) collective-permute-start(bf16[1,16,640]{2,1,0:T(8,128)(2,1)S(1)} %bitcast.49), channel_id=1, source_target_pairs={{0,4},{1,5},{2,6},{3,7},{4,0},{5,1},{6,2},{7,3},{8,12},{9,13},{10,... | collective-permute-start | bytes 61448 | tf_op jit(solution)/shard_map/ppermute | solution.py:434
  31.2 0.1 compare_select_fusion.2
  31.4 0.1 add.136
  31.5 0.2 select_reduce_fusion
  31.7 0.2 select_reduce_fusion.1
  31.9 0.9 fusion.5
  32.7 0.1 convert_reduce_fusion
  32.8 2.6 %collective-permute-done.3 = bf16[1,16,640]{2,1,0:T(8,128)(2,1)S(1)} collective-permute-done((bf16[1,16,640]{2,1,0:T(8,128)(2,1)S(1)}, bf16[1,16,640]{2,1,0:T(8,128)(2,1)S(1)}, u32[]{:S(2)}, u32[]{:S(2)}) %collective-permute-start.3) | collective-permute-done | bytes 20512 | tf_op jit(solution)/shard_map/ppermute | solution.py:434
  35.5 1.7 %collective-permute-start.7 = (bf16[4,16,640]{2,1,0:T(8,128)(2,1)S(1)}, bf16[4,16,640]{2,1,0:T(8,128)(2,1)S(1)}, u32[]{:S(2)}, u32[]{:S(2)}) collective-permute-start(bf16[4,16,640]{2,1,0:T(8,128)(2,1)S(1)} %pad_maximum_fusion.1), channel_id=1, source_target_pairs={{0,2},{1,3},{2,0},{3,1},{4,6},{5,7},{6,4},{7,5},{8,10},{9,11},{10,... | collective-permute-start | bytes 245768 | tf_op jit(solution)/shard_map/ppermute | solution.py:434
  37.1 0.1 select_reduce_fusion.4
  37.3 0.6 reshape.300.ids_ref
  37.9 2.2 %collective-permute-start.11 = (bf16[4,128,256]{2,1,0:T(8,128)(2,1)}, bf16[4,128,256]{2,1,0:T(8,128)(2,1)S(1)}, u32[]{:S(2)}, u32[]{:S(2)}) collective-permute-start(bf16[4,128,256]{2,1,0:T(8,128)(2,1)} %get-tuple-element.61), channel_id=1, source_target_pairs={{0,8},{1,9},{2,10},{3,11},{4,12},{5,13},{6,14},{7,15},{8,0},{9,1},... | collective-permute-start | bytes 786440 | tf_op jit(solution)/shard_map/ppermute | solution.py:434
  40.2 1.9 %collective-permute-start.9 = (bf16[8,128,256]{2,1,0:T(8,128)(2,1)}, bf16[8,128,256]{2,1,0:T(8,128)(2,1)S(1)}, u32[]{:S(2)}, u32[]{:S(2)}) collective-permute-start(bf16[8,128,256]{2,1,0:T(8,128)(2,1)} %get-tuple-element.55), channel_id=1, source_target_pairs={{0,4},{1,5},{2,6},{3,7},{4,0},{5,1},{6,2},{7,3},{8,12},{9,13},{10,... | collective-permute-start | bytes 1572872 | tf_op jit(solution)/shard_map/ppermute | solution.py:434
  42.1 1.1 collective-permute-start.10
  43.3 3.0 %next_pack.3 = (bf16[8,128,256]{2,1,0:T(8,128)(2,1)}, bf16[4,128,256]{2,1,0:T(8,128)(2,1)}, bf16[8,128,256]{2,1,0:T(8,128)(2,1)}) custom-call(s32[64]{0:T(128)} %get-tuple-element.41.order_ref.refs_1_, bf16[64,128,256]{2,1,0:T(8,128)(2,1)} %rest_0_.3, bf16[16,128,256]{2,1,0:T(8,128)(2,1)} %copy-done.4, bf16[16,128,256]{2,1,0:T(8,128)(2,1)} %copy-done.3), custom_call_target="tpu_custom_call" | custom-call | tf_op jit(solution)/shard_map/next_pack/pallas_call | solution.py:160
  46.3 4.7 %rows_and_parts.1 = (f32[4,16,128]{2,1,0:T(8,128)}, f32[8,256]{1,0:T(8,128)}, bf16[144,128]{1,0:T(8,128)(2,1)}) custom-call(s32[4]{0:T(128)} %copy-done.20, s32[16]{0:T(128)} %constant.99.clone.turn_ref, s32[64]{0:T(128)} %get-tuple-element.41.order_ref.refs_1_, s32[8]{0:T(128)} %reshape.300.ids_ref, s32[8]{0:T(128)} %lengths_ref.1, ...), custom_call_target="tpu_custom_call" | custom-call | tf_op jit(solution)/shard_map/rows_and_parts/pallas_call | solution.py:415
  51.1 0.6 collective-permute-start.13
  51.6 0.2 convert_reduce_fusion.1
  51.8 3.5 %collective-permute-start.12 = (bf16[4,128,256]{2,1,0:T(8,128)(2,1)}, bf16[4,128,256]{2,1,0:T(8,128)(2,1)S(1)}, u32[]{:S(2)}, u32[]{:S(2)}) collective-permute-start(bf16[4,128,256]{2,1,0:T(8,128)(2,1)} %get-tuple-element.62), channel_id=1, source_target_pairs={{0,12},{1,13},{2,14},{3,15},{4,8},{5,9},{6,10},{7,11},{8,4},{9,5},... | collective-permute-start | bytes 786440 | tf_op jit(solution)/shard_map/ppermute | solution.py:434
  55.4 0.7 select_reduce_fusion.3.refs_0_
  56.1 3.2 %collective-permute-done.9.refs_7_ = bf16[8,128,256]{2,1,0:T(8,128)(2,1)S(1)} collective-permute-done((bf16[8,128,256]{2,1,0:T(8,128)(2,1)}, bf16[8,128,256]{2,1,0:T(8,128)(2,1)S(1)}, u32[]{:S(2)}, u32[]{:S(2)}) %collective-permute-start.9) | collective-permute-done | bytes 524320 | tf_op jit(solution)/shard_map/ppermute | solution.py:434
  59.3 19.4 %collective-permute-start.14 = (bf16[144,128]{1,0:T(8,128)(2,1)}, bf16[144,128]{1,0:T(8,128)(2,1)S(1)}, u32[]{:S(2)}, u32[]{:S(2)}) collective-permute-start(bf16[144,128]{1,0:T(8,128)(2,1)} %get-tuple-element.65), channel_id=1, source_target_pairs={{0,14},{1,15},{2,12},{3,13},{4,10},{5,11},{6,8},{7,9},{8,6},{9,7},... | collective-permute-start | bytes 110600 | tf_op jit(solution)/shard_map/ppermute | solution.py:434
  78.7 1.2 gather_fusion
  79.9 5.9 %place_pages.5 = (bf16[64,128,256]{2,1,0:T(8,128)(2,1)}, f32[4,16,128]{2,1,0:T(8,128)}, f32[4,16,128]{2,1,0:T(8,128)}) custom-call(s32[64]{0:T(128)} %select_reduce_fusion.3.refs_0_, s32[64]{0:T(128)} %get-tuple-element.41.order_ref.refs_1_, s32[4]{0:T(128)} %gather_fusion, f32[8,256]{1,0:T(8,128)} %get-tuple-element.50.refs_3_, ...), custom_call_target="tpu_custom_call" | custom-call | tf_op jit(solution)/shard_map/place_pages/pallas_call | solution.py:319
  85.8 0.8 copy-done.7
  86.6 6.0 %place_pages.6 = (bf16[64,128,256]{2,1,0:T(8,128)(2,1)}, f32[4,16,128]{2,1,0:T(8,128)}, f32[4,16,128]{2,1,0:T(8,128)}) custom-call(s32[64]{0:T(128)} %select_reduce_fusion.3.refs_0_, s32[64]{0:T(128)} %get-tuple-element.41.order_ref.refs_1_, s32[4]{0:T(128)} %gather_fusion, f32[8,256]{1,0:T(8,128)} %get-tuple-element.50.refs_3_, ...), custom_call_target="tpu_custom_call", output_to_operand_aliasing={{0}: (9, {})} | custom-call | tf_op jit(solution)/shard_map/place_pages/pallas_call | solution.py:319
  92.7 0.7 copy-done.15
  93.3 0.2 copy-done.8
  93.5 6.0 %place_pages.7 = (bf16[64,128,256]{2,1,0:T(8,128)(2,1)}, f32[4,16,128]{2,1,0:T(8,128)}, f32[4,16,128]{2,1,0:T(8,128)}) custom-call(s32[64]{0:T(128)} %select_reduce_fusion.3.refs_0_, s32[64]{0:T(128)} %get-tuple-element.41.order_ref.refs_1_, s32[4]{0:T(128)} %gather_fusion, f32[8,256]{1,0:T(8,128)} %get-tuple-element.50.refs_3_, ...), custom_call_target="tpu_custom_call", output_to_operand_aliasing={{0}: (10, {})} | custom-call | tf_op jit(solution)/shard_map/place_pages/pallas_call | solution.py:319
  99.5 7.8 %collective-permute-start.16 = (bf16[4,128,256]{2,1,0:T(8,128)(2,1)}, bf16[4,128,256]{2,1,0:T(8,128)(2,1)S(1)}, u32[]{:S(2)}, u32[]{:S(2)}) collective-permute-start(bf16[4,128,256]{2,1,0:T(8,128)(2,1)} %get-tuple-element.75), channel_id=1, source_target_pairs={{0,14},{1,15},{2,12},{3,13},{4,10},{5,11},{6,8},{7,9},{8,6},{9,7},... | collective-permute-start | bytes 786440 | tf_op jit(solution)/shard_map/ppermute | solution.py:434
  107.3 0.8 gather_fusion.1
  108.1 0.8 copy-done.6
  108.9 4.4 %place_pages.8 = (bf16[64,128,256]{2,1,0:T(8,128)(2,1)}, f32[4,16,128]{2,1,0:T(8,128)}, f32[4,16,128]{2,1,0:T(8,128)}, bf16[4,16,128]{2,1,0:T(8,128)(2,1)}) custom-call(s32[64]{0:T(128)} %select_reduce_fusion.3.refs_0_, s32[64]{0:T(128)} %get-tuple-element.41.order_ref.refs_1_, s32[4]{0:T(128)} %gather_fusion, ...), custom_call_target="tpu_custom_call", output_to_operand_aliasing={{0}: (9, {})} | custom-call | tf_op jit(solution)/shard_map/place_pages/pallas_call | solution.py:319
  113.3 0.8 broadcast_in_dim_reshape.4
  114.1 3.3 %collective-permute-start.19 = (bf16[1,4,2,1024]{3,2,1,0:T(2,128)(2,1)S(1)}, bf16[1,4,2,1024]{3,2,1,0:T(2,128)(2,1)S(1)}, u32[]{:S(2)}, u32[]{:S(2)}) collective-permute-start(bf16[1,4,2,1024]{3,2,1,0:T(2,128)(2,1)S(1)} %broadcast_in_dim_reshape.4), channel_id=1, source_target_pairs={{0,12},{1,13},{2,14},{3,15},{4,8},{5,9},{6,10},{7,11},{8,4},{9,5},... | collective-permute-start | bytes 49160 | tf_op jit(solution)/shard_map/ppermute | solution.py:434
  117.4 0.5 collective-permute-start.18
  117.9 0.6 collective-permute-start.17
  118.5 3.4 %collective-permute-start.22 = (bf16[4,128,256]{2,1,0:T(8,128)(2,1)S(1)}, bf16[4,128,256]{2,1,0:T(8,128)(2,1)S(1)}, u32[]{:S(2)}, u32[]{:S(2)}) collective-permute-start(bf16[4,128,256]{2,1,0:T(8,128)(2,1)S(1)} %get-tuple-element.77), channel_id=1, source_target_pairs={{0,14},{1,15},{2,12},{3,13},{4,10},{5,11},{6,8},{7,9},{8,6},{9,7},... | collective-permute-start | bytes 786440 | tf_op jit(solution)/shard_map/ppermute | solution.py:434
  121.9 1.9 %collective-permute-done.18 = bf16[1,4,2,1024]{3,2,1,0:T(2,128)(2,1)S(1)} collective-permute-done((bf16[1,4,2,1024]{3,2,1,0:T(2,128)(2,1)S(1)}, bf16[1,4,2,1024]{3,2,1,0:T(2,128)(2,1)S(1)}, u32[]{:S(2)}, u32[]{:S(2)}) %collective-permute-start.18) | collective-permute-done | bytes 16416 | tf_op jit(solution)/shard_map/ppermute | solution.py:434
  123.8 0.1 pad_maximum_fusion.2
  123.9 1.2 collective-permute-start.20
  125.2 3.2 %collective-permute-done.20 = bf16[4,4,2,1024]{3,2,1,0:T(2,128)(2,1)S(1)} collective-permute-done((bf16[4,4,2,1024]{3,2,1,0:T(2,128)(2,1)S(1)}, bf16[4,4,2,1024]{3,2,1,0:T(2,128)(2,1)S(1)}, u32[]{:S(2)}, u32[]{:S(2)}) %collective-permute-start.20) | collective-permute-done | bytes 65568 | tf_op jit(solution)/shard_map/ppermute | solution.py:434
  128.4 0.1 constant_dynamic-update-slice_fusion.3
  128.6 1.3 collective-permute-done.21
  129.9 0.1 constant_dynamic-update-slice_fusion.8
  130.0 1.1 gather_fusion.2
  131.2 0.2 copy.19
  131.4 5.7 %convolution_convert_fusion.1 = bf16[16,512]{1,0:T(8,128)(2,1)S(1)} fusion(bf16[16,8192]{1,0:T(8,128)(2,1)S(1)} %bitcast.43, bf16[512,8192]{1,0:T(8,128)(2,1)} %param.10), kind=kOutput, calls=%fused_computation.4 | convolution fusion | flops 134225920 | bytes 8667136 | tf_op jit(solution)/shard_map/dot_general | solution.py:717
  137.1 0.6 reshape.304
  137.8 2.5 %place_pages.9 = bf16[64,128,256]{2,1,0:T(8,128)(2,1)} custom-call(s32[64]{0:T(128)} %select_reduce_fusion.3.refs_0_, s32[64]{0:T(128)} %get-tuple-element.41.order_ref.refs_1_, s32[4]{0:T(128)} %gather_fusion, f32[8,256]{1,0:T(8,128)} %get-tuple-element.50.refs_3_, bf16[4,128,256]{2,1,0:T(8,128)(2,1)} %copy-done.12, ...), custom_call_target="tpu_custom_call", output_to_operand_aliasing={{}: (6, {})} | custom-call | tf_op jit(solution)/shard_map/place_pages/pallas_call | solution.py:319
  (86 shorter events, 0.9 us)
Async XLA Ops:
  0.6 15.8 %copy-start.19 = (s32[64]{0:T(128)S(1)}, s32[64]{0:T(128)}, u32[]{:S(2)}) copy-start(s32[64]{0:T(128)} %units_ref.1) | copy-start | bytes 772
  0.6 14.7 %copy-start = (s32[8]{0:T(128)S(1)}, s32[8]{0:T(128)}, u32[]{:S(2)}) copy-start(s32[8]{0:T(128)} %lengths_ref.1) | copy-start | bytes 100
  0.7 14.8 %copy-start.16 = (bf16[8,2,8192]{2,1,0:T(2,128)(2,1)S(1)}, bf16[8,2,8192]{2,1,0:T(2,128)(2,1)}, u32[]{:S(2)}) copy-start(bf16[8,2,8192]{2,1,0:T(2,128)(2,1)} %param.8) | copy-start | bytes 786436
  5.5 26.0 %copy-start.18 = (s32[1024]{0:T(1024)S(1)}, s32[1024]{0:T(1024)}, u32[]{:S(2)}) copy-start(s32[1024]{0:T(1024)} %old_ref.1) | copy-start | bytes 12292
  5.5 4.9 %collective-permute-start = (bf16[16,128,256]{2,1,0:T(8,128)(2,1)}, bf16[16,128,256]{2,1,0:T(8,128)(2,1)S(1)}, u32[]{:S(2)}, u32[]{:S(2)}) collective-permute-start(bf16[16,128,256]{2,1,0:T(8,128)(2,1)} %get-tuple-element.42), channel_id=1, source_target_pairs={{0,1},{1,0},{2,3},{3,2},{4,5},{5,4},{6,7},{7,6},{8,9},{9,8},{10,11... | collective-permute-start | bytes 3145736 | tf_op jit(solution)/shard_map/ppermute | solution.py:434
  6.0 29.4 %collective-permute-start.5 = (bf16[4,128,256]{2,1,0:T(8,128)(2,1)}, bf16[4,128,256]{2,1,0:T(8,128)(2,1)S(1)}, u32[]{:S(2)}, u32[]{:S(2)}) collective-permute-start(bf16[4,128,256]{2,1,0:T(8,128)(2,1)} %get-tuple-element.47), channel_id=1, source_target_pairs={{0,8},{1,9},{2,10},{3,11},{4,12},{5,13},{6,14},{7,15},{8,0},{9,1},... | collective-permute-start | bytes 786440 | tf_op jit(solution)/shard_map/ppermute | solution.py:434
  10.4 1.0 copy-start.3
  15.1 4.6 %collective-permute-start.1 = (bf16[16,128,256]{2,1,0:T(8,128)(2,1)}, bf16[16,128,256]{2,1,0:T(8,128)(2,1)S(1)}, u32[]{:S(2)}, u32[]{:S(2)}) collective-permute-start(bf16[16,128,256]{2,1,0:T(8,128)(2,1)} %get-tuple-element.43), channel_id=1, source_target_pairs={{0,1},{1,0},{2,3},{3,2},{4,5},{5,4},{6,7},{7,6},{8,9},{9,8},{10,11... | collective-permute-start | bytes 3145736 | tf_op jit(solution)/shard_map/ppermute | solution.py:434
  16.6 18.9 %collective-permute-start.6 = (bf16[4,128,256]{2,1,0:T(8,128)(2,1)}, bf16[4,128,256]{2,1,0:T(8,128)(2,1)S(1)}, u32[]{:S(2)}, u32[]{:S(2)}) collective-permute-start(bf16[4,128,256]{2,1,0:T(8,128)(2,1)} %get-tuple-element.48), channel_id=1, source_target_pairs={{0,12},{1,13},{2,14},{3,15},{4,8},{5,9},{6,10},{7,11},{8,4},{9,5},... | collective-permute-start | bytes 786440 | tf_op jit(solution)/shard_map/ppermute | solution.py:434
  19.6 23.6 %copy-start.4 = (bf16[16,128,256]{2,1,0:T(8,128)(2,1)}, bf16[16,128,256]{2,1,0:T(8,128)(2,1)S(1)}, u32[]{:S(2)}) copy-start(bf16[16,128,256]{2,1,0:T(8,128)(2,1)S(1)} %collective-permute-done.1.passed_ref.rest_1_) | copy-start | bytes 3145732
  26.8 51.9 %copy-start.1 = (s32[8]{0:T(128)S(1)}, s32[8]{0:T(128)}, u32[]{:S(2)}) copy-start(s32[8]{0:T(128)} %lengths_ref.1) | copy-start | bytes 100
  26.8 6.0 %collective-permute-start.4 = (bf16[1,16,640]{2,1,0:T(8,128)(2,1)S(1)}, bf16[1,16,640]{2,1,0:T(8,128)(2,1)S(1)}, u32[]{:S(2)}, u32[]{:S(2)}) collective-permute-start(bf16[1,16,640]{2,1,0:T(8,128)(2,1)S(1)} %bitcast.47), channel_id=1, source_target_pairs={{0,12},{1,13},{2,14},{3,15},{4,8},{5,9},{6,10},{7,11},{8,4},{9,5},... | collective-permute-start | bytes 61448 | tf_op jit(solution)/shard_map/ppermute | solution.py:434
  28.2 7.2 %collective-permute-start.3 = (bf16[1,16,640]{2,1,0:T(8,128)(2,1)S(1)}, bf16[1,16,640]{2,1,0:T(8,128)(2,1)S(1)}, u32[]{:S(2)}, u32[]{:S(2)}) collective-permute-start(bf16[1,16,640]{2,1,0:T(8,128)(2,1)S(1)} %bitcast.48), channel_id=1, source_target_pairs={{0,8},{1,9},{2,10},{3,11},{4,12},{5,13},{6,14},{7,15},{8,0},{9,1},... | collective-permute-start | bytes 61448 | tf_op jit(solution)/shard_map/ppermute | solution.py:434
  28.2 7.2 %collective-permute-start.2 = (bf16[1,16,640]{2,1,0:T(8,128)(2,1)S(1)}, bf16[1,16,640]{2,1,0:T(8,128)(2,1)S(1)}, u32[]{:S(2)}, u32[]{:S(2)}) collective-permute-start(bf16[1,16,640]{2,1,0:T(8,128)(2,1)S(1)} %bitcast.49), channel_id=1, source_target_pairs={{0,4},{1,5},{2,6},{3,7},{4,0},{5,1},{6,2},{7,3},{8,12},{9,13},{10,... | collective-permute-start | bytes 61448 | tf_op jit(solution)/shard_map/ppermute | solution.py:434
  31.3 15.0 %copy-start.20 = (s32[4]{0:T(128)}, s32[4]{0:T(128)S(1)}, u32[]{:S(2)}) copy-start(s32[4]{0:T(128)S(1)} %get-tuple-element.81.units_ref) | copy-start | bytes 52
  35.4 44.5 %copy-start.10 = (bf16[4,128,256]{2,1,0:T(8,128)(2,1)}, bf16[4,128,256]{2,1,0:T(8,128)(2,1)S(1)}, u32[]{:S(2)}) copy-start(bf16[4,128,256]{2,1,0:T(8,128)(2,1)S(1)} %collective-permute-done.5.refs_7_) | copy-start | bytes 786436
  35.5 44.4 %copy-start.11 = (bf16[4,128,256]{2,1,0:T(8,128)(2,1)}, bf16[4,128,256]{2,1,0:T(8,128)(2,1)S(1)}, u32[]{:S(2)}) copy-start(bf16[4,128,256]{2,1,0:T(8,128)(2,1)S(1)} %collective-permute-done.6.refs_8_) | copy-start | bytes 786436
  35.5 4.6 %collective-permute-start.7 = (bf16[4,16,640]{2,1,0:T(8,128)(2,1)S(1)}, bf16[4,16,640]{2,1,0:T(8,128)(2,1)S(1)}, u32[]{:S(2)}, u32[]{:S(2)}) collective-permute-start(bf16[4,16,640]{2,1,0:T(8,128)(2,1)S(1)} %pad_maximum_fusion.1), channel_id=1, source_target_pairs={{0,2},{1,3},{2,0},{3,1},{4,6},{5,7},{6,4},{7,5},{8,10},{9,11},{10,... | collective-permute-start | bytes 245768 | tf_op jit(solution)/shard_map/ppermute | solution.py:434
  37.9 17.5 %collective-permute-start.11 = (bf16[4,128,256]{2,1,0:T(8,128)(2,1)}, bf16[4,128,256]{2,1,0:T(8,128)(2,1)S(1)}, u32[]{:S(2)}, u32[]{:S(2)}) collective-permute-start(bf16[4,128,256]{2,1,0:T(8,128)(2,1)} %get-tuple-element.61), channel_id=1, source_target_pairs={{0,8},{1,9},{2,10},{3,11},{4,12},{5,13},{6,14},{7,15},{8,0},{9,1},... | collective-permute-start | bytes 786440 | tf_op jit(solution)/shard_map/ppermute | solution.py:434
  40.1 3.1 %collective-permute-start.8 = (bf16[8,16,640]{2,1,0:T(8,128)(2,1)S(1)}, bf16[8,16,640]{2,1,0:T(8,128)(2,1)S(1)}, u32[]{:S(2)}, u32[]{:S(2)}) collective-permute-start(bf16[8,16,640]{2,1,0:T(8,128)(2,1)S(1)} %pad_maximum_fusion), channel_id=1, source_target_pairs={{0,1},{1,0},{2,3},{3,2},{4,5},{5,4},{6,7},{7,6},{8,9},{9,8},{10,11... | collective-permute-start | bytes 491528 | tf_op jit(solution)/shard_map/ppermute | solution.py:434
  40.2 19.2 %collective-permute-start.9 = (bf16[8,128,256]{2,1,0:T(8,128)(2,1)}, bf16[8,128,256]{2,1,0:T(8,128)(2,1)S(1)}, u32[]{:S(2)}, u32[]{:S(2)}) collective-permute-start(bf16[8,128,256]{2,1,0:T(8,128)(2,1)} %get-tuple-element.55), channel_id=1, source_target_pairs={{0,4},{1,5},{2,6},{3,7},{4,0},{5,1},{6,2},{7,3},{8,12},{9,13},{10,... | collective-permute-start | bytes 1572872 | tf_op jit(solution)/shard_map/ppermute | solution.py:434
  42.1 43.7 %collective-permute-start.10 = (bf16[8,128,256]{2,1,0:T(8,128)(2,1)}, bf16[8,128,256]{2,1,0:T(8,128)(2,1)S(1)}, u32[]{:S(2)}, u32[]{:S(2)}) collective-permute-start(bf16[8,128,256]{2,1,0:T(8,128)(2,1)} %get-tuple-element.57), channel_id=1, source_target_pairs={{0,6},{1,7},{2,4},{3,5},{4,2},{5,3},{6,0},{7,1},{8,14},{9,15},{10,... | collective-permute-start | bytes 1572872 | tf_op jit(solution)/shard_map/ppermute | solution.py:434
  43.3 3.0 %copy-start.9 = (bf16[16,16,640]{2,1,0:T(8,128)(2,1)}, bf16[16,16,640]{2,1,0:T(8,128)(2,1)S(1)}, u32[]{:S(2)}) copy-start(bf16[16,16,640]{2,1,0:T(8,128)(2,1)S(1)} %constant_dynamic-update-slice_fusion.rows_ref) | copy-start | bytes 983044
  51.1 41.6 %collective-permute-start.13 = (bf16[8,128,256]{2,1,0:T(8,128)(2,1)}, bf16[8,128,256]{2,1,0:T(8,128)(2,1)S(1)}, u32[]{:S(2)}, u32[]{:S(2)}) collective-permute-start(bf16[8,128,256]{2,1,0:T(8,128)(2,1)} %get-tuple-element.66), channel_id=1, source_target_pairs={{0,2},{1,3},{2,0},{3,1},{4,6},{5,7},{6,4},{7,5},{8,10},{9,11},{10,... | collective-permute-start | bytes 1572872 | tf_op jit(solution)/shard_map/ppermute | solution.py:434
  51.8 40.8 %collective-permute-start.12 = (bf16[4,128,256]{2,1,0:T(8,128)(2,1)}, bf16[4,128,256]{2,1,0:T(8,128)(2,1)S(1)}, u32[]{:S(2)}, u32[]{:S(2)}) collective-permute-start(bf16[4,128,256]{2,1,0:T(8,128)(2,1)} %get-tuple-element.62), channel_id=1, source_target_pairs={{0,12},{1,13},{2,14},{3,15},{4,8},{5,9},{6,10},{7,11},{8,4},{9,5},... | collective-permute-start | bytes 786440 | tf_op jit(solution)/shard_map/ppermute | solution.py:434
  55.4 37.3 %copy-start.13 = (bf16[4,128,256]{2,1,0:T(8,128)(2,1)}, bf16[4,128,256]{2,1,0:T(8,128)(2,1)S(1)}, u32[]{:S(2)}) copy-start(bf16[4,128,256]{2,1,0:T(8,128)(2,1)S(1)} %collective-permute-done.11.refs_7_) | copy-start | bytes 786436
  55.4 52.8 %collective-permute-start.15 = (bf16[8,128,256]{2,1,0:T(8,128)(2,1)}, bf16[8,128,256]{2,1,0:T(8,128)(2,1)S(1)}, u32[]{:S(2)}, u32[]{:S(2)}) collective-permute-start(bf16[8,128,256]{2,1,0:T(8,128)(2,1)} %get-tuple-element.71), channel_id=1, source_target_pairs={{0,10},{1,11},{2,8},{3,9},{4,14},{5,15},{6,12},{7,13},{8,2},{9,3},... | collective-permute-start | bytes 1572872 | tf_op jit(solution)/shard_map/ppermute | solution.py:434
  59.3 26.5 %copy-start.5 = (bf16[8,128,256]{2,1,0:T(8,128)(2,1)}, bf16[8,128,256]{2,1,0:T(8,128)(2,1)S(1)}, u32[]{:S(2)}) copy-start(bf16[8,128,256]{2,1,0:T(8,128)(2,1)S(1)} %collective-permute-done.9.refs_7_) | copy-start | bytes 1572868
  59.3 40.2 %collective-permute-start.14 = (bf16[144,128]{1,0:T(8,128)(2,1)}, bf16[144,128]{1,0:T(8,128)(2,1)S(1)}, u32[]{:S(2)}, u32[]{:S(2)}) collective-permute-start(bf16[144,128]{1,0:T(8,128)(2,1)} %get-tuple-element.65), channel_id=1, source_target_pairs={{0,14},{1,15},{2,12},{3,13},{4,10},{5,11},{6,8},{7,9},{8,6},{9,7},... | collective-permute-start | bytes 110600 | tf_op jit(solution)/shard_map/ppermute | solution.py:434
  79.9 27.4 %copy-start.2 = (s32[16]{0:T(128)S(1)}, s32[16]{0:T(128)}, u32[]{:S(2)}) copy-start(s32[16]{0:T(128)} %constant.99.clone.turn_ref) | copy-start | bytes 196
  85.8 0.8 copy-start.7
  92.6 0.7 copy-start.15
  92.6 0.9 copy-start.8
  99.5 8.6 %copy-start.17 = (bf16[144,128]{1,0:T(8,128)(2,1)}, bf16[144,128]{1,0:T(8,128)(2,1)S(1)}, u32[]{:S(2)}) copy-start(bf16[144,128]{1,0:T(8,128)(2,1)S(1)} %collective-permute-done.14.refs_7_) | copy-start | bytes 110596
  99.5 13.8 %collective-permute-start.16 = (bf16[4,128,256]{2,1,0:T(8,128)(2,1)}, bf16[4,128,256]{2,1,0:T(8,128)(2,1)S(1)}, u32[]{:S(2)}, u32[]{:S(2)}) collective-permute-start(bf16[4,128,256]{2,1,0:T(8,128)(2,1)} %get-tuple-element.75), channel_id=1, source_target_pairs={{0,14},{1,15},{2,12},{3,13},{4,10},{5,11},{6,8},{7,9},{8,6},{9,7},... | collective-permute-start | bytes 786440 | tf_op jit(solution)/shard_map/ppermute | solution.py:434
  108.1 0.8 copy-start.6
  113.3 24.5 %copy-start.12 = (bf16[4,128,256]{2,1,0:T(8,128)(2,1)}, bf16[4,128,256]{2,1,0:T(8,128)(2,1)S(1)}, u32[]{:S(2)}) copy-start(bf16[4,128,256]{2,1,0:T(8,128)(2,1)S(1)} %collective-permute-done.16.refs_4_) | copy-start | bytes 786436
  114.1 7.9 %collective-permute-start.19 = (bf16[1,4,2,1024]{3,2,1,0:T(2,128)(2,1)S(1)}, bf16[1,4,2,1024]{3,2,1,0:T(2,128)(2,1)S(1)}, u32[]{:S(2)}, u32[]{:S(2)}) collective-permute-start(bf16[1,4,2,1024]{3,2,1,0:T(2,128)(2,1)S(1)} %broadcast_in_dim_reshape.4), channel_id=1, source_target_pairs={{0,12},{1,13},{2,14},{3,15},{4,8},{5,9},{6,10},{7,11},{8,4},{9,5},... | collective-permute-start | bytes 49160 | tf_op jit(solution)/shard_map/ppermute | solution.py:434
  117.4 6.4 %collective-permute-start.18 = (bf16[1,4,2,1024]{3,2,1,0:T(2,128)(2,1)S(1)}, bf16[1,4,2,1024]{3,2,1,0:T(2,128)(2,1)S(1)}, u32[]{:S(2)}, u32[]{:S(2)}) collective-permute-start(bf16[1,4,2,1024]{3,2,1,0:T(2,128)(2,1)S(1)} %broadcast_in_dim_reshape.4), channel_id=1, source_target_pairs={{0,8},{1,9},{2,10},{3,11},{4,12},{5,13},{6,14},{7,15},{8,0},{9,1},... | collective-permute-start | bytes 49160 | tf_op jit(solution)/shard_map/ppermute | solution.py:434
  117.9 6.0 %collective-permute-start.17 = (bf16[1,4,2,1024]{3,2,1,0:T(2,128)(2,1)S(1)}, bf16[1,4,2,1024]{3,2,1,0:T(2,128)(2,1)S(1)}, u32[]{:S(2)}, u32[]{:S(2)}) collective-permute-start(bf16[1,4,2,1024]{3,2,1,0:T(2,128)(2,1)S(1)} %broadcast_in_dim_reshape.4), channel_id=1, source_target_pairs={{0,4},{1,5},{2,6},{3,7},{4,0},{5,1},{6,2},{7,3},{8,12},{9,13},{10,... | collective-permute-start | bytes 49160 | tf_op jit(solution)/shard_map/ppermute | solution.py:434
  118.5 12.9 %collective-permute-start.22 = (bf16[4,128,256]{2,1,0:T(8,128)(2,1)S(1)}, bf16[4,128,256]{2,1,0:T(8,128)(2,1)S(1)}, u32[]{:S(2)}, u32[]{:S(2)}) collective-permute-start(bf16[4,128,256]{2,1,0:T(8,128)(2,1)S(1)} %get-tuple-element.77), channel_id=1, source_target_pairs={{0,14},{1,15},{2,12},{3,13},{4,10},{5,11},{6,8},{7,9},{8,6},{9,7},... | collective-permute-start | bytes 786440 | tf_op jit(solution)/shard_map/ppermute | solution.py:434
  123.9 4.5 %collective-permute-start.20 = (bf16[4,4,2,1024]{3,2,1,0:T(2,128)(2,1)S(1)}, bf16[4,4,2,1024]{3,2,1,0:T(2,128)(2,1)S(1)}, u32[]{:S(2)}, u32[]{:S(2)}) collective-permute-start(bf16[4,4,2,1024]{3,2,1,0:T(2,128)(2,1)S(1)} %pad_maximum_fusion.2), channel_id=1, source_target_pairs={{0,2},{1,3},{2,0},{3,1},{4,6},{5,7},{6,4},{7,5},{8,10},{9,11},{10,... | collective-permute-start | bytes 196616 | tf_op jit(solution)/shard_map/ppermute | solution.py:434
  128.5 1.4 %collective-permute-start.21 = (bf16[8,4,2,1024]{3,2,1,0:T(2,128)(2,1)S(1)}, bf16[8,4,2,1024]{3,2,1,0:T(2,128)(2,1)S(1)}, u32[]{:S(2)}, u32[]{:S(2)}) collective-permute-start(bf16[8,4,2,1024]{3,2,1,0:T(2,128)(2,1)S(1)} %get-tuple-element.85), channel_id=1, source_target_pairs={{0,1},{1,0},{2,3},{3,2},{4,5},{5,4},{6,7},{7,6},{8,9},{9,8},{10,11... | collective-permute-start | bytes 393224 | tf_op jit(solution)/shard_map/ppermute | solution.py:434
  131.4 6.4 %copy-start.14 = (bf16[4,128,256]{2,1,0:T(8,128)(2,1)}, bf16[4,128,256]{2,1,0:T(8,128)(2,1)S(1)}, u32[]{:S(2)}) copy-start(bf16[4,128,256]{2,1,0:T(8,128)(2,1)S(1)} %collective-permute-done.22.refs_5_) | copy-start | bytes 786436

commit v9 on v8

--- a/solution.py
+++ b/solution.py
@@ -246,7 +246,7 @@
         total = jnp.sum(jnp.where(mine, sums, 0.0), axis=1, keepdims=True)
         weighted_ref[unit] += part_ref[n * QROWS : (n + 1) * QROWS, :].astype(jnp.float32)
         total_ref[unit] += jnp.broadcast_to(total, (QROWS, HD))
-    group = 4
+    group = 8
     for first in range(0, len(entries) if attends else 0, group):
         found = []
         for n in range(first, min(first + group, len(entries))):
@@ -641,6 +641,15 @@
             [],
             False,
         )
+        moved_d = send(after(chunk_d, moved_b2, sums[0], parts[0]), d)
+        new_cache, sums, _ = place(
+            [(moved_a2, [a + 1], 0), (moved_b2, [b + 1], 0), (moved_2, [near[0], near[0] + 1], 0)],
+            sums,
+            new_cache,
+            True,
+            [],
+            False,
+        )
         new_cache, sums, _ = place(
             [(moved_4, [near[1], near[1] + 1], 0), (moved_6, [near[2], near[2] + 1], 0)],
             sums,
@@ -649,15 +658,6 @@
             [],
             False,
         )
-        new_cache, sums, _ = place(
-            [(moved_a2, [a + 1], 0), (moved_b2, [b + 1], 0), (moved_2, [near[0], near[0] + 1], 0)],
-            sums,
-            new_cache,
-            True,
-            [],
-            False,
-        )
-        moved_d = send(after(chunk_d, moved_b2, sums[0], parts[0]), d)
         new_cache, sums, attended = place(
             [(moved_c, [c, c + 1], 0)], sums, new_cache, True, parts, True
         )

time: 142 us -> 151 us (1.063)
  waiting for transfers between devices: 12.2 us -> 39 us
  starting transfers between devices: 59.3 us -> 41.5 us
    ppermute x23, waiting for transfers between devices: 12.2 us -> 39 us  [swap(): return lax.ppermute(values, 'tp', [(i, i ^ key) for i in range(devices)])]
    ppermute x23, starting transfers between devices: 59.3 us -> 41.5 us  [swap(): return lax.ppermute(values, 'tp', [(i, i ^ key) for i in range(devices)])]
  transfers between devices with their start and end apart: 23 -> 23, of which waited for: 5 -> 8; matrix products, arithmetic and copies ran while one was open for 11% -> 11% of each run, Pallas kernels for 24% -> 23%
where the time goes in v9:
time: 151 us; the launch traced here: 150 us
  starting transfers between devices  41.5 us (27%)
  Pallas kernels  41.1 us (27%)
  waiting for transfers between devices  39 us (26%)
  matrix products  12.9 us (9%)
  local copies, waits for them, and re-layouts  11.1 us (7%)
  other arithmetic  2.83 us (2%)
    ppermute x23, starting transfers between devices, swap(): return lax.ppermute(values, 'tp', [(i, i ^ key) for i in range(devices)])  41.5 us
    ppermute x23, waiting for transfers between devices, swap(): return lax.ppermute(values, 'tp', [(i, i ^ key) for i in range(devices)])  39 us
    pallas_call x5, Pallas kernels, place_pages(): pl.pallas_call(functools.partial(place_kernel, entries, started, attends,...  24.7 us
    dot_general x1, matrix products, body(): lax.dot_general(flat_rows, qkv_weight, (((1,), (1,)), ((), ())), preferre...  7.16 us
    pallas_call x2, Pallas kernels, next_pack(): pl.pallas_call(functools.partial(next_pack_kernel, capacity, outs_pages,...  6.77 us
    dot_general x1, matrix products, body(): lax.dot_general(logical, out_weight, (((1,), (1,)), ((), ())), preferred_...  5.74 us
    pallas_call x1, Pallas kernels, first_pack(): pl.pallas_call(functools.partial(first_pack_kernel, devices, capacity, ou...  4.82 us
    pallas_call x1, Pallas kernels, rows_and_parts(): pl.pallas_call(functools.partial(rows_kernel, late), out_shape=(jax.Shape...  4.73 us
  transfers between devices with their start and end apart: 23, of which 8 were waited for; matrix products, arithmetic and copies ran while one was open for 11% of the time, Pallas kernels for 23%

profile of v9, /device:TPU:0, one launch (start us, length us, event | category | flops | bytes accessed | tf_op | source)
XLA Modules:
  0.0 149.7 jit_solution(15174645558566703050)
XLA Ops:
  0.7 4.8 %first_pack.1 = (bf16[4,128,256]{2,1,0:T(8,128)(2,1)}, bf16[16,128,256]{2,1,0:T(8,128)(2,1)}, s32[64]{0:T(128)}) custom-call(s32[64]{0:T(128)} %units_ref.1, s32[1024]{0:T(1024)} %old_ref.1, bf16[64,128,256]{2,1,0:T(8,128)(2,1)} %rest_0_.3), custom_call_target="tpu_custom_call" | custom-call | tf_op jit(solution)/shard_map/first_pack/pallas_call | solution.py:142
  5.5 0.5 collective-permute-start
  6.0 3.7 %collective-permute-start.5 = (bf16[4,128,256]{2,1,0:T(8,128)(2,1)}, bf16[4,128,256]{2,1,0:T(8,128)(2,1)S(1)}, u32[]{:S(2)}, u32[]{:S(2)}) collective-permute-start(bf16[4,128,256]{2,1,0:T(8,128)(2,1)} %get-tuple-element.47), channel_id=1, source_target_pairs={{0,8},{1,9},{2,10},{3,11},{4,12},{5,13},{6,14},{7,15},{8,0},{9,1},... | collective-permute-start | bytes 786440 | tf_op jit(solution)/shard_map/ppermute | solution.py:434
  9.7 0.8 reshape.299
  10.4 1.0 copy-done.3
  11.4 3.6 %next_pack.2 = (bf16[8,128,256]{2,1,0:T(8,128)(2,1)}, bf16[8,128,256]{2,1,0:T(8,128)(2,1)}, bf16[4,128,256]{2,1,0:T(8,128)(2,1)}, bf16[16,128,256]{2,1,0:T(8,128)(2,1)}) custom-call(s32[64]{0:T(128)} %get-tuple-element.41.order_ref.refs_1_, bf16[64,128,256]{2,1,0:T(8,128)(2,1)} %rest_0_.3, bf16[16,128,256]{2,1,0:T(8,128)(2,1)} %copy-done.3), custom_call_target="tpu_custom_call" | custom-call | tf_op jit(solution)/shard_map/next_pack/pallas_call | solution.py:160
  15.1 0.2 collective-permute-start.1
  15.5 0.1 reshape.298
  15.6 0.1 fusion.1
  15.8 0.7 pad_maximum_fusion.3
  16.4 0.1 select_reduce_fusion.2
  16.6 3.1 %collective-permute-start.6 = (bf16[4,128,256]{2,1,0:T(8,128)(2,1)}, bf16[4,128,256]{2,1,0:T(8,128)(2,1)S(1)}, u32[]{:S(2)}, u32[]{:S(2)}) collective-permute-start(bf16[4,128,256]{2,1,0:T(8,128)(2,1)} %get-tuple-element.48), channel_id=1, source_target_pairs={{0,12},{1,13},{2,14},{3,15},{4,8},{5,9},{6,10},{7,11},{8,4},{9,5},... | collective-permute-start | bytes 786440 | tf_op jit(solution)/shard_map/ppermute | solution.py:434
  19.6 7.2 %convolution_convert_fusion = bf16[16,640]{1,0:T(8,128)(2,1)S(1)} fusion(bf16[16,8192]{1,0:T(8,128)(2,1)S(1)} %reshape.298, bf16[640,8192]{1,0:T(8,128)(2,1)} %param.9), kind=kOutput, calls=%fused_computation.3 | convolution fusion | flops 167782400 | bytes 10768384 | tf_op jit(solution)/shard_map/dot_general | solution.py:542
  26.8 1.4 collective-permute-start.4
  28.2 3.0 %collective-permute-start.2 = (bf16[1,16,640]{2,1,0:T(8,128)(2,1)S(1)}, bf16[1,16,640]{2,1,0:T(8,128)(2,1)S(1)}, u32[]{:S(2)}, u32[]{:S(2)}) collective-permute-start(bf16[1,16,640]{2,1,0:T(8,128)(2,1)S(1)} %bitcast.49), channel_id=1, source_target_pairs={{0,4},{1,5},{2,6},{3,7},{4,0},{5,1},{6,2},{7,3},{8,12},{9,13},{10,... | collective-permute-start | bytes 61448 | tf_op jit(solution)/shard_map/ppermute | solution.py:434
  31.4 0.1 add.136
  31.5 0.2 select_reduce_fusion
  31.7 0.2 convert_reduce_fusion.1
  31.9 0.2 select_reduce_fusion.1
  32.0 0.9 fusion.5
  32.9 0.1 convert_reduce_fusion
  33.0 2.3 %collective-permute-done.3 = bf16[1,16,640]{2,1,0:T(8,128)(2,1)S(1)} collective-permute-done((bf16[1,16,640]{2,1,0:T(8,128)(2,1)S(1)}, bf16[1,16,640]{2,1,0:T(8,128)(2,1)S(1)}, u32[]{:S(2)}, u32[]{:S(2)}) %collective-permute-start.3) | collective-permute-done | bytes 20512 | tf_op jit(solution)/shard_map/ppermute | solution.py:434
  35.5 1.7 %collective-permute-start.7 = (bf16[4,16,640]{2,1,0:T(8,128)(2,1)S(1)}, bf16[4,16,640]{2,1,0:T(8,128)(2,1)S(1)}, u32[]{:S(2)}, u32[]{:S(2)}) collective-permute-start(bf16[4,16,640]{2,1,0:T(8,128)(2,1)S(1)} %pad_maximum_fusion.1), channel_id=1, source_target_pairs={{0,2},{1,3},{2,0},{3,1},{4,6},{5,7},{6,4},{7,5},{8,10},{9,11},{10,... | collective-permute-start | bytes 245768 | tf_op jit(solution)/shard_map/ppermute | solution.py:434
  37.1 0.1 select_reduce_fusion.4
  37.3 0.6 reshape.300.ids_ref
  37.9 2.2 %collective-permute-start.9 = (bf16[4,128,256]{2,1,0:T(8,128)(2,1)}, bf16[4,128,256]{2,1,0:T(8,128)(2,1)S(1)}, u32[]{:S(2)}, u32[]{:S(2)}) collective-permute-start(bf16[4,128,256]{2,1,0:T(8,128)(2,1)} %get-tuple-element.54), channel_id=1, source_target_pairs={{0,8},{1,9},{2,10},{3,11},{4,12},{5,13},{6,14},{7,15},{8,0},{9,1},... | collective-permute-start | bytes 786440 | tf_op jit(solution)/shard_map/ppermute | solution.py:434
  40.1 1.3 collective-permute-start.10
  41.5 0.6 collective-permute-start.12
  42.1 1.4 collective-permute-start.13
  43.6 3.1 %next_pack.3 = (bf16[8,128,256]{2,1,0:T(8,128)(2,1)}, bf16[4,128,256]{2,1,0:T(8,128)(2,1)}, bf16[8,128,256]{2,1,0:T(8,128)(2,1)}) custom-call(s32[64]{0:T(128)} %get-tuple-element.41.order_ref.refs_1_, bf16[64,128,256]{2,1,0:T(8,128)(2,1)} %rest_0_.3, bf16[16,128,256]{2,1,0:T(8,128)(2,1)} %copy-done.4, bf16[16,128,256]{2,1,0:T(8,128)(2,1)} %copy-done.3), custom_call_target="tpu_custom_call" | custom-call | tf_op jit(solution)/shard_map/next_pack/pallas_call | solution.py:160
  46.8 4.7 %rows_and_parts.1 = (f32[4,16,128]{2,1,0:T(8,128)}, f32[8,256]{1,0:T(8,128)}, bf16[144,128]{1,0:T(8,128)(2,1)}) custom-call(s32[4]{0:T(128)} %copy-done.20, s32[16]{0:T(128)} %constant.99.clone.turn_ref, s32[64]{0:T(128)} %get-tuple-element.41.order_ref.refs_1_, s32[8]{0:T(128)} %reshape.300.ids_ref, s32[8]{0:T(128)} %lengths_ref.1, ...), custom_call_target="tpu_custom_call" | custom-call | tf_op jit(solution)/shard_map/rows_and_parts/pallas_call | solution.py:415
  51.5 7.7 %collective-permute-done.9.refs_7_ = bf16[4,128,256]{2,1,0:T(8,128)(2,1)S(1)} collective-permute-done((bf16[4,128,256]{2,1,0:T(8,128)(2,1)}, bf16[4,128,256]{2,1,0:T(8,128)(2,1)S(1)}, u32[]{:S(2)}, u32[]{:S(2)}) %collective-permute-start.9) | collective-permute-done | bytes 262176 | tf_op jit(solution)/shard_map/ppermute | solution.py:434
  59.3 1.1 collective-permute-start.11
  60.4 0.6 select_reduce_fusion.3.refs_0_
  61.0 2.5 %collective-permute-start.14 = (bf16[144,128]{1,0:T(8,128)(2,1)}, bf16[144,128]{1,0:T(8,128)(2,1)S(1)}, u32[]{:S(2)}, u32[]{:S(2)}) collective-permute-start(bf16[144,128]{1,0:T(8,128)(2,1)} %get-tuple-element.58), channel_id=1, source_target_pairs={{0,14},{1,15},{2,12},{3,13},{4,10},{5,11},{6,8},{7,9},{8,6},{9,7},... | collective-permute-start | bytes 110600 | tf_op jit(solution)/shard_map/ppermute | solution.py:434
  63.5 1.2 gather_fusion
  64.7 6.0 %place_pages.5 = (bf16[64,128,256]{2,1,0:T(8,128)(2,1)}, f32[4,16,128]{2,1,0:T(8,128)}, f32[4,16,128]{2,1,0:T(8,128)}) custom-call(s32[64]{0:T(128)} %select_reduce_fusion.3.refs_0_, s32[64]{0:T(128)} %get-tuple-element.41.order_ref.refs_1_, s32[4]{0:T(128)} %gather_fusion, f32[8,256]{1,0:T(8,128)} %get-tuple-element.50.refs_3_, ...), custom_call_target="tpu_custom_call" | custom-call | tf_op jit(solution)/shard_map/place_pages/pallas_call | solution.py:319
  70.7 18.1 %collective-permute-done.14.refs_7_ = bf16[144,128]{1,0:T(8,128)(2,1)S(1)} collective-permute-done((bf16[144,128]{1,0:T(8,128)(2,1)}, bf16[144,128]{1,0:T(8,128)(2,1)S(1)}, u32[]{:S(2)}, u32[]{:S(2)}) %collective-permute-start.14) | collective-permute-done | bytes 36896 | tf_op jit(solution)/shard_map/ppermute | solution.py:434
  88.8 2.9 %collective-permute-start.16 = (bf16[4,128,256]{2,1,0:T(8,128)(2,1)}, bf16[4,128,256]{2,1,0:T(8,128)(2,1)S(1)}, u32[]{:S(2)}, u32[]{:S(2)}) collective-permute-start(bf16[4,128,256]{2,1,0:T(8,128)(2,1)} %get-tuple-element.75), channel_id=1, source_target_pairs={{0,14},{1,15},{2,12},{3,13},{4,10},{5,11},{6,8},{7,9},{8,6},{9,7},... | collective-permute-start | bytes 786440 | tf_op jit(solution)/shard_map/ppermute | solution.py:434
  91.7 0.8 gather_fusion.1
  92.5 6.8 %collective-permute-done.11.refs_9_ = bf16[8,128,256]{2,1,0:T(8,128)(2,1)S(1)} collective-permute-done((bf16[8,128,256]{2,1,0:T(8,128)(2,1)}, bf16[8,128,256]{2,1,0:T(8,128)(2,1)S(1)}, u32[]{:S(2)}, u32[]{:S(2)}) %collective-permute-start.11) | collective-permute-done | bytes 524320 | tf_op jit(solution)/shard_map/ppermute | solution.py:434
  99.3 0.8 copy-done.8
  100.1 5.9 %place_pages.6 = (bf16[64,128,256]{2,1,0:T(8,128)(2,1)}, f32[4,16,128]{2,1,0:T(8,128)}, f32[4,16,128]{2,1,0:T(8,128)}) custom-call(s32[64]{0:T(128)} %select_reduce_fusion.3.refs_0_, s32[64]{0:T(128)} %get-tuple-element.41.order_ref.refs_1_, s32[4]{0:T(128)} %gather_fusion, f32[8,256]{1,0:T(8,128)} %get-tuple-element.50.refs_3_, ...), custom_call_target="tpu_custom_call", output_to_operand_aliasing={{0}: (10, {})} | custom-call | tf_op jit(solution)/shard_map/place_pages/pallas_call | solution.py:319
  106.0 0.8 copy-done.5
  106.7 0.2 copy-done.6
  106.9 6.0 %place_pages.7 = (bf16[64,128,256]{2,1,0:T(8,128)(2,1)}, f32[4,16,128]{2,1,0:T(8,128)}, f32[4,16,128]{2,1,0:T(8,128)}) custom-call(s32[64]{0:T(128)} %select_reduce_fusion.3.refs_0_, s32[64]{0:T(128)} %get-tuple-element.41.order_ref.refs_1_, s32[4]{0:T(128)} %gather_fusion, f32[8,256]{1,0:T(8,128)} %get-tuple-element.50.refs_3_, ...), custom_call_target="tpu_custom_call", output_to_operand_aliasing={{0}: (9, {})} | custom-call | tf_op jit(solution)/shard_map/place_pages/pallas_call | solution.py:319
  112.9 0.8 copy-done.7
  113.7 4.4 %place_pages.8 = (bf16[64,128,256]{2,1,0:T(8,128)(2,1)}, f32[4,16,128]{2,1,0:T(8,128)}, f32[4,16,128]{2,1,0:T(8,128)}, bf16[4,16,128]{2,1,0:T(8,128)(2,1)}) custom-call(s32[64]{0:T(128)} %select_reduce_fusion.3.refs_0_, s32[64]{0:T(128)} %get-tuple-element.41.order_ref.refs_1_, s32[4]{0:T(128)} %gather_fusion, ...), custom_call_target="tpu_custom_call", output_to_operand_aliasing={{0}: (9, {})} | custom-call | tf_op jit(solution)/shard_map/place_pages/pallas_call | solution.py:319
  118.1 0.8 broadcast_in_dim_reshape.4
  118.9 5.1 %collective-permute-start.19 = (bf16[1,4,2,1024]{3,2,1,0:T(2,128)(2,1)S(1)}, bf16[1,4,2,1024]{3,2,1,0:T(2,128)(2,1)S(1)}, u32[]{:S(2)}, u32[]{:S(2)}) collective-permute-start(bf16[1,4,2,1024]{3,2,1,0:T(2,128)(2,1)S(1)} %broadcast_in_dim_reshape.4), channel_id=1, source_target_pairs={{0,12},{1,13},{2,14},{3,15},{4,8},{5,9},{6,10},{7,11},{8,4},{9,5},... | collective-permute-start | bytes 49160 | tf_op jit(solution)/shard_map/ppermute | solution.py:434
  124.0 1.3 collective-permute-start.18
  125.3 3.1 %collective-permute-start.22 = (bf16[4,128,256]{2,1,0:T(8,128)(2,1)S(1)}, bf16[4,128,256]{2,1,0:T(8,128)(2,1)S(1)}, u32[]{:S(2)}, u32[]{:S(2)}) collective-permute-start(bf16[4,128,256]{2,1,0:T(8,128)(2,1)S(1)} %get-tuple-element.77), channel_id=1, source_target_pairs={{0,14},{1,15},{2,12},{3,13},{4,10},{5,11},{6,8},{7,9},{8,6},{9,7},... | collective-permute-start | bytes 786440 | tf_op jit(solution)/shard_map/ppermute | solution.py:434
  128.5 0.2 collective-permute-done.18
  128.7 0.4 collective-permute-done.17
  129.0 0.1 pad_maximum_fusion.2
  129.1 6.3 %collective-permute-start.20 = (bf16[4,4,2,1024]{3,2,1,0:T(2,128)(2,1)S(1)}, bf16[4,4,2,1024]{3,2,1,0:T(2,128)(2,1)S(1)}, u32[]{:S(2)}, u32[]{:S(2)}) collective-permute-start(bf16[4,4,2,1024]{3,2,1,0:T(2,128)(2,1)S(1)} %pad_maximum_fusion.2), channel_id=1, source_target_pairs={{0,2},{1,3},{2,0},{3,1},{4,6},{5,7},{6,4},{7,5},{8,10},{9,11},{10,... | collective-permute-start | bytes 196616 | tf_op jit(solution)/shard_map/ppermute | solution.py:434
  135.5 2.2 %collective-permute-done.20 = bf16[4,4,2,1024]{3,2,1,0:T(2,128)(2,1)S(1)} collective-permute-done((bf16[4,4,2,1024]{3,2,1,0:T(2,128)(2,1)S(1)}, bf16[4,4,2,1024]{3,2,1,0:T(2,128)(2,1)S(1)}, u32[]{:S(2)}, u32[]{:S(2)}) %collective-permute-start.20) | collective-permute-done | bytes 65568 | tf_op jit(solution)/shard_map/ppermute | solution.py:434
  137.8 1.3 collective-permute-done.21
  139.1 0.1 constant_dynamic-update-slice_fusion.8
  139.2 1.1 gather_fusion.2
  140.4 0.2 copy.19
  140.6 5.7 %convolution_convert_fusion.1 = bf16[16,512]{1,0:T(8,128)(2,1)S(1)} fusion(bf16[16,8192]{1,0:T(8,128)(2,1)S(1)} %bitcast.43, bf16[512,8192]{1,0:T(8,128)(2,1)} %param.10), kind=kOutput, calls=%fused_computation.4 | convolution fusion | flops 134225920 | bytes 8667136 | tf_op jit(solution)/shard_map/dot_general | solution.py:717
  146.3 0.6 reshape.304
  147.0 2.5 %place_pages.9 = bf16[64,128,256]{2,1,0:T(8,128)(2,1)} custom-call(s32[64]{0:T(128)} %select_reduce_fusion.3.refs_0_, s32[64]{0:T(128)} %get-tuple-element.41.order_ref.refs_1_, s32[4]{0:T(128)} %gather_fusion, f32[8,256]{1,0:T(8,128)} %get-tuple-element.50.refs_3_, bf16[4,128,256]{2,1,0:T(8,128)(2,1)} %copy-done.11, ...), custom_call_target="tpu_custom_call", output_to_operand_aliasing={{}: (6, {})} | custom-call | tf_op jit(solution)/shard_map/place_pages/pallas_call | solution.py:319
  (86 shorter events, 1.0 us)
Async XLA Ops:
  0.6 15.8 %copy-start.19 = (s32[64]{0:T(128)S(1)}, s32[64]{0:T(128)}, u32[]{:S(2)}) copy-start(s32[64]{0:T(128)} %units_ref.1) | copy-start | bytes 772
  0.6 14.7 %copy-start = (s32[8]{0:T(128)S(1)}, s32[8]{0:T(128)}, u32[]{:S(2)}) copy-start(s32[8]{0:T(128)} %lengths_ref.1) | copy-start | bytes 100
  0.7 14.8 %copy-start.16 = (bf16[8,2,8192]{2,1,0:T(2,128)(2,1)S(1)}, bf16[8,2,8192]{2,1,0:T(2,128)(2,1)}, u32[]{:S(2)}) copy-start(bf16[8,2,8192]{2,1,0:T(2,128)(2,1)} %param.8) | copy-start | bytes 786436
  5.5 26.0 %copy-start.18 = (s32[1024]{0:T(1024)S(1)}, s32[1024]{0:T(1024)}, u32[]{:S(2)}) copy-start(s32[1024]{0:T(1024)} %old_ref.1) | copy-start | bytes 12292
  5.5 4.9 %collective-permute-start = (bf16[16,128,256]{2,1,0:T(8,128)(2,1)}, bf16[16,128,256]{2,1,0:T(8,128)(2,1)S(1)}, u32[]{:S(2)}, u32[]{:S(2)}) collective-permute-start(bf16[16,128,256]{2,1,0:T(8,128)(2,1)} %get-tuple-element.42), channel_id=1, source_target_pairs={{0,1},{1,0},{2,3},{3,2},{4,5},{5,4},{6,7},{7,6},{8,9},{9,8},{10,11... | collective-permute-start | bytes 3145736 | tf_op jit(solution)/shard_map/ppermute | solution.py:434
  6.0 29.4 %collective-permute-start.5 = (bf16[4,128,256]{2,1,0:T(8,128)(2,1)}, bf16[4,128,256]{2,1,0:T(8,128)(2,1)S(1)}, u32[]{:S(2)}, u32[]{:S(2)}) collective-permute-start(bf16[4,128,256]{2,1,0:T(8,128)(2,1)} %get-tuple-element.47), channel_id=1, source_target_pairs={{0,8},{1,9},{2,10},{3,11},{4,12},{5,13},{6,14},{7,15},{8,0},{9,1},... | collective-permute-start | bytes 786440 | tf_op jit(solution)/shard_map/ppermute | solution.py:434
  10.4 1.0 copy-start.3
  15.1 4.6 %collective-permute-start.1 = (bf16[16,128,256]{2,1,0:T(8,128)(2,1)}, bf16[16,128,256]{2,1,0:T(8,128)(2,1)S(1)}, u32[]{:S(2)}, u32[]{:S(2)}) collective-permute-start(bf16[16,128,256]{2,1,0:T(8,128)(2,1)} %get-tuple-element.43), channel_id=1, source_target_pairs={{0,1},{1,0},{2,3},{3,2},{4,5},{5,4},{6,7},{7,6},{8,9},{9,8},{10,11... | collective-permute-start | bytes 3145736 | tf_op jit(solution)/shard_map/ppermute | solution.py:434
  16.6 18.9 %collective-permute-start.6 = (bf16[4,128,256]{2,1,0:T(8,128)(2,1)}, bf16[4,128,256]{2,1,0:T(8,128)(2,1)S(1)}, u32[]{:S(2)}, u32[]{:S(2)}) collective-permute-start(bf16[4,128,256]{2,1,0:T(8,128)(2,1)} %get-tuple-element.48), channel_id=1, source_target_pairs={{0,12},{1,13},{2,14},{3,15},{4,8},{5,9},{6,10},{7,11},{8,4},{9,5},... | collective-permute-start | bytes 786440 | tf_op jit(solution)/shard_map/ppermute | solution.py:434
  19.6 23.9 %copy-start.4 = (bf16[16,128,256]{2,1,0:T(8,128)(2,1)}, bf16[16,128,256]{2,1,0:T(8,128)(2,1)S(1)}, u32[]{:S(2)}) copy-start(bf16[16,128,256]{2,1,0:T(8,128)(2,1)S(1)} %collective-permute-done.1.passed_ref.rest_1_) | copy-start | bytes 3145732
  26.8 36.7 %copy-start.1 = (s32[8]{0:T(128)S(1)}, s32[8]{0:T(128)}, u32[]{:S(2)}) copy-start(s32[8]{0:T(128)} %lengths_ref.1) | copy-start | bytes 100
  26.8 6.2 %collective-permute-start.4 = (bf16[1,16,640]{2,1,0:T(8,128)(2,1)S(1)}, bf16[1,16,640]{2,1,0:T(8,128)(2,1)S(1)}, u32[]{:S(2)}, u32[]{:S(2)}) collective-permute-start(bf16[1,16,640]{2,1,0:T(8,128)(2,1)S(1)} %bitcast.47), channel_id=1, source_target_pairs={{0,12},{1,13},{2,14},{3,15},{4,8},{5,9},{6,10},{7,11},{8,4},{9,5},... | collective-permute-start | bytes 61448 | tf_op jit(solution)/shard_map/ppermute | solution.py:434
  28.2 7.2 %collective-permute-start.3 = (bf16[1,16,640]{2,1,0:T(8,128)(2,1)S(1)}, bf16[1,16,640]{2,1,0:T(8,128)(2,1)S(1)}, u32[]{:S(2)}, u32[]{:S(2)}) collective-permute-start(bf16[1,16,640]{2,1,0:T(8,128)(2,1)S(1)} %bitcast.48), channel_id=1, source_target_pairs={{0,8},{1,9},{2,10},{3,11},{4,12},{5,13},{6,14},{7,15},{8,0},{9,1},... | collective-permute-start | bytes 61448 | tf_op jit(solution)/shard_map/ppermute | solution.py:434
  28.2 7.2 %collective-permute-start.2 = (bf16[1,16,640]{2,1,0:T(8,128)(2,1)S(1)}, bf16[1,16,640]{2,1,0:T(8,128)(2,1)S(1)}, u32[]{:S(2)}, u32[]{:S(2)}) collective-permute-start(bf16[1,16,640]{2,1,0:T(8,128)(2,1)S(1)} %bitcast.49), channel_id=1, source_target_pairs={{0,4},{1,5},{2,6},{3,7},{4,0},{5,1},{6,2},{7,3},{8,12},{9,13},{10,... | collective-permute-start | bytes 61448 | tf_op jit(solution)/shard_map/ppermute | solution.py:434
  31.3 15.5 %copy-start.20 = (s32[4]{0:T(128)}, s32[4]{0:T(128)S(1)}, u32[]{:S(2)}) copy-start(s32[4]{0:T(128)S(1)} %get-tuple-element.81.units_ref) | copy-start | bytes 52
  35.4 29.3 %copy-start.10 = (bf16[4,128,256]{2,1,0:T(8,128)(2,1)}, bf16[4,128,256]{2,1,0:T(8,128)(2,1)S(1)}, u32[]{:S(2)}) copy-start(bf16[4,128,256]{2,1,0:T(8,128)(2,1)S(1)} %collective-permute-done.5.refs_7_) | copy-start | bytes 786436
  35.5 29.3 %copy-start.12 = (bf16[4,128,256]{2,1,0:T(8,128)(2,1)}, bf16[4,128,256]{2,1,0:T(8,128)(2,1)S(1)}, u32[]{:S(2)}) copy-start(bf16[4,128,256]{2,1,0:T(8,128)(2,1)S(1)} %collective-permute-done.6.refs_8_) | copy-start | bytes 786436
  35.5 5.9 %collective-permute-start.7 = (bf16[4,16,640]{2,1,0:T(8,128)(2,1)S(1)}, bf16[4,16,640]{2,1,0:T(8,128)(2,1)S(1)}, u32[]{:S(2)}, u32[]{:S(2)}) collective-permute-start(bf16[4,16,640]{2,1,0:T(8,128)(2,1)S(1)} %pad_maximum_fusion.1), channel_id=1, source_target_pairs={{0,2},{1,3},{2,0},{3,1},{4,6},{5,7},{6,4},{7,5},{8,10},{9,11},{10,... | collective-permute-start | bytes 245768 | tf_op jit(solution)/shard_map/ppermute | solution.py:434
  37.9 21.4 %collective-permute-start.9 = (bf16[4,128,256]{2,1,0:T(8,128)(2,1)}, bf16[4,128,256]{2,1,0:T(8,128)(2,1)S(1)}, u32[]{:S(2)}, u32[]{:S(2)}) collective-permute-start(bf16[4,128,256]{2,1,0:T(8,128)(2,1)} %get-tuple-element.54), channel_id=1, source_target_pairs={{0,8},{1,9},{2,10},{3,11},{4,12},{5,13},{6,14},{7,15},{8,0},{9,1},... | collective-permute-start | bytes 786440 | tf_op jit(solution)/shard_map/ppermute | solution.py:434
  40.1 20.9 %collective-permute-start.10 = (bf16[4,128,256]{2,1,0:T(8,128)(2,1)}, bf16[4,128,256]{2,1,0:T(8,128)(2,1)S(1)}, u32[]{:S(2)}, u32[]{:S(2)}) collective-permute-start(bf16[4,128,256]{2,1,0:T(8,128)(2,1)} %get-tuple-element.55), channel_id=1, source_target_pairs={{0,12},{1,13},{2,14},{3,15},{4,8},{5,9},{6,10},{7,11},{8,4},{9,5},... | collective-permute-start | bytes 786440 | tf_op jit(solution)/shard_map/ppermute | solution.py:434
  41.4 2.1 %collective-permute-start.8 = (bf16[8,16,640]{2,1,0:T(8,128)(2,1)S(1)}, bf16[8,16,640]{2,1,0:T(8,128)(2,1)S(1)}, u32[]{:S(2)}, u32[]{:S(2)}) collective-permute-start(bf16[8,16,640]{2,1,0:T(8,128)(2,1)S(1)} %pad_maximum_fusion), channel_id=1, source_target_pairs={{0,1},{1,0},{2,3},{3,2},{4,5},{5,4},{6,7},{7,6},{8,9},{9,8},{10,11... | collective-permute-start | bytes 491528 | tf_op jit(solution)/shard_map/ppermute | solution.py:434
  41.5 64.5 %collective-permute-start.12 = (bf16[8,128,256]{2,1,0:T(8,128)(2,1)}, bf16[8,128,256]{2,1,0:T(8,128)(2,1)S(1)}, u32[]{:S(2)}, u32[]{:S(2)}) collective-permute-start(bf16[8,128,256]{2,1,0:T(8,128)(2,1)} %get-tuple-element.64), channel_id=1, source_target_pairs={{0,4},{1,5},{2,6},{3,7},{4,0},{5,1},{6,2},{7,3},{8,12},{9,13},{10,... | collective-permute-start | bytes 1572872 | tf_op jit(solution)/shard_map/ppermute | solution.py:434
  42.1 63.9 %collective-permute-start.13 = (bf16[8,128,256]{2,1,0:T(8,128)(2,1)}, bf16[8,128,256]{2,1,0:T(8,128)(2,1)S(1)}, u32[]{:S(2)}, u32[]{:S(2)}) collective-permute-start(bf16[8,128,256]{2,1,0:T(8,128)(2,1)} %get-tuple-element.66), channel_id=1, source_target_pairs={{0,6},{1,7},{2,4},{3,5},{4,2},{5,3},{6,0},{7,1},{8,14},{9,15},{10,... | collective-permute-start | bytes 1572872 | tf_op jit(solution)/shard_map/ppermute | solution.py:434
  43.6 3.2 %copy-start.9 = (bf16[16,16,640]{2,1,0:T(8,128)(2,1)}, bf16[16,16,640]{2,1,0:T(8,128)(2,1)S(1)}, u32[]{:S(2)}) copy-start(bf16[16,16,640]{2,1,0:T(8,128)(2,1)S(1)} %constant_dynamic-update-slice_fusion.rows_ref) | copy-start | bytes 983044
  43.6 48.1 %copy-start.2 = (s32[16]{0:T(128)S(1)}, s32[16]{0:T(128)}, u32[]{:S(2)}) copy-start(s32[16]{0:T(128)} %constant.99.clone.turn_ref) | copy-start | bytes 196
  59.3 40.0 %copy-start.13 = (bf16[4,128,256]{2,1,0:T(8,128)(2,1)}, bf16[4,128,256]{2,1,0:T(8,128)(2,1)S(1)}, u32[]{:S(2)}) copy-start(bf16[4,128,256]{2,1,0:T(8,128)(2,1)S(1)} %collective-permute-done.9.refs_7_) | copy-start | bytes 786436
  59.3 53.6 %collective-permute-start.15 = (bf16[8,128,256]{2,1,0:T(8,128)(2,1)}, bf16[8,128,256]{2,1,0:T(8,128)(2,1)S(1)}, u32[]{:S(2)}, u32[]{:S(2)}) collective-permute-start(bf16[8,128,256]{2,1,0:T(8,128)(2,1)} %get-tuple-element.71), channel_id=1, source_target_pairs={{0,10},{1,11},{2,8},{3,9},{4,14},{5,15},{6,12},{7,13},{8,2},{9,3},... | collective-permute-start | bytes 1572872 | tf_op jit(solution)/shard_map/ppermute | solution.py:434
  59.3 40.0 %collective-permute-start.11 = (bf16[8,128,256]{2,1,0:T(8,128)(2,1)}, bf16[8,128,256]{2,1,0:T(8,128)(2,1)S(1)}, u32[]{:S(2)}, u32[]{:S(2)}) collective-permute-start(bf16[8,128,256]{2,1,0:T(8,128)(2,1)} %get-tuple-element.59), channel_id=1, source_target_pairs={{0,2},{1,3},{2,0},{3,1},{4,6},{5,7},{6,4},{7,5},{8,10},{9,11},{10,... | collective-permute-start | bytes 1572872 | tf_op jit(solution)/shard_map/ppermute | solution.py:434
  61.0 38.3 %copy-start.14 = (bf16[4,128,256]{2,1,0:T(8,128)(2,1)}, bf16[4,128,256]{2,1,0:T(8,128)(2,1)S(1)}, u32[]{:S(2)}) copy-start(bf16[4,128,256]{2,1,0:T(8,128)(2,1)S(1)} %collective-permute-done.10.refs_8_) | copy-start | bytes 786436
  61.0 27.8 %collective-permute-start.14 = (bf16[144,128]{1,0:T(8,128)(2,1)}, bf16[144,128]{1,0:T(8,128)(2,1)S(1)}, u32[]{:S(2)}, u32[]{:S(2)}) collective-permute-start(bf16[144,128]{1,0:T(8,128)(2,1)} %get-tuple-element.58), channel_id=1, source_target_pairs={{0,14},{1,15},{2,12},{3,13},{4,10},{5,11},{6,8},{7,9},{8,6},{9,7},... | collective-permute-start | bytes 110600 | tf_op jit(solution)/shard_map/ppermute | solution.py:434
  88.8 24.1 %copy-start.17 = (bf16[144,128]{1,0:T(8,128)(2,1)}, bf16[144,128]{1,0:T(8,128)(2,1)S(1)}, u32[]{:S(2)}) copy-start(bf16[144,128]{1,0:T(8,128)(2,1)S(1)} %collective-permute-done.14.refs_7_) | copy-start | bytes 110596
  88.8 29.3 %collective-permute-start.16 = (bf16[4,128,256]{2,1,0:T(8,128)(2,1)}, bf16[4,128,256]{2,1,0:T(8,128)(2,1)S(1)}, u32[]{:S(2)}, u32[]{:S(2)}) collective-permute-start(bf16[4,128,256]{2,1,0:T(8,128)(2,1)} %get-tuple-element.75), channel_id=1, source_target_pairs={{0,14},{1,15},{2,12},{3,13},{4,10},{5,11},{6,8},{7,9},{8,6},{9,7},... | collective-permute-start | bytes 786440 | tf_op jit(solution)/shard_map/ppermute | solution.py:434
  99.3 0.8 copy-start.8
  105.9 0.8 copy-start.5
  106.0 0.9 copy-start.6
  112.9 0.8 copy-start.7
  118.1 28.9 %copy-start.11 = (bf16[4,128,256]{2,1,0:T(8,128)(2,1)}, bf16[4,128,256]{2,1,0:T(8,128)(2,1)S(1)}, u32[]{:S(2)}) copy-start(bf16[4,128,256]{2,1,0:T(8,128)(2,1)S(1)} %collective-permute-done.16.refs_4_) | copy-start | bytes 786436
  118.9 9.6 %collective-permute-start.19 = (bf16[1,4,2,1024]{3,2,1,0:T(2,128)(2,1)S(1)}, bf16[1,4,2,1024]{3,2,1,0:T(2,128)(2,1)S(1)}, u32[]{:S(2)}, u32[]{:S(2)}) collective-permute-start(bf16[1,4,2,1024]{3,2,1,0:T(2,128)(2,1)S(1)} %broadcast_in_dim_reshape.4), channel_id=1, source_target_pairs={{0,12},{1,13},{2,14},{3,15},{4,8},{5,9},{6,10},{7,11},{8,4},{9,5},... | collective-permute-start | bytes 49160 | tf_op jit(solution)/shard_map/ppermute | solution.py:434
  124.0 4.6 %collective-permute-start.18 = (bf16[1,4,2,1024]{3,2,1,0:T(2,128)(2,1)S(1)}, bf16[1,4,2,1024]{3,2,1,0:T(2,128)(2,1)S(1)}, u32[]{:S(2)}, u32[]{:S(2)}) collective-permute-start(bf16[1,4,2,1024]{3,2,1,0:T(2,128)(2,1)S(1)} %broadcast_in_dim_reshape.4), channel_id=1, source_target_pairs={{0,8},{1,9},{2,10},{3,11},{4,12},{5,13},{6,14},{7,15},{8,0},{9,1},... | collective-permute-start | bytes 49160 | tf_op jit(solution)/shard_map/ppermute | solution.py:434
  125.3 3.7 %collective-permute-start.17 = (bf16[1,4,2,1024]{3,2,1,0:T(2,128)(2,1)S(1)}, bf16[1,4,2,1024]{3,2,1,0:T(2,128)(2,1)S(1)}, u32[]{:S(2)}, u32[]{:S(2)}) collective-permute-start(bf16[1,4,2,1024]{3,2,1,0:T(2,128)(2,1)S(1)} %broadcast_in_dim_reshape.4), channel_id=1, source_target_pairs={{0,4},{1,5},{2,6},{3,7},{4,0},{5,1},{6,2},{7,3},{8,12},{9,13},{10,... | collective-permute-start | bytes 49160 | tf_op jit(solution)/shard_map/ppermute | solution.py:434
  125.3 15.3 %collective-permute-start.22 = (bf16[4,128,256]{2,1,0:T(8,128)(2,1)S(1)}, bf16[4,128,256]{2,1,0:T(8,128)(2,1)S(1)}, u32[]{:S(2)}, u32[]{:S(2)}) collective-permute-start(bf16[4,128,256]{2,1,0:T(8,128)(2,1)S(1)} %get-tuple-element.77), channel_id=1, source_target_pairs={{0,14},{1,15},{2,12},{3,13},{4,10},{5,11},{6,8},{7,9},{8,6},{9,7},... | collective-permute-start | bytes 786440 | tf_op jit(solution)/shard_map/ppermute | solution.py:434
  129.1 8.5 %collective-permute-start.20 = (bf16[4,4,2,1024]{3,2,1,0:T(2,128)(2,1)S(1)}, bf16[4,4,2,1024]{3,2,1,0:T(2,128)(2,1)S(1)}, u32[]{:S(2)}, u32[]{:S(2)}) collective-permute-start(bf16[4,4,2,1024]{3,2,1,0:T(2,128)(2,1)S(1)} %pad_maximum_fusion.2), channel_id=1, source_target_pairs={{0,2},{1,3},{2,0},{3,1},{4,6},{5,7},{6,4},{7,5},{8,10},{9,11},{10,... | collective-permute-start | bytes 196616 | tf_op jit(solution)/shard_map/ppermute | solution.py:434
  137.7 1.4 collective-permute-start.21
  140.6 6.4 %copy-start.15 = (bf16[4,128,256]{2,1,0:T(8,128)(2,1)}, bf16[4,128,256]{2,1,0:T(8,128)(2,1)S(1)}, u32[]{:S(2)}) copy-start(bf16[4,128,256]{2,1,0:T(8,128)(2,1)S(1)} %collective-permute-done.22.refs_5_) | copy-start | bytes 786436

commit v10 on v7

--- a/solution.py
+++ b/solution.py
@@ -476,7 +476,7 @@
     if pairwise:
         half, quarter = devices // 2, devices // 4
         a, b = half, half + quarter
-        c, d = a + 2, b + 2
+        c, d, b = a + 2, b, b + 2
         near = list(range(2, half, 2))
         (chunk_a, cross_near), order = first_pack(
             new_units,
@@ -709,6 +709,8 @@
         .transpose(0, 2, 1, 3)
         .reshape(requests * 2, HEADS * HD)
     )
+    if pairwise:
+        logical = after(logical, moved_d2)
     mixed_rows = lax.dot_general(
         logical, out_weight, (((1,), (1,)), ((), ())), preferred_element_type=jnp.float32
     )

time: 138 us -> 145 us (1.051)
  the two profiles are of different devices: /device:TPU:8 before, /device:TPU:0 now
where the time goes in v10:
time: 145 us; the launch traced here: 143 us
  starting transfers between devices  43.8 us (30%)
  Pallas kernels  41.1 us (28%)
  waiting for transfers between devices  26.5 us (18%)
  matrix products  12.9 us (9%)
  local copies, waits for them, and re-layouts  11 us (8%)
  other arithmetic  6.23 us (4%)
    ppermute x23, starting transfers between devices, swap(): return lax.ppermute(values, 'tp', [(i, i ^ key) for i in range(devices)])  43.8 us
    ppermute x23, waiting for transfers between devices, swap(): return lax.ppermute(values, 'tp', [(i, i ^ key) for i in range(devices)])  26.5 us
    pallas_call x5, Pallas kernels, place_pages(): pl.pallas_call(functools.partial(place_kernel, entries, started, attends,...  24.9 us
    dot_general x1, matrix products, body(): lax.dot_general(flat_rows, qkv_weight, (((1,), (1,)), ((), ())), preferre...  7.16 us
    pallas_call x2, Pallas kernels, next_pack(): pl.pallas_call(functools.partial(next_pack_kernel, capacity, outs_pages,...  6.61 us
    dot_general x1, matrix products, body(): lax.dot_general(logical, out_weight, (((1,), (1,)), ((), ())), preferred_...  5.74 us
    pallas_call x1, Pallas kernels, first_pack(): pl.pallas_call(functools.partial(first_pack_kernel, devices, capacity, ou...  4.82 us
    pallas_call x1, Pallas kernels, rows_and_parts(): pl.pallas_call(functools.partial(rows_kernel, late), out_shape=(jax.Shape...  4.73 us
  transfers between devices with their start and end apart: 23, of which 8 were waited for; matrix products, arithmetic and copies ran while one was open for 14% of the time, Pallas kernels for 24%

profile of v10, /device:TPU:0, one launch (start us, length us, event | category | flops | bytes accessed | tf_op | source)
XLA Modules:
  0.0 142.8 jit_solution(779799514298736752)
XLA Ops:
  0.6 4.8 %first_pack.1 = (bf16[4,128,256]{2,1,0:T(8,128)(2,1)}, bf16[16,128,256]{2,1,0:T(8,128)(2,1)}, s32[64]{0:T(128)}) custom-call(s32[64]{0:T(128)} %units_ref.1, s32[1024]{0:T(1024)} %old_ref.1, bf16[64,128,256]{2,1,0:T(8,128)(2,1)} %rest_0_.3), custom_call_target="tpu_custom_call" | custom-call | tf_op jit(solution)/shard_map/first_pack/pallas_call | solution.py:142
  5.5 4.1 %collective-permute-start.5 = (bf16[4,128,256]{2,1,0:T(8,128)(2,1)}, bf16[4,128,256]{2,1,0:T(8,128)(2,1)S(1)}, u32[]{:S(2)}, u32[]{:S(2)}) collective-permute-start(bf16[4,128,256]{2,1,0:T(8,128)(2,1)} %get-tuple-element.40), channel_id=1, source_target_pairs={{0,8},{1,9},{2,10},{3,11},{4,12},{5,13},{6,14},{7,15},{8,0},{9,1},... | collective-permute-start | bytes 786440 | tf_op jit(solution)/shard_map/ppermute | solution.py:434
  9.6 0.8 reshape.298
  10.3 0.7 compare_select_fusion.2
  11.3 0.8 select_reduce_fusion.2
  12.0 0.8 select_reduce_fusion.1
  12.9 0.9 select_reduce_fusion
  13.8 0.7 add_convert_fusion
  14.5 1.0 copy-done.2
  15.5 3.6 %next_pack.2 = (bf16[8,128,256]{2,1,0:T(8,128)(2,1)}, bf16[8,128,256]{2,1,0:T(8,128)(2,1)}, bf16[4,128,256]{2,1,0:T(8,128)(2,1)}, bf16[16,128,256]{2,1,0:T(8,128)(2,1)}) custom-call(s32[64]{0:T(128)} %get-tuple-element.36.order_ref.refs_1_, bf16[64,128,256]{2,1,0:T(8,128)(2,1)} %rest_0_.3, bf16[16,128,256]{2,1,0:T(8,128)(2,1)} %copy-done.2), custom_call_target="tpu_custom_call" | custom-call | tf_op jit(solution)/shard_map/next_pack/pallas_call | solution.py:160
  19.1 0.6 collective-permute-start.1
  19.9 0.2 convert_reduce_fusion.1
  20.1 0.1 fusion.1
  20.3 2.4 %collective-permute-start.6 = (bf16[4,128,256]{2,1,0:T(8,128)(2,1)}, bf16[4,128,256]{2,1,0:T(8,128)(2,1)S(1)}, u32[]{:S(2)}, u32[]{:S(2)}) collective-permute-start(bf16[4,128,256]{2,1,0:T(8,128)(2,1)} %get-tuple-element.41), channel_id=1, source_target_pairs={{0,14},{1,15},{2,12},{3,13},{4,10},{5,11},{6,8},{7,9},{8,6},{9,7},... | collective-permute-start | bytes 786440 | tf_op jit(solution)/shard_map/ppermute | solution.py:434
  22.6 7.2 %convolution_convert_fusion = bf16[16,640]{1,0:T(8,128)(2,1)S(1)} fusion(bf16[16,8192]{1,0:T(8,128)(2,1)S(1)} %reshape.300, bf16[640,8192]{1,0:T(8,128)(2,1)} %param.9), kind=kOutput, calls=%fused_computation.3 | convolution fusion | flops 167782400 | bytes 10768384 | tf_op jit(solution)/shard_map/dot_general | solution.py:572
  29.8 2.5 %collective-permute-start.4 = (bf16[1,16,640]{2,1,0:T(8,128)(2,1)S(1)}, bf16[1,16,640]{2,1,0:T(8,128)(2,1)S(1)}, u32[]{:S(2)}, u32[]{:S(2)}) collective-permute-start(bf16[1,16,640]{2,1,0:T(8,128)(2,1)S(1)} %bitcast.47), channel_id=1, source_target_pairs={{0,12},{1,13},{2,14},{3,15},{4,8},{5,9},{6,10},{7,11},{8,4},{9,5},... | collective-permute-start | bytes 61448 | tf_op jit(solution)/shard_map/ppermute | solution.py:434
  32.3 0.1 collective-permute-start.3
  32.4 1.8 %collective-permute-start.2 = (bf16[1,16,640]{2,1,0:T(8,128)(2,1)S(1)}, bf16[1,16,640]{2,1,0:T(8,128)(2,1)S(1)}, u32[]{:S(2)}, u32[]{:S(2)}) collective-permute-start(bf16[1,16,640]{2,1,0:T(8,128)(2,1)S(1)} %bitcast.49), channel_id=1, source_target_pairs={{0,4},{1,5},{2,6},{3,7},{4,0},{5,1},{6,2},{7,3},{8,12},{9,13},{10,... | collective-permute-start | bytes 61448 | tf_op jit(solution)/shard_map/ppermute | solution.py:434
  34.2 0.7 pad_maximum_fusion.3
  34.9 0.6 collective-permute-done.4
  35.5 3.0 %collective-permute-start.9 = (bf16[8,128,256]{2,1,0:T(8,128)(2,1)}, bf16[8,128,256]{2,1,0:T(8,128)(2,1)S(1)}, u32[]{:S(2)}, u32[]{:S(2)}) collective-permute-start(bf16[8,128,256]{2,1,0:T(8,128)(2,1)} %get-tuple-element.47), channel_id=1, source_target_pairs={{0,4},{1,5},{2,6},{3,7},{4,0},{5,1},{6,2},{7,3},{8,12},{9,13},{10,... | collective-permute-start | bytes 1572872 | tf_op jit(solution)/shard_map/ppermute | solution.py:434
  38.5 1.5 %collective-permute-start.7 = (bf16[4,16,640]{2,1,0:T(8,128)(2,1)S(1)}, bf16[4,16,640]{2,1,0:T(8,128)(2,1)S(1)}, u32[]{:S(2)}, u32[]{:S(2)}) collective-permute-start(bf16[4,16,640]{2,1,0:T(8,128)(2,1)S(1)} %pad_maximum_fusion.1), channel_id=1, source_target_pairs={{0,2},{1,3},{2,0},{3,1},{4,6},{5,7},{6,4},{7,5},{8,10},{9,11},{10,... | collective-permute-start | bytes 245768 | tf_op jit(solution)/shard_map/ppermute | solution.py:434
  40.1 0.9 fusion.5
  41.0 1.0 collective-permute-start.11
  42.0 1.1 collective-permute-done.7
  43.2 1.3 collective-permute-done.8
  44.6 3.0 %next_pack.3 = (bf16[8,128,256]{2,1,0:T(8,128)(2,1)}, bf16[4,128,256]{2,1,0:T(8,128)(2,1)}, bf16[8,128,256]{2,1,0:T(8,128)(2,1)}) custom-call(s32[64]{0:T(128)} %get-tuple-element.36.order_ref.refs_1_, bf16[64,128,256]{2,1,0:T(8,128)(2,1)} %rest_0_.3, bf16[16,128,256]{2,1,0:T(8,128)(2,1)} %copy-done.3, bf16[16,128,256]{2,1,0:T(8,128)(2,1)} %copy-done.2), custom_call_target="tpu_custom_call" | custom-call | tf_op jit(solution)/shard_map/next_pack/pallas_call | solution.py:160
  47.6 1.5 %collective-permute-start.13 = (bf16[8,128,256]{2,1,0:T(8,128)(2,1)}, bf16[8,128,256]{2,1,0:T(8,128)(2,1)S(1)}, u32[]{:S(2)}, u32[]{:S(2)}) collective-permute-start(bf16[8,128,256]{2,1,0:T(8,128)(2,1)} %get-tuple-element.55), channel_id=1, source_target_pairs={{0,2},{1,3},{2,0},{3,1},{4,6},{5,7},{6,4},{7,5},{8,10},{9,11},{10,... | collective-permute-start | bytes 1572872 | tf_op jit(solution)/shard_map/ppermute | solution.py:434
  49.1 0.1 convert_reduce_fusion
  49.2 2.4 %collective-permute-start.12 = (bf16[4,128,256]{2,1,0:T(8,128)(2,1)}, bf16[4,128,256]{2,1,0:T(8,128)(2,1)S(1)}, u32[]{:S(2)}, u32[]{:S(2)}) collective-permute-start(bf16[4,128,256]{2,1,0:T(8,128)(2,1)} %get-tuple-element.53), channel_id=1, source_target_pairs={{0,14},{1,15},{2,12},{3,13},{4,10},{5,11},{6,8},{7,9},{8,6},{9,7},... | collective-permute-start | bytes 786440 | tf_op jit(solution)/shard_map/ppermute | solution.py:434
  51.6 0.1 select_reduce_fusion.4
  51.8 0.6 reshape.299.ids_ref
  52.4 4.7 %rows_and_parts.1 = (f32[4,16,128]{2,1,0:T(8,128)}, f32[8,256]{1,0:T(8,128)}, bf16[144,128]{1,0:T(8,128)(2,1)}) custom-call(s32[4]{0:T(128)} %copy-done.18, s32[16]{0:T(128)} %constant.99.clone.turn_ref, s32[64]{0:T(128)} %get-tuple-element.36.order_ref.refs_1_, s32[8]{0:T(128)} %reshape.299.ids_ref, s32[8]{0:T(128)} %lengths_ref.1, ...), custom_call_target="tpu_custom_call" | custom-call | tf_op jit(solution)/shard_map/rows_and_parts/pallas_call | solution.py:415
  57.1 16.6 %collective-permute-done.11.refs_7_ = bf16[4,128,256]{2,1,0:T(8,128)(2,1)S(1)} collective-permute-done((bf16[4,128,256]{2,1,0:T(8,128)(2,1)}, bf16[4,128,256]{2,1,0:T(8,128)(2,1)S(1)}, u32[]{:S(2)}, u32[]{:S(2)}) %collective-permute-start.11) | collective-permute-done | bytes 262176 | tf_op jit(solution)/shard_map/ppermute | solution.py:434
  73.7 2.5 %collective-permute-start.15 = (bf16[8,128,256]{2,1,0:T(8,128)(2,1)}, bf16[8,128,256]{2,1,0:T(8,128)(2,1)S(1)}, u32[]{:S(2)}, u32[]{:S(2)}) collective-permute-start(bf16[8,128,256]{2,1,0:T(8,128)(2,1)} %get-tuple-element.61), channel_id=1, source_target_pairs={{0,10},{1,11},{2,8},{3,9},{4,14},{5,15},{6,12},{7,13},{8,2},{9,3},... | collective-permute-start | bytes 1572872 | tf_op jit(solution)/shard_map/ppermute | solution.py:434
  76.3 0.7 select_reduce_fusion.3.refs_0_
  76.9 1.1 collective-permute-start.14
  78.1 1.2 gather_fusion
  79.3 6.0 %place_pages.5 = (bf16[64,128,256]{2,1,0:T(8,128)(2,1)}, f32[4,16,128]{2,1,0:T(8,128)}, f32[4,16,128]{2,1,0:T(8,128)}) custom-call(s32[64]{0:T(128)} %select_reduce_fusion.3.refs_0_, s32[64]{0:T(128)} %get-tuple-element.36.order_ref.refs_1_, s32[4]{0:T(128)} %gather_fusion, f32[8,256]{1,0:T(8,128)} %get-tuple-element.43.refs_3_, ...), custom_call_target="tpu_custom_call" | custom-call | tf_op jit(solution)/shard_map/place_pages/pallas_call | solution.py:319
  85.3 0.8 copy-done.5
  86.1 6.0 %place_pages.6 = (bf16[64,128,256]{2,1,0:T(8,128)(2,1)}, f32[4,16,128]{2,1,0:T(8,128)}, f32[4,16,128]{2,1,0:T(8,128)}) custom-call(s32[64]{0:T(128)} %select_reduce_fusion.3.refs_0_, s32[64]{0:T(128)} %get-tuple-element.36.order_ref.refs_1_, s32[4]{0:T(128)} %gather_fusion, f32[8,256]{1,0:T(8,128)} %get-tuple-element.43.refs_3_, ...), custom_call_target="tpu_custom_call", output_to_operand_aliasing={{0}: (9, {})} | custom-call | tf_op jit(solution)/shard_map/place_pages/pallas_call | solution.py:319
  92.2 0.7 copy-done.14
  92.8 0.2 copy-done.6
  93.0 6.0 %place_pages.7 = (bf16[64,128,256]{2,1,0:T(8,128)(2,1)}, f32[4,16,128]{2,1,0:T(8,128)}, f32[4,16,128]{2,1,0:T(8,128)}) custom-call(s32[64]{0:T(128)} %select_reduce_fusion.3.refs_0_, s32[64]{0:T(128)} %get-tuple-element.36.order_ref.refs_1_, s32[4]{0:T(128)} %gather_fusion, f32[8,256]{1,0:T(8,128)} %get-tuple-element.43.refs_3_, ...), custom_call_target="tpu_custom_call", output_to_operand_aliasing={{0}: (10, {})} | custom-call | tf_op jit(solution)/shard_map/place_pages/pallas_call | solution.py:319
  99.0 2.6 %collective-permute-start.16 = (bf16[4,128,256]{2,1,0:T(8,128)(2,1)S(1)}, bf16[4,128,256]{2,1,0:T(8,128)(2,1)S(1)}, u32[]{:S(2)}, u32[]{:S(2)}) collective-permute-start(bf16[4,128,256]{2,1,0:T(8,128)(2,1)S(1)} %copy-done.19), channel_id=1, source_target_pairs={{0,12},{1,13},{2,14},{3,15},{4,8},{5,9},{6,10},{7,11},{8,4},{9,5},... | collective-permute-start | bytes 786440 | tf_op jit(solution)/shard_map/ppermute | solution.py:434
  101.7 0.8 gather_fusion.1
  102.5 1.5 %collective-permute-done.15.refs_8_ = bf16[8,128,256]{2,1,0:T(8,128)(2,1)S(1)} collective-permute-done((bf16[8,128,256]{2,1,0:T(8,128)(2,1)}, bf16[8,128,256]{2,1,0:T(8,128)(2,1)S(1)}, u32[]{:S(2)}, u32[]{:S(2)}) %collective-permute-start.15) | collective-permute-done | bytes 524320 | tf_op jit(solution)/shard_map/ppermute | solution.py:434
  104.0 0.8 copy-done.7
  104.8 4.4 %place_pages.8 = (bf16[64,128,256]{2,1,0:T(8,128)(2,1)}, f32[4,16,128]{2,1,0:T(8,128)}, f32[4,16,128]{2,1,0:T(8,128)}, bf16[4,16,128]{2,1,0:T(8,128)(2,1)}) custom-call(s32[64]{0:T(128)} %select_reduce_fusion.3.refs_0_, s32[64]{0:T(128)} %get-tuple-element.36.order_ref.refs_1_, s32[4]{0:T(128)} %gather_fusion, ...), custom_call_target="tpu_custom_call", output_to_operand_aliasing={{0}: (9, {})} | custom-call | tf_op jit(solution)/shard_map/place_pages/pallas_call | solution.py:319
  109.2 0.8 broadcast_in_dim_reshape.4
  110.0 2.8 %collective-permute-start.19 = (bf16[1,4,2,1024]{3,2,1,0:T(2,128)(2,1)S(1)}, bf16[1,4,2,1024]{3,2,1,0:T(2,128)(2,1)S(1)}, u32[]{:S(2)}, u32[]{:S(2)}) collective-permute-start(bf16[1,4,2,1024]{3,2,1,0:T(2,128)(2,1)S(1)} %broadcast_in_dim_reshape.4), channel_id=1, source_target_pairs={{0,12},{1,13},{2,14},{3,15},{4,8},{5,9},{6,10},{7,11},{8,4},{9,5},... | collective-permute-start | bytes 49160 | tf_op jit(solution)/shard_map/ppermute | solution.py:434
  112.8 7.0 %collective-permute-start.18 = (bf16[1,4,2,1024]{3,2,1,0:T(2,128)(2,1)S(1)}, bf16[1,4,2,1024]{3,2,1,0:T(2,128)(2,1)S(1)}, u32[]{:S(2)}, u32[]{:S(2)}) collective-permute-start(bf16[1,4,2,1024]{3,2,1,0:T(2,128)(2,1)S(1)} %broadcast_in_dim_reshape.4), channel_id=1, source_target_pairs={{0,8},{1,9},{2,10},{3,11},{4,12},{5,13},{6,14},{7,15},{8,0},{9,1},... | collective-permute-start | bytes 49160 | tf_op jit(solution)/shard_map/ppermute | solution.py:434
  119.8 0.3 collective-permute-start.17
  120.1 2.4 %collective-permute-start.22 = (bf16[4,128,256]{2,1,0:T(8,128)(2,1)S(1)}, bf16[4,128,256]{2,1,0:T(8,128)(2,1)S(1)}, u32[]{:S(2)}, u32[]{:S(2)}) collective-permute-start(bf16[4,128,256]{2,1,0:T(8,128)(2,1)S(1)} %copy-done.16), channel_id=1, source_target_pairs={{0,12},{1,13},{2,14},{3,15},{4,8},{5,9},{6,10},{7,11},{8,4},{9,5},... | collective-permute-start | bytes 786440 | tf_op jit(solution)/shard_map/ppermute | solution.py:434
  122.6 1.8 %collective-permute-done.17 = bf16[1,4,2,1024]{3,2,1,0:T(2,128)(2,1)S(1)} collective-permute-done((bf16[1,4,2,1024]{3,2,1,0:T(2,128)(2,1)S(1)}, bf16[1,4,2,1024]{3,2,1,0:T(2,128)(2,1)S(1)}, u32[]{:S(2)}, u32[]{:S(2)}) %collective-permute-start.17) | collective-permute-done | bytes 16416 | tf_op jit(solution)/shard_map/ppermute | solution.py:434
  124.4 0.1 pad_maximum_fusion.2
  124.5 4.0 %collective-permute-start.20 = (bf16[4,4,2,1024]{3,2,1,0:T(2,128)(2,1)S(1)}, bf16[4,4,2,1024]{3,2,1,0:T(2,128)(2,1)S(1)}, u32[]{:S(2)}, u32[]{:S(2)}) collective-permute-start(bf16[4,4,2,1024]{3,2,1,0:T(2,128)(2,1)S(1)} %pad_maximum_fusion.2), channel_id=1, source_target_pairs={{0,2},{1,3},{2,0},{3,1},{4,6},{5,7},{6,4},{7,5},{8,10},{9,11},{10,... | collective-permute-start | bytes 196616 | tf_op jit(solution)/shard_map/ppermute | solution.py:434
  128.6 2.2 %collective-permute-done.20 = bf16[4,4,2,1024]{3,2,1,0:T(2,128)(2,1)S(1)} collective-permute-done((bf16[4,4,2,1024]{3,2,1,0:T(2,128)(2,1)S(1)}, bf16[4,4,2,1024]{3,2,1,0:T(2,128)(2,1)S(1)}, u32[]{:S(2)}, u32[]{:S(2)}) %collective-permute-start.20) | collective-permute-done | bytes 65568 | tf_op jit(solution)/shard_map/ppermute | solution.py:434
  130.9 1.3 collective-permute-done.21
  132.3 1.1 gather_fusion.2
  133.5 0.2 copy.19
  133.7 5.7 %convolution_convert_fusion.1 = bf16[16,512]{1,0:T(8,128)(2,1)S(1)} fusion(bf16[16,8192]{1,0:T(8,128)(2,1)S(1)} %bitcast.43, bf16[512,8192]{1,0:T(8,128)(2,1)} %param.10), kind=kOutput, calls=%fused_computation.4 | convolution fusion | flops 134225920 | bytes 8667136 | tf_op jit(solution)/shard_map/dot_general | solution.py:714
  139.4 0.6 reshape.304
  140.1 2.5 %place_pages.9 = bf16[64,128,256]{2,1,0:T(8,128)(2,1)} custom-call(s32[64]{0:T(128)} %select_reduce_fusion.3.refs_0_, s32[64]{0:T(128)} %get-tuple-element.36.order_ref.refs_1_, s32[4]{0:T(128)} %gather_fusion, f32[8,256]{1,0:T(8,128)} %get-tuple-element.43.refs_3_, bf16[4,128,256]{2,1,0:T(8,128)(2,1)} %copy-done.11, ...), custom_call_target="tpu_custom_call", output_to_operand_aliasing={{}: (6, {})} | custom-call | tf_op jit(solution)/shard_map/place_pages/pallas_call | solution.py:319
  (85 shorter events, 1.2 us)
Async XLA Ops:
  0.6 19.2 %copy-start.15 = (bf16[8,2,8192]{2,1,0:T(2,128)(2,1)S(1)}, bf16[8,2,8192]{2,1,0:T(2,128)(2,1)}, u32[]{:S(2)}) copy-start(bf16[8,2,8192]{2,1,0:T(2,128)(2,1)} %param.8) | copy-start | bytes 786436
  5.5 33.0 %collective-permute-start.5 = (bf16[4,128,256]{2,1,0:T(8,128)(2,1)}, bf16[4,128,256]{2,1,0:T(8,128)(2,1)S(1)}, u32[]{:S(2)}, u32[]{:S(2)}) collective-permute-start(bf16[4,128,256]{2,1,0:T(8,128)(2,1)} %get-tuple-element.40), channel_id=1, source_target_pairs={{0,8},{1,9},{2,10},{3,11},{4,12},{5,13},{6,14},{7,15},{8,0},{9,1},... | collective-permute-start | bytes 786440 | tf_op jit(solution)/shard_map/ppermute | solution.py:434
  9.6 4.9 %collective-permute-start = (bf16[16,128,256]{2,1,0:T(8,128)(2,1)}, bf16[16,128,256]{2,1,0:T(8,128)(2,1)S(1)}, u32[]{:S(2)}, u32[]{:S(2)}) collective-permute-start(bf16[16,128,256]{2,1,0:T(8,128)(2,1)} %get-tuple-element.37), channel_id=1, source_target_pairs={{0,1},{1,0},{2,3},{3,2},{4,5},{5,4},{6,7},{7,6},{8,9},{9,8},{10,11... | collective-permute-start | bytes 3145736 | tf_op jit(solution)/shard_map/ppermute | solution.py:434
  11.1 27.4 %copy-start.18 = (s32[4]{0:T(128)}, s32[4]{0:T(128)S(1)}, u32[]{:S(2)}) copy-start(s32[4]{0:T(128)S(1)} %get-tuple-element.71.units_ref) | copy-start | bytes 52
  14.5 1.0 copy-start.2
  19.1 3.5 %collective-permute-start.1 = (bf16[16,128,256]{2,1,0:T(8,128)(2,1)}, bf16[16,128,256]{2,1,0:T(8,128)(2,1)S(1)}, u32[]{:S(2)}, u32[]{:S(2)}) collective-permute-start(bf16[16,128,256]{2,1,0:T(8,128)(2,1)} %get-tuple-element.38), channel_id=1, source_target_pairs={{0,1},{1,0},{2,3},{3,2},{4,5},{5,4},{6,7},{7,6},{8,9},{9,8},{10,11... | collective-permute-start | bytes 3145736 | tf_op jit(solution)/shard_map/ppermute | solution.py:434
  20.3 18.3 %collective-permute-start.6 = (bf16[4,128,256]{2,1,0:T(8,128)(2,1)}, bf16[4,128,256]{2,1,0:T(8,128)(2,1)S(1)}, u32[]{:S(2)}, u32[]{:S(2)}) collective-permute-start(bf16[4,128,256]{2,1,0:T(8,128)(2,1)} %get-tuple-element.41), channel_id=1, source_target_pairs={{0,14},{1,15},{2,12},{3,13},{4,10},{5,11},{6,8},{7,9},{8,6},{9,7},... | collective-permute-start | bytes 786440 | tf_op jit(solution)/shard_map/ppermute | solution.py:434
  22.6 21.9 %copy-start.3 = (bf16[16,128,256]{2,1,0:T(8,128)(2,1)}, bf16[16,128,256]{2,1,0:T(8,128)(2,1)S(1)}, u32[]{:S(2)}) copy-start(bf16[16,128,256]{2,1,0:T(8,128)(2,1)S(1)} %collective-permute-done.1.passed_ref.rest_1_) | copy-start | bytes 3145732
  29.8 48.3 %copy-start = (s32[8]{0:T(128)S(1)}, s32[8]{0:T(128)}, u32[]{:S(2)}) copy-start(s32[8]{0:T(128)} %lengths_ref.1) | copy-start | bytes 100
  29.8 5.7 %collective-permute-start.4 = (bf16[1,16,640]{2,1,0:T(8,128)(2,1)S(1)}, bf16[1,16,640]{2,1,0:T(8,128)(2,1)S(1)}, u32[]{:S(2)}, u32[]{:S(2)}) collective-permute-start(bf16[1,16,640]{2,1,0:T(8,128)(2,1)S(1)} %bitcast.47), channel_id=1, source_target_pairs={{0,12},{1,13},{2,14},{3,15},{4,8},{5,9},{6,10},{7,11},{8,4},{9,5},... | collective-permute-start | bytes 61448 | tf_op jit(solution)/shard_map/ppermute | solution.py:434
  32.3 6.2 %collective-permute-start.3 = (bf16[1,16,640]{2,1,0:T(8,128)(2,1)S(1)}, bf16[1,16,640]{2,1,0:T(8,128)(2,1)S(1)}, u32[]{:S(2)}, u32[]{:S(2)}) collective-permute-start(bf16[1,16,640]{2,1,0:T(8,128)(2,1)S(1)} %bitcast.48), channel_id=1, source_target_pairs={{0,8},{1,9},{2,10},{3,11},{4,12},{5,13},{6,14},{7,15},{8,0},{9,1},... | collective-permute-start | bytes 61448 | tf_op jit(solution)/shard_map/ppermute | solution.py:434
  32.4 6.0 %collective-permute-start.2 = (bf16[1,16,640]{2,1,0:T(8,128)(2,1)S(1)}, bf16[1,16,640]{2,1,0:T(8,128)(2,1)S(1)}, u32[]{:S(2)}, u32[]{:S(2)}) collective-permute-start(bf16[1,16,640]{2,1,0:T(8,128)(2,1)S(1)} %bitcast.49), channel_id=1, source_target_pairs={{0,4},{1,5},{2,6},{3,7},{4,0},{5,1},{6,2},{7,3},{8,12},{9,13},{10,... | collective-permute-start | bytes 61448 | tf_op jit(solution)/shard_map/ppermute | solution.py:434
  35.5 41.4 %collective-permute-start.9 = (bf16[8,128,256]{2,1,0:T(8,128)(2,1)}, bf16[8,128,256]{2,1,0:T(8,128)(2,1)S(1)}, u32[]{:S(2)}, u32[]{:S(2)}) collective-permute-start(bf16[8,128,256]{2,1,0:T(8,128)(2,1)} %get-tuple-element.47), channel_id=1, source_target_pairs={{0,4},{1,5},{2,6},{3,7},{4,0},{5,1},{6,2},{7,3},{8,12},{9,13},{10,... | collective-permute-start | bytes 1572872 | tf_op jit(solution)/shard_map/ppermute | solution.py:434
  38.5 46.8 %collective-permute-start.10 = (bf16[8,128,256]{2,1,0:T(8,128)(2,1)}, bf16[8,128,256]{2,1,0:T(8,128)(2,1)S(1)}, u32[]{:S(2)}, u32[]{:S(2)}) collective-permute-start(bf16[8,128,256]{2,1,0:T(8,128)(2,1)} %get-tuple-element.48), channel_id=1, source_target_pairs={{0,6},{1,7},{2,4},{3,5},{4,2},{5,3},{6,0},{7,1},{8,14},{9,15},{10,... | collective-permute-start | bytes 1572872 | tf_op jit(solution)/shard_map/ppermute | solution.py:434
  38.5 40.7 %copy-start.9 = (bf16[4,128,256]{2,1,0:T(8,128)(2,1)}, bf16[4,128,256]{2,1,0:T(8,128)(2,1)S(1)}, u32[]{:S(2)}) copy-start(bf16[4,128,256]{2,1,0:T(8,128)(2,1)S(1)} %collective-permute-done.5.refs_7_) | copy-start | bytes 786436
  38.5 40.7 %copy-start.10 = (bf16[4,128,256]{2,1,0:T(8,128)(2,1)}, bf16[4,128,256]{2,1,0:T(8,128)(2,1)S(1)}, u32[]{:S(2)}) copy-start(bf16[4,128,256]{2,1,0:T(8,128)(2,1)S(1)} %collective-permute-done.6.refs_8_) | copy-start | bytes 786436
  38.5 4.5 %collective-permute-start.7 = (bf16[4,16,640]{2,1,0:T(8,128)(2,1)S(1)}, bf16[4,16,640]{2,1,0:T(8,128)(2,1)S(1)}, u32[]{:S(2)}, u32[]{:S(2)}) collective-permute-start(bf16[4,16,640]{2,1,0:T(8,128)(2,1)S(1)} %pad_maximum_fusion.1), channel_id=1, source_target_pairs={{0,2},{1,3},{2,0},{3,1},{4,6},{5,7},{6,4},{7,5},{8,10},{9,11},{10,... | collective-permute-start | bytes 245768 | tf_op jit(solution)/shard_map/ppermute | solution.py:434
  41.0 32.7 %collective-permute-start.11 = (bf16[4,128,256]{2,1,0:T(8,128)(2,1)}, bf16[4,128,256]{2,1,0:T(8,128)(2,1)S(1)}, u32[]{:S(2)}, u32[]{:S(2)}) collective-permute-start(bf16[4,128,256]{2,1,0:T(8,128)(2,1)} %get-tuple-element.52), channel_id=1, source_target_pairs={{0,8},{1,9},{2,10},{3,11},{4,12},{5,13},{6,14},{7,15},{8,0},{9,1},... | collective-permute-start | bytes 786440 | tf_op jit(solution)/shard_map/ppermute | solution.py:434
  43.1 1.5 %collective-permute-start.8 = (bf16[8,16,640]{2,1,0:T(8,128)(2,1)S(1)}, bf16[8,16,640]{2,1,0:T(8,128)(2,1)S(1)}, u32[]{:S(2)}, u32[]{:S(2)}) collective-permute-start(bf16[8,16,640]{2,1,0:T(8,128)(2,1)S(1)} %pad_maximum_fusion), channel_id=1, source_target_pairs={{0,1},{1,0},{2,3},{3,2},{4,5},{5,4},{6,7},{7,6},{8,9},{9,8},{10,11... | collective-permute-start | bytes 491528 | tf_op jit(solution)/shard_map/ppermute | solution.py:434
  44.6 7.8 %copy-start.8 = (bf16[16,16,640]{2,1,0:T(8,128)(2,1)}, bf16[16,16,640]{2,1,0:T(8,128)(2,1)S(1)}, u32[]{:S(2)}) copy-start(bf16[16,16,640]{2,1,0:T(8,128)(2,1)S(1)} %constant_dynamic-update-slice_fusion.rows_ref) | copy-start | bytes 983044
  47.6 44.6 %collective-permute-start.13 = (bf16[8,128,256]{2,1,0:T(8,128)(2,1)}, bf16[8,128,256]{2,1,0:T(8,128)(2,1)S(1)}, u32[]{:S(2)}, u32[]{:S(2)}) collective-permute-start(bf16[8,128,256]{2,1,0:T(8,128)(2,1)} %get-tuple-element.55), channel_id=1, source_target_pairs={{0,2},{1,3},{2,0},{3,1},{4,6},{5,7},{6,4},{7,5},{8,10},{9,11},{10,... | collective-permute-start | bytes 1572872 | tf_op jit(solution)/shard_map/ppermute | solution.py:434
  49.2 42.9 %collective-permute-start.12 = (bf16[4,128,256]{2,1,0:T(8,128)(2,1)}, bf16[4,128,256]{2,1,0:T(8,128)(2,1)S(1)}, u32[]{:S(2)}, u32[]{:S(2)}) collective-permute-start(bf16[4,128,256]{2,1,0:T(8,128)(2,1)} %get-tuple-element.53), channel_id=1, source_target_pairs={{0,14},{1,15},{2,12},{3,13},{4,10},{5,11},{6,8},{7,9},{8,6},{9,7},... | collective-permute-start | bytes 786440 | tf_op jit(solution)/shard_map/ppermute | solution.py:434
  73.7 18.4 %copy-start.12 = (bf16[4,128,256]{2,1,0:T(8,128)(2,1)}, bf16[4,128,256]{2,1,0:T(8,128)(2,1)S(1)}, u32[]{:S(2)}) copy-start(bf16[4,128,256]{2,1,0:T(8,128)(2,1)S(1)} %collective-permute-done.11.refs_7_) | copy-start | bytes 786436
  73.7 30.3 %collective-permute-start.15 = (bf16[8,128,256]{2,1,0:T(8,128)(2,1)}, bf16[8,128,256]{2,1,0:T(8,128)(2,1)S(1)}, u32[]{:S(2)}, u32[]{:S(2)}) collective-permute-start(bf16[8,128,256]{2,1,0:T(8,128)(2,1)} %get-tuple-element.61), channel_id=1, source_target_pairs={{0,10},{1,11},{2,8},{3,9},{4,14},{5,15},{6,12},{7,13},{8,2},{9,3},... | collective-permute-start | bytes 1572872 | tf_op jit(solution)/shard_map/ppermute | solution.py:434
  76.9 8.4 %copy-start.4 = (bf16[8,128,256]{2,1,0:T(8,128)(2,1)}, bf16[8,128,256]{2,1,0:T(8,128)(2,1)S(1)}, u32[]{:S(2)}) copy-start(bf16[8,128,256]{2,1,0:T(8,128)(2,1)S(1)} %collective-permute-done.9.refs_7_) | copy-start | bytes 1572868
  76.9 22.0 %collective-permute-start.14 = (bf16[144,128]{1,0:T(8,128)(2,1)}, bf16[144,128]{1,0:T(8,128)(2,1)S(1)}, u32[]{:S(2)}, u32[]{:S(2)}) collective-permute-start(bf16[144,128]{1,0:T(8,128)(2,1)} %get-tuple-element.59), channel_id=1, source_target_pairs={{0,12},{1,13},{2,14},{3,15},{4,8},{5,9},{6,10},{7,11},{8,4},{9,5},... | collective-permute-start | bytes 110600 | tf_op jit(solution)/shard_map/ppermute | solution.py:434
  79.2 19.7 %copy-start.19 = (bf16[4,128,256]{2,1,0:T(8,128)(2,1)S(1)}, bf16[4,128,256]{2,1,0:T(8,128)(2,1)}, u32[]{:S(2)}) copy-start(bf16[4,128,256]{2,1,0:T(8,128)(2,1)} %get-tuple-element.65) | copy-start | bytes 786436
  79.3 22.4 %copy-start.1 = (s32[16]{0:T(128)S(1)}, s32[16]{0:T(128)}, u32[]{:S(2)}) copy-start(s32[16]{0:T(128)} %constant.99.clone.turn_ref) | copy-start | bytes 196
  85.3 34.8 %copy-start.16 = (bf16[4,128,256]{2,1,0:T(8,128)(2,1)S(1)}, bf16[4,128,256]{2,1,0:T(8,128)(2,1)}, u32[]{:S(2)}) copy-start(bf16[4,128,256]{2,1,0:T(8,128)(2,1)} %get-tuple-element.67) | copy-start | bytes 786436
  85.3 0.8 copy-start.5
  92.1 0.7 copy-start.14
  92.1 0.9 copy-start.6
  99.0 5.0 %copy-start.17 = (bf16[144,128]{1,0:T(8,128)(2,1)}, bf16[144,128]{1,0:T(8,128)(2,1)S(1)}, u32[]{:S(2)}) copy-start(bf16[144,128]{1,0:T(8,128)(2,1)S(1)} %collective-permute-done.14.refs_7_) | copy-start | bytes 110596
  99.0 10.2 %collective-permute-start.16 = (bf16[4,128,256]{2,1,0:T(8,128)(2,1)S(1)}, bf16[4,128,256]{2,1,0:T(8,128)(2,1)S(1)}, u32[]{:S(2)}, u32[]{:S(2)}) collective-permute-start(bf16[4,128,256]{2,1,0:T(8,128)(2,1)S(1)} %copy-done.19), channel_id=1, source_target_pairs={{0,12},{1,13},{2,14},{3,15},{4,8},{5,9},{6,10},{7,11},{8,4},{9,5},... | collective-permute-start | bytes 786440 | tf_op jit(solution)/shard_map/ppermute | solution.py:434
  104.0 0.8 copy-start.7
  109.2 30.9 %copy-start.11 = (bf16[4,128,256]{2,1,0:T(8,128)(2,1)}, bf16[4,128,256]{2,1,0:T(8,128)(2,1)S(1)}, u32[]{:S(2)}) copy-start(bf16[4,128,256]{2,1,0:T(8,128)(2,1)S(1)} %collective-permute-done.16.refs_4_) | copy-start | bytes 786436
  110.0 12.6 %collective-permute-start.19 = (bf16[1,4,2,1024]{3,2,1,0:T(2,128)(2,1)S(1)}, bf16[1,4,2,1024]{3,2,1,0:T(2,128)(2,1)S(1)}, u32[]{:S(2)}, u32[]{:S(2)}) collective-permute-start(bf16[1,4,2,1024]{3,2,1,0:T(2,128)(2,1)S(1)} %broadcast_in_dim_reshape.4), channel_id=1, source_target_pairs={{0,12},{1,13},{2,14},{3,15},{4,8},{5,9},{6,10},{7,11},{8,4},{9,5},... | collective-permute-start | bytes 49160 | tf_op jit(solution)/shard_map/ppermute | solution.py:434
  112.8 9.8 %collective-permute-start.18 = (bf16[1,4,2,1024]{3,2,1,0:T(2,128)(2,1)S(1)}, bf16[1,4,2,1024]{3,2,1,0:T(2,128)(2,1)S(1)}, u32[]{:S(2)}, u32[]{:S(2)}) collective-permute-start(bf16[1,4,2,1024]{3,2,1,0:T(2,128)(2,1)S(1)} %broadcast_in_dim_reshape.4), channel_id=1, source_target_pairs={{0,8},{1,9},{2,10},{3,11},{4,12},{5,13},{6,14},{7,15},{8,0},{9,1},... | collective-permute-start | bytes 49160 | tf_op jit(solution)/shard_map/ppermute | solution.py:434
  119.8 4.6 %collective-permute-start.17 = (bf16[1,4,2,1024]{3,2,1,0:T(2,128)(2,1)S(1)}, bf16[1,4,2,1024]{3,2,1,0:T(2,128)(2,1)S(1)}, u32[]{:S(2)}, u32[]{:S(2)}) collective-permute-start(bf16[1,4,2,1024]{3,2,1,0:T(2,128)(2,1)S(1)} %broadcast_in_dim_reshape.4), channel_id=1, source_target_pairs={{0,4},{1,5},{2,6},{3,7},{4,0},{5,1},{6,2},{7,3},{8,12},{9,13},{10,... | collective-permute-start | bytes 49160 | tf_op jit(solution)/shard_map/ppermute | solution.py:434
  120.1 13.5 %collective-permute-start.22 = (bf16[4,128,256]{2,1,0:T(8,128)(2,1)S(1)}, bf16[4,128,256]{2,1,0:T(8,128)(2,1)S(1)}, u32[]{:S(2)}, u32[]{:S(2)}) collective-permute-start(bf16[4,128,256]{2,1,0:T(8,128)(2,1)S(1)} %copy-done.16), channel_id=1, source_target_pairs={{0,12},{1,13},{2,14},{3,15},{4,8},{5,9},{6,10},{7,11},{8,4},{9,5},... | collective-permute-start | bytes 786440 | tf_op jit(solution)/shard_map/ppermute | solution.py:434
  124.5 6.2 %collective-permute-start.20 = (bf16[4,4,2,1024]{3,2,1,0:T(2,128)(2,1)S(1)}, bf16[4,4,2,1024]{3,2,1,0:T(2,128)(2,1)S(1)}, u32[]{:S(2)}, u32[]{:S(2)}) collective-permute-start(bf16[4,4,2,1024]{3,2,1,0:T(2,128)(2,1)S(1)} %pad_maximum_fusion.2), channel_id=1, source_target_pairs={{0,2},{1,3},{2,0},{3,1},{4,6},{5,7},{6,4},{7,5},{8,10},{9,11},{10,... | collective-permute-start | bytes 196616 | tf_op jit(solution)/shard_map/ppermute | solution.py:434
  130.8 1.4 collective-permute-start.21
  133.7 6.4 %copy-start.13 = (bf16[4,128,256]{2,1,0:T(8,128)(2,1)}, bf16[4,128,256]{2,1,0:T(8,128)(2,1)S(1)}, u32[]{:S(2)}) copy-start(bf16[4,128,256]{2,1,0:T(8,128)(2,1)S(1)} %collective-permute-done.22.refs_5_) | copy-start | bytes 786436

commit v11 on v10

--- a/solution.py
+++ b/solution.py
@@ -476,7 +476,7 @@
     if pairwise:
         half, quarter = devices // 2, devices // 4
         a, b = half, half + quarter
-        c, d, b = a + 2, b, b + 2
+        c, d = a + 2, b + 2
         near = list(range(2, half, 2))
         (chunk_a, cross_near), order = first_pack(
             new_units,
@@ -604,7 +604,7 @@
             capacity,
             [own(c) + passed(1, 2), own(d), own(near[0]) + passed(2, 1)],
         )
-        moved_2 = send(chunk_2, near[0])
+        moved_2 = send(after(chunk_2, sent), near[0])
         moved_c = send(after(chunk_c, moved_a2, sent), c)
 
         def place(groups, sums, cache, attends, parts, finish):

time: 145 us -> 142 us (0.979)
  waiting for transfers between devices: 26.5 us -> 29.6 us
  starting transfers between devices: 43.8 us -> 41 us
  other arithmetic: 6.23 us -> 4.18 us
    ppermute x23, waiting for transfers between devices: 26.5 us -> 29.6 us  [swap(): return lax.ppermute(values, 'tp', [(i, i ^ key) for i in range(devices)])]
    ppermute x23, starting transfers between devices: 43.8 us -> 41 us  [swap(): return lax.ppermute(values, 'tp', [(i, i ^ key) for i in range(devices)])]
  transfers between devices with their start and end apart: 23 -> 23, of which waited for: 8 -> 10; matrix products, arithmetic and copies ran while one was open for 14% -> 12% of each run, Pallas kernels for 24% -> 24%
where the time goes in v11:
time: 142 us; the launch traced here: 141 us
  Pallas kernels  41 us (29%)
  starting transfers between devices  41 us (29%)
  waiting for transfers between devices  29.6 us (21%)
  matrix products  12.9 us (9%)
  local copies, waits for them, and re-layouts  10.9 us (8%)
  other arithmetic  4.18 us (3%)
    ppermute x23, starting transfers between devices, swap(): return lax.ppermute(values, 'tp', [(i, i ^ key) for i in range(devices)])  41 us
    ppermute x23, waiting for transfers between devices, swap(): return lax.ppermute(values, 'tp', [(i, i ^ key) for i in range(devices)])  29.6 us
    pallas_call x5, Pallas kernels, place_pages(): pl.pallas_call(functools.partial(place_kernel, entries, started, attends,...  24.8 us
    dot_general x1, matrix products, body(): lax.dot_general(flat_rows, qkv_weight, (((1,), (1,)), ((), ())), preferre...  7.16 us
    pallas_call x2, Pallas kernels, next_pack(): pl.pallas_call(functools.partial(next_pack_kernel, capacity, outs_pages,...  6.62 us
    dot_general x1, matrix products, body(): lax.dot_general(logical, out_weight, (((1,), (1,)), ((), ())), preferred_...  5.74 us
    pallas_call x1, Pallas kernels, first_pack(): pl.pallas_call(functools.partial(first_pack_kernel, devices, capacity, ou...  4.82 us
    pallas_call x1, Pallas kernels, rows_and_parts(): pl.pallas_call(functools.partial(rows_kernel, late), out_shape=(jax.Shape...  4.74 us
  transfers between devices with their start and end apart: 23, of which 10 were waited for; matrix products, arithmetic and copies ran while one was open for 12% of the time, Pallas kernels for 24%

profile of v11, /device:TPU:0, one launch (start us, length us, event | category | flops | bytes accessed | tf_op | source)
XLA Modules:
  0.0 140.7 jit_solution(16362374040487229880)
XLA Ops:
  0.7 4.8 %first_pack.1 = (bf16[4,128,256]{2,1,0:T(8,128)(2,1)}, bf16[16,128,256]{2,1,0:T(8,128)(2,1)}, s32[64]{0:T(128)}) custom-call(s32[64]{0:T(128)} %units_ref.1, s32[1024]{0:T(1024)} %old_ref.1, bf16[64,128,256]{2,1,0:T(8,128)(2,1)} %rest_0_.3), custom_call_target="tpu_custom_call" | custom-call | tf_op jit(solution)/shard_map/first_pack/pallas_call | solution.py:142
  5.5 4.1 %collective-permute-start.5 = (bf16[4,128,256]{2,1,0:T(8,128)(2,1)}, bf16[4,128,256]{2,1,0:T(8,128)(2,1)S(1)}, u32[]{:S(2)}, u32[]{:S(2)}) collective-permute-start(bf16[4,128,256]{2,1,0:T(8,128)(2,1)} %get-tuple-element.41), channel_id=1, source_target_pairs={{0,8},{1,9},{2,10},{3,11},{4,12},{5,13},{6,14},{7,15},{8,0},{9,1},... | collective-permute-start | bytes 786440 | tf_op jit(solution)/shard_map/ppermute | solution.py:434
  9.6 0.7 compare_select_fusion.2
  10.3 0.7 add_convert_fusion
  11.1 0.8 reshape.298
  12.0 0.1 fusion.1
  12.2 0.3 collective-permute-done.rest_1_.refs_6_.rest_2_
  12.5 1.0 copy-done.2
  13.5 3.6 %next_pack.2 = (bf16[8,128,256]{2,1,0:T(8,128)(2,1)}, bf16[8,128,256]{2,1,0:T(8,128)(2,1)}, bf16[4,128,256]{2,1,0:T(8,128)(2,1)}, bf16[16,128,256]{2,1,0:T(8,128)(2,1)}) custom-call(s32[64]{0:T(128)} %get-tuple-element.37.order_ref.refs_1_, bf16[64,128,256]{2,1,0:T(8,128)(2,1)} %rest_0_.3, bf16[16,128,256]{2,1,0:T(8,128)(2,1)} %copy-done.2), custom_call_target="tpu_custom_call" | custom-call | tf_op jit(solution)/shard_map/next_pack/pallas_call | solution.py:160
  17.1 0.3 collective-permute-start.1
  17.6 0.7 pad_maximum_fusion.3
  18.2 0.2 select_reduce_fusion.1
  18.4 0.1 convert_reduce_fusion
  18.6 0.2 select_reduce_fusion
  18.8 0.2 convert_reduce_fusion.1
  19.0 1.4 %collective-permute-start.6 = (bf16[4,128,256]{2,1,0:T(8,128)(2,1)}, bf16[4,128,256]{2,1,0:T(8,128)(2,1)S(1)}, u32[]{:S(2)}, u32[]{:S(2)}) collective-permute-start(bf16[4,128,256]{2,1,0:T(8,128)(2,1)} %get-tuple-element.42), channel_id=1, source_target_pairs={{0,12},{1,13},{2,14},{3,15},{4,8},{5,9},{6,10},{7,11},{8,4},{9,5},... | collective-permute-start | bytes 786440 | tf_op jit(solution)/shard_map/ppermute | solution.py:434
  20.4 7.2 %convolution_convert_fusion = bf16[16,640]{1,0:T(8,128)(2,1)S(1)} fusion(bf16[16,8192]{1,0:T(8,128)(2,1)S(1)} %reshape.300, bf16[640,8192]{1,0:T(8,128)(2,1)} %param.9), kind=kOutput, calls=%fused_computation.3 | convolution fusion | flops 167782400 | bytes 10768384 | tf_op jit(solution)/shard_map/dot_general | solution.py:572
  27.5 2.5 %collective-permute-start.4 = (bf16[1,16,640]{2,1,0:T(8,128)(2,1)S(1)}, bf16[1,16,640]{2,1,0:T(8,128)(2,1)S(1)}, u32[]{:S(2)}, u32[]{:S(2)}) collective-permute-start(bf16[1,16,640]{2,1,0:T(8,128)(2,1)S(1)} %bitcast.47), channel_id=1, source_target_pairs={{0,12},{1,13},{2,14},{3,15},{4,8},{5,9},{6,10},{7,11},{8,4},{9,5},... | collective-permute-start | bytes 61448 | tf_op jit(solution)/shard_map/ppermute | solution.py:434
  30.0 0.2 collective-permute-start.3
  30.2 1.7 %collective-permute-start.2 = (bf16[1,16,640]{2,1,0:T(8,128)(2,1)S(1)}, bf16[1,16,640]{2,1,0:T(8,128)(2,1)S(1)}, u32[]{:S(2)}, u32[]{:S(2)}) collective-permute-start(bf16[1,16,640]{2,1,0:T(8,128)(2,1)S(1)} %bitcast.49), channel_id=1, source_target_pairs={{0,4},{1,5},{2,6},{3,7},{4,0},{5,1},{6,2},{7,3},{8,12},{9,13},{10,... | collective-permute-start | bytes 61448 | tf_op jit(solution)/shard_map/ppermute | solution.py:434
  31.9 0.1 select_reduce_fusion.4
  32.1 0.7 reshape.299.ids_ref
  32.8 0.4 collective-permute-done.4
  33.2 3.3 %collective-permute-start.9 = (bf16[8,128,256]{2,1,0:T(8,128)(2,1)}, bf16[8,128,256]{2,1,0:T(8,128)(2,1)S(1)}, u32[]{:S(2)}, u32[]{:S(2)}) collective-permute-start(bf16[8,128,256]{2,1,0:T(8,128)(2,1)} %get-tuple-element.48), channel_id=1, source_target_pairs={{0,4},{1,5},{2,6},{3,7},{4,0},{5,1},{6,2},{7,3},{8,12},{9,13},{10,... | collective-permute-start | bytes 1572872 | tf_op jit(solution)/shard_map/ppermute | solution.py:434
  36.5 1.0 collective-permute-start.10
  37.5 0.6 collective-permute-start.7
  38.1 0.8 fusion.5
  38.9 2.5 %collective-permute-start.11 = (bf16[4,128,256]{2,1,0:T(8,128)(2,1)S(1)}, bf16[4,128,256]{2,1,0:T(8,128)(2,1)S(1)}, u32[]{:S(2)}, u32[]{:S(2)}) collective-permute-start(bf16[4,128,256]{2,1,0:T(8,128)(2,1)S(1)} %get-tuple-element.53), channel_id=1, source_target_pairs={{0,8},{1,9},{2,10},{3,11},{4,12},{5,13},{6,14},{7,15},{8,0},{9,1},... | collective-permute-start | bytes 786440 | tf_op jit(solution)/shard_map/ppermute | solution.py:434
  41.4 0.6 collective-permute-done.7
  42.1 1.3 collective-permute-done.8
  43.5 3.0 %next_pack.3 = (bf16[8,128,256]{2,1,0:T(8,128)(2,1)}, bf16[4,128,256]{2,1,0:T(8,128)(2,1)}, bf16[8,128,256]{2,1,0:T(8,128)(2,1)}) custom-call(s32[64]{0:T(128)} %get-tuple-element.37.order_ref.refs_1_, bf16[64,128,256]{2,1,0:T(8,128)(2,1)} %rest_0_.3, bf16[16,128,256]{2,1,0:T(8,128)(2,1)} %copy-done.3, bf16[16,128,256]{2,1,0:T(8,128)(2,1)} %copy-done.2), custom_call_target="tpu_custom_call" | custom-call | tf_op jit(solution)/shard_map/next_pack/pallas_call | solution.py:160
  46.6 4.7 %rows_and_parts.1 = (f32[4,16,128]{2,1,0:T(8,128)}, f32[8,256]{1,0:T(8,128)}, bf16[144,128]{1,0:T(8,128)(2,1)}) custom-call(s32[4]{0:T(128)} %copy-done.19, s32[16]{0:T(128)} %constant.99.clone.turn_ref, s32[64]{0:T(128)} %get-tuple-element.37.order_ref.refs_1_, s32[8]{0:T(128)} %reshape.299.ids_ref, s32[8]{0:T(128)} %lengths_ref.1, ...), custom_call_target="tpu_custom_call" | custom-call | tf_op jit(solution)/shard_map/rows_and_parts/pallas_call | solution.py:415
  51.3 1.0 collective-permute-start.13
  52.3 1.9 %collective-permute-start.12 = (bf16[4,128,256]{2,1,0:T(8,128)(2,1)}, bf16[4,128,256]{2,1,0:T(8,128)(2,1)S(1)}, u32[]{:S(2)}, u32[]{:S(2)}) collective-permute-start(bf16[4,128,256]{2,1,0:T(8,128)(2,1)} %get-tuple-element.54), channel_id=1, source_target_pairs={{0,12},{1,13},{2,14},{3,15},{4,8},{5,9},{6,10},{7,11},{8,4},{9,5},... | collective-permute-start | bytes 786440 | tf_op jit(solution)/shard_map/ppermute | solution.py:434
  54.3 11.7 %collective-permute-done.11.refs_7_ = bf16[4,128,256]{2,1,0:T(8,128)(2,1)S(1)} collective-permute-done((bf16[4,128,256]{2,1,0:T(8,128)(2,1)S(1)}, bf16[4,128,256]{2,1,0:T(8,128)(2,1)S(1)}, u32[]{:S(2)}, u32[]{:S(2)}) %collective-permute-start.11) | collective-permute-done | bytes 262176 | tf_op jit(solution)/shard_map/ppermute | solution.py:434
  66.0 4.4 %collective-permute-start.15 = (bf16[8,128,256]{2,1,0:T(8,128)(2,1)}, bf16[8,128,256]{2,1,0:T(8,128)(2,1)S(1)}, u32[]{:S(2)}, u32[]{:S(2)}) collective-permute-start(bf16[8,128,256]{2,1,0:T(8,128)(2,1)} %get-tuple-element.63), channel_id=1, source_target_pairs={{0,10},{1,11},{2,8},{3,9},{4,14},{5,15},{6,12},{7,13},{8,2},{9,3},... | collective-permute-start | bytes 1572872 | tf_op jit(solution)/shard_map/ppermute | solution.py:434
  70.4 0.7 select_reduce_fusion.3.refs_0_
  71.0 1.9 %collective-permute-start.14 = (bf16[144,128]{1,0:T(8,128)(2,1)}, bf16[144,128]{1,0:T(8,128)(2,1)S(1)}, u32[]{:S(2)}, u32[]{:S(2)}) collective-permute-start(bf16[144,128]{1,0:T(8,128)(2,1)} %get-tuple-element.57), channel_id=1, source_target_pairs={{0,14},{1,15},{2,12},{3,13},{4,10},{5,11},{6,8},{7,9},{8,6},{9,7},... | collective-permute-start | bytes 110600 | tf_op jit(solution)/shard_map/ppermute | solution.py:434
  73.0 1.1 gather_fusion
  74.1 6.0 %place_pages.5 = (bf16[64,128,256]{2,1,0:T(8,128)(2,1)}, f32[4,16,128]{2,1,0:T(8,128)}, f32[4,16,128]{2,1,0:T(8,128)}) custom-call(s32[64]{0:T(128)} %select_reduce_fusion.3.refs_0_, s32[64]{0:T(128)} %get-tuple-element.37.order_ref.refs_1_, s32[4]{0:T(128)} %gather_fusion, f32[8,256]{1,0:T(8,128)} %get-tuple-element.44.refs_3_, ...), custom_call_target="tpu_custom_call" | custom-call | tf_op jit(solution)/shard_map/place_pages/pallas_call | solution.py:319
  80.1 0.8 copy-done.5
  80.9 6.0 %place_pages.6 = (bf16[64,128,256]{2,1,0:T(8,128)(2,1)}, f32[4,16,128]{2,1,0:T(8,128)}, f32[4,16,128]{2,1,0:T(8,128)}) custom-call(s32[64]{0:T(128)} %select_reduce_fusion.3.refs_0_, s32[64]{0:T(128)} %get-tuple-element.37.order_ref.refs_1_, s32[4]{0:T(128)} %gather_fusion, f32[8,256]{1,0:T(8,128)} %get-tuple-element.44.refs_3_, ...), custom_call_target="tpu_custom_call", output_to_operand_aliasing={{0}: (9, {})} | custom-call | tf_op jit(solution)/shard_map/place_pages/pallas_call | solution.py:319
  87.0 0.7 copy-done.14
  87.6 0.2 copy-done.7
  87.8 5.9 %place_pages.7 = (bf16[64,128,256]{2,1,0:T(8,128)(2,1)}, f32[4,16,128]{2,1,0:T(8,128)}, f32[4,16,128]{2,1,0:T(8,128)}) custom-call(s32[64]{0:T(128)} %select_reduce_fusion.3.refs_0_, s32[64]{0:T(128)} %get-tuple-element.37.order_ref.refs_1_, s32[4]{0:T(128)} %gather_fusion, f32[8,256]{1,0:T(8,128)} %get-tuple-element.44.refs_3_, ...), custom_call_target="tpu_custom_call", output_to_operand_aliasing={{0}: (10, {})} | custom-call | tf_op jit(solution)/shard_map/place_pages/pallas_call | solution.py:319
  93.7 2.9 %collective-permute-start.16 = (bf16[4,128,256]{2,1,0:T(8,128)(2,1)}, bf16[4,128,256]{2,1,0:T(8,128)(2,1)S(1)}, u32[]{:S(2)}, u32[]{:S(2)}) collective-permute-start(bf16[4,128,256]{2,1,0:T(8,128)(2,1)} %get-tuple-element.67), channel_id=1, source_target_pairs={{0,14},{1,15},{2,12},{3,13},{4,10},{5,11},{6,8},{7,9},{8,6},{9,7},... | collective-permute-start | bytes 786440 | tf_op jit(solution)/shard_map/ppermute | solution.py:434
  96.6 0.8 gather_fusion.1
  97.4 2.6 %collective-permute-done.15.refs_8_ = bf16[8,128,256]{2,1,0:T(8,128)(2,1)S(1)} collective-permute-done((bf16[8,128,256]{2,1,0:T(8,128)(2,1)}, bf16[8,128,256]{2,1,0:T(8,128)(2,1)S(1)}, u32[]{:S(2)}, u32[]{:S(2)}) %collective-permute-start.15) | collective-permute-done | bytes 524320 | tf_op jit(solution)/shard_map/ppermute | solution.py:434
  100.0 0.8 copy-done.6
  100.8 4.4 %place_pages.8 = (bf16[64,128,256]{2,1,0:T(8,128)(2,1)}, f32[4,16,128]{2,1,0:T(8,128)}, f32[4,16,128]{2,1,0:T(8,128)}, bf16[4,16,128]{2,1,0:T(8,128)(2,1)}) custom-call(s32[64]{0:T(128)} %select_reduce_fusion.3.refs_0_, s32[64]{0:T(128)} %get-tuple-element.37.order_ref.refs_1_, s32[4]{0:T(128)} %gather_fusion, ...), custom_call_target="tpu_custom_call", output_to_operand_aliasing={{0}: (9, {})} | custom-call | tf_op jit(solution)/shard_map/place_pages/pallas_call | solution.py:319
  105.3 0.8 broadcast_in_dim_reshape.4
  106.0 5.3 %collective-permute-start.19 = (bf16[1,4,2,1024]{3,2,1,0:T(2,128)(2,1)S(1)}, bf16[1,4,2,1024]{3,2,1,0:T(2,128)(2,1)S(1)}, u32[]{:S(2)}, u32[]{:S(2)}) collective-permute-start(bf16[1,4,2,1024]{3,2,1,0:T(2,128)(2,1)S(1)} %broadcast_in_dim_reshape.4), channel_id=1, source_target_pairs={{0,12},{1,13},{2,14},{3,15},{4,8},{5,9},{6,10},{7,11},{8,4},{9,5},... | collective-permute-start | bytes 49160 | tf_op jit(solution)/shard_map/ppermute | solution.py:434
  111.3 4.7 %collective-permute-start.18 = (bf16[1,4,2,1024]{3,2,1,0:T(2,128)(2,1)S(1)}, bf16[1,4,2,1024]{3,2,1,0:T(2,128)(2,1)S(1)}, u32[]{:S(2)}, u32[]{:S(2)}) collective-permute-start(bf16[1,4,2,1024]{3,2,1,0:T(2,128)(2,1)S(1)} %broadcast_in_dim_reshape.4), channel_id=1, source_target_pairs={{0,8},{1,9},{2,10},{3,11},{4,12},{5,13},{6,14},{7,15},{8,0},{9,1},... | collective-permute-start | bytes 49160 | tf_op jit(solution)/shard_map/ppermute | solution.py:434
  116.0 1.1 collective-permute-start.22
  117.1 2.2 %collective-permute-done.18 = bf16[1,4,2,1024]{3,2,1,0:T(2,128)(2,1)S(1)} collective-permute-done((bf16[1,4,2,1024]{3,2,1,0:T(2,128)(2,1)S(1)}, bf16[1,4,2,1024]{3,2,1,0:T(2,128)(2,1)S(1)}, u32[]{:S(2)}, u32[]{:S(2)}) %collective-permute-start.18) | collective-permute-done | bytes 16416 | tf_op jit(solution)/shard_map/ppermute | solution.py:434
  119.3 4.9 %collective-permute-done.17 = bf16[1,4,2,1024]{3,2,1,0:T(2,128)(2,1)S(1)} collective-permute-done((bf16[1,4,2,1024]{3,2,1,0:T(2,128)(2,1)S(1)}, bf16[1,4,2,1024]{3,2,1,0:T(2,128)(2,1)S(1)}, u32[]{:S(2)}, u32[]{:S(2)}) %collective-permute-start.17) | collective-permute-done | bytes 16416 | tf_op jit(solution)/shard_map/ppermute | solution.py:434
  124.2 0.1 pad_maximum_fusion.2
  124.5 4.2 %collective-permute-done.20 = bf16[4,4,2,1024]{3,2,1,0:T(2,128)(2,1)S(1)} collective-permute-done((bf16[4,4,2,1024]{3,2,1,0:T(2,128)(2,1)S(1)}, bf16[4,4,2,1024]{3,2,1,0:T(2,128)(2,1)S(1)}, u32[]{:S(2)}, u32[]{:S(2)}) %collective-permute-start.20) | collective-permute-done | bytes 65568 | tf_op jit(solution)/shard_map/ppermute | solution.py:434
  128.9 1.3 collective-permute-done.21
  130.3 1.1 gather_fusion.2
  131.5 0.2 copy.19
  131.6 5.7 %convolution_convert_fusion.1 = bf16[16,512]{1,0:T(8,128)(2,1)S(1)} fusion(bf16[16,8192]{1,0:T(8,128)(2,1)S(1)} %bitcast.43, bf16[512,8192]{1,0:T(8,128)(2,1)} %param.10), kind=kOutput, calls=%fused_computation.4 | convolution fusion | flops 134225920 | bytes 8667136 | tf_op jit(solution)/shard_map/dot_general | solution.py:714
  137.4 0.6 reshape.304
  138.0 2.6 %place_pages.9 = bf16[64,128,256]{2,1,0:T(8,128)(2,1)} custom-call(s32[64]{0:T(128)} %select_reduce_fusion.3.refs_0_, s32[64]{0:T(128)} %get-tuple-element.37.order_ref.refs_1_, s32[4]{0:T(128)} %gather_fusion, f32[8,256]{1,0:T(8,128)} %get-tuple-element.44.refs_3_, bf16[4,128,256]{2,1,0:T(8,128)(2,1)} %copy-done.11, ...), custom_call_target="tpu_custom_call", output_to_operand_aliasing={{}: (6, {})} | custom-call | tf_op jit(solution)/shard_map/place_pages/pallas_call | solution.py:319
  (85 shorter events, 1.3 us)
Async XLA Ops:
  0.6 17.6 %copy-start.18 = (s32[64]{0:T(128)S(1)}, s32[64]{0:T(128)}, u32[]{:S(2)}) copy-start(s32[64]{0:T(128)} %units_ref.1) | copy-start | bytes 772
  0.6 17.9 %copy-start.17 = (s32[1024]{0:T(1024)S(1)}, s32[1024]{0:T(1024)}, u32[]{:S(2)}) copy-start(s32[1024]{0:T(1024)} %old_ref.1) | copy-start | bytes 12292
  0.7 16.8 %copy-start.15 = (bf16[8,2,8192]{2,1,0:T(2,128)(2,1)S(1)}, bf16[8,2,8192]{2,1,0:T(2,128)(2,1)}, u32[]{:S(2)}) copy-start(bf16[8,2,8192]{2,1,0:T(2,128)(2,1)} %param.8) | copy-start | bytes 786436
  5.5 32.0 %collective-permute-start.5 = (bf16[4,128,256]{2,1,0:T(8,128)(2,1)}, bf16[4,128,256]{2,1,0:T(8,128)(2,1)S(1)}, u32[]{:S(2)}, u32[]{:S(2)}) collective-permute-start(bf16[4,128,256]{2,1,0:T(8,128)(2,1)} %get-tuple-element.41), channel_id=1, source_target_pairs={{0,8},{1,9},{2,10},{3,11},{4,12},{5,13},{6,14},{7,15},{8,0},{9,1},... | collective-permute-start | bytes 786440 | tf_op jit(solution)/shard_map/ppermute | solution.py:434
  9.6 2.9 %collective-permute-start = (bf16[16,128,256]{2,1,0:T(8,128)(2,1)}, bf16[16,128,256]{2,1,0:T(8,128)(2,1)S(1)}, u32[]{:S(2)}, u32[]{:S(2)}) collective-permute-start(bf16[16,128,256]{2,1,0:T(8,128)(2,1)} %get-tuple-element.38), channel_id=1, source_target_pairs={{0,1},{1,0},{2,3},{3,2},{4,5},{5,4},{6,7},{7,6},{8,9},{9,8},{10,11... | collective-permute-start | bytes 3145736 | tf_op jit(solution)/shard_map/ppermute | solution.py:434
  10.3 27.1 %copy-start.19 = (s32[4]{0:T(128)}, s32[4]{0:T(128)S(1)}, u32[]{:S(2)}) copy-start(s32[4]{0:T(128)S(1)} %get-tuple-element.73.units_ref) | copy-start | bytes 52
  12.5 1.0 copy-start.2
  17.1 3.3 %collective-permute-start.1 = (bf16[16,128,256]{2,1,0:T(8,128)(2,1)}, bf16[16,128,256]{2,1,0:T(8,128)(2,1)S(1)}, u32[]{:S(2)}, u32[]{:S(2)}) collective-permute-start(bf16[16,128,256]{2,1,0:T(8,128)(2,1)} %get-tuple-element.39), channel_id=1, source_target_pairs={{0,1},{1,0},{2,3},{3,2},{4,5},{5,4},{6,7},{7,6},{8,9},{9,8},{10,11... | collective-permute-start | bytes 3145736 | tf_op jit(solution)/shard_map/ppermute | solution.py:434
  19.0 18.5 %collective-permute-start.6 = (bf16[4,128,256]{2,1,0:T(8,128)(2,1)}, bf16[4,128,256]{2,1,0:T(8,128)(2,1)S(1)}, u32[]{:S(2)}, u32[]{:S(2)}) collective-permute-start(bf16[4,128,256]{2,1,0:T(8,128)(2,1)} %get-tuple-element.42), channel_id=1, source_target_pairs={{0,12},{1,13},{2,14},{3,15},{4,8},{5,9},{6,10},{7,11},{8,4},{9,5},... | collective-permute-start | bytes 786440 | tf_op jit(solution)/shard_map/ppermute | solution.py:434
  20.4 23.1 %copy-start.3 = (bf16[16,128,256]{2,1,0:T(8,128)(2,1)}, bf16[16,128,256]{2,1,0:T(8,128)(2,1)S(1)}, u32[]{:S(2)}) copy-start(bf16[16,128,256]{2,1,0:T(8,128)(2,1)S(1)} %collective-permute-done.1.passed_ref.rest_1_) | copy-start | bytes 3145732
  27.5 45.4 %copy-start = (s32[8]{0:T(128)S(1)}, s32[8]{0:T(128)}, u32[]{:S(2)}) copy-start(s32[8]{0:T(128)} %lengths_ref.1) | copy-start | bytes 100
  27.5 5.6 %collective-permute-start.4 = (bf16[1,16,640]{2,1,0:T(8,128)(2,1)S(1)}, bf16[1,16,640]{2,1,0:T(8,128)(2,1)S(1)}, u32[]{:S(2)}, u32[]{:S(2)}) collective-permute-start(bf16[1,16,640]{2,1,0:T(8,128)(2,1)S(1)} %bitcast.47), channel_id=1, source_target_pairs={{0,12},{1,13},{2,14},{3,15},{4,8},{5,9},{6,10},{7,11},{8,4},{9,5},... | collective-permute-start | bytes 61448 | tf_op jit(solution)/shard_map/ppermute | solution.py:434
  30.0 6.4 %collective-permute-start.3 = (bf16[1,16,640]{2,1,0:T(8,128)(2,1)S(1)}, bf16[1,16,640]{2,1,0:T(8,128)(2,1)S(1)}, u32[]{:S(2)}, u32[]{:S(2)}) collective-permute-start(bf16[1,16,640]{2,1,0:T(8,128)(2,1)S(1)} %bitcast.48), channel_id=1, source_target_pairs={{0,8},{1,9},{2,10},{3,11},{4,12},{5,13},{6,14},{7,15},{8,0},{9,1},... | collective-permute-start | bytes 61448 | tf_op jit(solution)/shard_map/ppermute | solution.py:434
  30.2 7.2 %collective-permute-start.2 = (bf16[1,16,640]{2,1,0:T(8,128)(2,1)S(1)}, bf16[1,16,640]{2,1,0:T(8,128)(2,1)S(1)}, u32[]{:S(2)}, u32[]{:S(2)}) collective-permute-start(bf16[1,16,640]{2,1,0:T(8,128)(2,1)S(1)} %bitcast.49), channel_id=1, source_target_pairs={{0,4},{1,5},{2,6},{3,7},{4,0},{5,1},{6,2},{7,3},{8,12},{9,13},{10,... | collective-permute-start | bytes 61448 | tf_op jit(solution)/shard_map/ppermute | solution.py:434
  33.2 37.9 %collective-permute-start.9 = (bf16[8,128,256]{2,1,0:T(8,128)(2,1)}, bf16[8,128,256]{2,1,0:T(8,128)(2,1)S(1)}, u32[]{:S(2)}, u32[]{:S(2)}) collective-permute-start(bf16[8,128,256]{2,1,0:T(8,128)(2,1)} %get-tuple-element.48), channel_id=1, source_target_pairs={{0,4},{1,5},{2,6},{3,7},{4,0},{5,1},{6,2},{7,3},{8,12},{9,13},{10,... | collective-permute-start | bytes 1572872 | tf_op jit(solution)/shard_map/ppermute | solution.py:434
  36.5 43.6 %collective-permute-start.10 = (bf16[8,128,256]{2,1,0:T(8,128)(2,1)}, bf16[8,128,256]{2,1,0:T(8,128)(2,1)S(1)}, u32[]{:S(2)}, u32[]{:S(2)}) collective-permute-start(bf16[8,128,256]{2,1,0:T(8,128)(2,1)} %get-tuple-element.49), channel_id=1, source_target_pairs={{0,6},{1,7},{2,4},{3,5},{4,2},{5,3},{6,0},{7,1},{8,14},{9,15},{10,... | collective-permute-start | bytes 1572872 | tf_op jit(solution)/shard_map/ppermute | solution.py:434
  37.5 36.6 %copy-start.9 = (bf16[4,128,256]{2,1,0:T(8,128)(2,1)}, bf16[4,128,256]{2,1,0:T(8,128)(2,1)S(1)}, u32[]{:S(2)}) copy-start(bf16[4,128,256]{2,1,0:T(8,128)(2,1)S(1)} %collective-permute-done.5.refs_7_) | copy-start | bytes 786436
  37.5 36.6 %copy-start.10 = (bf16[4,128,256]{2,1,0:T(8,128)(2,1)}, bf16[4,128,256]{2,1,0:T(8,128)(2,1)S(1)}, u32[]{:S(2)}) copy-start(bf16[4,128,256]{2,1,0:T(8,128)(2,1)S(1)} %collective-permute-done.6.refs_8_) | copy-start | bytes 786436
  37.5 4.5 %collective-permute-start.7 = (bf16[4,16,640]{2,1,0:T(8,128)(2,1)S(1)}, bf16[4,16,640]{2,1,0:T(8,128)(2,1)S(1)}, u32[]{:S(2)}, u32[]{:S(2)}) collective-permute-start(bf16[4,16,640]{2,1,0:T(8,128)(2,1)S(1)} %pad_maximum_fusion.1), channel_id=1, source_target_pairs={{0,2},{1,3},{2,0},{3,1},{4,6},{5,7},{6,4},{7,5},{8,10},{9,11},{10,... | collective-permute-start | bytes 245768 | tf_op jit(solution)/shard_map/ppermute | solution.py:434
  38.9 27.1 %collective-permute-start.11 = (bf16[4,128,256]{2,1,0:T(8,128)(2,1)S(1)}, bf16[4,128,256]{2,1,0:T(8,128)(2,1)S(1)}, u32[]{:S(2)}, u32[]{:S(2)}) collective-permute-start(bf16[4,128,256]{2,1,0:T(8,128)(2,1)S(1)} %get-tuple-element.53), channel_id=1, source_target_pairs={{0,8},{1,9},{2,10},{3,11},{4,12},{5,13},{6,14},{7,15},{8,0},{9,1},... | collective-permute-start | bytes 786440 | tf_op jit(solution)/shard_map/ppermute | solution.py:434
  42.0 1.5 %collective-permute-start.8 = (bf16[8,16,640]{2,1,0:T(8,128)(2,1)S(1)}, bf16[8,16,640]{2,1,0:T(8,128)(2,1)S(1)}, u32[]{:S(2)}, u32[]{:S(2)}) collective-permute-start(bf16[8,16,640]{2,1,0:T(8,128)(2,1)S(1)} %pad_maximum_fusion), channel_id=1, source_target_pairs={{0,1},{1,0},{2,3},{3,2},{4,5},{5,4},{6,7},{7,6},{8,9},{9,8},{10,11... | collective-permute-start | bytes 491528 | tf_op jit(solution)/shard_map/ppermute | solution.py:434
  43.5 3.0 %copy-start.8 = (bf16[16,16,640]{2,1,0:T(8,128)(2,1)}, bf16[16,16,640]{2,1,0:T(8,128)(2,1)S(1)}, u32[]{:S(2)}) copy-start(bf16[16,16,640]{2,1,0:T(8,128)(2,1)S(1)} %constant_dynamic-update-slice_fusion.rows_ref) | copy-start | bytes 983044
  51.3 35.6 %collective-permute-start.13 = (bf16[8,128,256]{2,1,0:T(8,128)(2,1)}, bf16[8,128,256]{2,1,0:T(8,128)(2,1)S(1)}, u32[]{:S(2)}, u32[]{:S(2)}) collective-permute-start(bf16[8,128,256]{2,1,0:T(8,128)(2,1)} %get-tuple-element.58), channel_id=1, source_target_pairs={{0,2},{1,3},{2,0},{3,1},{4,6},{5,7},{6,4},{7,5},{8,10},{9,11},{10,... | collective-permute-start | bytes 1572872 | tf_op jit(solution)/shard_map/ppermute | solution.py:434
  52.3 34.6 %collective-permute-start.12 = (bf16[4,128,256]{2,1,0:T(8,128)(2,1)}, bf16[4,128,256]{2,1,0:T(8,128)(2,1)S(1)}, u32[]{:S(2)}, u32[]{:S(2)}) collective-permute-start(bf16[4,128,256]{2,1,0:T(8,128)(2,1)} %get-tuple-element.54), channel_id=1, source_target_pairs={{0,12},{1,13},{2,14},{3,15},{4,8},{5,9},{6,10},{7,11},{8,4},{9,5},... | collective-permute-start | bytes 786440 | tf_op jit(solution)/shard_map/ppermute | solution.py:434
  66.0 21.0 %copy-start.12 = (bf16[4,128,256]{2,1,0:T(8,128)(2,1)}, bf16[4,128,256]{2,1,0:T(8,128)(2,1)S(1)}, u32[]{:S(2)}) copy-start(bf16[4,128,256]{2,1,0:T(8,128)(2,1)S(1)} %collective-permute-done.11.refs_7_) | copy-start | bytes 786436
  66.0 34.0 %collective-permute-start.15 = (bf16[8,128,256]{2,1,0:T(8,128)(2,1)}, bf16[8,128,256]{2,1,0:T(8,128)(2,1)S(1)}, u32[]{:S(2)}, u32[]{:S(2)}) collective-permute-start(bf16[8,128,256]{2,1,0:T(8,128)(2,1)} %get-tuple-element.63), channel_id=1, source_target_pairs={{0,10},{1,11},{2,8},{3,9},{4,14},{5,15},{6,12},{7,13},{8,2},{9,3},... | collective-permute-start | bytes 1572872 | tf_op jit(solution)/shard_map/ppermute | solution.py:434
  71.0 9.1 %copy-start.4 = (bf16[8,128,256]{2,1,0:T(8,128)(2,1)}, bf16[8,128,256]{2,1,0:T(8,128)(2,1)S(1)}, u32[]{:S(2)}) copy-start(bf16[8,128,256]{2,1,0:T(8,128)(2,1)S(1)} %collective-permute-done.9.refs_7_) | copy-start | bytes 1572868
  71.0 22.6 %collective-permute-start.14 = (bf16[144,128]{1,0:T(8,128)(2,1)}, bf16[144,128]{1,0:T(8,128)(2,1)S(1)}, u32[]{:S(2)}, u32[]{:S(2)}) collective-permute-start(bf16[144,128]{1,0:T(8,128)(2,1)} %get-tuple-element.57), channel_id=1, source_target_pairs={{0,14},{1,15},{2,12},{3,13},{4,10},{5,11},{6,8},{7,9},{8,6},{9,7},... | collective-permute-start | bytes 110600 | tf_op jit(solution)/shard_map/ppermute | solution.py:434
  74.1 22.5 %copy-start.1 = (s32[16]{0:T(128)S(1)}, s32[16]{0:T(128)}, u32[]{:S(2)}) copy-start(s32[16]{0:T(128)} %constant.99.clone.turn_ref) | copy-start | bytes 196
  80.1 0.8 copy-start.5
  86.9 0.7 copy-start.14
  87.0 0.9 copy-start.7
  93.7 6.4 %copy-start.16 = (bf16[144,128]{1,0:T(8,128)(2,1)}, bf16[144,128]{1,0:T(8,128)(2,1)S(1)}, u32[]{:S(2)}) copy-start(bf16[144,128]{1,0:T(8,128)(2,1)S(1)} %collective-permute-done.14.refs_7_) | copy-start | bytes 110596
  93.7 11.5 %collective-permute-start.16 = (bf16[4,128,256]{2,1,0:T(8,128)(2,1)}, bf16[4,128,256]{2,1,0:T(8,128)(2,1)S(1)}, u32[]{:S(2)}, u32[]{:S(2)}) collective-permute-start(bf16[4,128,256]{2,1,0:T(8,128)(2,1)} %get-tuple-element.67), channel_id=1, source_target_pairs={{0,14},{1,15},{2,12},{3,13},{4,10},{5,11},{6,8},{7,9},{8,6},{9,7},... | collective-permute-start | bytes 786440 | tf_op jit(solution)/shard_map/ppermute | solution.py:434
  100.0 0.8 copy-start.6
  105.2 32.8 %copy-start.11 = (bf16[4,128,256]{2,1,0:T(8,128)(2,1)}, bf16[4,128,256]{2,1,0:T(8,128)(2,1)S(1)}, u32[]{:S(2)}) copy-start(bf16[4,128,256]{2,1,0:T(8,128)(2,1)S(1)} %collective-permute-done.16.refs_4_) | copy-start | bytes 786436
  106.0 11.1 %collective-permute-start.19 = (bf16[1,4,2,1024]{3,2,1,0:T(2,128)(2,1)S(1)}, bf16[1,4,2,1024]{3,2,1,0:T(2,128)(2,1)S(1)}, u32[]{:S(2)}, u32[]{:S(2)}) collective-permute-start(bf16[1,4,2,1024]{3,2,1,0:T(2,128)(2,1)S(1)} %broadcast_in_dim_reshape.4), channel_id=1, source_target_pairs={{0,12},{1,13},{2,14},{3,15},{4,8},{5,9},{6,10},{7,11},{8,4},{9,5},... | collective-permute-start | bytes 49160 | tf_op jit(solution)/shard_map/ppermute | solution.py:434
  111.3 8.0 %collective-permute-start.18 = (bf16[1,4,2,1024]{3,2,1,0:T(2,128)(2,1)S(1)}, bf16[1,4,2,1024]{3,2,1,0:T(2,128)(2,1)S(1)}, u32[]{:S(2)}, u32[]{:S(2)}) collective-permute-start(bf16[1,4,2,1024]{3,2,1,0:T(2,128)(2,1)S(1)} %broadcast_in_dim_reshape.4), channel_id=1, source_target_pairs={{0,8},{1,9},{2,10},{3,11},{4,12},{5,13},{6,14},{7,15},{8,0},{9,1},... | collective-permute-start | bytes 49160 | tf_op jit(solution)/shard_map/ppermute | solution.py:434
  116.0 8.2 %collective-permute-start.17 = (bf16[1,4,2,1024]{3,2,1,0:T(2,128)(2,1)S(1)}, bf16[1,4,2,1024]{3,2,1,0:T(2,128)(2,1)S(1)}, u32[]{:S(2)}, u32[]{:S(2)}) collective-permute-start(bf16[1,4,2,1024]{3,2,1,0:T(2,128)(2,1)S(1)} %broadcast_in_dim_reshape.4), channel_id=1, source_target_pairs={{0,4},{1,5},{2,6},{3,7},{4,0},{5,1},{6,2},{7,3},{8,12},{9,13},{10,... | collective-permute-start | bytes 49160 | tf_op jit(solution)/shard_map/ppermute | solution.py:434
  116.0 15.6 %collective-permute-start.22 = (bf16[4,128,256]{2,1,0:T(8,128)(2,1)S(1)}, bf16[4,128,256]{2,1,0:T(8,128)(2,1)S(1)}, u32[]{:S(2)}, u32[]{:S(2)}) collective-permute-start(bf16[4,128,256]{2,1,0:T(8,128)(2,1)S(1)} %get-tuple-element.69), channel_id=1, source_target_pairs={{0,14},{1,15},{2,12},{3,13},{4,10},{5,11},{6,8},{7,9},{8,6},{9,7},... | collective-permute-start | bytes 786440 | tf_op jit(solution)/shard_map/ppermute | solution.py:434
  124.3 4.3 %collective-permute-start.20 = (bf16[4,4,2,1024]{3,2,1,0:T(2,128)(2,1)S(1)}, bf16[4,4,2,1024]{3,2,1,0:T(2,128)(2,1)S(1)}, u32[]{:S(2)}, u32[]{:S(2)}) collective-permute-start(bf16[4,4,2,1024]{3,2,1,0:T(2,128)(2,1)S(1)} %pad_maximum_fusion.2), channel_id=1, source_target_pairs={{0,2},{1,3},{2,0},{3,1},{4,6},{5,7},{6,4},{7,5},{8,10},{9,11},{10,... | collective-permute-start | bytes 196616 | tf_op jit(solution)/shard_map/ppermute | solution.py:434
  128.8 1.4 %collective-permute-start.21 = (bf16[8,4,2,1024]{3,2,1,0:T(2,128)(2,1)S(1)}, bf16[8,4,2,1024]{3,2,1,0:T(2,128)(2,1)S(1)}, u32[]{:S(2)}, u32[]{:S(2)}) collective-permute-start(bf16[8,4,2,1024]{3,2,1,0:T(2,128)(2,1)S(1)} %get-tuple-element.77), channel_id=1, source_target_pairs={{0,1},{1,0},{2,3},{3,2},{4,5},{5,4},{6,7},{7,6},{8,9},{9,8},{10,11... | collective-permute-start | bytes 393224 | tf_op jit(solution)/shard_map/ppermute | solution.py:434
  131.6 6.4 %copy-start.13 = (bf16[4,128,256]{2,1,0:T(8,128)(2,1)}, bf16[4,128,256]{2,1,0:T(8,128)(2,1)S(1)}, u32[]{:S(2)}) copy-start(bf16[4,128,256]{2,1,0:T(8,128)(2,1)S(1)} %collective-permute-done.22.refs_5_) | copy-start | bytes 786436

commit v12 on v7

--- a/solution.py
+++ b/solution.py
@@ -19,6 +19,7 @@
 QROWS = 2 * GROUP
 PER_UNIT = MAXCTX // PAGE
 VMEM_LIMIT = 56 * 1024 * 1024
+PLACE_LIMIT = 16 * 1024 * 1024
 
 rope_base = 10000.0
 
@@ -327,7 +328,7 @@
             pltpu.SemaphoreType.DMA((count,)),
             pltpu.SemaphoreType.DMA((count,)),
         ],
-        compiler_params=pltpu.CompilerParams(vmem_limit_bytes=VMEM_LIMIT),
+        compiler_params=pltpu.CompilerParams(vmem_limit_bytes=PLACE_LIMIT if started else VMEM_LIMIT),
         name="place_pages",
     )(*args)
     return result[0], result[1:3], result[3] if finish else None
@@ -660,9 +661,8 @@
         )
         attended = after(attended, moved_d)
         moved_d2 = send(after(piece(cross_far, 3), attended), d)
-        new_cache, _, _ = place(
-            [(moved_d, [d], 0), (moved_d2, [d + 1], 0)], None, new_cache, False, [], False
-        )
+        new_cache, _, _ = place([(moved_d, [d], 0)], None, new_cache, False, [], False)
+        new_cache, _, _ = place([(moved_d2, [d + 1], 0)], None, new_cache, False, [], False)
     else:
         own_requests, own_heads = own_units // KVH, own_units % KVH
         positions = own_lengths[:, None] + jnp.arange(2, dtype=jnp.int32)[None, :]

time: 138 us -> 137 us (level)
  the two profiles are of different devices: /device:TPU:8 before, /device:TPU:0 now
where the time goes in v12:
time: 137 us; the launch traced here: 135 us
  Pallas kernels  41.4 us (30%)
  starting transfers between devices  38 us (28%)
  waiting for transfers between devices  23.3 us (17%)
  matrix products  12.8 us (9%)
  local copies, waits for them, and re-layouts  12.2 us (9%)
  other arithmetic  6.16 us (4%)
    ppermute x23, starting transfers between devices, swap(): return lax.ppermute(values, 'tp', [(i, i ^ key) for i in range(devices)])  38 us
    pallas_call x6, Pallas kernels, place_pages(): pl.pallas_call(functools.partial(place_kernel, entries, started, attends,...  25.1 us
    ppermute x23, waiting for transfers between devices, swap(): return lax.ppermute(values, 'tp', [(i, i ^ key) for i in range(devices)])  23.3 us
    dot_general x1, matrix products, body(): lax.dot_general(flat_rows, qkv_weight, (((1,), (1,)), ((), ())), preferre...  7.16 us
    pallas_call x2, Pallas kernels, next_pack(): pl.pallas_call(functools.partial(next_pack_kernel, capacity, outs_pages,...  6.7 us
    dot_general x1, matrix products, body(): lax.dot_general(logical, out_weight, (((1,), (1,)), ((), ())), preferred_...  5.64 us
    unnamed x49, local copies, waits for them, and re-layouts  5.57 us
    pallas_call x1, Pallas kernels, first_pack(): pl.pallas_call(functools.partial(first_pack_kernel, devices, capacity, ou...  4.82 us
  transfers between devices with their start and end apart: 23, of which 9 were waited for; matrix products, arithmetic and copies ran while one was open for 19% of the time, Pallas kernels for 26%

profile of v12, /device:TPU:0, one launch (start us, length us, event | category | flops | bytes accessed | tf_op | source)
XLA Modules:
  0.0 135.1 jit_solution(18246521307433968502)
XLA Ops:
  0.6 4.8 %first_pack.1 = (bf16[4,128,256]{2,1,0:T(8,128)(2,1)}, bf16[16,128,256]{2,1,0:T(8,128)(2,1)}, s32[64]{0:T(128)}) custom-call(s32[64]{0:T(128)} %units_ref.1, s32[1024]{0:T(1024)} %old_ref.1, bf16[64,128,256]{2,1,0:T(8,128)(2,1)} %rest_0_.3), custom_call_target="tpu_custom_call" | custom-call | tf_op jit(solution)/shard_map/first_pack/pallas_call | solution.py:143
  5.5 4.1 %collective-permute-start.5 = (bf16[4,128,256]{2,1,0:T(8,128)(2,1)}, bf16[4,128,256]{2,1,0:T(8,128)(2,1)S(1)}, u32[]{:S(2)}, u32[]{:S(2)}) collective-permute-start(bf16[4,128,256]{2,1,0:T(8,128)(2,1)} %get-tuple-element.39), channel_id=1, source_target_pairs={{0,8},{1,9},{2,10},{3,11},{4,12},{5,13},{6,14},{7,15},{8,0},{9,1},... | collective-permute-start | bytes 786440 | tf_op jit(solution)/shard_map/ppermute | solution.py:435
  9.6 0.8 reshape.298
  10.3 0.7 compare_select_fusion.2
  11.3 0.8 select_reduce_fusion.2
  12.0 0.8 select_reduce_fusion.1
  12.9 0.9 select_reduce_fusion
  13.8 0.7 add_convert_fusion
  14.5 1.0 copy-done.13
  15.5 3.6 %next_pack.2 = (bf16[8,128,256]{2,1,0:T(8,128)(2,1)}, bf16[8,128,256]{2,1,0:T(8,128)(2,1)}, bf16[4,128,256]{2,1,0:T(8,128)(2,1)}, bf16[16,128,256]{2,1,0:T(8,128)(2,1)}) custom-call(s32[64]{0:T(128)} %get-tuple-element.35.order_ref.refs_1_, bf16[64,128,256]{2,1,0:T(8,128)(2,1)} %rest_0_.3, bf16[16,128,256]{2,1,0:T(8,128)(2,1)} %copy-done.13), custom_call_target="tpu_custom_call" | custom-call | tf_op jit(solution)/shard_map/next_pack/pallas_call | solution.py:161
  19.1 0.6 collective-permute-start.1
  19.9 0.2 convert_reduce_fusion.1
  20.1 0.1 fusion.1
  20.3 1.4 %collective-permute-start.6 = (bf16[4,128,256]{2,1,0:T(8,128)(2,1)}, bf16[4,128,256]{2,1,0:T(8,128)(2,1)S(1)}, u32[]{:S(2)}, u32[]{:S(2)}) collective-permute-start(bf16[4,128,256]{2,1,0:T(8,128)(2,1)} %get-tuple-element.40), channel_id=1, source_target_pairs={{0,12},{1,13},{2,14},{3,15},{4,8},{5,9},{6,10},{7,11},{8,4},{9,5},... | collective-permute-start | bytes 786440 | tf_op jit(solution)/shard_map/ppermute | solution.py:435
  21.7 0.5 collective-permute-done.1.passed_ref.rest_1_
  22.2 7.2 %convolution_convert_fusion = bf16[16,640]{1,0:T(8,128)(2,1)S(1)} fusion(bf16[16,8192]{1,0:T(8,128)(2,1)S(1)} %reshape.300, bf16[640,8192]{1,0:T(8,128)(2,1)} %param.9), kind=kOutput, calls=%fused_computation.3 | convolution fusion | flops 167782400 | bytes 10768384 | tf_op jit(solution)/shard_map/dot_general | solution.py:573
  29.4 2.0 %collective-permute-start.4 = (bf16[1,16,640]{2,1,0:T(8,128)(2,1)S(1)}, bf16[1,16,640]{2,1,0:T(8,128)(2,1)S(1)}, u32[]{:S(2)}, u32[]{:S(2)}) collective-permute-start(bf16[1,16,640]{2,1,0:T(8,128)(2,1)S(1)} %bitcast.47), channel_id=1, source_target_pairs={{0,12},{1,13},{2,14},{3,15},{4,8},{5,9},{6,10},{7,11},{8,4},{9,5},... | collective-permute-start | bytes 61448 | tf_op jit(solution)/shard_map/ppermute | solution.py:435
  31.3 1.1 collective-permute-start.3
  32.4 1.3 collective-permute-start.2
  33.8 0.7 pad_maximum_fusion.3
  34.5 0.5 collective-permute-done.4
  35.0 2.5 %collective-permute-start.9 = (bf16[8,128,256]{2,1,0:T(8,128)(2,1)}, bf16[8,128,256]{2,1,0:T(8,128)(2,1)S(1)}, u32[]{:S(2)}, u32[]{:S(2)}) collective-permute-start(bf16[8,128,256]{2,1,0:T(8,128)(2,1)} %get-tuple-element.46), channel_id=1, source_target_pairs={{0,4},{1,5},{2,6},{3,7},{4,0},{5,1},{6,2},{7,3},{8,12},{9,13},{10,... | collective-permute-start | bytes 1572872 | tf_op jit(solution)/shard_map/ppermute | solution.py:435
  37.5 1.0 collective-permute-start.10
  38.5 0.6 collective-permute-start.7
  39.2 0.9 fusion.5
  40.1 1.5 %collective-permute-start.11 = (bf16[4,128,256]{2,1,0:T(8,128)(2,1)}, bf16[4,128,256]{2,1,0:T(8,128)(2,1)S(1)}, u32[]{:S(2)}, u32[]{:S(2)}) collective-permute-start(bf16[4,128,256]{2,1,0:T(8,128)(2,1)} %get-tuple-element.51), channel_id=1, source_target_pairs={{0,8},{1,9},{2,10},{3,11},{4,12},{5,13},{6,14},{7,15},{8,0},{9,1},... | collective-permute-start | bytes 786440 | tf_op jit(solution)/shard_map/ppermute | solution.py:435
  41.6 1.5 %collective-permute-done.7 = bf16[4,16,640]{2,1,0:T(8,128)(2,1)S(1)} collective-permute-done((bf16[4,16,640]{2,1,0:T(8,128)(2,1)S(1)}, bf16[4,16,640]{2,1,0:T(8,128)(2,1)S(1)}, u32[]{:S(2)}, u32[]{:S(2)}) %collective-permute-start.7) | collective-permute-done | bytes 81952 | tf_op jit(solution)/shard_map/ppermute | solution.py:435
  43.2 1.3 collective-permute-done.8
  44.6 3.1 %next_pack.3 = (bf16[8,128,256]{2,1,0:T(8,128)(2,1)}, bf16[4,128,256]{2,1,0:T(8,128)(2,1)}, bf16[8,128,256]{2,1,0:T(8,128)(2,1)}) custom-call(s32[64]{0:T(128)} %get-tuple-element.35.order_ref.refs_1_, bf16[64,128,256]{2,1,0:T(8,128)(2,1)} %rest_0_.3, bf16[16,128,256]{2,1,0:T(8,128)(2,1)} %copy-done.14, bf16[16,128,256]{2,1,0:T(8,128)(2,1)} %copy-done.13), custom_call_target="tpu_custom_call" | custom-call | tf_op jit(solution)/shard_map/next_pack/pallas_call | solution.py:161
  47.7 0.6 collective-permute-start.13
  48.4 2.4 %collective-permute-start.12 = (bf16[4,128,256]{2,1,0:T(8,128)(2,1)}, bf16[4,128,256]{2,1,0:T(8,128)(2,1)S(1)}, u32[]{:S(2)}, u32[]{:S(2)}) collective-permute-start(bf16[4,128,256]{2,1,0:T(8,128)(2,1)} %get-tuple-element.52), channel_id=1, source_target_pairs={{0,12},{1,13},{2,14},{3,15},{4,8},{5,9},{6,10},{7,11},{8,4},{9,5},... | collective-permute-start | bytes 786440 | tf_op jit(solution)/shard_map/ppermute | solution.py:435
  50.8 0.1 select_reduce_fusion.4
  51.0 0.7 reshape.299.ids_ref
  51.6 4.7 %rows_and_parts.1 = (f32[4,16,128]{2,1,0:T(8,128)}, f32[8,256]{1,0:T(8,128)}, bf16[144,128]{1,0:T(8,128)(2,1)}) custom-call(s32[4]{0:T(128)} %copy-done.20, s32[16]{0:T(128)} %constant.99.clone.turn_ref, s32[64]{0:T(128)} %get-tuple-element.35.order_ref.refs_1_, s32[8]{0:T(128)} %reshape.299.ids_ref, s32[8]{0:T(128)} %lengths_ref.1, ...), custom_call_target="tpu_custom_call" | custom-call | tf_op jit(solution)/shard_map/rows_and_parts/pallas_call | solution.py:416
  56.4 10.8 %collective-permute-done.11.refs_7_ = bf16[4,128,256]{2,1,0:T(8,128)(2,1)S(1)} collective-permute-done((bf16[4,128,256]{2,1,0:T(8,128)(2,1)}, bf16[4,128,256]{2,1,0:T(8,128)(2,1)S(1)}, u32[]{:S(2)}, u32[]{:S(2)}) %collective-permute-start.11) | collective-permute-done | bytes 262176 | tf_op jit(solution)/shard_map/ppermute | solution.py:435
  67.1 4.3 %collective-permute-start.15 = (bf16[8,128,256]{2,1,0:T(8,128)(2,1)}, bf16[8,128,256]{2,1,0:T(8,128)(2,1)S(1)}, u32[]{:S(2)}, u32[]{:S(2)}) collective-permute-start(bf16[8,128,256]{2,1,0:T(8,128)(2,1)} %get-tuple-element.60), channel_id=1, source_target_pairs={{0,10},{1,11},{2,8},{3,9},{4,14},{5,15},{6,12},{7,13},{8,2},{9,3},... | collective-permute-start | bytes 1572872 | tf_op jit(solution)/shard_map/ppermute | solution.py:435
  71.4 0.6 select_reduce_fusion.3.refs_0_
  72.1 0.9 collective-permute-start.14
  72.9 1.2 gather_fusion
  74.2 6.0 %place_pages.6 = (bf16[64,128,256]{2,1,0:T(8,128)(2,1)}, f32[4,16,128]{2,1,0:T(8,128)}, f32[4,16,128]{2,1,0:T(8,128)}) custom-call(s32[64]{0:T(128)} %select_reduce_fusion.3.refs_0_, s32[64]{0:T(128)} %get-tuple-element.35.order_ref.refs_1_, s32[4]{0:T(128)} %gather_fusion, f32[8,256]{1,0:T(8,128)} %get-tuple-element.42.refs_3_, ...), custom_call_target="tpu_custom_call" | custom-call | tf_op jit(solution)/shard_map/place_pages/pallas_call | solution.py:320
  80.2 0.7 copy-done
  81.0 0.7 copy-done.2
  81.7 0.8 copy-done.5
  82.4 0.8 copy-done.6
  83.2 0.6 copy-done.7
  83.8 0.7 copy-done.9
  84.4 5.8 %place_pages.7 = (bf16[64,128,256]{2,1,0:T(8,128)(2,1)}, f32[4,16,128]{2,1,0:T(8,128)S(1)}, f32[4,16,128]{2,1,0:T(8,128)S(1)}) custom-call(s32[64]{0:T(128)S(1)} %copy-done.9, s32[64]{0:T(128)S(1)} %copy-done.4, s32[4]{0:T(128)S(1)} %copy-done.7, f32[8,256]{1,0:T(8,128)S(1)} %copy-done.2, ...), custom_call_target="tpu_custom_call", output_to_operand_aliasing={{0}: (9, {})} | custom-call | tf_op jit(solution)/shard_map/place_pages/pallas_call | solution.py:320
  90.2 5.7 %place_pages.8 = (bf16[64,128,256]{2,1,0:T(8,128)(2,1)}, f32[4,16,128]{2,1,0:T(8,128)S(1)}, f32[4,16,128]{2,1,0:T(8,128)S(1)}) custom-call(s32[64]{0:T(128)S(1)} %copy-done.9, s32[64]{0:T(128)S(1)} %copy-done.4, s32[4]{0:T(128)S(1)} %copy-done.7, f32[8,256]{1,0:T(8,128)S(1)} %copy-done.2, ...), custom_call_target="tpu_custom_call", output_to_operand_aliasing={{0}: (10, {})} | custom-call | tf_op jit(solution)/shard_map/place_pages/pallas_call | solution.py:320
  96.0 3.9 %collective-permute-start.16 = (bf16[4,128,256]{2,1,0:T(8,128)(2,1)}, bf16[4,128,256]{2,1,0:T(8,128)(2,1)S(1)}, u32[]{:S(2)}, u32[]{:S(2)}) collective-permute-start(bf16[4,128,256]{2,1,0:T(8,128)(2,1)} %get-tuple-element.64), channel_id=1, source_target_pairs={{0,14},{1,15},{2,12},{3,13},{4,10},{5,11},{6,8},{7,9},{8,6},{9,7},... | collective-permute-start | bytes 786440 | tf_op jit(solution)/shard_map/ppermute | solution.py:435
  99.9 0.8 gather_fusion.1
  100.7 4.2 %place_pages.9 = (bf16[64,128,256]{2,1,0:T(8,128)(2,1)}, f32[4,16,128]{2,1,0:T(8,128)}, f32[4,16,128]{2,1,0:T(8,128)}, bf16[4,16,128]{2,1,0:T(8,128)(2,1)S(1)}) custom-call(s32[64]{0:T(128)S(1)} %copy-done.10, s32[64]{0:T(128)S(1)} %copy-done.4, s32[4]{0:T(128)S(1)} %copy-done.8, f32[8,256]{1,0:T(8,128)S(1)} %copy-done.3, ...), custom_call_target="tpu_custom_call", output_to_operand_aliasing={{0}: (9, {})} | custom-call | tf_op jit(solution)/shard_map/place_pages/pallas_call | solution.py:320
  104.9 0.7 collective-permute-done.16.refs_4_
  105.6 3.0 %collective-permute-start.19 = (bf16[1,4,2,1024]{3,2,1,0:T(2,128)(2,1)S(1)}, bf16[1,4,2,1024]{3,2,1,0:T(2,128)(2,1)S(1)}, u32[]{:S(2)}, u32[]{:S(2)}) collective-permute-start(bf16[1,4,2,1024]{3,2,1,0:T(2,128)(2,1)S(1)} %broadcast_in_dim_reshape.4), channel_id=1, source_target_pairs={{0,12},{1,13},{2,14},{3,15},{4,8},{5,9},{6,10},{7,11},{8,4},{9,5},... | collective-permute-start | bytes 49160 | tf_op jit(solution)/shard_map/ppermute | solution.py:435
  108.6 4.6 %collective-permute-start.18 = (bf16[1,4,2,1024]{3,2,1,0:T(2,128)(2,1)S(1)}, bf16[1,4,2,1024]{3,2,1,0:T(2,128)(2,1)S(1)}, u32[]{:S(2)}, u32[]{:S(2)}) collective-permute-start(bf16[1,4,2,1024]{3,2,1,0:T(2,128)(2,1)S(1)} %broadcast_in_dim_reshape.4), channel_id=1, source_target_pairs={{0,8},{1,9},{2,10},{3,11},{4,12},{5,13},{6,14},{7,15},{8,0},{9,1},... | collective-permute-start | bytes 49160 | tf_op jit(solution)/shard_map/ppermute | solution.py:435
  113.3 2.0 %collective-permute-done.18 = bf16[1,4,2,1024]{3,2,1,0:T(2,128)(2,1)S(1)} collective-permute-done((bf16[1,4,2,1024]{3,2,1,0:T(2,128)(2,1)S(1)}, bf16[1,4,2,1024]{3,2,1,0:T(2,128)(2,1)S(1)}, u32[]{:S(2)}, u32[]{:S(2)}) %collective-permute-start.18) | collective-permute-done | bytes 16416 | tf_op jit(solution)/shard_map/ppermute | solution.py:435
  115.3 1.7 %collective-permute-done.17 = bf16[1,4,2,1024]{3,2,1,0:T(2,128)(2,1)S(1)} collective-permute-done((bf16[1,4,2,1024]{3,2,1,0:T(2,128)(2,1)S(1)}, bf16[1,4,2,1024]{3,2,1,0:T(2,128)(2,1)S(1)}, u32[]{:S(2)}, u32[]{:S(2)}) %collective-permute-start.17) | collective-permute-done | bytes 16416 | tf_op jit(solution)/shard_map/ppermute | solution.py:435
  117.3 4.2 %collective-permute-done.20 = bf16[4,4,2,1024]{3,2,1,0:T(2,128)(2,1)S(1)} collective-permute-done((bf16[4,4,2,1024]{3,2,1,0:T(2,128)(2,1)S(1)}, bf16[4,4,2,1024]{3,2,1,0:T(2,128)(2,1)S(1)}, u32[]{:S(2)}, u32[]{:S(2)}) %collective-permute-start.20) | collective-permute-done | bytes 65568 | tf_op jit(solution)/shard_map/ppermute | solution.py:435
  121.6 2.1 %collective-permute-start.22 = (bf16[4,128,256]{2,1,0:T(8,128)(2,1)S(1)}, bf16[4,128,256]{2,1,0:T(8,128)(2,1)S(1)}, u32[]{:S(2)}, u32[]{:S(2)}) collective-permute-start(bf16[4,128,256]{2,1,0:T(8,128)(2,1)S(1)} %copy-done.19), channel_id=1, source_target_pairs={{0,14},{1,15},{2,12},{3,13},{4,10},{5,11},{6,8},{7,9},{8,6},{9,7},... | collective-permute-start | bytes 786440 | tf_op jit(solution)/shard_map/ppermute | solution.py:435
  123.7 1.7 %place_pages.10.refs_5_ = bf16[64,128,256]{2,1,0:T(8,128)(2,1)} custom-call(s32[64]{0:T(128)S(1)} %copy-done.10, s32[64]{0:T(128)S(1)} %copy-done.4, s32[4]{0:T(128)S(1)} %copy-done.8, f32[8,256]{1,0:T(8,128)S(1)} %copy-done.3, bf16[4,128,256]{2,1,0:T(8,128)(2,1)S(1)} %collective-permute-done.16.refs_4_, ...), custom_call_target="tpu_custom_call", output_to_operand_aliasing={{}: (5, {})} | custom-call | tf_op jit(solution)/shard_map/place_pages/pallas_call | solution.py:320
  125.6 1.1 gather_fusion.2
  126.7 0.2 copy.20
  126.9 5.6 %convolution_convert_fusion.1 = bf16[16,512]{1,0:T(8,128)(2,1)S(1)} fusion(bf16[16,8192]{1,0:T(8,128)(2,1)S(1)} %bitcast.43, bf16[512,8192]{1,0:T(8,128)(2,1)} %param.10), kind=kOutput, calls=%fused_computation.4 | convolution fusion | flops 134225920 | bytes 8667136 | tf_op jit(solution)/shard_map/dot_general | solution.py:712
  132.5 0.6 reshape.304
  133.2 1.7 %place_pages.11 = bf16[64,128,256]{2,1,0:T(8,128)(2,1)} custom-call(s32[64]{0:T(128)S(1)} %copy-done.10, s32[64]{0:T(128)S(1)} %copy-done.4, s32[4]{0:T(128)S(1)} %copy-done.8, f32[8,256]{1,0:T(8,128)S(1)} %copy-done.3, bf16[4,128,256]{2,1,0:T(8,128)(2,1)S(1)} %collective-permute-done.22.refs_4_, ...), custom_call_target="tpu_custom_call", output_to_operand_aliasing={{}: (5, {})} | custom-call | tf_op jit(solution)/shard_map/place_pages/pallas_call | solution.py:320
  (88 shorter events, 1.5 us)
Async XLA Ops:
  0.6 19.2 %copy-start.18 = (bf16[8,2,8192]{2,1,0:T(2,128)(2,1)S(1)}, bf16[8,2,8192]{2,1,0:T(2,128)(2,1)}, u32[]{:S(2)}) copy-start(bf16[8,2,8192]{2,1,0:T(2,128)(2,1)} %param.8) | copy-start | bytes 786436
  5.5 33.0 %collective-permute-start.5 = (bf16[4,128,256]{2,1,0:T(8,128)(2,1)}, bf16[4,128,256]{2,1,0:T(8,128)(2,1)S(1)}, u32[]{:S(2)}, u32[]{:S(2)}) collective-permute-start(bf16[4,128,256]{2,1,0:T(8,128)(2,1)} %get-tuple-element.39), channel_id=1, source_target_pairs={{0,8},{1,9},{2,10},{3,11},{4,12},{5,13},{6,14},{7,15},{8,0},{9,1},... | collective-permute-start | bytes 786440 | tf_op jit(solution)/shard_map/ppermute | solution.py:435
  9.6 4.9 %collective-permute-start = (bf16[16,128,256]{2,1,0:T(8,128)(2,1)}, bf16[16,128,256]{2,1,0:T(8,128)(2,1)S(1)}, u32[]{:S(2)}, u32[]{:S(2)}) collective-permute-start(bf16[16,128,256]{2,1,0:T(8,128)(2,1)} %get-tuple-element.36), channel_id=1, source_target_pairs={{0,1},{1,0},{2,3},{3,2},{4,5},{5,4},{6,7},{7,6},{8,9},{9,8},{10,11... | collective-permute-start | bytes 3145736 | tf_op jit(solution)/shard_map/ppermute | solution.py:435
  11.1 27.4 %copy-start.20 = (s32[4]{0:T(128)}, s32[4]{0:T(128)S(1)}, u32[]{:S(2)}) copy-start(s32[4]{0:T(128)S(1)} %get-tuple-element.69.units_ref) | copy-start | bytes 52
  14.5 1.0 copy-start.13
  19.1 3.1 %collective-permute-start.1 = (bf16[16,128,256]{2,1,0:T(8,128)(2,1)}, bf16[16,128,256]{2,1,0:T(8,128)(2,1)S(1)}, u32[]{:S(2)}, u32[]{:S(2)}) collective-permute-start(bf16[16,128,256]{2,1,0:T(8,128)(2,1)} %get-tuple-element.37), channel_id=1, source_target_pairs={{0,1},{1,0},{2,3},{3,2},{4,5},{5,4},{6,7},{7,6},{8,9},{9,8},{10,11... | collective-permute-start | bytes 3145736 | tf_op jit(solution)/shard_map/ppermute | solution.py:435
  20.3 18.3 %collective-permute-start.6 = (bf16[4,128,256]{2,1,0:T(8,128)(2,1)}, bf16[4,128,256]{2,1,0:T(8,128)(2,1)S(1)}, u32[]{:S(2)}, u32[]{:S(2)}) collective-permute-start(bf16[4,128,256]{2,1,0:T(8,128)(2,1)} %get-tuple-element.40), channel_id=1, source_target_pairs={{0,12},{1,13},{2,14},{3,15},{4,8},{5,9},{6,10},{7,11},{8,4},{9,5},... | collective-permute-start | bytes 786440 | tf_op jit(solution)/shard_map/ppermute | solution.py:435
  22.2 22.3 %copy-start.14 = (bf16[16,128,256]{2,1,0:T(8,128)(2,1)}, bf16[16,128,256]{2,1,0:T(8,128)(2,1)S(1)}, u32[]{:S(2)}) copy-start(bf16[16,128,256]{2,1,0:T(8,128)(2,1)S(1)} %collective-permute-done.1.passed_ref.rest_1_) | copy-start | bytes 3145732
  29.4 43.6 %copy-start.11 = (s32[8]{0:T(128)S(1)}, s32[8]{0:T(128)}, u32[]{:S(2)}) copy-start(s32[8]{0:T(128)} %lengths_ref.1) | copy-start | bytes 100
  29.4 5.6 %collective-permute-start.4 = (bf16[1,16,640]{2,1,0:T(8,128)(2,1)S(1)}, bf16[1,16,640]{2,1,0:T(8,128)(2,1)S(1)}, u32[]{:S(2)}, u32[]{:S(2)}) collective-permute-start(bf16[1,16,640]{2,1,0:T(8,128)(2,1)S(1)} %bitcast.47), channel_id=1, source_target_pairs={{0,12},{1,13},{2,14},{3,15},{4,8},{5,9},{6,10},{7,11},{8,4},{9,5},... | collective-permute-start | bytes 61448 | tf_op jit(solution)/shard_map/ppermute | solution.py:435
  31.3 6.2 %collective-permute-start.3 = (bf16[1,16,640]{2,1,0:T(8,128)(2,1)S(1)}, bf16[1,16,640]{2,1,0:T(8,128)(2,1)S(1)}, u32[]{:S(2)}, u32[]{:S(2)}) collective-permute-start(bf16[1,16,640]{2,1,0:T(8,128)(2,1)S(1)} %bitcast.48), channel_id=1, source_target_pairs={{0,8},{1,9},{2,10},{3,11},{4,12},{5,13},{6,14},{7,15},{8,0},{9,1},... | collective-permute-start | bytes 61448 | tf_op jit(solution)/shard_map/ppermute | solution.py:435
  32.4 6.0 %collective-permute-start.2 = (bf16[1,16,640]{2,1,0:T(8,128)(2,1)S(1)}, bf16[1,16,640]{2,1,0:T(8,128)(2,1)S(1)}, u32[]{:S(2)}, u32[]{:S(2)}) collective-permute-start(bf16[1,16,640]{2,1,0:T(8,128)(2,1)S(1)} %bitcast.49), channel_id=1, source_target_pairs={{0,4},{1,5},{2,6},{3,7},{4,0},{5,1},{6,2},{7,3},{8,12},{9,13},{10,... | collective-permute-start | bytes 61448 | tf_op jit(solution)/shard_map/ppermute | solution.py:435
  35.0 37.0 %collective-permute-start.9 = (bf16[8,128,256]{2,1,0:T(8,128)(2,1)}, bf16[8,128,256]{2,1,0:T(8,128)(2,1)S(1)}, u32[]{:S(2)}, u32[]{:S(2)}) collective-permute-start(bf16[8,128,256]{2,1,0:T(8,128)(2,1)} %get-tuple-element.46), channel_id=1, source_target_pairs={{0,4},{1,5},{2,6},{3,7},{4,0},{5,1},{6,2},{7,3},{8,12},{9,13},{10,... | collective-permute-start | bytes 1572872 | tf_op jit(solution)/shard_map/ppermute | solution.py:435
  37.5 42.7 %collective-permute-start.10 = (bf16[8,128,256]{2,1,0:T(8,128)(2,1)}, bf16[8,128,256]{2,1,0:T(8,128)(2,1)S(1)}, u32[]{:S(2)}, u32[]{:S(2)}) collective-permute-start(bf16[8,128,256]{2,1,0:T(8,128)(2,1)} %get-tuple-element.47), channel_id=1, source_target_pairs={{0,6},{1,7},{2,4},{3,5},{4,2},{5,3},{6,0},{7,1},{8,14},{9,15},{10,... | collective-permute-start | bytes 1572872 | tf_op jit(solution)/shard_map/ppermute | solution.py:435
  38.5 35.6 %copy-start.16 = (bf16[4,128,256]{2,1,0:T(8,128)(2,1)}, bf16[4,128,256]{2,1,0:T(8,128)(2,1)S(1)}, u32[]{:S(2)}) copy-start(bf16[4,128,256]{2,1,0:T(8,128)(2,1)S(1)} %collective-permute-done.5.refs_7_) | copy-start | bytes 786436
  38.5 35.6 %copy-start.17 = (bf16[4,128,256]{2,1,0:T(8,128)(2,1)}, bf16[4,128,256]{2,1,0:T(8,128)(2,1)S(1)}, u32[]{:S(2)}) copy-start(bf16[4,128,256]{2,1,0:T(8,128)(2,1)S(1)} %collective-permute-done.6.refs_8_) | copy-start | bytes 786436
  38.5 4.5 %collective-permute-start.7 = (bf16[4,16,640]{2,1,0:T(8,128)(2,1)S(1)}, bf16[4,16,640]{2,1,0:T(8,128)(2,1)S(1)}, u32[]{:S(2)}, u32[]{:S(2)}) collective-permute-start(bf16[4,16,640]{2,1,0:T(8,128)(2,1)S(1)} %pad_maximum_fusion.1), channel_id=1, source_target_pairs={{0,2},{1,3},{2,0},{3,1},{4,6},{5,7},{6,4},{7,5},{8,10},{9,11},{10,... | collective-permute-start | bytes 245768 | tf_op jit(solution)/shard_map/ppermute | solution.py:435
  40.1 27.1 %collective-permute-start.11 = (bf16[4,128,256]{2,1,0:T(8,128)(2,1)}, bf16[4,128,256]{2,1,0:T(8,128)(2,1)S(1)}, u32[]{:S(2)}, u32[]{:S(2)}) collective-permute-start(bf16[4,128,256]{2,1,0:T(8,128)(2,1)} %get-tuple-element.51), channel_id=1, source_target_pairs={{0,8},{1,9},{2,10},{3,11},{4,12},{5,13},{6,14},{7,15},{8,0},{9,1},... | collective-permute-start | bytes 786440 | tf_op jit(solution)/shard_map/ppermute | solution.py:435
  43.1 1.5 %collective-permute-start.8 = (bf16[8,16,640]{2,1,0:T(8,128)(2,1)S(1)}, bf16[8,16,640]{2,1,0:T(8,128)(2,1)S(1)}, u32[]{:S(2)}, u32[]{:S(2)}) collective-permute-start(bf16[8,16,640]{2,1,0:T(8,128)(2,1)S(1)} %pad_maximum_fusion), channel_id=1, source_target_pairs={{0,1},{1,0},{2,3},{3,2},{4,5},{5,4},{6,7},{7,6},{8,9},{9,8},{10,11... | collective-permute-start | bytes 491528 | tf_op jit(solution)/shard_map/ppermute | solution.py:435
  44.6 7.1 %copy-start.15 = (bf16[16,16,640]{2,1,0:T(8,128)(2,1)}, bf16[16,16,640]{2,1,0:T(8,128)(2,1)S(1)}, u32[]{:S(2)}) copy-start(bf16[16,16,640]{2,1,0:T(8,128)(2,1)S(1)} %constant_dynamic-update-slice_fusion.rows_ref) | copy-start | bytes 983044
  44.6 35.6 %copy-start.4 = (s32[64]{0:T(128)S(1)}, s32[64]{0:T(128)}, u32[]{:S(2)}) copy-start(s32[64]{0:T(128)} %get-tuple-element.35.order_ref.refs_1_) | copy-start | bytes 772
  47.7 42.5 %collective-permute-start.13 = (bf16[8,128,256]{2,1,0:T(8,128)(2,1)}, bf16[8,128,256]{2,1,0:T(8,128)(2,1)S(1)}, u32[]{:S(2)}, u32[]{:S(2)}) collective-permute-start(bf16[8,128,256]{2,1,0:T(8,128)(2,1)} %get-tuple-element.54), channel_id=1, source_target_pairs={{0,2},{1,3},{2,0},{3,1},{4,6},{5,7},{6,4},{7,5},{8,10},{9,11},{10,... | collective-permute-start | bytes 1572872 | tf_op jit(solution)/shard_map/ppermute | solution.py:435
  48.4 41.8 %collective-permute-start.12 = (bf16[4,128,256]{2,1,0:T(8,128)(2,1)}, bf16[4,128,256]{2,1,0:T(8,128)(2,1)S(1)}, u32[]{:S(2)}, u32[]{:S(2)}) collective-permute-start(bf16[4,128,256]{2,1,0:T(8,128)(2,1)} %get-tuple-element.52), channel_id=1, source_target_pairs={{0,12},{1,13},{2,14},{3,15},{4,8},{5,9},{6,10},{7,11},{8,4},{9,5},... | collective-permute-start | bytes 786440 | tf_op jit(solution)/shard_map/ppermute | solution.py:435
  67.1 33.5 %collective-permute-start.15 = (bf16[8,128,256]{2,1,0:T(8,128)(2,1)}, bf16[8,128,256]{2,1,0:T(8,128)(2,1)S(1)}, u32[]{:S(2)}, u32[]{:S(2)}) collective-permute-start(bf16[8,128,256]{2,1,0:T(8,128)(2,1)} %get-tuple-element.60), channel_id=1, source_target_pairs={{0,10},{1,11},{2,8},{3,9},{4,14},{5,15},{6,12},{7,13},{8,2},{9,3},... | collective-permute-start | bytes 1572872 | tf_op jit(solution)/shard_map/ppermute | solution.py:435
  72.1 23.9 %collective-permute-start.14 = (bf16[144,128]{1,0:T(8,128)(2,1)}, bf16[144,128]{1,0:T(8,128)(2,1)S(1)}, u32[]{:S(2)}, u32[]{:S(2)}) collective-permute-start(bf16[144,128]{1,0:T(8,128)(2,1)} %get-tuple-element.58), channel_id=1, source_target_pairs={{0,14},{1,15},{2,12},{3,13},{4,10},{5,11},{6,8},{7,9},{8,6},{9,7},... | collective-permute-start | bytes 110600 | tf_op jit(solution)/shard_map/ppermute | solution.py:435
  74.1 25.8 %copy-start.12 = (s32[16]{0:T(128)S(1)}, s32[16]{0:T(128)}, u32[]{:S(2)}) copy-start(s32[16]{0:T(128)} %constant.99.clone.turn_ref) | copy-start | bytes 196
  74.1 26.6 %copy-start.1 = (f32[4,16,128]{2,1,0:T(8,128)S(1)}, f32[4,16,128]{2,1,0:T(8,128)}, u32[]{:S(2)}) copy-start(f32[4,16,128]{2,1,0:T(8,128)} %get-tuple-element.43.refs_4_) | copy-start | bytes 98308
  74.1 26.6 %copy-start.3 = (f32[8,256]{1,0:T(8,128)S(1)}, f32[8,256]{1,0:T(8,128)}, u32[]{:S(2)}) copy-start(f32[8,256]{1,0:T(8,128)} %get-tuple-element.42.refs_3_) | copy-start | bytes 24580
  74.1 26.6 %copy-start.8 = (s32[4]{0:T(128)S(1)}, s32[4]{0:T(128)}, u32[]{:S(2)}) copy-start(s32[4]{0:T(128)} %gather_fusion) | copy-start | bytes 52
  74.1 26.6 %copy-start.10 = (s32[64]{0:T(128)S(1)}, s32[64]{0:T(128)}, u32[]{:S(2)}) copy-start(s32[64]{0:T(128)} %select_reduce_fusion.3.refs_0_) | copy-start | bytes 772
  74.2 47.5 %copy-start.19 = (bf16[4,128,256]{2,1,0:T(8,128)(2,1)S(1)}, bf16[4,128,256]{2,1,0:T(8,128)(2,1)}, u32[]{:S(2)}) copy-start(bf16[4,128,256]{2,1,0:T(8,128)(2,1)} %get-tuple-element.66) | copy-start | bytes 786436
  80.2 0.8 copy-start
  81.0 0.7 copy-start.2
  81.6 0.8 copy-start.5
  82.4 0.8 copy-start.6
  83.2 0.6 copy-start.7
  83.8 0.7 copy-start.9
  96.0 9.6 %collective-permute-start.16 = (bf16[4,128,256]{2,1,0:T(8,128)(2,1)}, bf16[4,128,256]{2,1,0:T(8,128)(2,1)S(1)}, u32[]{:S(2)}, u32[]{:S(2)}) collective-permute-start(bf16[4,128,256]{2,1,0:T(8,128)(2,1)} %get-tuple-element.64), channel_id=1, source_target_pairs={{0,14},{1,15},{2,12},{3,13},{4,10},{5,11},{6,8},{7,9},{8,6},{9,7},... | collective-permute-start | bytes 786440 | tf_op jit(solution)/shard_map/ppermute | solution.py:435
  105.6 7.6 %collective-permute-start.19 = (bf16[1,4,2,1024]{3,2,1,0:T(2,128)(2,1)S(1)}, bf16[1,4,2,1024]{3,2,1,0:T(2,128)(2,1)S(1)}, u32[]{:S(2)}, u32[]{:S(2)}) collective-permute-start(bf16[1,4,2,1024]{3,2,1,0:T(2,128)(2,1)S(1)} %broadcast_in_dim_reshape.4), channel_id=1, source_target_pairs={{0,12},{1,13},{2,14},{3,15},{4,8},{5,9},{6,10},{7,11},{8,4},{9,5},... | collective-permute-start | bytes 49160 | tf_op jit(solution)/shard_map/ppermute | solution.py:435
  108.6 6.7 %collective-permute-start.18 = (bf16[1,4,2,1024]{3,2,1,0:T(2,128)(2,1)S(1)}, bf16[1,4,2,1024]{3,2,1,0:T(2,128)(2,1)S(1)}, u32[]{:S(2)}, u32[]{:S(2)}) collective-permute-start(bf16[1,4,2,1024]{3,2,1,0:T(2,128)(2,1)S(1)} %broadcast_in_dim_reshape.4), channel_id=1, source_target_pairs={{0,8},{1,9},{2,10},{3,11},{4,12},{5,13},{6,14},{7,15},{8,0},{9,1},... | collective-permute-start | bytes 49160 | tf_op jit(solution)/shard_map/ppermute | solution.py:435
  113.2 3.7 %collective-permute-start.17 = (bf16[1,4,2,1024]{3,2,1,0:T(2,128)(2,1)S(1)}, bf16[1,4,2,1024]{3,2,1,0:T(2,128)(2,1)S(1)}, u32[]{:S(2)}, u32[]{:S(2)}) collective-permute-start(bf16[1,4,2,1024]{3,2,1,0:T(2,128)(2,1)S(1)} %broadcast_in_dim_reshape.4), channel_id=1, source_target_pairs={{0,4},{1,5},{2,6},{3,7},{4,0},{5,1},{6,2},{7,3},{8,12},{9,13},{10,... | collective-permute-start | bytes 49160 | tf_op jit(solution)/shard_map/ppermute | solution.py:435
  117.1 4.3 %collective-permute-start.20 = (bf16[4,4,2,1024]{3,2,1,0:T(2,128)(2,1)S(1)}, bf16[4,4,2,1024]{3,2,1,0:T(2,128)(2,1)S(1)}, u32[]{:S(2)}, u32[]{:S(2)}) collective-permute-start(bf16[4,4,2,1024]{3,2,1,0:T(2,128)(2,1)S(1)} %pad_maximum_fusion.2), channel_id=1, source_target_pairs={{0,2},{1,3},{2,0},{3,1},{4,6},{5,7},{6,4},{7,5},{8,10},{9,11},{10,... | collective-permute-start | bytes 196616 | tf_op jit(solution)/shard_map/ppermute | solution.py:435
  121.5 3.9 %collective-permute-start.21 = (bf16[8,4,2,1024]{3,2,1,0:T(2,128)(2,1)S(1)}, bf16[8,4,2,1024]{3,2,1,0:T(2,128)(2,1)S(1)}, u32[]{:S(2)}, u32[]{:S(2)}) collective-permute-start(bf16[8,4,2,1024]{3,2,1,0:T(2,128)(2,1)S(1)} %get-tuple-element.73), channel_id=1, source_target_pairs={{0,1},{1,0},{2,3},{3,2},{4,5},{5,4},{6,7},{7,6},{8,9},{9,8},{10,11... | collective-permute-start | bytes 393224 | tf_op jit(solution)/shard_map/ppermute | solution.py:435
  121.6 11.6 %collective-permute-start.22 = (bf16[4,128,256]{2,1,0:T(8,128)(2,1)S(1)}, bf16[4,128,256]{2,1,0:T(8,128)(2,1)S(1)}, u32[]{:S(2)}, u32[]{:S(2)}) collective-permute-start(bf16[4,128,256]{2,1,0:T(8,128)(2,1)S(1)} %copy-done.19), channel_id=1, source_target_pairs={{0,14},{1,15},{2,12},{3,13},{4,10},{5,11},{6,8},{7,9},{8,6},{9,7},... | collective-permute-start | bytes 786440 | tf_op jit(solution)/shard_map/ppermute | solution.py:435

commit v13 on v12

--- a/solution.py
+++ b/solution.py
@@ -543,6 +543,14 @@
     else:
         table = source_dev * capacity + rank
 
+    flat_rows = hidden_states.reshape(requests * 2, D)
+    if pairwise:
+        flat_rows = after(flat_rows, cross_far)
+    own_part = lax.dot_general(
+        flat_rows, qkv_weight, (((1,), (1,)), ((), ())), preferred_element_type=jnp.float32
+    ).astype(jnp.bfloat16)
+    if pairwise:
+        new_units, old_pages, _ = lax.optimization_barrier((new_units, old_pages, own_part))
     slot_index = jnp.sum(
         jnp.where(
             new_units[None, :] == jnp.arange(total_units, dtype=jnp.int32)[:, None],
@@ -567,12 +575,6 @@
         picked = chosen[:, None, :] & (ranks[:, None, :] == wants)
         late_ids = jnp.sum(jnp.where(picked, ids[:, None, :], 0), axis=-1)
         late_ids = late_ids.reshape(2 * capacity).astype(jnp.int32)
-    flat_rows = hidden_states.reshape(requests * 2, D)
-    if pairwise:
-        flat_rows = after(flat_rows, cross_far)
-    own_part = lax.dot_general(
-        flat_rows, qkv_weight, (((1,), (1,)), ((), ())), preferred_element_type=jnp.float32
-    ).astype(jnp.bfloat16)
     if pairwise:
         positions = context_lengths[:, None] + jnp.arange(2, dtype=jnp.int32)[None, :]
         cosine, sine = rope_tables(positions.reshape(2 * requests))

time: 137 us -> 134 us (0.978)
  other arithmetic: 6.16 us -> 4.15 us
    unnamed x49 -> x51, local copies, waits for them, and re-layouts: 5.57 us -> 5.47 us
  transfers between devices with their start and end apart: 23 -> 23, of which waited for: 9 -> 9; matrix products, arithmetic and copies ran while one was open for 19% -> 17% of each run, Pallas kernels for 26% -> 26%
where the time goes in v13:
time: 134 us; the launch traced here: 132 us
  Pallas kernels  41.5 us (31%)
  starting transfers between devices  38.3 us (29%)
  waiting for transfers between devices  22.7 us (17%)
  matrix products  12.8 us (10%)
  local copies, waits for them, and re-layouts  11.4 us (9%)
  other arithmetic  4.15 us (3%)
    ppermute x23, starting transfers between devices, swap(): return lax.ppermute(values, 'tp', [(i, i ^ key) for i in range(devices)])  38.3 us
    pallas_call x6, Pallas kernels, place_pages(): pl.pallas_call(functools.partial(place_kernel, entries, started, attends,...  25 us
    ppermute x23, waiting for transfers between devices, swap(): return lax.ppermute(values, 'tp', [(i, i ^ key) for i in range(devices)])  22.7 us
    dot_general x1, matrix products, body(): lax.dot_general(flat_rows, qkv_weight, (((1,), (1,)), ((), ())), preferre...  7.16 us
    pallas_call x2, Pallas kernels, next_pack(): pl.pallas_call(functools.partial(next_pack_kernel, capacity, outs_pages,...  6.89 us
    dot_general x1, matrix products, body(): lax.dot_general(logical, out_weight, (((1,), (1,)), ((), ())), preferred_...  5.64 us
    unnamed x51, local copies, waits for them, and re-layouts  5.47 us
    pallas_call x1, Pallas kernels, first_pack(): pl.pallas_call(functools.partial(first_pack_kernel, devices, capacity, ou...  4.82 us
  transfers between devices with their start and end apart: 23, of which 9 were waited for; matrix products, arithmetic and copies ran while one was open for 17% of the time, Pallas kernels for 26%

profile of v13, /device:TPU:0, one launch (start us, length us, event | category | flops | bytes accessed | tf_op | source)
XLA Modules:
  0.0 132.1 jit_solution(7189474593925449106)
XLA Ops:
  0.7 4.8 %first_pack.1 = (bf16[4,128,256]{2,1,0:T(8,128)(2,1)}, bf16[16,128,256]{2,1,0:T(8,128)(2,1)}, s32[64]{0:T(128)}) custom-call(s32[64]{0:T(128)} %units_ref.1, s32[1024]{0:T(1024)} %old_ref.1, bf16[64,128,256]{2,1,0:T(8,128)(2,1)} %rest_0_.3), custom_call_target="tpu_custom_call" | custom-call | tf_op jit(solution)/shard_map/first_pack/pallas_call | solution.py:143
  5.5 4.1 %collective-permute-start.5 = (bf16[4,128,256]{2,1,0:T(8,128)(2,1)}, bf16[4,128,256]{2,1,0:T(8,128)(2,1)S(1)}, u32[]{:S(2)}, u32[]{:S(2)}) collective-permute-start(bf16[4,128,256]{2,1,0:T(8,128)(2,1)} %get-tuple-element.43), channel_id=1, source_target_pairs={{0,8},{1,9},{2,10},{3,11},{4,12},{5,13},{6,14},{7,15},{8,0},{9,1},... | collective-permute-start | bytes 786440 | tf_op jit(solution)/shard_map/ppermute | solution.py:435
  9.6 0.7 compare_select_fusion.2
  10.5 0.7 add_convert_fusion
  11.2 1.3 collective-permute-done.rest_1_.refs_6_.rest_2_
  12.5 1.0 copy-done.12
  13.5 3.8 %next_pack.2 = (bf16[8,128,256]{2,1,0:T(8,128)(2,1)}, bf16[8,128,256]{2,1,0:T(8,128)(2,1)}, bf16[4,128,256]{2,1,0:T(8,128)(2,1)}, bf16[16,128,256]{2,1,0:T(8,128)(2,1)}) custom-call(s32[64]{0:T(128)} %get-tuple-element.37.order_ref.refs_1_, bf16[64,128,256]{2,1,0:T(8,128)(2,1)} %rest_0_.3, bf16[16,128,256]{2,1,0:T(8,128)(2,1)} %copy-done.12), custom_call_target="tpu_custom_call" | custom-call | tf_op jit(solution)/shard_map/next_pack/pallas_call | solution.py:161
  17.2 0.2 collective-permute-start.1
  17.5 1.2 gather_fusion
  18.9 0.1 fusion.1
  19.0 0.7 pad_maximum_fusion.3
  19.7 0.2 select_reduce_fusion
  19.9 0.2 convert_reduce_fusion.1
  20.1 1.4 %collective-permute-start.6 = (bf16[4,128,256]{2,1,0:T(8,128)(2,1)}, bf16[4,128,256]{2,1,0:T(8,128)(2,1)}, u32[]{:S(2)}, u32[]{:S(2)}) collective-permute-start(bf16[4,128,256]{2,1,0:T(8,128)(2,1)} %get-tuple-element.44), channel_id=1, source_target_pairs={{0,12},{1,13},{2,14},{3,15},{4,8},{5,9},{6,10},{7,11},{8,4},{9,5},... | collective-permute-start | bytes 786440 | tf_op jit(solution)/shard_map/ppermute | solution.py:435
  21.6 7.2 %convolution_convert_fusion = bf16[16,640]{1,0:T(8,128)(2,1)S(1)} fusion(bf16[16,8192]{1,0:T(8,128)(2,1)S(1)} %reshape.298, bf16[640,8192]{1,0:T(8,128)(2,1)} %param.9), kind=kOutput, calls=%fused_computation.3 | convolution fusion | flops 167782400 | bytes 10768384 | tf_op jit(solution)/shard_map/dot_general | solution.py:549
  28.7 2.5 %collective-permute-start.4 = (bf16[1,16,640]{2,1,0:T(8,128)(2,1)S(1)}, bf16[1,16,640]{2,1,0:T(8,128)(2,1)S(1)}, u32[]{:S(2)}, u32[]{:S(2)}) collective-permute-start(bf16[1,16,640]{2,1,0:T(8,128)(2,1)S(1)} %bitcast.47), channel_id=1, source_target_pairs={{0,12},{1,13},{2,14},{3,15},{4,8},{5,9},{6,10},{7,11},{8,4},{9,5},... | collective-permute-start | bytes 61448 | tf_op jit(solution)/shard_map/ppermute | solution.py:435
  31.2 1.9 %collective-permute-start.2 = (bf16[1,16,640]{2,1,0:T(8,128)(2,1)S(1)}, bf16[1,16,640]{2,1,0:T(8,128)(2,1)S(1)}, u32[]{:S(2)}, u32[]{:S(2)}) collective-permute-start(bf16[1,16,640]{2,1,0:T(8,128)(2,1)S(1)} %bitcast.49), channel_id=1, source_target_pairs={{0,4},{1,5},{2,6},{3,7},{4,0},{5,1},{6,2},{7,3},{8,12},{9,13},{10,... | collective-permute-start | bytes 61448 | tf_op jit(solution)/shard_map/ppermute | solution.py:435
  33.1 0.9 fusion.5
  34.2 0.2 collective-permute-start.9
  34.4 0.5 copy-done.15
  34.9 3.8 %collective-permute-start.10 = (bf16[8,128,256]{2,1,0:T(8,128)(2,1)}, bf16[8,128,256]{2,1,0:T(8,128)(2,1)S(1)}, u32[]{:S(2)}, u32[]{:S(2)}) collective-permute-start(bf16[8,128,256]{2,1,0:T(8,128)(2,1)} %get-tuple-element.51), channel_id=1, source_target_pairs={{0,6},{1,7},{2,4},{3,5},{4,2},{5,3},{6,0},{7,1},{8,14},{9,15},{10,... | collective-permute-start | bytes 1572872 | tf_op jit(solution)/shard_map/ppermute | solution.py:435
  38.7 0.2 collective-permute-start.11
  38.9 1.3 %collective-permute-start.12 = (bf16[4,128,256]{2,1,0:T(8,128)(2,1)}, bf16[4,128,256]{2,1,0:T(8,128)(2,1)S(1)}, u32[]{:S(2)}, u32[]{:S(2)}) collective-permute-start(bf16[4,128,256]{2,1,0:T(8,128)(2,1)} %get-tuple-element.56), channel_id=1, source_target_pairs={{0,12},{1,13},{2,14},{3,15},{4,8},{5,9},{6,10},{7,11},{8,4},{9,5},... | collective-permute-start | bytes 786440 | tf_op jit(solution)/shard_map/ppermute | solution.py:435
  40.3 1.5 %collective-permute-start.7 = (bf16[4,16,640]{2,1,0:T(8,128)(2,1)S(1)}, bf16[4,16,640]{2,1,0:T(8,128)(2,1)S(1)}, u32[]{:S(2)}, u32[]{:S(2)}) collective-permute-start(bf16[4,16,640]{2,1,0:T(8,128)(2,1)S(1)} %pad_maximum_fusion.1), channel_id=1, source_target_pairs={{0,2},{1,3},{2,0},{3,1},{4,6},{5,7},{6,4},{7,5},{8,10},{9,11},{10,... | collective-permute-start | bytes 245768 | tf_op jit(solution)/shard_map/ppermute | solution.py:435
  41.8 0.2 select_reduce_fusion.1
  42.0 2.8 %collective-permute-done.7 = bf16[4,16,640]{2,1,0:T(8,128)(2,1)S(1)} collective-permute-done((bf16[4,16,640]{2,1,0:T(8,128)(2,1)S(1)}, bf16[4,16,640]{2,1,0:T(8,128)(2,1)S(1)}, u32[]{:S(2)}, u32[]{:S(2)}) %collective-permute-start.7) | collective-permute-done | bytes 81952 | tf_op jit(solution)/shard_map/ppermute | solution.py:435
  44.9 1.3 %collective-permute-done.8 = bf16[8,16,640]{2,1,0:T(8,128)(2,1)S(1)} collective-permute-done((bf16[8,16,640]{2,1,0:T(8,128)(2,1)S(1)}, bf16[8,16,640]{2,1,0:T(8,128)(2,1)S(1)}, u32[]{:S(2)}, u32[]{:S(2)}) %collective-permute-start.8) | collective-permute-done | bytes 163872 | tf_op jit(solution)/shard_map/ppermute | solution.py:435
  46.3 3.1 %next_pack.3 = (bf16[8,128,256]{2,1,0:T(8,128)(2,1)}, bf16[4,128,256]{2,1,0:T(8,128)(2,1)}, bf16[8,128,256]{2,1,0:T(8,128)(2,1)}) custom-call(s32[64]{0:T(128)} %get-tuple-element.37.order_ref.refs_1_, bf16[64,128,256]{2,1,0:T(8,128)(2,1)} %rest_0_.3, bf16[16,128,256]{2,1,0:T(8,128)(2,1)} %copy-done.13, bf16[16,128,256]{2,1,0:T(8,128)(2,1)} %copy-done.12), custom_call_target="tpu_custom_call" | custom-call | tf_op jit(solution)/shard_map/next_pack/pallas_call | solution.py:161
  49.5 1.5 %collective-permute-start.13 = (bf16[8,128,256]{2,1,0:T(8,128)(2,1)}, bf16[8,128,256]{2,1,0:T(8,128)(2,1)S(1)}, u32[]{:S(2)}, u32[]{:S(2)}) collective-permute-start(bf16[8,128,256]{2,1,0:T(8,128)(2,1)} %get-tuple-element.58), channel_id=1, source_target_pairs={{0,2},{1,3},{2,0},{3,1},{4,6},{5,7},{6,4},{7,5},{8,10},{9,11},{10,... | collective-permute-start | bytes 1572872 | tf_op jit(solution)/shard_map/ppermute | solution.py:435
  51.0 0.1 convert_reduce_fusion
  51.1 0.1 select_reduce_fusion.4
  51.3 0.6 reshape.300.ids_ref
  51.9 4.7 %rows_and_parts.1 = (f32[4,16,128]{2,1,0:T(8,128)}, f32[8,256]{1,0:T(8,128)}, bf16[144,128]{1,0:T(8,128)(2,1)}) custom-call(s32[4]{0:T(128)} %copy-done.20, s32[16]{0:T(128)} %constant.99.clone.turn_ref, s32[64]{0:T(128)} %get-tuple-element.37.order_ref.refs_1_, s32[8]{0:T(128)} %reshape.300.ids_ref, s32[8]{0:T(128)} %lengths_ref.1, ...), custom_call_target="tpu_custom_call" | custom-call | tf_op jit(solution)/shard_map/rows_and_parts/pallas_call | solution.py:416
  56.7 7.3 %collective-permute-done.11.refs_7_ = bf16[4,128,256]{2,1,0:T(8,128)(2,1)S(1)} collective-permute-done((bf16[4,128,256]{2,1,0:T(8,128)(2,1)}, bf16[4,128,256]{2,1,0:T(8,128)(2,1)S(1)}, u32[]{:S(2)}, u32[]{:S(2)}) %collective-permute-start.11) | collective-permute-done | bytes 262176 | tf_op jit(solution)/shard_map/ppermute | solution.py:435
  63.9 4.2 %collective-permute-start.15 = (bf16[8,128,256]{2,1,0:T(8,128)(2,1)}, bf16[8,128,256]{2,1,0:T(8,128)(2,1)S(1)}, u32[]{:S(2)}, u32[]{:S(2)}) collective-permute-start(bf16[8,128,256]{2,1,0:T(8,128)(2,1)} %get-tuple-element.64), channel_id=1, source_target_pairs={{0,10},{1,11},{2,8},{3,9},{4,14},{5,15},{6,12},{7,13},{8,2},{9,3},... | collective-permute-start | bytes 1572872 | tf_op jit(solution)/shard_map/ppermute | solution.py:435
  68.2 0.6 select_reduce_fusion.3.refs_0_
  68.8 2.4 %collective-permute-start.14 = (bf16[144,128]{1,0:T(8,128)(2,1)}, bf16[144,128]{1,0:T(8,128)(2,1)S(1)}, u32[]{:S(2)}, u32[]{:S(2)}) collective-permute-start(bf16[144,128]{1,0:T(8,128)(2,1)} %get-tuple-element.62), channel_id=1, source_target_pairs={{0,14},{1,15},{2,12},{3,13},{4,10},{5,11},{6,8},{7,9},{8,6},{9,7},... | collective-permute-start | bytes 110600 | tf_op jit(solution)/shard_map/ppermute | solution.py:435
  71.3 5.9 %place_pages.6 = (bf16[64,128,256]{2,1,0:T(8,128)(2,1)}, f32[4,16,128]{2,1,0:T(8,128)}, f32[4,16,128]{2,1,0:T(8,128)}) custom-call(s32[64]{0:T(128)} %select_reduce_fusion.3.refs_0_, s32[64]{0:T(128)} %get-tuple-element.37.order_ref.refs_1_, s32[4]{0:T(128)} %gather_fusion, f32[8,256]{1,0:T(8,128)} %get-tuple-element.46.refs_3_, ...), custom_call_target="tpu_custom_call" | custom-call | tf_op jit(solution)/shard_map/place_pages/pallas_call | solution.py:320
  77.3 0.7 copy-done
  78.0 0.7 copy-done.2
  78.7 0.8 copy-done.5
  79.5 0.8 copy-done.6
  80.2 0.7 copy-done.8
  80.9 5.8 %place_pages.7 = (bf16[64,128,256]{2,1,0:T(8,128)(2,1)}, f32[4,16,128]{2,1,0:T(8,128)S(1)}, f32[4,16,128]{2,1,0:T(8,128)S(1)}) custom-call(s32[64]{0:T(128)S(1)} %copy-done.8, s32[64]{0:T(128)S(1)} %copy-done.4, s32[4]{0:T(128)S(1)} %copy-done.7, f32[8,256]{1,0:T(8,128)S(1)} %copy-done.2, ...), custom_call_target="tpu_custom_call", output_to_operand_aliasing={{0}: (9, {})} | custom-call | tf_op jit(solution)/shard_map/place_pages/pallas_call | solution.py:320
  86.7 5.7 %place_pages.8 = (bf16[64,128,256]{2,1,0:T(8,128)(2,1)}, f32[4,16,128]{2,1,0:T(8,128)S(1)}, f32[4,16,128]{2,1,0:T(8,128)S(1)}) custom-call(s32[64]{0:T(128)S(1)} %copy-done.8, s32[64]{0:T(128)S(1)} %copy-done.4, s32[4]{0:T(128)S(1)} %copy-done.7, f32[8,256]{1,0:T(8,128)S(1)} %copy-done.2, ...), custom_call_target="tpu_custom_call", output_to_operand_aliasing={{0}: (10, {})} | custom-call | tf_op jit(solution)/shard_map/place_pages/pallas_call | solution.py:320
  92.4 2.4 %collective-permute-start.16 = (bf16[4,128,256]{2,1,0:T(8,128)(2,1)S(1)}, bf16[4,128,256]{2,1,0:T(8,128)(2,1)S(1)}, u32[]{:S(2)}, u32[]{:S(2)}) collective-permute-start(bf16[4,128,256]{2,1,0:T(8,128)(2,1)S(1)} %copy-done.21), channel_id=1, source_target_pairs={{0,14},{1,15},{2,12},{3,13},{4,10},{5,11},{6,8},{7,9},{8,6},{9,7},... | collective-permute-start | bytes 786440 | tf_op jit(solution)/shard_map/ppermute | solution.py:435
  94.9 0.8 gather_fusion.1
  95.7 2.4 %collective-permute-done.15.refs_8_ = bf16[8,128,256]{2,1,0:T(8,128)(2,1)S(1)} collective-permute-done((bf16[8,128,256]{2,1,0:T(8,128)(2,1)}, bf16[8,128,256]{2,1,0:T(8,128)(2,1)S(1)}, u32[]{:S(2)}, u32[]{:S(2)}) %collective-permute-start.15) | collective-permute-done | bytes 524320 | tf_op jit(solution)/shard_map/ppermute | solution.py:435
  98.1 4.2 %place_pages.9 = (bf16[64,128,256]{2,1,0:T(8,128)(2,1)}, f32[4,16,128]{2,1,0:T(8,128)}, f32[4,16,128]{2,1,0:T(8,128)}, bf16[4,16,128]{2,1,0:T(8,128)(2,1)S(1)}) custom-call(s32[64]{0:T(128)S(1)} %copy-done.9, s32[64]{0:T(128)S(1)} %copy-done.4, s32[4]{0:T(128)S(1)} %copy-done.7, f32[8,256]{1,0:T(8,128)S(1)} %copy-done.3, ...), custom_call_target="tpu_custom_call", output_to_operand_aliasing={{0}: (9, {})} | custom-call | tf_op jit(solution)/shard_map/place_pages/pallas_call | solution.py:320
  102.3 1.5 %collective-permute-start.19 = (bf16[1,4,2,1024]{3,2,1,0:T(2,128)(2,1)S(1)}, bf16[1,4,2,1024]{3,2,1,0:T(2,128)(2,1)S(1)}, u32[]{:S(2)}, u32[]{:S(2)}) collective-permute-start(bf16[1,4,2,1024]{3,2,1,0:T(2,128)(2,1)S(1)} %broadcast_in_dim_reshape.4), channel_id=1, source_target_pairs={{0,12},{1,13},{2,14},{3,15},{4,8},{5,9},{6,10},{7,11},{8,4},{9,5},... | collective-permute-start | bytes 49160 | tf_op jit(solution)/shard_map/ppermute | solution.py:435
  103.8 6.4 %collective-permute-start.18 = (bf16[1,4,2,1024]{3,2,1,0:T(2,128)(2,1)S(1)}, bf16[1,4,2,1024]{3,2,1,0:T(2,128)(2,1)S(1)}, u32[]{:S(2)}, u32[]{:S(2)}) collective-permute-start(bf16[1,4,2,1024]{3,2,1,0:T(2,128)(2,1)S(1)} %broadcast_in_dim_reshape.4), channel_id=1, source_target_pairs={{0,8},{1,9},{2,10},{3,11},{4,12},{5,13},{6,14},{7,15},{8,0},{9,1},... | collective-permute-start | bytes 49160 | tf_op jit(solution)/shard_map/ppermute | solution.py:435
  110.3 1.9 %collective-permute-done.18 = bf16[1,4,2,1024]{3,2,1,0:T(2,128)(2,1)S(1)} collective-permute-done((bf16[1,4,2,1024]{3,2,1,0:T(2,128)(2,1)S(1)}, bf16[1,4,2,1024]{3,2,1,0:T(2,128)(2,1)S(1)}, u32[]{:S(2)}, u32[]{:S(2)}) %collective-permute-start.18) | collective-permute-done | bytes 16416 | tf_op jit(solution)/shard_map/ppermute | solution.py:435
  112.1 1.9 %collective-permute-done.17 = bf16[1,4,2,1024]{3,2,1,0:T(2,128)(2,1)S(1)} collective-permute-done((bf16[1,4,2,1024]{3,2,1,0:T(2,128)(2,1)S(1)}, bf16[1,4,2,1024]{3,2,1,0:T(2,128)(2,1)S(1)}, u32[]{:S(2)}, u32[]{:S(2)}) %collective-permute-start.17) | collective-permute-done | bytes 16416 | tf_op jit(solution)/shard_map/ppermute | solution.py:435
  114.0 0.1 pad_maximum_fusion.2
  114.1 0.9 collective-permute-start.20
  115.0 3.4 %collective-permute-done.20 = bf16[4,4,2,1024]{3,2,1,0:T(2,128)(2,1)S(1)} collective-permute-done((bf16[4,4,2,1024]{3,2,1,0:T(2,128)(2,1)S(1)}, bf16[4,4,2,1024]{3,2,1,0:T(2,128)(2,1)S(1)}, u32[]{:S(2)}, u32[]{:S(2)}) %collective-permute-start.20) | collective-permute-done | bytes 65568 | tf_op jit(solution)/shard_map/ppermute | solution.py:435
  118.6 1.7 %collective-permute-start.22 = (bf16[4,128,256]{2,1,0:T(8,128)(2,1)S(1)}, bf16[4,128,256]{2,1,0:T(8,128)(2,1)S(1)}, u32[]{:S(2)}, u32[]{:S(2)}) collective-permute-start(bf16[4,128,256]{2,1,0:T(8,128)(2,1)S(1)} %copy-done.17), channel_id=1, source_target_pairs={{0,14},{1,15},{2,12},{3,13},{4,10},{5,11},{6,8},{7,9},{8,6},{9,7},... | collective-permute-start | bytes 786440 | tf_op jit(solution)/shard_map/ppermute | solution.py:435
  120.3 1.7 %place_pages.10.refs_5_ = bf16[64,128,256]{2,1,0:T(8,128)(2,1)} custom-call(s32[64]{0:T(128)S(1)} %copy-done.9, s32[64]{0:T(128)S(1)} %copy-done.4, s32[4]{0:T(128)S(1)} %copy-done.7, f32[8,256]{1,0:T(8,128)S(1)} %copy-done.3, bf16[4,128,256]{2,1,0:T(8,128)(2,1)S(1)} %collective-permute-done.16.refs_4_, ...), custom_call_target="tpu_custom_call", output_to_operand_aliasing={{}: (5, {})} | custom-call | tf_op jit(solution)/shard_map/place_pages/pallas_call | solution.py:320
  122.1 1.1 gather_fusion.2
  123.3 0.2 copy.20
  123.5 5.6 %convolution_convert_fusion.1 = bf16[16,512]{1,0:T(8,128)(2,1)S(1)} fusion(bf16[16,8192]{1,0:T(8,128)(2,1)S(1)} %bitcast.43, bf16[512,8192]{1,0:T(8,128)(2,1)} %param.10), kind=kOutput, calls=%fused_computation.4 | convolution fusion | flops 134225920 | bytes 8667136 | tf_op jit(solution)/shard_map/dot_general | solution.py:714
  129.1 0.6 reshape.304
  129.8 0.4 collective-permute-done.22.refs_4_
  130.2 1.7 %place_pages.11 = bf16[64,128,256]{2,1,0:T(8,128)(2,1)} custom-call(s32[64]{0:T(128)S(1)} %copy-done.9, s32[64]{0:T(128)S(1)} %copy-done.4, s32[4]{0:T(128)S(1)} %copy-done.7, f32[8,256]{1,0:T(8,128)S(1)} %copy-done.3, bf16[4,128,256]{2,1,0:T(8,128)(2,1)S(1)} %collective-permute-done.22.refs_4_, ...), custom_call_target="tpu_custom_call", output_to_operand_aliasing={{}: (5, {})} | custom-call | tf_op jit(solution)/shard_map/place_pages/pallas_call | solution.py:320
  (90 shorter events, 1.4 us)
Async XLA Ops:
  0.6 19.1 %copy-start.18 = (s32[1024]{0:T(1024)S(1)}, s32[1024]{0:T(1024)}, u32[]{:S(2)}) copy-start(s32[1024]{0:T(1024)} %old_ref.1) | copy-start | bytes 12292
  0.6 16.9 %copy-start.10 = (s32[8]{0:T(128)S(1)}, s32[8]{0:T(128)}, u32[]{:S(2)}) copy-start(s32[8]{0:T(128)} %lengths_ref.1) | copy-start | bytes 100
  0.7 18.2 %copy-start.16 = (bf16[8,2,8192]{2,1,0:T(2,128)(2,1)S(1)}, bf16[8,2,8192]{2,1,0:T(2,128)(2,1)}, u32[]{:S(2)}) copy-start(bf16[8,2,8192]{2,1,0:T(2,128)(2,1)} %param.8) | copy-start | bytes 786436
  5.5 28.7 %collective-permute-start.5 = (bf16[4,128,256]{2,1,0:T(8,128)(2,1)}, bf16[4,128,256]{2,1,0:T(8,128)(2,1)S(1)}, u32[]{:S(2)}, u32[]{:S(2)}) collective-permute-start(bf16[4,128,256]{2,1,0:T(8,128)(2,1)} %get-tuple-element.43), channel_id=1, source_target_pairs={{0,8},{1,9},{2,10},{3,11},{4,12},{5,13},{6,14},{7,15},{8,0},{9,1},... | collective-permute-start | bytes 786440 | tf_op jit(solution)/shard_map/ppermute | solution.py:435
  9.6 2.9 %collective-permute-start = (bf16[16,128,256]{2,1,0:T(8,128)(2,1)}, bf16[16,128,256]{2,1,0:T(8,128)(2,1)S(1)}, u32[]{:S(2)}, u32[]{:S(2)}) collective-permute-start(bf16[16,128,256]{2,1,0:T(8,128)(2,1)} %get-tuple-element.38), channel_id=1, source_target_pairs={{0,1},{1,0},{2,3},{3,2},{4,5},{5,4},{6,7},{7,6},{8,9},{9,8},{10,11... | collective-permute-start | bytes 3145736 | tf_op jit(solution)/shard_map/ppermute | solution.py:435
  10.3 18.4 %copy-start.20 = (s32[4]{0:T(128)}, s32[4]{0:T(128)S(1)}, u32[]{:S(2)}) copy-start(s32[4]{0:T(128)S(1)} %get-tuple-element.73.units_ref) | copy-start | bytes 52
  12.5 1.0 copy-start.12
  13.5 28.3 %copy-start.19 = (s32[64]{0:T(128)S(1)}, s32[64]{0:T(128)}, u32[]{:S(2)}) copy-start(s32[64]{0:T(128)} %units_ref.1) | copy-start | bytes 772
  17.2 4.4 %collective-permute-start.1 = (bf16[16,128,256]{2,1,0:T(8,128)(2,1)}, bf16[16,128,256]{2,1,0:T(8,128)(2,1)S(1)}, u32[]{:S(2)}, u32[]{:S(2)}) collective-permute-start(bf16[16,128,256]{2,1,0:T(8,128)(2,1)} %get-tuple-element.39), channel_id=1, source_target_pairs={{0,1},{1,0},{2,3},{3,2},{4,5},{5,4},{6,7},{7,6},{8,9},{9,8},{10,11... | collective-permute-start | bytes 3145736 | tf_op jit(solution)/shard_map/ppermute | solution.py:435
  20.1 20.1 %collective-permute-start.6 = (bf16[4,128,256]{2,1,0:T(8,128)(2,1)}, bf16[4,128,256]{2,1,0:T(8,128)(2,1)}, u32[]{:S(2)}, u32[]{:S(2)}) collective-permute-start(bf16[4,128,256]{2,1,0:T(8,128)(2,1)} %get-tuple-element.44), channel_id=1, source_target_pairs={{0,12},{1,13},{2,14},{3,15},{4,8},{5,9},{6,10},{7,11},{8,4},{9,5},... | collective-permute-start | bytes 786440 | tf_op jit(solution)/shard_map/ppermute | solution.py:435
  21.6 24.7 %copy-start.13 = (bf16[16,128,256]{2,1,0:T(8,128)(2,1)}, bf16[16,128,256]{2,1,0:T(8,128)(2,1)S(1)}, u32[]{:S(2)}) copy-start(bf16[16,128,256]{2,1,0:T(8,128)(2,1)S(1)} %collective-permute-done.1.passed_ref.rest_1_) | copy-start | bytes 3145732
  28.7 5.6 %collective-permute-start.4 = (bf16[1,16,640]{2,1,0:T(8,128)(2,1)S(1)}, bf16[1,16,640]{2,1,0:T(8,128)(2,1)S(1)}, u32[]{:S(2)}, u32[]{:S(2)}) collective-permute-start(bf16[1,16,640]{2,1,0:T(8,128)(2,1)S(1)} %bitcast.47), channel_id=1, source_target_pairs={{0,12},{1,13},{2,14},{3,15},{4,8},{5,9},{6,10},{7,11},{8,4},{9,5},... | collective-permute-start | bytes 61448 | tf_op jit(solution)/shard_map/ppermute | solution.py:435
  31.2 7.5 %collective-permute-start.3 = (bf16[1,16,640]{2,1,0:T(8,128)(2,1)S(1)}, bf16[1,16,640]{2,1,0:T(8,128)(2,1)S(1)}, u32[]{:S(2)}, u32[]{:S(2)}) collective-permute-start(bf16[1,16,640]{2,1,0:T(8,128)(2,1)S(1)} %bitcast.48), channel_id=1, source_target_pairs={{0,8},{1,9},{2,10},{3,11},{4,12},{5,13},{6,14},{7,15},{8,0},{9,1},... | collective-permute-start | bytes 61448 | tf_op jit(solution)/shard_map/ppermute | solution.py:435
  31.2 7.6 %collective-permute-start.2 = (bf16[1,16,640]{2,1,0:T(8,128)(2,1)S(1)}, bf16[1,16,640]{2,1,0:T(8,128)(2,1)S(1)}, u32[]{:S(2)}, u32[]{:S(2)}) collective-permute-start(bf16[1,16,640]{2,1,0:T(8,128)(2,1)S(1)} %bitcast.49), channel_id=1, source_target_pairs={{0,4},{1,5},{2,6},{3,7},{4,0},{5,1},{6,2},{7,3},{8,12},{9,13},{10,... | collective-permute-start | bytes 61448 | tf_op jit(solution)/shard_map/ppermute | solution.py:435
  34.2 0.7 copy-start.15
  34.2 34.6 %collective-permute-start.9 = (bf16[8,128,256]{2,1,0:T(8,128)(2,1)}, bf16[8,128,256]{2,1,0:T(8,128)(2,1)S(1)}, u32[]{:S(2)}, u32[]{:S(2)}) collective-permute-start(bf16[8,128,256]{2,1,0:T(8,128)(2,1)} %get-tuple-element.50), channel_id=1, source_target_pairs={{0,4},{1,5},{2,6},{3,7},{4,0},{5,1},{6,2},{7,3},{8,12},{9,13},{10,... | collective-permute-start | bytes 1572872 | tf_op jit(solution)/shard_map/ppermute | solution.py:435
  34.9 42.3 %collective-permute-start.10 = (bf16[8,128,256]{2,1,0:T(8,128)(2,1)}, bf16[8,128,256]{2,1,0:T(8,128)(2,1)S(1)}, u32[]{:S(2)}, u32[]{:S(2)}) collective-permute-start(bf16[8,128,256]{2,1,0:T(8,128)(2,1)} %get-tuple-element.51), channel_id=1, source_target_pairs={{0,6},{1,7},{2,4},{3,5},{4,2},{5,3},{6,0},{7,1},{8,14},{9,15},{10,... | collective-permute-start | bytes 1572872 | tf_op jit(solution)/shard_map/ppermute | solution.py:435
  38.7 25.3 %collective-permute-start.11 = (bf16[4,128,256]{2,1,0:T(8,128)(2,1)}, bf16[4,128,256]{2,1,0:T(8,128)(2,1)S(1)}, u32[]{:S(2)}, u32[]{:S(2)}) collective-permute-start(bf16[4,128,256]{2,1,0:T(8,128)(2,1)} %get-tuple-element.55), channel_id=1, source_target_pairs={{0,8},{1,9},{2,10},{3,11},{4,12},{5,13},{6,14},{7,15},{8,0},{9,1},... | collective-permute-start | bytes 786440 | tf_op jit(solution)/shard_map/ppermute | solution.py:435
  38.9 47.8 %collective-permute-start.12 = (bf16[4,128,256]{2,1,0:T(8,128)(2,1)}, bf16[4,128,256]{2,1,0:T(8,128)(2,1)S(1)}, u32[]{:S(2)}, u32[]{:S(2)}) collective-permute-start(bf16[4,128,256]{2,1,0:T(8,128)(2,1)} %get-tuple-element.56), channel_id=1, source_target_pairs={{0,12},{1,13},{2,14},{3,15},{4,8},{5,9},{6,10},{7,11},{8,4},{9,5},... | collective-permute-start | bytes 786440 | tf_op jit(solution)/shard_map/ppermute | solution.py:435
  40.3 4.5 %collective-permute-start.7 = (bf16[4,16,640]{2,1,0:T(8,128)(2,1)S(1)}, bf16[4,16,640]{2,1,0:T(8,128)(2,1)S(1)}, u32[]{:S(2)}, u32[]{:S(2)}) collective-permute-start(bf16[4,16,640]{2,1,0:T(8,128)(2,1)S(1)} %pad_maximum_fusion.1), channel_id=1, source_target_pairs={{0,2},{1,3},{2,0},{3,1},{4,6},{5,7},{6,4},{7,5},{8,10},{9,11},{10,... | collective-permute-start | bytes 245768 | tf_op jit(solution)/shard_map/ppermute | solution.py:435
  44.8 1.5 %collective-permute-start.8 = (bf16[8,16,640]{2,1,0:T(8,128)(2,1)S(1)}, bf16[8,16,640]{2,1,0:T(8,128)(2,1)S(1)}, u32[]{:S(2)}, u32[]{:S(2)}) collective-permute-start(bf16[8,16,640]{2,1,0:T(8,128)(2,1)S(1)} %pad_maximum_fusion), channel_id=1, source_target_pairs={{0,1},{1,0},{2,3},{3,2},{4,5},{5,4},{6,7},{7,6},{8,9},{9,8},{10,11... | collective-permute-start | bytes 491528 | tf_op jit(solution)/shard_map/ppermute | solution.py:435
  46.3 5.6 %copy-start.14 = (bf16[16,16,640]{2,1,0:T(8,128)(2,1)}, bf16[16,16,640]{2,1,0:T(8,128)(2,1)S(1)}, u32[]{:S(2)}) copy-start(bf16[16,16,640]{2,1,0:T(8,128)(2,1)S(1)} %constant_dynamic-update-slice_fusion.rows_ref) | copy-start | bytes 983044
  46.3 30.9 %copy-start.4 = (s32[64]{0:T(128)S(1)}, s32[64]{0:T(128)}, u32[]{:S(2)}) copy-start(s32[64]{0:T(128)} %get-tuple-element.37.order_ref.refs_1_) | copy-start | bytes 772
  46.3 30.9 %copy-start.7 = (s32[4]{0:T(128)S(1)}, s32[4]{0:T(128)}, u32[]{:S(2)}) copy-start(s32[4]{0:T(128)} %gather_fusion) | copy-start | bytes 52
  49.5 37.2 %collective-permute-start.13 = (bf16[8,128,256]{2,1,0:T(8,128)(2,1)}, bf16[8,128,256]{2,1,0:T(8,128)(2,1)S(1)}, u32[]{:S(2)}, u32[]{:S(2)}) collective-permute-start(bf16[8,128,256]{2,1,0:T(8,128)(2,1)} %get-tuple-element.58), channel_id=1, source_target_pairs={{0,2},{1,3},{2,0},{3,1},{4,6},{5,7},{6,4},{7,5},{8,10},{9,11},{10,... | collective-permute-start | bytes 1572872 | tf_op jit(solution)/shard_map/ppermute | solution.py:435
  56.6 35.8 %copy-start.21 = (bf16[4,128,256]{2,1,0:T(8,128)(2,1)S(1)}, bf16[4,128,256]{2,1,0:T(8,128)(2,1)}, u32[]{:S(2)}) copy-start(bf16[4,128,256]{2,1,0:T(8,128)(2,1)} %get-tuple-element.68) | copy-start | bytes 786436
  56.6 38.2 %copy-start.11 = (s32[16]{0:T(128)S(1)}, s32[16]{0:T(128)}, u32[]{:S(2)}) copy-start(s32[16]{0:T(128)} %constant.99.clone.turn_ref) | copy-start | bytes 196
  63.9 34.2 %collective-permute-start.15 = (bf16[8,128,256]{2,1,0:T(8,128)(2,1)}, bf16[8,128,256]{2,1,0:T(8,128)(2,1)S(1)}, u32[]{:S(2)}, u32[]{:S(2)}) collective-permute-start(bf16[8,128,256]{2,1,0:T(8,128)(2,1)} %get-tuple-element.64), channel_id=1, source_target_pairs={{0,10},{1,11},{2,8},{3,9},{4,14},{5,15},{6,12},{7,13},{8,2},{9,3},... | collective-permute-start | bytes 1572872 | tf_op jit(solution)/shard_map/ppermute | solution.py:435
  68.8 23.6 %collective-permute-start.14 = (bf16[144,128]{1,0:T(8,128)(2,1)}, bf16[144,128]{1,0:T(8,128)(2,1)S(1)}, u32[]{:S(2)}, u32[]{:S(2)}) collective-permute-start(bf16[144,128]{1,0:T(8,128)(2,1)} %get-tuple-element.62), channel_id=1, source_target_pairs={{0,14},{1,15},{2,12},{3,13},{4,10},{5,11},{6,8},{7,9},{8,6},{9,7},... | collective-permute-start | bytes 110600 | tf_op jit(solution)/shard_map/ppermute | solution.py:435
  71.3 26.8 %copy-start.1 = (f32[4,16,128]{2,1,0:T(8,128)S(1)}, f32[4,16,128]{2,1,0:T(8,128)}, u32[]{:S(2)}) copy-start(f32[4,16,128]{2,1,0:T(8,128)} %get-tuple-element.47.refs_4_) | copy-start | bytes 98308
  71.3 26.8 %copy-start.3 = (f32[8,256]{1,0:T(8,128)S(1)}, f32[8,256]{1,0:T(8,128)}, u32[]{:S(2)}) copy-start(f32[8,256]{1,0:T(8,128)} %get-tuple-element.46.refs_3_) | copy-start | bytes 24580
  71.3 26.8 %copy-start.9 = (s32[64]{0:T(128)S(1)}, s32[64]{0:T(128)}, u32[]{:S(2)}) copy-start(s32[64]{0:T(128)} %select_reduce_fusion.3.refs_0_) | copy-start | bytes 772
  71.3 47.3 %copy-start.17 = (bf16[4,128,256]{2,1,0:T(8,128)(2,1)S(1)}, bf16[4,128,256]{2,1,0:T(8,128)(2,1)}, u32[]{:S(2)}) copy-start(bf16[4,128,256]{2,1,0:T(8,128)(2,1)} %get-tuple-element.70) | copy-start | bytes 786436
  77.2 0.8 copy-start
  78.0 0.7 copy-start.2
  78.7 0.8 copy-start.5
  79.5 0.8 copy-start.6
  80.2 0.7 copy-start.8
  92.4 9.9 %collective-permute-start.16 = (bf16[4,128,256]{2,1,0:T(8,128)(2,1)S(1)}, bf16[4,128,256]{2,1,0:T(8,128)(2,1)S(1)}, u32[]{:S(2)}, u32[]{:S(2)}) collective-permute-start(bf16[4,128,256]{2,1,0:T(8,128)(2,1)S(1)} %copy-done.21), channel_id=1, source_target_pairs={{0,14},{1,15},{2,12},{3,13},{4,10},{5,11},{6,8},{7,9},{8,6},{9,7},... | collective-permute-start | bytes 786440 | tf_op jit(solution)/shard_map/ppermute | solution.py:435
  102.3 7.9 %collective-permute-start.19 = (bf16[1,4,2,1024]{3,2,1,0:T(2,128)(2,1)S(1)}, bf16[1,4,2,1024]{3,2,1,0:T(2,128)(2,1)S(1)}, u32[]{:S(2)}, u32[]{:S(2)}) collective-permute-start(bf16[1,4,2,1024]{3,2,1,0:T(2,128)(2,1)S(1)} %broadcast_in_dim_reshape.4), channel_id=1, source_target_pairs={{0,12},{1,13},{2,14},{3,15},{4,8},{5,9},{6,10},{7,11},{8,4},{9,5},... | collective-permute-start | bytes 49160 | tf_op jit(solution)/shard_map/ppermute | solution.py:435
  103.8 8.3 %collective-permute-start.18 = (bf16[1,4,2,1024]{3,2,1,0:T(2,128)(2,1)S(1)}, bf16[1,4,2,1024]{3,2,1,0:T(2,128)(2,1)S(1)}, u32[]{:S(2)}, u32[]{:S(2)}) collective-permute-start(bf16[1,4,2,1024]{3,2,1,0:T(2,128)(2,1)S(1)} %broadcast_in_dim_reshape.4), channel_id=1, source_target_pairs={{0,8},{1,9},{2,10},{3,11},{4,12},{5,13},{6,14},{7,15},{8,0},{9,1},... | collective-permute-start | bytes 49160 | tf_op jit(solution)/shard_map/ppermute | solution.py:435
  110.2 3.7 %collective-permute-start.17 = (bf16[1,4,2,1024]{3,2,1,0:T(2,128)(2,1)S(1)}, bf16[1,4,2,1024]{3,2,1,0:T(2,128)(2,1)S(1)}, u32[]{:S(2)}, u32[]{:S(2)}) collective-permute-start(bf16[1,4,2,1024]{3,2,1,0:T(2,128)(2,1)S(1)} %broadcast_in_dim_reshape.4), channel_id=1, source_target_pairs={{0,4},{1,5},{2,6},{3,7},{4,0},{5,1},{6,2},{7,3},{8,12},{9,13},{10,... | collective-permute-start | bytes 49160 | tf_op jit(solution)/shard_map/ppermute | solution.py:435
  114.1 4.3 %collective-permute-start.20 = (bf16[4,4,2,1024]{3,2,1,0:T(2,128)(2,1)S(1)}, bf16[4,4,2,1024]{3,2,1,0:T(2,128)(2,1)S(1)}, u32[]{:S(2)}, u32[]{:S(2)}) collective-permute-start(bf16[4,4,2,1024]{3,2,1,0:T(2,128)(2,1)S(1)} %pad_maximum_fusion.2), channel_id=1, source_target_pairs={{0,2},{1,3},{2,0},{3,1},{4,6},{5,7},{6,4},{7,5},{8,10},{9,11},{10,... | collective-permute-start | bytes 196616 | tf_op jit(solution)/shard_map/ppermute | solution.py:435
  118.5 3.5 %collective-permute-start.21 = (bf16[8,4,2,1024]{3,2,1,0:T(2,128)(2,1)S(1)}, bf16[8,4,2,1024]{3,2,1,0:T(2,128)(2,1)S(1)}, u32[]{:S(2)}, u32[]{:S(2)}) collective-permute-start(bf16[8,4,2,1024]{3,2,1,0:T(2,128)(2,1)S(1)} %get-tuple-element.77), channel_id=1, source_target_pairs={{0,1},{1,0},{2,3},{3,2},{4,5},{5,4},{6,7},{7,6},{8,9},{9,8},{10,11... | collective-permute-start | bytes 393224 | tf_op jit(solution)/shard_map/ppermute | solution.py:435
  118.6 11.6 %collective-permute-start.22 = (bf16[4,128,256]{2,1,0:T(8,128)(2,1)S(1)}, bf16[4,128,256]{2,1,0:T(8,128)(2,1)S(1)}, u32[]{:S(2)}, u32[]{:S(2)}) collective-permute-start(bf16[4,128,256]{2,1,0:T(8,128)(2,1)S(1)} %copy-done.17), channel_id=1, source_target_pairs={{0,14},{1,15},{2,12},{3,13},{4,10},{5,11},{6,8},{7,9},{8,6},{9,7},... | collective-permute-start | bytes 786440 | tf_op jit(solution)/shard_map/ppermute | solution.py:435
